TPU v7x, 32 devices: a whole 2x2x4 slice. The times are simulated.
32 devices in a mesh: dp: 8 (over y, x, core), tensor: 4 (over z).
Axes of the slice: x: 2, y: 2, z: 4, core: 2. Of those that a mesh axis runs over, the one named last changes fastest.
Arguments:
- text_input: bfloat16 [12288, 768], P('dp'), may hold values from -6 to 6
- layout_input: bfloat16 [12288, 192], P('dp'), may hold values from -6 to 6
- block_starts: int32 [24], P('dp'), may hold values from 0 to 1920
- intersection_flags: int32 [24, 512], P('dp'), may hold values from 0 to 1, as said below
- text_cotangent: bfloat16 [12288, 768], P(('dp', 'tensor')), may hold values from -6 to 6
- layout_cotangent: bfloat16 [12288, 192], P(('dp', 'tensor')), may hold values from -6 to 6
- text_project: bfloat16 [768, 2304], replicated, may hold values from -0.21875 to 0.21875
- text_biases: float32 [4, 768], replicated, may hold values from -4 to 4
- text_dense: bfloat16 [768, 768], replicated, may hold values from -1.75 to 1.75
- text_gains: float32 [2, 768], replicated, may hold values from 0.5 to 1.5
- text_shifts: float32 [2, 768], replicated, may hold values from -4 to 4
- text_widen: bfloat16 [768, 3072], P(None, 'tensor'), may hold values from -0.21875 to 0.21875
- text_hidden_bias: float32 [3072], P('tensor'), may hold values from -4 to 4
- text_narrow: bfloat16 [3072, 768], P('tensor'), may hold values from -0.109375 to 0.109375
- layout_project: bfloat16 [192, 576], replicated, may hold values from -0.4375 to 0.4375
- layout_biases: float32 [4, 192], replicated, may hold values from -4 to 4
- layout_dense: bfloat16 [192, 192], replicated, may hold values from -2.5 to 2.5
- layout_gains: float32 [2, 192], replicated, may hold values from 0.5 to 1.5
- layout_shifts: float32 [2, 192], replicated, may hold values from -4 to 4
- layout_widen: bfloat16 [192, 768], P(None, 'tensor'), may hold values from -0.4375 to 0.4375
- layout_hidden_bias: float32 [768], P('tensor'), may hold values from -4 to 4
- layout_narrow: bfloat16 [768, 192], P('tensor'), may hold values from -0.21875 to 0.21875
Outputs:
- text_result: bfloat16 [12288, 768], P(('dp', 'tensor'))
- layout_result: bfloat16 [12288, 192], P(('dp', 'tensor'))
- text_input_grad: float32 [12288, 768], P('dp')
- layout_input_grad: float32 [12288, 192], P('dp')
- grad_text_project: float32 [768, 2304], replicated
- grad_text_biases: float32 [4, 768], replicated
- grad_text_dense: float32 [768, 768], replicated
- grad_text_gains: float32 [2, 768], replicated
- grad_text_shifts: float32 [2, 768], replicated
- grad_text_widen: float32 [768, 3072], P(None, 'tensor')
- grad_text_hidden_bias: float32 [3072], P('tensor')
- grad_text_narrow: float32 [3072, 768], P('tensor')
- grad_layout_project: float32 [192, 576], replicated
- grad_layout_biases: float32 [4, 192], replicated
- grad_layout_dense: float32 [192, 192], replicated
- grad_layout_gains: float32 [2, 192], replicated
- grad_layout_shifts: float32 [2, 192], replicated
- grad_layout_widen: float32 [192, 768], P(None, 'tensor')
- grad_layout_hidden_bias: float32 [768], P('tensor')
- grad_layout_narrow: float32 [768, 192], P('tensor')
Inputs may be any that keep to these rules, and one draw needn't show every extreme that they name: `intersection_flags`: in every block the flagged rows form a leading run.
All inputs are finite; a program needn't handle non-finite values.
Results may differ from a plain program's by a relative error of at most 0.013.
The roundings to bfloat16 on the way count: a program that leaves them out, or rounds other values in their place, can miss the bound.
Values may be sent and summed in bfloat16 or wider, within the bound.
No kernel may reach another device: no remote copies, remote signals or barrier semaphores. Data moves between devices by JAX's collectives and lax.ppermute only.
A program may use at most 192 MiB of HBM per device.

v0:
```python
import math

import jax
import jax.numpy as jnp
from jax import lax
from jax.sharding import PartitionSpec as P

HEADS = 12
DOC = 2048


epsilon = 1e-05
masked_score = -1e30


def layer_norm(values, gain_row, shift_row):
    centre = values - jnp.mean(values, axis=-1, keepdims=True)
    spread = jnp.mean(centre * centre, axis=-1, keepdims=True)
    return centre * lax.rsqrt(spread + epsilon) * gain_row + shift_row


def gelu_exact(values):
    return jax.nn.gelu(values, approximate=False)


def joint_scores(text_query, text_key, layout_query, layout_key, valid_keys):
    text_scale = 1.0 / math.sqrt(text_query.shape[-1])
    layout_scale = 1.0 / math.sqrt(layout_query.shape[-1])
    joined = (
        jnp.einsum("qhd,khd->hqk", text_query, text_key, preferred_element_type=jnp.float32)
        * text_scale
    )
    joined = (
        joined
        + jnp.einsum("qhd,khd->hqk", layout_query, layout_key, preferred_element_type=jnp.float32)
        * layout_scale
    )
    return (jnp.where(valid_keys[None, None, :], joined, masked_score), text_scale, layout_scale)


def attend_forward(block_items):
    text_query, text_key, text_value, layout_query, layout_key, layout_value, valid_keys = (
        block_items
    )
    scores, text_scale, layout_scale = joint_scores(
        text_query, text_key, layout_query, layout_key, valid_keys
    )
    highest = jnp.max(scores, axis=-1, keepdims=True)
    exponent = jnp.exp(scores - highest)
    totals = jnp.sum(exponent, axis=-1, keepdims=True)
    rounded = (exponent / totals).astype(jnp.bfloat16)
    text_context = jnp.einsum(
        "hqk,khd->qhd", rounded, text_value, preferred_element_type=jnp.float32
    )
    layout_context = jnp.einsum(
        "hqk,khd->qhd", rounded, layout_value, preferred_element_type=jnp.float32
    )
    return (
        text_context.astype(jnp.bfloat16),
        layout_context.astype(jnp.bfloat16),
        (highest + jnp.log(totals))[..., 0],
    )


def attend_backward(block_items):
    (
        text_query,
        text_key,
        text_value,
        layout_query,
        layout_key,
        layout_value,
        valid_keys,
        log_total,
        text_dctx,
        layout_dctx,
    ) = block_items
    scores, text_scale, layout_scale = joint_scores(
        text_query, text_key, layout_query, layout_key, valid_keys
    )
    attention = jnp.exp(scores - log_total[..., None])
    rounded = attention.astype(jnp.bfloat16)
    dprobs = jnp.einsum("qhd,khd->hqk", text_dctx, text_value, preferred_element_type=jnp.float32)
    dprobs = dprobs + jnp.einsum(
        "qhd,khd->hqk", layout_dctx, layout_value, preferred_element_type=jnp.float32
    )
    row_inner = jnp.sum(attention * dprobs, axis=-1, keepdims=True)
    dscores = (attention * (dprobs - row_inner)).astype(jnp.bfloat16)
    text_dquery = (
        jnp.einsum("hqk,khd->qhd", dscores, text_key, preferred_element_type=jnp.float32)
        * text_scale
    )
    text_dkey = (
        jnp.einsum("hqk,qhd->khd", dscores, text_query, preferred_element_type=jnp.float32)
        * text_scale
    )
    text_dvalue = jnp.einsum("hqk,qhd->khd", rounded, text_dctx, preferred_element_type=jnp.float32)
    layout_dquery = (
        jnp.einsum("hqk,khd->qhd", dscores, layout_key, preferred_element_type=jnp.float32)
        * layout_scale
    )
    layout_dkey = (
        jnp.einsum("hqk,qhd->khd", dscores, layout_query, preferred_element_type=jnp.float32)
        * layout_scale
    )
    layout_dvalue = jnp.einsum(
        "hqk,qhd->khd", rounded, layout_dctx, preferred_element_type=jnp.float32
    )
    return (text_dquery, text_dkey, text_dvalue, layout_dquery, layout_dkey, layout_dvalue)


def stream_heads(source, project, biases, blocks, head_count):
    features = source.shape[1]
    joint_bias = jnp.concatenate([biases[0], jnp.zeros_like(biases[0]), biases[1]])
    projected = (jnp.dot(source, project, preferred_element_type=jnp.float32) + joint_bias).astype(
        jnp.bfloat16
    )
    return projected.reshape(blocks, -1, 3, head_count, features // head_count)


def stream_middle(source, context, dense, biases, gains, shifts, widen, hidden_bias, narrow):
    branch = jnp.dot(context, dense, preferred_element_type=jnp.float32) + biases[2]
    first_sum = source.astype(jnp.float32) + branch
    normed = layer_norm(first_sum, gains[0], shifts[0])
    normed_low = normed.astype(jnp.bfloat16)
    hidden = jnp.dot(normed_low, widen, preferred_element_type=jnp.float32) + hidden_bias
    active = gelu_exact(hidden).astype(jnp.bfloat16)
    partial_out = jnp.dot(active, narrow, preferred_element_type=jnp.float32)
    return (first_sum, normed, normed_low, hidden, active, partial_out)


def ffn_backward(upstream, active, hidden, normed_low, widen, narrow):
    grad_narrow = jnp.einsum("rf,rd->fd", active, upstream, preferred_element_type=jnp.float32)
    dactive = jnp.einsum("rd,fd->rf", upstream, narrow, preferred_element_type=jnp.float32)
    gelu_pull = jax.vjp(gelu_exact, hidden)[1]
    dhidden = gelu_pull(dactive)[0].astype(jnp.bfloat16)
    grad_widen = jnp.einsum("rd,rf->df", normed_low, dhidden, preferred_element_type=jnp.float32)
    grad_hidden = jnp.sum(dhidden, axis=0, dtype=jnp.float32)
    dnormed = jnp.einsum("rf,df->rd", dhidden, widen, preferred_element_type=jnp.float32)
    grad_out_bias = jnp.sum(upstream, axis=0, dtype=jnp.float32)
    return (grad_narrow, grad_widen, grad_hidden, dnormed, grad_out_bias)


def stream_dense_back(dfirst, context, dense):
    dbranch = dfirst.astype(jnp.bfloat16)
    grad_dense = jnp.einsum("rc,rd->cd", context, dbranch, preferred_element_type=jnp.float32)
    grad_branch = jnp.sum(dbranch, axis=0, dtype=jnp.float32)
    dcontext = jnp.einsum("rd,cd->rc", dbranch, dense, preferred_element_type=jnp.float32).astype(
        jnp.bfloat16
    )
    return (grad_dense, grad_branch, dcontext)


def stream_input_back(source, project, dfirst, dquery, dkey, dvalue, total_rows):
    features = source.shape[1]
    dprojected = jnp.concatenate(
        [
            dquery.reshape(total_rows, features),
            dkey.reshape(total_rows, features),
            dvalue.reshape(total_rows, features),
        ],
        axis=1,
    ).astype(jnp.bfloat16)
    grad_project = jnp.einsum("rw,rv->wv", source, dprojected, preferred_element_type=jnp.float32)
    grad_query_bias = jnp.sum(dprojected[:, :features], axis=0, dtype=jnp.float32)
    grad_value_bias = jnp.sum(dprojected[:, 2 * features :], axis=0, dtype=jnp.float32)
    input_grad = dfirst + jnp.einsum(
        "rv,wv->rw", dprojected, project, preferred_element_type=jnp.float32
    )
    return (grad_project, grad_query_bias, grad_value_bias, input_grad)


def per_device(
    text_input,
    layout_input,
    block_starts,
    intersection_flags,
    text_cotangent,
    layout_cotangent,
    text_project,
    text_biases,
    text_dense,
    text_gains,
    text_shifts,
    text_widen,
    text_hidden_bias,
    text_narrow,
    layout_project,
    layout_biases,
    layout_dense,
    layout_gains,
    layout_shifts,
    layout_widen,
    layout_hidden_bias,
    layout_narrow,
):
    blocks, length = intersection_flags.shape
    total_rows = blocks * length
    groups = lax.axis_size("tensor")
    share = total_rows // groups
    offset = lax.axis_index("tensor") * share
    position = jnp.arange(length, dtype=jnp.int32)
    valid_keys = block_starts[:, None] + position[None, :] < DOC
    kept_rows = jnp.logical_and(valid_keys, intersection_flags == 0).reshape(total_rows)
    kept_share = lax.dynamic_slice_in_dim(kept_rows, offset, share, 0).astype(jnp.float32)
    text_heads = stream_heads(text_input, text_project, text_biases, blocks, HEADS)
    layout_heads = stream_heads(layout_input, layout_project, layout_biases, blocks, HEADS)
    head_items = (
        text_heads[:, :, 0],
        text_heads[:, :, 1],
        text_heads[:, :, 2],
        layout_heads[:, :, 0],
        layout_heads[:, :, 1],
        layout_heads[:, :, 2],
        valid_keys,
    )
    text_ctx, layout_ctx, log_total = lax.map(attend_forward, head_items)
    text_context = text_ctx.reshape(total_rows, -1)
    layout_context = layout_ctx.reshape(total_rows, -1)
    text_first, text_normed, text_low, text_hidden, text_active, text_partial = stream_middle(
        text_input,
        text_context,
        text_dense,
        text_biases,
        text_gains,
        text_shifts,
        text_widen,
        text_hidden_bias,
        text_narrow,
    )
    layout_first, layout_normed, layout_low, layout_hidden, layout_active, layout_partial = (
        stream_middle(
            layout_input,
            layout_context,
            layout_dense,
            layout_biases,
            layout_gains,
            layout_shifts,
            layout_widen,
            layout_hidden_bias,
            layout_narrow,
        )
    )
    text_sum, layout_sum = (
        lax.psum_scatter(text_partial, "tensor", scatter_dimension=0, tiled=True),
        lax.psum_scatter(layout_partial, "tensor", scatter_dimension=0, tiled=True),
    )
    text_second = (
        lax.dynamic_slice_in_dim(text_normed, offset, share, 0) + text_sum + text_biases[3]
    )
    layout_second = (
        lax.dynamic_slice_in_dim(layout_normed, offset, share, 0) + layout_sum + layout_biases[3]
    )
    text_result = layer_norm(text_second, text_gains[1], text_shifts[1]).astype(jnp.bfloat16)
    layout_result = layer_norm(layout_second, layout_gains[1], layout_shifts[1]).astype(
        jnp.bfloat16
    )
    text_upstream = text_cotangent.astype(jnp.float32) * kept_share[:, None]
    layout_upstream = layout_cotangent.astype(jnp.float32) * kept_share[:, None]
    text_pull_two = jax.vjp(layer_norm, text_second, text_gains[1], text_shifts[1])[1]
    text_dsecond, text_gain_two, text_shift_two = text_pull_two(text_upstream)
    layout_pull_two = jax.vjp(layer_norm, layout_second, layout_gains[1], layout_shifts[1])[1]
    layout_dsecond, layout_gain_two, layout_shift_two = layout_pull_two(layout_upstream)
    text_dfull, layout_dfull = (
        lax.all_gather(text_dsecond.astype(jnp.bfloat16), "tensor", axis=0, tiled=True),
        lax.all_gather(layout_dsecond.astype(jnp.bfloat16), "tensor", axis=0, tiled=True),
    )
    text_gnarrow, text_gwiden, text_ghidden, text_dnormed, text_gout = ffn_backward(
        text_dfull, text_active, text_hidden, text_low, text_widen, text_narrow
    )
    layout_gnarrow, layout_gwiden, layout_ghidden, layout_dnormed, layout_gout = ffn_backward(
        layout_dfull, layout_active, layout_hidden, layout_low, layout_widen, layout_narrow
    )
    text_dpart, layout_dpart = (
        lax.psum_scatter(text_dnormed, "tensor", scatter_dimension=0, tiled=True),
        lax.psum_scatter(layout_dnormed, "tensor", scatter_dimension=0, tiled=True),
    )
    text_norm_two = jnp.stack([text_gain_two, text_shift_two])
    layout_norm_two = jnp.stack([layout_gain_two, layout_shift_two])
    text_dall, layout_dall, text_norm_all, layout_norm_all = (
        lax.all_gather(text_dsecond + text_dpart, "tensor", axis=0, tiled=True),
        lax.all_gather(layout_dsecond + layout_dpart, "tensor", axis=0, tiled=True),
        lax.all_gather(text_norm_two, "tensor", axis=0, tiled=True),
        lax.all_gather(layout_norm_two, "tensor", axis=0, tiled=True),
    )
    text_norm_sum = jnp.sum(text_norm_all.reshape(groups, 2, -1), axis=0)
    layout_norm_sum = jnp.sum(layout_norm_all.reshape(groups, 2, -1), axis=0)
    text_pull_one = jax.vjp(layer_norm, text_first, text_gains[0], text_shifts[0])[1]
    text_dfirst, text_gain_one, text_shift_one = text_pull_one(text_dall)
    layout_pull_one = jax.vjp(layer_norm, layout_first, layout_gains[0], layout_shifts[0])[1]
    layout_dfirst, layout_gain_one, layout_shift_one = layout_pull_one(layout_dall)
    text_gdense, text_gbranch, text_dcontext = stream_dense_back(
        text_dfirst, text_context, text_dense
    )
    layout_gdense, layout_gbranch, layout_dcontext = stream_dense_back(
        layout_dfirst, layout_context, layout_dense
    )
    back_items = head_items + (
        log_total,
        text_dcontext.reshape(text_ctx.shape),
        layout_dcontext.reshape(layout_ctx.shape),
    )
    text_dq, text_dk, text_dv, layout_dq, layout_dk, layout_dv = lax.map(
        attend_backward, back_items
    )
    text_gproject, text_gquery, text_gvalue, text_input_grad = stream_input_back(
        text_input, text_project, text_dfirst, text_dq, text_dk, text_dv, total_rows
    )
    layout_gproject, layout_gquery, layout_gvalue, layout_input_grad = stream_input_back(
        layout_input, layout_project, layout_dfirst, layout_dq, layout_dk, layout_dv, total_rows
    )
    text_gbiases = jnp.stack([text_gquery, text_gvalue, text_gbranch, text_gout])
    layout_gbiases = jnp.stack([layout_gquery, layout_gvalue, layout_gbranch, layout_gout])
    text_ggains = jnp.stack([text_gain_one, text_norm_sum[0]])
    text_gshifts = jnp.stack([text_shift_one, text_norm_sum[1]])
    layout_ggains = jnp.stack([layout_gain_one, layout_norm_sum[0]])
    layout_gshifts = jnp.stack([layout_shift_one, layout_norm_sum[1]])
    (
        text_gproject,
        text_gbiases,
        text_gdense,
        text_ggains,
        text_gshifts,
        text_gwiden,
        text_ghidden,
        text_gnarrow,
        layout_gproject,
        layout_gbiases,
        layout_gdense,
        layout_ggains,
        layout_gshifts,
        layout_gwiden,
        layout_ghidden,
        layout_gnarrow,
    ) = lax.psum(
        (
            text_gproject,
            text_gbiases,
            text_gdense,
            text_ggains,
            text_gshifts,
            text_gwiden,
            text_ghidden,
            text_gnarrow,
            layout_gproject,
            layout_gbiases,
            layout_gdense,
            layout_ggains,
            layout_gshifts,
            layout_gwiden,
            layout_ghidden,
            layout_gnarrow,
        ),
        "dp",
    )
    return (
        text_result,
        layout_result,
        text_input_grad,
        layout_input_grad,
        text_gproject,
        text_gbiases,
        text_gdense,
        text_ggains,
        text_gshifts,
        text_gwiden,
        text_ghidden,
        text_gnarrow,
        layout_gproject,
        layout_gbiases,
        layout_gdense,
        layout_ggains,
        layout_gshifts,
        layout_gwiden,
        layout_ghidden,
        layout_gnarrow,
    )


def solution(mesh):
    placed = (
        P("dp", None),
        P("dp", None),
        P("dp"),
        P("dp", None),
        P(("dp", "tensor"), None),
        P(("dp", "tensor"), None),
        P(),
        P(),
        P(),
        P(),
        P(),
        P(None, "tensor"),
        P("tensor"),
        P("tensor", None),
        P(),
        P(),
        P(),
        P(),
        P(),
        P(None, "tensor"),
        P("tensor"),
        P("tensor", None),
    )
    return jax.shard_map(
        per_device,
        mesh=mesh,
        in_specs=placed,
        out_specs=(
            P(("dp", "tensor"), None),
            P(("dp", "tensor"), None),
            P("dp", None),
            P("dp", None),
            P(),
            P(),
            P(),
            P(),
            P(),
            P(None, "tensor"),
            P("tensor"),
            P("tensor", None),
            P(),
            P(),
            P(),
            P(),
            P(),
            P(None, "tensor"),
            P("tensor"),
            P("tensor", None),
        ),
        check_vma=False,
    )
```

profile of v0, /device:TPU:9, one launch (start us, length us, event | category | flops | bytes accessed | tf_op | source)
XLA Modules:
  0.0 1067.3 jit_solution(6313889922349163424)
XLA Ops:
  13.3 5.2 reshape.264
  24.0 4.3 copy.114
  28.3 9.2 add_convert_fusion
  37.4 10.3 copy.115
  47.7 17.2 %reshape.263 = bf16[3,512,3,12,64]{1,0,4,3,2:T(4,128)(2,1)} reshape(bf16[1536,2304]{0,1:T(8,128)(2,1)} %copy.115) | data formatting | bytes 14155776 | tf_op jit(solution)/shard_map/reshape | solution.py:118
  64.9 6.4 slice_bitcast_fusion
  78.2 80.3 %while.34 = (s32[]{:T(128)}, bf16[3,512,12,64]{1,3,2,0:T(8,128)(2,1)}, bf16[3,512,12,16]{1,3,2,0:T(8,128)(2,1)}, f32[3,12,512]{2,1,0:T(8,128)}, bf16[3,512,12,64...) while((s32[]{:T(128)}, ...), condition=%wide.region_3.4_spmd, body=%wide.region_0.3_spmd.sunk | while | flops 1038575616 | bytes 109524728 | solution.py:217
  78.3 7.7 fusion.220
  86.1 8.2 fusion.221
  105.0 7.7 fusion.220
  112.7 8.2 fusion.221
  131.6 7.7 fusion.220
  139.4 8.2 fusion.221
  158.4 3.7 copy.122
  170.6 13.7 %multiply_convert_fusion.1 = (bf16[1536,768]{1,0:T(8,128)(2,1)S(1)}, f32[1536,768]{1,0:T(8,128)}, f32[1536,768]{1,0:T(8,128)}) fusion(f32[768]{0:T(1024)S(1)} %copy-done.111, bf16[768,768]{1,0:T(8,128)(2,1)S(1)} %copy-done.107, f32[1536,768]{0,1:T(8,128)S(1)} %multiply_add_fusion), kind=kOutput, calls=%fused_computation.103 | convolution fusion | flops 1890975744 | bytes 17697792 | tf_op jit(solution)/shard_map/dot_general | solution.py:126
  185.7 4.3 fusion.122
  194.9 4.0 multiply_convert_fusion.2
  204.7 72.0 %reduce-scatter.5.cloned.1.call-done = f32[384,768]{0,1:T(8,128)} async-done(((f32[1536,768]{0,1:T(8,128)}), f32[384,768]{0,1:T(8,128)}) %reduce-scatter.5.cloned.1.call-update) | async-done | bytes 1179664 | tf_op jit(solution)/shard_map/reduce_scatter | solution.py:245
  283.0 23.7 %reduce-scatter.7.cloned.1.call-done = f32[384,192]{0,1:T(8,128)} async-done(((f32[1536,192]{0,1:T(8,128)}), f32[384,192]{0,1:T(8,128)}) %reduce-scatter.7.cloned.1.call-update) | async-done | bytes 294928 | tf_op jit(solution)/shard_map/reduce_scatter | solution.py:246
  311.9 20.6 %all_gather.20 = bf16[1536,192]{0,1:T(8,128)(2,1)S(1)} all-gather(bf16[384,192]{0,1:T(8,128)(2,1)S(1)} %add_convert_fusion.9), channel_id=1, replica_groups=mesh['dp'=8,'tensor'=4] {'tensor'}, dimensions={0}, use_global_device_ids=true | all-gather | bytes 737280 | tf_op jit(solution)/shard_map/all_gather | solution.py:266
  336.6 28.6 %all-gather.6.cloned.1.call-done = bf16[1536,768]{0,1:T(8,128)(2,1)} async-done(((bf16[384,768]{0,1:T(8,128)(2,1)}), bf16[1536,768]{0,1:T(8,128)(2,1)}) %all-gather.6.cloned.1.call-update) | async-done | bytes 2359312 | tf_op jit(solution)/shard_map/all_gather | solution.py:265
  365.1 9.2 convert_reduce_fusion
  375.8 4.2 fusion.124
  380.0 14.9 %reduce-scatter.11.cloned.1.call-done = f32[384,192]{0,1:T(8,128)} async-done(((f32[1536,192]{0,1:T(8,128)}), f32[384,192]{0,1:T(8,128)}) %reduce-scatter.11.cloned.1.call-update) | async-done | bytes 294928 | tf_op jit(solution)/shard_map/reduce_scatter | solution.py:276
  397.1 86.6 %reduce-scatter.9.cloned.1.call-done = f32[384,768]{0,1:T(8,128)} async-done(((f32[1536,768]{0,1:T(8,128)}), f32[384,768]{0,1:T(8,128)}) %reduce-scatter.9.cloned.1.call-update) | async-done | bytes 1179664 | tf_op jit(solution)/shard_map/reduce_scatter | solution.py:275
  483.7 3.6 add_add_fusion.6
  492.2 23.8 %all-gather.10.cloned.1.call-done = f32[1536,192]{0,1:T(8,128)} async-done(((f32[384,192]{0,1:T(8,128)}), f32[1536,192]{0,1:T(8,128)}) %all-gather.10.cloned.1.call-update) | async-done | bytes 1179664 | tf_op jit(solution)/shard_map/all_gather | solution.py:282
  529.7 6.0 fusion.126
  535.7 3.4 fusion.93
  539.1 65.7 %all-gather.8.cloned.1.call-done = f32[1536,768]{0,1:T(8,128)} async-done(((f32[384,768]{0,1:T(8,128)}), f32[1536,768]{0,1:T(8,128)}) %all-gather.8.cloned.1.call-update) | async-done | bytes 4718608 | tf_op jit(solution)/shard_map/all_gather | solution.py:281
  604.8 5.4 multiply_reduce_fusion.1
  610.2 3.6 fusion.109
  617.2 3.4 fusion.125
  620.7 3.5 convolution_convert_fusion.2
  624.1 8.2 reshape.292
  632.3 7.3 copy.132
  639.6 165.8 %while.35 = (s32[]{:T(128)}, bf16[3,512,12,64]{1,3,2,0:T(8,128)(2,1)}, bf16[3,512,12,64]{1,3,2,0:T(8,128)(2,1)}, bf16[3,512,12,64]{1,3,2,0:T(8,128)(2,1)}, bf16[...) while((s32[]{:T(128)}, ...), condition=%wide.region_26.27_spmd, body=%wide.region_24.26_spmd.sunk | while | flops 2558453760 | bytes 234696672 | solution.py:303
  644.0 7.4 convolution_add_fusion.5
  651.4 7.8 fusion.244
  659.2 10.9 %multiply_reduce_fusion.14 = (f32[12,512]{1,0:T(8,128)S(1)}, f32[12,512,512]{1,2,0:T(8,128)S(1)}) fusion(f32[12,512,512]{1,2,0:T(8,128)} %convolution_add_fusion.5, f32[12,512]{1,0:T(8,128)S(1)} %dynamic-slice_bitcast_fusion.2, bf16[3,512,12,16]{1,3,2,0:T(8,128)(2,1)S(1)} %copy-done.6, s32[]{:T(128)S(6)} %copy.195, ...), kind=kOutput, calls=%fused_computation.30.clone.1 | convolution fusion | flops 122677248 | bytes 38200832 | tf_op jit(solution)/shard_map/while/body/eval_jaxpr/qhd,khd->hqk/dot_general | solution.py:35
  670.1 6.9 multiply_convert_fusion.4
  683.2 3.4 bitcast_dynamic-update-slice_fusion.11
  686.7 4.8 bitcast_dynamic-update-slice_fusion.10
  699.1 7.4 convolution_add_fusion.5
  706.5 7.8 fusion.244
  714.3 10.9 %multiply_reduce_fusion.14 = (f32[12,512]{1,0:T(8,128)S(1)}, f32[12,512,512]{1,2,0:T(8,128)S(1)}) fusion(f32[12,512,512]{1,2,0:T(8,128)} %convolution_add_fusion.5, f32[12,512]{1,0:T(8,128)S(1)} %dynamic-slice_bitcast_fusion.2, bf16[3,512,12,16]{1,3,2,0:T(8,128)(2,1)S(1)} %copy-done.6, s32[]{:T(128)S(6)} %copy.195, ...), kind=kOutput, calls=%fused_computation.30.clone.1 | convolution fusion | flops 122677248 | bytes 38200832 | tf_op jit(solution)/shard_map/while/body/eval_jaxpr/qhd,khd->hqk/dot_general | solution.py:35
  725.2 6.9 multiply_convert_fusion.4
  738.3 3.4 bitcast_dynamic-update-slice_fusion.11
  741.8 4.7 bitcast_dynamic-update-slice_fusion.10
  754.2 7.4 convolution_add_fusion.5
  761.6 7.8 fusion.244
  769.4 10.9 %multiply_reduce_fusion.14 = (f32[12,512]{1,0:T(8,128)S(1)}, f32[12,512,512]{1,2,0:T(8,128)S(1)}) fusion(f32[12,512,512]{1,2,0:T(8,128)} %convolution_add_fusion.5, f32[12,512]{1,0:T(8,128)S(1)} %dynamic-slice_bitcast_fusion.2, bf16[3,512,12,16]{1,3,2,0:T(8,128)(2,1)S(1)} %copy-done.6, s32[]{:T(128)S(6)} %copy.195, ...), kind=kOutput, calls=%fused_computation.30.clone.1 | convolution fusion | flops 122677248 | bytes 38200832 | tf_op jit(solution)/shard_map/while/body/eval_jaxpr/qhd,khd->hqk/dot_general | solution.py:35
  780.3 6.9 multiply_convert_fusion.4
  793.4 3.4 bitcast_dynamic-update-slice_fusion.11
  796.9 4.8 bitcast_dynamic-update-slice_fusion.10
  828.1 7.7 convolution_bitcast_fusion
  836.4 10.0 all-gather.1
  850.9 10.1 all-gather
  873.0 11.4 %add_add_fusion.2 = f32[1536,768]{0,1:T(8,128)} fusion(f32[1536,768]{0,1:T(8,128)} %copy-done.11, bf16[768,2304]{1,0:T(8,128)(2,1)S(1)} %copy-done, bf16[1536,2304]{0,1:T(8,128)(2,1)} %copy-done.41, f32[1536]{0:T(1024)S(1)} %copy-done.83), kind=kOutput, calls=%fused_computation.120 | convolution fusion | flops 5438177280 | bytes 20060160 | tf_op jit(solution)/shard_map/rv,wv->rw/dot_general | solution.py:167
  884.4 6.1 copy.144
  897.0 27.8 %all-reduce = (f32[4,768]{1,0:T(4,128)}, f32[2,768]{1,0:T(2,128)}, f32[2,768]{1,0:T(2,128)}, f32[768]{0:T(1024)}, f32[4,192]{1,0:T(4,128)}, /*index=5*/f32[2,192]{1,0:T(2,128)}, f32[2,192]{1,0:T(2,128)}, f32[192]{0:T(256)}) all-reduce(f32[4,768]{1,0:T(4,128)} %pad_maximum_fusion.1, ...), channel_id=1, replica_groups=mesh['dp'=8,'tensor'=4] {'dp'}, use_global_device_ids=true, to_apply=%region_32.33 | all-reduce | flops 8640 | bytes 69120 | tf_op jit(solution)/shard_map/psum | solution.py:335
  924.9 3.5 convolution_add_fusion.3
  928.4 113.8 %all-reduce.4.cloned.1.call-done = (f32[768,2304]{0,1:T(8,128)}, f32[768,768]{1,0:T(8,128)}, f32[768,768]{1,0:T(8,128)}, f32[768,768]{1,0:T(8,128)}, f32[192,576...) async-done(((f32[768,2304]{0,1:T(8,128)}, f32[768,768]{1,0:T(8,128)}, f32[768,768]{1,0:T(8,128)}, f32[768,768]{1,0:T(8,128)}, ...) | async-done | bytes 15040528 | tf_op jit(solution)/shard_map/psum | solution.py:335
  1042.2 8.0 copy.145
  (479 shorter events, 208.8 us)
Async XLA Ops:
  7.2 21.1 %copy-start = (bf16[768,2304]{1,0:T(8,128)(2,1)S(1)}, bf16[768,2304]{1,0:T(8,128)(2,1)}, u32[]{:S(2)}) copy-start(bf16[768,2304]{1,0:T(8,128)(2,1)} %param.32) | copy-start | bytes 10616836
  7.2 269.5 %reduce-scatter.5.cloned.1.call-start = ((), (), s32[]{:S(2)}) async-start(), calls=%async_computation.4 | async-start | bytes 5898240 | tf_op jit(solution)/shard_map/reduce_scatter | solution.py:245
  163.0 4.2 copy-start.30
  170.6 13.7 %copy-start.15 = (f32[1536,768]{0,1:T(8,128)}, f32[1536,768]{0,1:T(8,128)S(1)}, u32[]{:S(2)}) copy-start(f32[1536,768]{0,1:T(8,128)S(1)} %multiply_add_fusion) | copy-start | bytes 14155780
  170.6 15.1 %copy-start.106 = (bf16[768,768]{1,0:T(8,128)(2,1)S(1)}, bf16[768,768]{1,0:T(8,128)(2,1)}, u32[]{:S(2)}) copy-start(bf16[768,768]{1,0:T(8,128)(2,1)} %param.39) | copy-start | bytes 3538948
  190.1 116.6 %reduce-scatter.7.cloned.1.call-start = ((), (), s32[]{:S(2)}) async-start(), calls=%async_computation.5 | async-start | bytes 1474560 | tf_op jit(solution)/shard_map/reduce_scatter | solution.py:246
  192.7 6.2 copy-start.2
  194.9 4.0 copy-start.16
  194.9 4.8 copy-start.64
  201.1 164.0 %all-gather.6.cloned.1.call-start = ((), (), s32[]{:S(2)}) async-start(), calls=%async_computation.6 | async-start | bytes 2949120 | tf_op jit(solution)/shard_map/all_gather | solution.py:265
  283.0 112.0 %reduce-scatter.11.cloned.1.call-start = ((), (), s32[]{:S(2)}) async-start(), calls=%async_computation.9 | async-start | bytes 1474560 | tf_op jit(solution)/shard_map/reduce_scatter | solution.py:276
  306.7 25.9 %copy-start.65 = (bf16[192,192]{1,0:T(8,128)(2,1)S(1)}, bf16[192,192]{1,0:T(8,128)(2,1)}, u32[]{:S(2)}) copy-start(bf16[192,192]{1,0:T(8,128)(2,1)} %param.47) | copy-start | bytes 221188
  306.7 25.9 %copy-start.113 = (f32[1536,192]{0,1:T(8,128)S(1)}, f32[1536,192]{0,1:T(8,128)}, u32[]{:S(2)}) copy-start(f32[1536,192]{0,1:T(8,128)} %get-tuple-element.424) | copy-start | bytes 3538948
  306.7 25.9 %copy-start.114 = (f32[1536,192]{0,1:T(8,128)S(1)}, f32[1536,192]{0,1:T(8,128)}, u32[]{:S(2)}) copy-start(f32[1536,192]{0,1:T(8,128)} %get-tuple-element.466) | copy-start | bytes 3538948
  308.0 24.5 %copy-start.76 = (f32[384]{0:T(512)}, f32[384]{0:T(512)S(1)}, u32[]{:S(2)}) copy-start(f32[384]{0:T(512)S(1)} %broadcast_multiply_fusion.2) | copy-start | bytes 4612
  309.2 23.4 %copy-start.78 = (f32[384]{0:T(512)}, f32[384]{0:T(512)S(1)}, u32[]{:S(2)}) copy-start(f32[384]{0:T(512)S(1)} %get-tuple-element.451) | copy-start | bytes 4612
  309.2 23.4 %copy-start.79 = (f32[384]{0:T(512)}, f32[384]{0:T(512)S(1)}, u32[]{:S(2)}) copy-start(f32[384]{0:T(512)S(1)} %get-tuple-element.452) | copy-start | bytes 4612
  310.9 21.7 %copy-start.84 = (f32[384]{0:T(512)}, f32[384]{0:T(512)S(1)}, u32[]{:S(2)}) copy-start(f32[384]{0:T(512)S(1)} %negate_multiply_fusion.4) | copy-start | bytes 4612
  336.1 147.7 %reduce-scatter.9.cloned.1.call-start = ((), (), s32[]{:S(2)}) async-start(), calls=%async_computation.7 | async-start | bytes 5898240 | tf_op jit(solution)/shard_map/reduce_scatter | solution.py:275
  365.1 10.6 copy-start.108
  380.0 136.0 %all-gather.10.cloned.1.call-start = ((), (), s32[]{:S(2)}) async-start(), calls=%async_computation.10 | async-start | bytes 1474560 | tf_op jit(solution)/shard_map/all_gather | solution.py:282
  397.1 207.7 %all-gather.8.cloned.1.call-start = ((), (), s32[]{:S(2)}) async-start(), calls=%async_computation.8 | async-start | bytes 5898240 | tf_op jit(solution)/shard_map/all_gather | solution.py:281
  487.4 28.6 %copy-start.92 = (f32[1,192]{1,0:T(1,128)S(1)}, f32[1,192]{1,0:T(1,128)}, u32[]{:S(2)}) copy-start(f32[1,192]{1,0:T(1,128)} %copy-done.91) | copy-start | bytes 2308
  487.4 554.8 %all-reduce.4.cloned.1.call-start = ((), (), s32[]{:S(2)}) async-start(), calls=%async_computation.11 | async-start | bytes 30474240 | tf_op jit(solution)/shard_map/psum | solution.py:335
  525.1 10.6 slice-start
  529.7 6.0 slice-start.1
  529.7 6.0 copy-start.116
  535.7 69.1 %copy-start.55 = (f32[1536]{0:T(1024)S(1)}, f32[1536]{0:T(1024)}, u32[]{:S(2)}) copy-start(f32[1536]{0:T(1024)} %copy-done.54) | copy-start | bytes 18436
  535.7 69.1 %copy-start.75 = (f32[768]{0:T(1024)S(1)}, f32[768]{0:T(1024)}, u32[]{:S(2)}) copy-start(f32[768]{0:T(1024)} %copy-done.74) | copy-start | bytes 9220
  604.8 5.4 copy-start.71
  604.8 5.4 copy-start.10
  604.8 5.4 copy-start.62
  617.2 3.4 copy-start.110
  651.4 7.8 copy-start.5
  651.4 7.8 copy-start.6
  670.1 6.9 copy-start.46
  683.2 3.4 copy-start.45
  686.6 4.8 copy-start.33
  686.7 4.8 copy-start.36
  706.5 7.8 copy-start.5
  706.5 7.8 copy-start.6
  725.2 6.9 copy-start.46
  738.3 3.4 copy-start.45
  741.8 4.8 copy-start.33
  741.8 4.8 copy-start.36
  761.6 7.8 copy-start.5
  761.6 7.8 copy-start.6
  780.3 6.9 copy-start.46
  793.4 3.4 copy-start.45
  796.8 4.8 copy-start.33
  796.8 4.8 copy-start.36
  816.1 7.4 copy-start.7
  835.8 15.0 %copy-start.87 = (f32[768]{0:T(1024)S(1)}, f32[768]{0:T(1024)}, u32[]{:S(2)}) copy-start(f32[768]{0:T(1024)} %get-tuple-element.318) | copy-start | bytes 9220
  835.8 15.0 %copy-start.86 = (f32[768]{0:T(1024)S(1)}, f32[768]{0:T(1024)}, u32[]{:S(2)}) copy-start(f32[768]{0:T(1024)} %get-tuple-element.323) | copy-start | bytes 9220
  850.8 16.9 %copy-start.88 = (f32[768]{0:T(1024)S(1)}, f32[768]{0:T(1024)}, u32[]{:S(2)}) copy-start(f32[768]{0:T(1024)} %get-tuple-element.315) | copy-start | bytes 9220
  850.9 16.3 %copy-start.89 = (f32[768]{0:T(1024)S(1)}, f32[768]{0:T(1024)}, u32[]{:S(2)}) copy-start(f32[768]{0:T(1024)} %get-tuple-element.313) | copy-start | bytes 9220
  862.4 6.0 copy-start.90
  867.2 4.9 copy-start.9
  868.9 4.0 copy-start.83
  884.4 8.6 copy-start.99
  884.4 8.6 copy-start.101
  884.4 40.4 %copy-start.69 = (f32[1536]{0:T(1024)S(1)}, f32[1536]{0:T(1024)}, u32[]{:S(2)}) copy-start(f32[1536]{0:T(1024)} %copy-done.68) | copy-start | bytes 18436
  1050.1 3.4 copy-start.26
  1056.0 3.6 copy-start.56
  (92 other events, 172.5 us)
Sparse Core Ops, SparseCore 0:
  190.2 86.4 reduce-scatter.4
  279.0 27.6 reduce-scatter.6
  308.3 56.7 all-gather.5
  367.9 27.0 reduce-scatter.10
  397.7 85.9 reduce-scatter.8
  485.7 30.1 all-gather.9
  518.1 86.6 all-gather.7
  836.0 206.1 all-reduce.3
where the time goes:
time: 1080 us; the launch traced here: 1070 us
  waiting for transfers between devices  429 us (40%)
  matrix products  302 us (28%)
  local copies, waits for them, and re-layouts  165 us (15%)
  other arithmetic  83.9 us (8%)
  blocking collectives  68.6 us (6%)
  between operations  15.6 us (1%)
    psum x1, waiting for transfers between devices, per_device(): lax.psum((text_gproject, text_gbiases, text_gdense, text_ggains, text_gsh...  114 us
    reduce_scatter x1, waiting for transfers between devices, per_device(): lax.psum_scatter(text_dnormed, 'tensor', scatter_dimension=0, tiled=True)  86.6 us
    reduce_scatter x1, waiting for transfers between devices, per_device(): lax.psum_scatter(text_partial, 'tensor', scatter_dimension=0, tiled=True)  72 us
    all_gather x1, waiting for transfers between devices, per_device(): lax.all_gather(text_dsecond + text_dpart, 'tensor', axis=0, tiled=True)  65.7 us
    unnamed x236, local copies, waits for them, and re-layouts  57.6 us
    dot_general x6, matrix products, joint_scores(): jnp.einsum('qhd,khd->hqk', layout_query, layout_key, preferred_element_ty...  57.4 us
    dot_general x6, matrix products, joint_scores(): jnp.einsum('qhd,khd->hqk', text_query, text_key, preferred_element_type=j...  46.6 us
    all_gather x1, waiting for transfers between devices, per_device(): lax.all_gather(text_dsecond.astype(jnp.bfloat16), 'tensor', axis=0, tiled...  28.6 us
  transfers between devices with their start and end apart: 8, of which 8 were waited for; matrix products, arithmetic and copies ran while one was open for 11% of the time, Pallas kernels for 0%

commit v1 on v0

v1 whole, which is shorter than its diff:
```python
import functools
import math

import jax
import jax.numpy as jnp
from jax import lax
from jax.experimental import pallas as pl
from jax.experimental.pallas import tpu as pltpu
from jax.sharding import PartitionSpec as P

HEADS = 12
DOC = 2048
LANES = 128
epsilon = 1e-05
masked_score = -1e30
F32 = jnp.float32
BF = jnp.bfloat16

OWN, WINDOW, SHIFT, LOCAL, LIMIT, FLAGGED, PLACE = 0, 1, 2, 3, 6, 9, 12
SCALARS = 16


def nn(a, b):
    return lax.dot_general(a, b, (((1,), (0,)), ((), ())), preferred_element_type=F32)


def nt(a, b):
    return lax.dot_general(a, b, (((1,), (1,)), ((), ())), preferred_element_type=F32)


def tn(a, b):
    return lax.dot_general(a, b, (((0,), (0,)), ((), ())), preferred_element_type=F32)


def mean(values):
    return jnp.mean(values, axis=-1, keepdims=True)


def column_sum(values):
    return jnp.sum(values.astype(F32), axis=0, keepdims=True)


def normalised(values):
    centre = values - mean(values)
    scale = lax.rsqrt(mean(centre * centre) + epsilon)
    return centre * scale, scale


def norm_back(upstream, normal, scale, gain_row):
    u = upstream * gain_row
    return scale * (u - mean(u) - normal * mean(u * normal))


def lanes_of(start):
    return pl.ds(pl.multiple_of(start, LANES), LANES)


def head_masks(pair, text_scale, layout_scale):
    lane = lax.broadcasted_iota(jnp.int32, (1, LANES), 1)
    first = 32 * pair - LANES * (pair // 4)
    text_a = jnp.where(lane < 64, text_scale, 0.0)
    text_b = jnp.where(lane < 64, 0.0, text_scale)
    layout_a = jnp.where((lane >= first) & (lane < first + 16), layout_scale, 0.0)
    layout_b = jnp.where((lane >= first + 16) & (lane < first + 32), layout_scale, 0.0)
    return text_a, layout_a, text_b, layout_b


def stack_heads(text, layout, masks):
    text_a, layout_a, text_b, layout_b = (m.astype(BF) for m in masks)
    upper = jnp.concatenate([text * text_a, layout * layout_a], axis=1)
    lower = jnp.concatenate([text * text_b, layout * layout_b], axis=1)
    return jnp.concatenate([upper, lower], axis=0)


def unstack_heads(stacked, masks):
    text_a, layout_a, text_b, layout_b = masks
    upper, lower = stacked[:LANES], stacked[LANES:]
    text = upper[:, :LANES] * text_a + lower[:, :LANES] * text_b
    layout = upper[:, LANES:] * layout_a + lower[:, LANES:] * layout_b
    return text, layout


def pair_scores(stacked, keys, limit):
    scores = nt(stacked, keys)
    key = lax.broadcasted_iota(jnp.int32, (1, scores.shape[1]), 1)
    return jnp.where(key < limit, scores, masked_score)


def attend_kernel(
    info, xt, xl, wt, wl, bt, bl, dense_t, dense_l, gt, st, gl, sl,
    qt, kt, vt, ql, kl, vl, ct, cl, first_t, first_l, low_t, low_l, lse,
    q_scr, k_scr, v_scr, ql_scr, kl_scr, vl_scr, cl_scr,
):
    own_rows, width = first_t.shape
    layout_width = first_l.shape[1]
    wide = ql.shape[1]
    window = kt.shape[0]
    block = window // 2
    own = pl.multiple_of(info[OWN], LANES)
    start = pl.multiple_of(info[WINDOW], LANES)

    for i in range(own_rows // LANES):
        rows = pl.ds(i * LANES, LANES)
        from_rows = pl.ds(pl.multiple_of(own + i * LANES, LANES), LANES)
        q = (nn(xt[from_rows, :], wt[:, :width]) + bt[0:1, :]).astype(BF)
        q_scr[rows, :] = q
        qt[rows, :] = q
        q = (nn(xl[from_rows, :], wl[:, :wide]) + bl[0:1, :]).astype(BF)
        ql_scr[rows, :] = q
        ql[rows, :] = q

    def project(i, carry):
        rows = pl.ds(pl.multiple_of(i * 256, 256), 256)
        from_rows = pl.ds(pl.multiple_of(start + i * 256, 256), 256)
        x = xt[from_rows, :]
        k = nn(x, wt[:, width : 2 * width]).astype(BF)
        k_scr[rows, :] = k
        kt[rows, :] = k
        v = (nn(x, wt[:, 2 * width :]) + bt[1:2, :]).astype(BF)
        v_scr[rows, :] = v
        vt[rows, :] = v
        x = xl[from_rows, :]
        k = nn(x, wl[:, wide : 2 * wide]).astype(BF)
        kl_scr[rows, :] = k
        kl[rows, :] = k
        v = (nn(x, wl[:, 2 * wide :]) + bl[1:2, :]).astype(BF)
        vl_scr[rows, :] = v
        vl[rows, :] = v
        return carry

    lax.fori_loop(0, window // 256, project, 0)
    cl_scr[...] = jnp.zeros_like(cl_scr)
    lse[...] = jnp.zeros_like(lse)
    lane = lax.broadcasted_iota(jnp.int32, (1, LANES), 1)

    def one_pair(pair, carry):
        text_lanes = lanes_of(pair * LANES)
        group_lanes = lanes_of((pair // 4) * LANES)
        scaled = head_masks(pair, 0.125, 0.25)
        plain = head_masks(pair, 1.0, 1.0)
        for j in range(own_rows // LANES):
            rows = pl.ds(j * LANES, LANES)
            keys_at = pl.ds(pl.multiple_of(info[LOCAL + j] * block, block), block)
            stacked = stack_heads(q_scr[rows, text_lanes], ql_scr[rows, group_lanes], scaled)
            keys = jnp.concatenate([k_scr[keys_at, text_lanes], kl_scr[keys_at, group_lanes]], axis=1)
            values = jnp.concatenate([v_scr[keys_at, text_lanes], vl_scr[keys_at, group_lanes]], axis=1)
            scores = pair_scores(stacked, keys, info[LIMIT + j])
            highest = jnp.max(scores, axis=-1, keepdims=True)
            exponent = jnp.exp(scores - highest)
            totals = jnp.sum(exponent, axis=-1, keepdims=True)
            probs = (exponent * (1.0 / totals)).astype(BF)
            text, layout = unstack_heads(nn(probs, values), plain)
            ct[rows, text_lanes] = text.astype(BF)
            cl_scr[rows, group_lanes] += layout
            log_total = highest + jnp.log(totals)
            lse[rows, :] = (
                lse[rows, :]
                + jnp.where(lane == 2 * pair, log_total[:LANES], 0.0)
                + jnp.where(lane == 2 * pair + 1, log_total[LANES:], 0.0)
            )
        return carry

    lax.fori_loop(0, HEADS // 2, one_pair, 0)

    for i in range(own_rows // LANES):
        rows = pl.ds(i * LANES, LANES)
        from_rows = pl.ds(pl.multiple_of(own + i * LANES, LANES), LANES)
        first = xt[from_rows, :].astype(F32) + (nn(ct[rows, :], dense_t[...]) + bt[2:3, :])
        first_t[rows, :] = first
        low_t[rows, :] = (normalised(first)[0] * gt[0:1, :] + st[0:1, :]).astype(BF)
        context = cl_scr[rows, :layout_width].astype(BF)
        cl[rows, :] = context
        first = xl[from_rows, :].astype(F32) + (nn(context, dense_l[...]) + bl[2:3, :layout_width])
        first_l[rows, :] = first
        low_l[rows, :] = (normalised(first)[0] * gl[0:1, :] + sl[0:1, :]).astype(BF)


def gelu_both(hidden):
    below = 0.5 * (1.0 + lax.erf(hidden * math.sqrt(0.5)))
    density = jnp.exp(-0.5 * hidden * hidden) * (1.0 / math.sqrt(2.0 * math.pi))
    return hidden * below, below + hidden * density


def ffn_stream(first, low, widen, hidden_bias, narrow, out_bias, gain, shift, cot, keep, dense, scratch, outs):
    gprime, second = scratch
    result, dout_ref, active, dhid, dfirst, dbranch, dcontext, sums, hidden_sums = outs
    shards = widen.shape[0]
    hid = widen.shape[2]
    wide = dcontext.shape[1]
    width = first.shape[1]
    step = 256 if hid % 256 == 0 else hid
    xh_one, scale_one = normalised(first[...])
    second[...] = xh_one * gain[0:1, :] + shift[0:1, :] + out_bias

    def forward(i, carry):
        for n in range(hid // step):
            cols = pl.ds(n * step, step)
            hidden = nn(low[...], widen[i, :, cols]) + hidden_bias[i, :, cols]
            value, slope = gelu_both(hidden)
            active[i, :, cols] = value.astype(BF)
            gprime[i, :, cols] = slope
        second[...] += nn(active[i], narrow[i])
        return carry

    lax.fori_loop(0, shards, forward, 0)
    xh_two, scale_two = normalised(second[...])
    result[...] = (xh_two * gain[1:2, :] + shift[1:2, :]).astype(BF)
    upstream = cot[...].astype(F32) * keep
    dsecond = norm_back(upstream, xh_two, scale_two, gain[1:2, :])
    dout_ref[...] = dsecond.astype(BF)
    sums[0:1, :] = column_sum(upstream * xh_two)
    sums[1:2, :] = column_sum(upstream)
    sums[2:3, :] = column_sum(dout_ref[...])
    second[...] = dsecond

    def backward(i, carry):
        for n in range(hid // step):
            cols = pl.ds(n * step, step)
            dactive = nt(dout_ref[...], narrow[i, cols, :])
            dhidden = (dactive * gprime[i, :, cols]).astype(BF)
            dhid[i, :, cols] = dhidden
            hidden_sums[i, :, cols] = column_sum(dhidden)
        second[...] += nt(dhid[i], widen[i])
        return carry

    lax.fori_loop(0, shards, backward, 0)
    dnormed = second[...]
    xh_one, scale_one = normalised(first[...])
    back = norm_back(dnormed, xh_one, scale_one, gain[0:1, :])
    sums[3:4, :] = column_sum(dnormed * xh_one)
    sums[4:5, :] = column_sum(dnormed)
    dfirst[...] = back
    dbranch[...] = back.astype(BF)
    sums[5:6, :] = column_sum(dbranch[...])
    sums[6:8, :] = jnp.zeros((2, width), F32)
    dc = nt(dbranch[...], dense[...]).astype(BF)
    dcontext[:, :width] = dc
    if wide > width:
        dcontext[:, width:] = jnp.zeros((dc.shape[0], wide - width), BF)


def ffn_kernel(info, *refs):
    (first_t, low_t, widen_t, hb_t, narrow_t, bt, gt, st, cot_t, dense_t) = refs[:10]
    (first_l, low_l, widen_l, hb_l, narrow_l, bl, gl, sl, cot_l, dense_l) = refs[10:20]
    outs_t, outs_l = refs[20:29], refs[29:38]
    gp_t, sec_t, gp_l, sec_l = refs[38:]
    row = lax.broadcasted_iota(jnp.int32, (LANES, 1), 0)
    keep = []
    for j in range(first_t.shape[0] // LANES):
        place = row + info[PLACE + j]
        keep.append(jnp.where((place >= info[FLAGGED + j]) & (place < info[LIMIT + j]), 1.0, 0.0))
    keep = jnp.concatenate(keep, axis=0)
    ffn_stream(first_t, low_t, widen_t, hb_t, narrow_t, bt[3:4, :], gt, st, cot_t, keep, dense_t, (gp_t, sec_t), outs_t)
    ffn_stream(first_l, low_l, widen_l, hb_l, narrow_l, bl[3:4, :], gl, sl, cot_l, keep, dense_l, (gp_l, sec_l), outs_l)


def weight_grads_kernel(active, dout, low, dhid, active_l, dout_l, low_l, dhid_l, gn, gw, gn_l, gw_l):
    gn[0] = tn(active[0], dout[...]).astype(BF)
    gw[0] = tn(low[...], dhid[0]).astype(BF)
    gn_l[0] = tn(active_l[0], dout_l[...])
    gw_l[0] = tn(low_l[...], dhid_l[0])


def attend_back_kernel(
    info, qt, kt, vt, ql, kl, vl, dct, dcl, lse,
    dq, dk, dv, dq_l, dk_l, dv_l,
    k_acc, v_acc, kl_acc, vl_acc, ql_acc,
):
    own_rows = qt.shape[0]
    window = kt.shape[0]
    block = window // 2
    pad = (dk.shape[0] - window) // 2
    for acc in (k_acc, v_acc, kl_acc, vl_acc, ql_acc):
        acc[...] = jnp.zeros_like(acc)
    for out in (dk, dv, dk_l, dv_l):
        edge = jnp.zeros((pad, out.shape[1]), BF)
        out[:pad, :] = edge
        out[pad + window :, :] = edge
    lane = lax.broadcasted_iota(jnp.int32, (1, LANES), 1)

    def one_pair(pair, carry):
        text_lanes = lanes_of(pair * LANES)
        group_lanes = lanes_of((pair // 4) * LANES)
        scaled = head_masks(pair, 0.125, 0.25)
        plain = head_masks(pair, 1.0, 1.0)
        for j in range(own_rows // LANES):
            rows = pl.ds(j * LANES, LANES)
            keys_at = pl.ds(pl.multiple_of(info[LOCAL + j] * block, block), block)
            stacked = stack_heads(qt[rows, text_lanes], ql[rows, group_lanes], scaled)
            keys = jnp.concatenate([kt[keys_at, text_lanes], kl[keys_at, group_lanes]], axis=1)
            values = jnp.concatenate([vt[keys_at, text_lanes], vl[keys_at, group_lanes]], axis=1)
            dcs = stack_heads(dct[rows, text_lanes], dcl[rows, group_lanes], plain)
            logs = lse[rows, :]
            log_total = jnp.concatenate(
                [
                    jnp.sum(jnp.where(lane == 2 * pair, logs, 0.0), axis=1, keepdims=True),
                    jnp.sum(jnp.where(lane == 2 * pair + 1, logs, 0.0), axis=1, keepdims=True),
                ],
                axis=0,
            )
            probs = jnp.exp(pair_scores(stacked, keys, info[LIMIT + j]) - log_total)
            dprobs = nt(dcs, values)
            inner = jnp.sum(probs * dprobs, axis=1, keepdims=True)
            dscores = (probs * (dprobs - inner)).astype(BF)
            text, layout = unstack_heads(nn(dscores, keys), scaled)
            dq[rows, text_lanes] = text.astype(BF)
            ql_acc[rows, group_lanes] += layout
            both = tn(dscores, stacked)
            k_acc[keys_at, text_lanes] += both[:, :LANES]
            kl_acc[keys_at, group_lanes] += both[:, LANES:]
            both = tn(probs.astype(BF), dcs)
            v_acc[keys_at, text_lanes] += both[:, :LANES]
            vl_acc[keys_at, group_lanes] += both[:, LANES:]
        return carry

    lax.fori_loop(0, HEADS // 2, one_pair, 0)
    middle = pl.ds(pad, window)
    dk[middle, :] = k_acc[...].astype(BF)
    dv[middle, :] = v_acc[...].astype(BF)
    dk_l[middle, :] = kl_acc[...].astype(BF)
    dv_l[middle, :] = vl_acc[...].astype(BF)
    dq_l[...] = ql_acc[...].astype(BF)


def project_back_kernel(
    info, xt, xl, wt, wl, dq, dk, dv, dq_l, dk_l, dv_l, dfirst_t, dfirst_l, ct, cl, db_t, db_l,
    side, own_grad, gp, gd, gp_l, gd_l, sums, sums_l,
):
    own_rows, width = dq.shape
    wide = dq_l.shape[1]
    layout_width = xl.shape[1]
    pad = own_rows
    window = dk.shape[0] - 2 * pad
    own = pl.multiple_of(info[OWN], LANES)
    start = pl.multiple_of(info[WINDOW], LANES)
    shift = pl.multiple_of(info[SHIFT], LANES)

    def rows_grad(at):
        rows = pl.ds(pl.multiple_of(shift + at, LANES), LANES)
        text = nt(dk[rows, :], wt[:, width : 2 * width]) + nt(dv[rows, :], wt[:, 2 * width :])
        layout = nt(dk_l[rows, :], wl[:, wide : 2 * wide]) + nt(dv_l[rows, :], wl[:, 2 * wide :])
        return text, layout

    def part(i, carry):
        at = i * LANES
        to = pl.ds(pl.multiple_of(at, LANES), LANES)
        text, layout = rows_grad(at)
        side[0, to, :width] = text.astype(BF)
        side[0, to, width:] = layout.astype(BF)
        text, layout = rows_grad(at + 2 * own_rows)
        side[1, to, :width] = text.astype(BF)
        side[1, to, width:] = layout.astype(BF)
        text, layout = rows_grad(at + own_rows)
        own_grad[to, :width] = dfirst_t[to, :] + text + nt(dq[to, :], wt[:, :width])
        own_grad[to, width:] = dfirst_l[to, :] + layout + nt(dq_l[to, :], wl[:, :wide])
        return carry

    lax.fori_loop(0, own_rows // LANES, part, 0)
    x_own = xt[pl.ds(own, own_rows), :]
    x_win = xt[pl.ds(start, window), :]
    middle = pl.ds(pad, window)
    gp[0] = tn(x_own, dq[...]).astype(BF)
    gp[1] = tn(x_win, dk[middle, :]).astype(BF)
    gp[2] = tn(x_win, dv[middle, :]).astype(BF)
    gd[...] = tn(ct[...], db_t[...]).astype(BF)
    x_own = xl[pl.ds(own, own_rows), :]
    x_win = xl[pl.ds(start, window), :]
    gp_l[0] = tn(x_own, dq_l[...])
    gp_l[1] = tn(x_win, dk_l[middle, :])
    gp_l[2] = tn(x_win, dv_l[middle, :])
    gd_l[...] = tn(cl[...], db_l[...])
    sums[0:1, :] = column_sum(dq[...])
    sums[1:2, :] = column_sum(dv[middle, :])
    sums_l[0:1, :] = column_sum(dq_l[...])
    sums_l[1:2, :] = column_sum(dv_l[middle, :])


def call(kernel, operands, outs, scratch=(), grid=None, in_specs=None, out_specs=None, flops=0, name=None):
    operands = tuple(operands)
    if in_specs is None:
        in_specs = [pl.BlockSpec(memory_space=pltpu.SMEM)]
        in_specs += [pl.BlockSpec(memory_space=pltpu.VMEM)] * (len(operands) - 1)
    if out_specs is None:
        out_specs = [pl.BlockSpec(memory_space=pltpu.VMEM)] * len(outs)
    moved = sum(math.prod(o.shape) * o.dtype.itemsize for o in tuple(operands) + tuple(outs))
    extra = {} if grid is None else {"grid": grid}
    return pl.pallas_call(
        kernel,
        out_shape=outs,
        in_specs=in_specs,
        out_specs=out_specs,
        scratch_shapes=list(scratch),
        cost_estimate=pl.CostEstimate(flops=flops, bytes_accessed=moved, transcendentals=0),
        compiler_params=pltpu.CompilerParams(vmem_limit_bytes=56 << 20),
        name=name,
        **extra,
    )(*operands)


def shape(dims, dtype=BF):
    return jax.ShapeDtypeStruct(dims, dtype)


def per_device(
    text_input, layout_input, block_starts, intersection_flags, text_cotangent, layout_cotangent,
    text_project, text_biases, text_dense, text_gains, text_shifts, text_widen, text_hidden_bias, text_narrow,
    layout_project, layout_biases, layout_dense, layout_gains, layout_shifts, layout_widen, layout_hidden_bias,
    layout_narrow,
):
    blocks, length = intersection_flags.shape
    total = blocks * length
    groups = lax.axis_size("tensor")
    planes = lax.axis_size("dp")
    own = total // groups
    tiles = own // LANES
    width = text_input.shape[1]
    layout_width = layout_input.shape[1]
    wide = 2 * LANES
    window = 2 * length
    t = lax.axis_index("tensor").astype(jnp.int32)
    me = lax.axis_index("dp").astype(jnp.int32)

    flagged = jnp.sum(intersection_flags, axis=1, dtype=jnp.int32)
    base = jnp.minimum((t * own) // length, blocks - 2)
    tile_rows = t * own + LANES * jnp.arange(tiles, dtype=jnp.int32)
    tile_block = tile_rows // length
    pick = tile_block[:, None] == jnp.arange(blocks, dtype=jnp.int32)[None, :]
    limit = DOC - jnp.sum(jnp.where(pick, block_starts[None, :], 0), axis=1)
    flags_of = jnp.sum(jnp.where(pick, flagged[None, :], 0), axis=1)
    info = jnp.concatenate(
        [
            jnp.stack([t * own, base * length, t * own - base * length]),
            tile_block - base,
            limit,
            flags_of,
            tile_rows - tile_block * length,
            jnp.zeros((1,), jnp.int32),
        ]
    ).astype(jnp.int32)

    piece = text_widen.shape[0] // planes
    mine = jnp.concatenate(
        [
            lax.dynamic_slice_in_dim(text_widen, me * piece, piece, 0),
            lax.dynamic_slice_in_dim(text_narrow, me * piece, piece, 0),
        ],
        axis=0,
    )
    gathered = lax.all_gather(mine, ("tensor", "dp"), axis=0, tiled=False)
    gathered = gathered.reshape(groups, planes, 2, piece, width)
    widen_t = gathered[:, :, 0].reshape(groups, width, -1)
    narrow_t = gathered[:, :, 1].reshape(groups, -1, width)
    small = lax.all_gather(jnp.concatenate([layout_widen, layout_narrow], axis=0), "tensor", axis=0, tiled=False)
    widen_l, narrow_l = small[:, :layout_width], small[:, layout_width:]
    hidden_bias = lax.all_gather(
        jnp.concatenate([text_hidden_bias, layout_hidden_bias])[None, :], "tensor", axis=0, tiled=False
    )
    split = text_hidden_bias.shape[0]
    hb_t, hb_l = hidden_bias[:, :, :split], hidden_bias[:, :, split:]

    def pad_parts(values):
        rows = values.shape[0]
        parts = values.reshape(rows, -1, layout_width)
        return jnp.pad(parts, ((0, 0), (0, 0), (0, wide - layout_width))).reshape(rows, -1)

    wl = pad_parts(layout_project)
    bl = pad_parts(layout_biases)

    qkv_macs = (own + 2 * window) * width * width
    unit = 2 * 36 // groups * length * length * 256
    (qt, kt, vt, ql, kl, vl, ct, cl, first_t, first_l, low_t, low_l, lse) = call(
        attend_kernel,
        (info, text_input, layout_input, text_project, wl, text_biases, bl, text_dense, layout_dense,
         text_gains, text_shifts, layout_gains, layout_shifts),
        (
            shape((own, width)), shape((window, width)), shape((window, width)),
            shape((own, wide)), shape((window, wide)), shape((window, wide)),
            shape((own, width)), shape((own, layout_width)),
            shape((own, width), F32), shape((own, layout_width), F32),
            shape((own, width)), shape((own, layout_width)), shape((own, LANES), F32),
        ),
        scratch=(
            pltpu.VMEM((own, width), BF), pltpu.VMEM((window, width), BF), pltpu.VMEM((window, width), BF),
            pltpu.VMEM((own, wide), BF), pltpu.VMEM((window, wide), BF), pltpu.VMEM((window, wide), BF),
            pltpu.VMEM((own, wide), F32),
        ),
        flops=2 * (qkv_macs + 2 * unit), name="attend",
    )

    hid = text_narrow.shape[0]
    hid_l = layout_narrow.shape[0]
    stream_outs = lambda w, h, pw: (
        shape((own, w)), shape((own, w)), shape((groups, own, h)), shape((groups, own, h)),
        shape((own, w), F32), shape((own, w)), shape((own, pw)), shape((8, w), F32), shape((groups, 1, h), F32),
    )
    outs = call(
        ffn_kernel,
        (info,
         first_t, low_t, widen_t, hb_t, narrow_t, text_biases, text_gains, text_shifts, text_cotangent, text_dense,
         first_l, low_l, widen_l, hb_l, narrow_l, layout_biases, layout_gains, layout_shifts, layout_cotangent,
         layout_dense),
        stream_outs(width, hid, width) + stream_outs(layout_width, hid_l, wide),
        scratch=(
            pltpu.VMEM((groups, own, hid), F32), pltpu.VMEM((own, width), F32),
            pltpu.VMEM((groups, own, hid_l), F32), pltpu.VMEM((own, layout_width), F32),
        ),
        flops=2 * 4 * groups * own * width * hid, name="feed_forward",
    )
    result_t, dout_t, active_t, dhid_t, dfirst_t, db_t, dc_t, sums_t, hsum_t = outs[:9]
    result_l, dout_l, active_l, dhid_l, dfirst_l, db_l, dc_l, sums_l, hsum_l = outs[9:]

    vm = lambda block, index: pl.BlockSpec(block, index)
    whole = lambda w: vm((own, w), lambda k: (0, 0))
    shard = lambda *dims: vm((1, *dims), lambda k: (k, 0, 0))
    gn, gw, gn_l, gw_l = call(
        weight_grads_kernel,
        (active_t, dout_t, low_t, dhid_t, active_l, dout_l, low_l, dhid_l),
        (shape((groups, hid, width)), shape((groups, width, hid)),
         shape((groups, hid_l, layout_width), F32), shape((groups, layout_width, hid_l), F32)),
        grid=(groups,),
        in_specs=[shard(own, hid), whole(width), whole(width), shard(own, hid),
                  shard(own, hid_l), whole(layout_width), whole(layout_width), shard(own, hid_l)],
        out_specs=[shard(hid, width), shard(width, hid), shard(hid_l, layout_width), shard(layout_width, hid_l)],
        flops=2 * 2 * groups * own * width * hid, name="weight_grads",
    )

    padded = window + 2 * own
    dq, dk, dv, dq_l, dk_l, dv_l = call(
        attend_back_kernel,
        (info, qt, kt, vt, ql, kl, vl, dc_t, dc_l, lse),
        (shape((own, width)), shape((padded, width)), shape((padded, width)),
         shape((own, wide)), shape((padded, wide)), shape((padded, wide))),
        scratch=(pltpu.VMEM((window, width), F32), pltpu.VMEM((window, width), F32),
                 pltpu.VMEM((window, wide), F32), pltpu.VMEM((window, wide), F32), pltpu.VMEM((own, wide), F32)),
        flops=2 * 5 * unit, name="attend_back",
    )
    side, own_grad, gp, gd, gp_l, gd_l, psums_t, psums_l = call(
        project_back_kernel,
        (info, text_input, layout_input, text_project, wl, dq, dk, dv, dq_l, dk_l, dv_l, dfirst_t, dfirst_l,
         ct, cl, db_t, db_l),
        (shape((2, own, width + layout_width)), shape((own, width + layout_width), F32),
         shape((3, width, width)), shape((width, width)),
         shape((3, layout_width, wide), F32), shape((layout_width, layout_width), F32),
         shape((2, width), F32), shape((2, wide), F32)),
        flops=2 * 2 * qkv_macs, name="project_back",
    )

    to_left = [(i + 1, i) for i in range(groups - 1)]
    to_right = [(i, i + 1) for i in range(groups - 1)]
    from_right = lax.ppermute(side[0], "tensor", to_left)
    from_left = lax.ppermute(side[1], "tensor", to_right)
    own_sum = (own_grad + from_right.astype(F32) + from_left.astype(F32)).astype(BF)
    all_rows = lax.all_gather(own_sum, "tensor", axis=0, tiled=True).astype(F32)
    text_grad, layout_grad = all_rows[:, :width], all_rows[:, width:]

    both = ("tensor", "dp")
    sharded = jnp.concatenate([gn, gw], axis=1).reshape(-1, width)
    sharded = lax.psum_scatter(sharded, both, scatter_dimension=0, tiled=True)
    sharded = lax.all_gather(sharded, "dp", axis=0, tiled=True).astype(F32)
    g_narrow, g_widen = sharded[:hid], sharded[hid:]
    copied = jnp.concatenate([gp.reshape(-1, width), gd], axis=0)
    copied = lax.psum(copied, both).astype(F32)
    g_project = jnp.concatenate([copied[i * width : (i + 1) * width] for i in range(3)], axis=1)
    g_dense = copied[3 * width :]

    w = layout_width
    small = lax.psum((gn_l, gw_l, gp_l[:, :, :w], gd_l, sums_t, hsum_t, sums_l, hsum_l, psums_t, psums_l[:, :w]), both)
    gn_l, gw_l, gp_l, gd_l, sums_t, hsum_t, sums_l, hsum_l, psums_t, psums_l = small
    at = lambda v: lax.dynamic_index_in_dim(v, t, 0, keepdims=False)
    g_project_l = jnp.concatenate([gp_l[0], gp_l[1], gp_l[2]], axis=1)

    def vectors(sums, psums):
        biases = jnp.stack([psums[0], psums[1], sums[5], sums[2]])
        return biases, jnp.stack([sums[3], sums[0]]), jnp.stack([sums[4], sums[1]])

    bias_t, gain_t, shift_t = vectors(sums_t, psums_t)
    bias_l, gain_l, shift_l = vectors(sums_l, psums_l)
    return (
        result_t, result_l, text_grad, layout_grad,
        g_project, bias_t, g_dense, gain_t, shift_t, g_widen, at(hsum_t)[0], g_narrow,
        g_project_l, bias_l, gd_l, gain_l, shift_l, at(gw_l), at(hsum_l)[0], at(gn_l),
    )


def solution(mesh):
    rows = P(("dp", "tensor"), None)
    weights = (P(), P(), P(), P(), P(), P(None, "tensor"), P("tensor"), P("tensor", None))
    return jax.shard_map(
        per_device,
        mesh=mesh,
        in_specs=(P("dp", None), P("dp", None), P("dp"), P("dp", None), rows, rows) + weights + weights,
        out_specs=(rows, rows, P("dp", None), P("dp", None)) + weights + weights,
        check_vma=False,
    )
```

time: 1080 us -> 706 us (0.65)
  matrix products: 302 us -> 0 us
  local copies, waits for them, and re-layouts: 165 us -> 48.3 us
  Pallas kernels: 0 us -> 97.5 us
  other arithmetic: 83.9 us -> 23.7 us
    dot_general x66 -> x0, matrix products: 302 us -> none  [the longest x6 57.4 us: joint_scores(): jnp.einsum('qhd,khd->hqk', layout_query, layout_key, preferred_element_ty...]
    reduce_scatter x4 -> x1, waiting for transfers between devices: 197 us -> 51.3 us  [per_device(): sharded = lax.psum_scatter(sharded, both, scatter_dimension=0, tiled=True)]
    psum x1 -> x2, waiting for transfers between devices: 114 us -> 241 us  [the longest x1 144 us: per_device(): copied = lax.psum(copied, both).astype(F32)]
    pallas_call x0 -> x5, Pallas kernels: none -> 97.5 us  [call(): pl.pallas_call(kernel, out_shape=outs, in_specs=in_specs, out_specs=out_s...]
    unnamed x236 -> x44, local copies, waits for them, and re-layouts: 57.6 us -> 11.3 us
    reduce_sum x25 -> x2, other arithmetic: 38.8 us -> 1 us  [the longest x1 0.82 us: per_device(): flagged = jnp.sum(intersection_flags, axis=1, dtype=jnp.int32)]
    ppermute x0 -> x2, waiting for transfers between devices: none -> 35.7 us  [the longest x1 35.7 us: per_device(): from_right = lax.ppermute(side[0], 'tensor', to_left)]
    reshape x9 -> x2, local copies, waits for them, and re-layouts: 34.6 us -> 1.47 us  [pad_parts(): jnp.pad(parts, ((0, 0), (0, 0), (0, wide - layout_width))).reshape(rows, -1)]
  transfers between devices with their start and end apart: 8 -> 8, of which waited for: 8 -> 7; matrix products, arithmetic and copies ran while one was open for 11% -> 7% of each run, Pallas kernels for 0% -> 9%
where the time goes in v1:
time: 706 us; the launch traced here: 704 us
  waiting for transfers between devices  434 us (61%)
  Pallas kernels  97.5 us (14%)
  blocking collectives  79.1 us (11%)
  local copies, waits for them, and re-layouts  48.3 us (7%)
  other arithmetic  23.7 us (3%)
  between operations  15.1 us (2%)
    psum x1, waiting for transfers between devices, per_device(): copied = lax.psum(copied, both).astype(F32)  144 us
    pallas_call x5, Pallas kernels, call(): pl.pallas_call(kernel, out_shape=outs, in_specs=in_specs, out_specs=out_s...  97.5 us
    psum x1, waiting for transfers between devices, per_device(): lax.psum((gn_l, gw_l, gp_l[:, :, :w], gd_l, sums_t, hsum_t, sums_l, hsum_...  96.6 us
    all_gather x1, waiting for transfers between devices, per_device(): all_rows = lax.all_gather(own_sum, 'tensor', axis=0, tiled=True).astype(F32)  56.6 us
    reduce_scatter x1, waiting for transfers between devices, per_device(): sharded = lax.psum_scatter(sharded, both, scatter_dimension=0, tiled=True)  51.3 us
    psum x1, blocking collectives, per_device(): lax.psum((gn_l, gw_l, gp_l[:, :, :w], gd_l, sums_t, hsum_t, sums_l, hsum_...  41.6 us
    ppermute x1, waiting for transfers between devices, per_device(): from_right = lax.ppermute(side[0], 'tensor', to_left)  35.7 us
    all_gather x1, waiting for transfers between devices, per_device(): gathered = lax.all_gather(mine, ('tensor', 'dp'), axis=0, tiled=False)  25.5 us
  transfers between devices with their start and end apart: 8, of which 7 were waited for; matrix products, arithmetic and copies ran while one was open for 7% of the time, Pallas kernels for 9%

profile of v1, /device:TPU:9, one launch (start us, length us, event | category | flops | bytes accessed | tf_op | source)
XLA Modules:
  0.0 703.8 jit_solution(8300343030973080446)
XLA Ops:
  7.3 1.1 constant_dynamic-slice_fusion.1
  8.4 0.7 pad_maximum_fusion.4
  9.2 1.2 dynamic-slice
  11.1 0.8 maximum_dynamic-update-slice_fusion
  11.9 12.1 %all-reduce.2 = f32[3840]{0:T(1024)S(1)} all-reduce(f32[3840]{0:T(1024)S(1)} %maximum_dynamic-update-slice_fusion), channel_id=3, replica_groups=mesh['dp'=8,'tensor'=4] {'tensor'}, use_global_device_ids=true, to_apply=%add.2 | all-reduce | flops 3840 | bytes 30720
  24.1 0.6 slice.139.refs_3_
  24.7 0.6 slice.142.refs_13_
  25.3 0.8 reduce_sum.28
  26.2 1.1 copy.71
  27.3 0.9 copy.84.wl
  28.2 1.2 copy.73.xl
  29.4 0.8 copy.76.refs_18_
  30.2 0.2 select_reduce_fusion
  30.4 0.6 concatenate.24.info
  31.0 0.6 pad_bitcast_fusion.bl
  31.7 25.3 %all-gather.2 = bf16[1536,192]{1,0:T(8,128)(2,1)S(1)} all-gather(bf16[384,192]{1,0:T(8,128)(2,1)S(1)} %pad_maximum_fusion.5), channel_id=4, replica_groups=mesh['dp'=8,'tensor'=4] {'tensor'}, dimensions={0}, use_global_device_ids=true | all-gather | bytes 737280 | tf_op jit(solution)/shard_map/all_gather | solution.py:453
  57.0 1.0 fusion.3
  58.0 19.0 %attend.1 = (bf16[384,768]{1,0:T(8,128)(2,1)}, bf16[1024,768]{1,0:T(8,128)(2,1)}, bf16[1024,768]{1,0:T(8,128)(2,1)}, bf16[384,256]{1,0:T(8,128)(2,1)}, bf16[1024...) custom-call(s32[16]{0:T(128)} %concatenate.24.info, ...), custom_call_target="tpu_custom_call" | custom-call | flops 7700742144 | bytes 16194624 | tf_op jit(solution)/shard_map/attend/pallas_call | solution.py:387
  77.0 25.5 %all-gather.11.cloned.1.call-done = bf16[6144,768]{1,0:T(8,128)(2,1)} async-done(((bf16[192,768]{1,0:T(8,128)(2,1)}), bf16[6144,768]{1,0:T(8,128)(2,1)}) %all-gather.11.cloned.1.call-update) | async-done | bytes 9437200 | tf_op jit(solution)/shard_map/all_gather | solution.py:449
  102.5 8.1 %fusion = (bf16[4,8,1,96,768]{4,3,2,1,0:T(8,128)(2,1)}, bf16[4,8,1,96,768]{4,3,2,1,0:T(8,128)(2,1)}) fusion(bf16[4,8,2,96,768]{4,3,2,1,0:T(8,128)(2,1)} %bitcast.37), kind=kLoop, calls=%fused_computation.37 | loop fusion | bytes 18874368 | tf_op jit(solution)/shard_map/slice | solution.py:452
  110.6 27.1 %feed_forward.1 = (bf16[384,768]{1,0:T(8,128)(2,1)}, bf16[384,768]{1,0:T(8,128)(2,1)}, bf16[4,384,768]{2,1,0:T(8,128)(2,1)}, bf16[4,384,768]{2,1,0:T(8,128)(2,1)...) custom-call(s32[16]{0:T(128)} %concatenate.24.info, ...), custom_call_target="tpu_custom_call" | custom-call | flops 7247757312 | bytes 24692800 | tf_op jit(solution)/shard_map/feed_forward/pallas_call | solution.py:387
  137.7 9.6 %weight_grads.1 = (bf16[4,768,768]{2,1,0:T(8,128)(2,1)}, bf16[4,768,768]{2,1,0:T(8,128)(2,1)}, f32[4,192,192]{2,1,0:T(8,128)}, f32[4,192,192]{2,1,0:T(8,128)}) custom-call(bf16[4,384,768]{2,1,0:T(8,128)(2,1)} %get-tuple-element.102.active, bf16[384,768]{1,0:T(8,128)(2,1)} %get-tuple-element.103.dout, bf16[384,768]{1,0:T(8,128)(2,1)} %get-tuple-element.70.refs_1_.low, ...), custom_call_target="tpu_custom_call" | custom-call | flops 3623878656 | bytes 17989632 | tf_op jit(solution)/shard_map/weight_grads/pallas_call | solution.py:387
  147.3 7.6 %pad_maximum_fusion = bf16[4,1536,768]{2,1,0:T(8,128)(2,1)} fusion(bf16[4,768,768]{2,1,0:T(8,128)(2,1)} %get-tuple-element.109, bf16[4,768,768]{2,1,0:T(8,128)(2,1)} %get-tuple-element.108), kind=kLoop, calls=%fused_computation | loop fusion | flops 18874368 | bytes 18874368 | tf_op jit(solution)/shard_map/concatenate | solution.py:557
  154.9 0.3 all-reduce.10.cloned.1.call-start
  155.2 19.5 %attend_back.1 = (bf16[384,768]{1,0:T(8,128)(2,1)}, bf16[1792,768]{1,0:T(8,128)(2,1)}, bf16[1792,768]{1,0:T(8,128)(2,1)}, bf16[384,256]{1,0:T(8,128)(2,1)}, bf16...) custom-call(s32[16]{0:T(128)} %concatenate.24.info, bf16[384,768]{1,0:T(8,128)(2,1)} %get-tuple-element.75.qt, ...), custom_call_target="tpu_custom_call" | custom-call | flops 12079595520 | bytes 14090304 | tf_op jit(solution)/shard_map/attend_back/pallas_call | solution.py:387
  174.7 22.3 %project_back.1 = (bf16[2,384,960]{2,1,0:T(8,128)(2,1)}, f32[384,960]{1,0:T(8,128)}, bf16[3,768,768]{2,1,0:T(8,128)(2,1)}, bf16[768,768]{1,0:T(8,128)(2,1)}, f32...) custom-call(s32[16]{0:T(128)} %concatenate.24.info, bf16[1536,768]{1,0:T(8,128)(2,1)} %xt.3, ...), custom_call_target="tpu_custom_call" | custom-call | flops 5737807872 | bytes 26271808 | tf_op jit(solution)/shard_map/project_back/pallas_call | solution.py:387
  197.1 1.2 copy-done.3
  198.3 4.5 pad_maximum_fusion.2
  202.8 1.3 copy-done.1
  204.2 0.1 slice_bitcast_fusion.1
  204.3 1.2 copy.78
  205.4 2.3 collective-permute-start
  207.7 1.2 copy.80
  208.9 3.3 collective-permute-start.1
  212.1 35.7 %collective-permute-done = bf16[384,960]{0,1:T(8,128)(2,1)S(1)} collective-permute-done((bf16[384,960]{0,1:T(8,128)(2,1)}, bf16[384,960]{0,1:T(8,128)(2,1)S(1)}, u32[]{:S(2)}, u32[]{:S(2)}) %collective-permute-start) | collective-permute-done | bytes 737312 | tf_op jit(solution)/shard_map/ppermute | solution.py:550
  247.8 0.3 copy.79
  248.1 1.4 copy.81
  249.6 1.2 add_convert_fusion
  250.9 51.3 %reduce-scatter.2.cloned.1.call-done = bf16[192,768]{1,0:T(8,128)(2,1)} async-done(((bf16[6144,768]{1,0:T(8,128)(2,1)}), bf16[192,768]{1,0:T(8,128)(2,1)}) %reduce-scatter.2.cloned.1.call-update) | async-done | bytes 294928 | tf_op jit(solution)/shard_map/reduce_scatter | solution.py:558
  302.2 0.8 copy.82
  303.1 41.6 %all-reduce.3 = (f32[8,768]{1,0:T(8,128)S(1)}, f32[2,768]{1,0:T(2,128)S(1)}, f32[4,1,768]{2,1,0:T(1,128)S(1)}, f32[8,192]{1,0:T(8,128)S(1)}, f32[2,192]{1,0:T(2,128)S(1)}, /*index=5*/f32[4,1,192]{2,1,0:T(1,128)S(1)}) all-reduce(f32[8,768]{1,0:T(8,128)S(1)} %copy-done.10, ...), channel_id=1, replica_groups=mesh['dp'=8,'tensor'=4] {'tensor','dp'}, use_global_device_ids=true, to_apply=%region_5.6 | all-reduce | flops 13440 | bytes 107520 | tf_op jit(solution)/shard_map/psum | solution.py:567
  344.7 0.6 dynamic-slice_reduce_fusion
  345.3 0.6 constant_dynamic-slice_fusion
  345.9 0.6 pad_maximum_fusion.11
  346.5 0.6 pad_maximum_fusion.10
  347.1 0.6 pad_maximum_fusion.9
  347.7 0.6 pad_maximum_fusion.8
  348.3 0.6 pad_maximum_fusion.7
  348.9 0.6 pad_maximum_fusion.6
  349.5 96.6 %all-reduce.10.cloned.1.call-done = (f32[3,192,192]{2,1,0:T(8,128)}, f32[192,192]{1,0:T(8,128)}, f32[4,192,192]{2,1,0:T(8,128)}, f32[4,192,192]{2,1,0:T(8,128)}) async-done(((f32[3,192,192]{2,1,0:T(8,128)}, f32[192,192]{1,0:T(8,128)}, f32[4,192,192]{2,1,0:T(8,128)}, f32[4,192,192]{2,1,0:T(8,128)}), (f32[3,192,192]{2,1,0:T(8,128)}, f32[192,192]{1,0:T(8,128)}, f32[4,192,192]{2,1,0:T(8,128)}, ...) | async-done | bytes 1769488 | tf_op jit(solution)/shard_map/psum | solution.py:567
  446.1 1.6 dynamic-slice_bitcast_fusion
  447.8 1.6 dynamic-slice_bitcast_fusion.1
  449.4 1.2 slice_bitcast_fusion.4
  450.5 0.9 pad_maximum_fusion.3
  451.5 144.0 %all-reduce.8.cloned.1.call-done = bf16[3072,768]{1,0:T(8,128)(2,1)} async-done(((bf16[3072,768]{1,0:T(8,128)(2,1)}), bf16[3072,768]{1,0:T(8,128)(2,1)}) %all-reduce.8.cloned.1.call-update) | async-done | bytes 4718608 | tf_op jit(solution)/shard_map/psum | solution.py:562
  595.5 4.4 fusion.1
  599.9 3.2 pad_maximum_fusion.1
  603.1 56.6 %all-gather.7.cloned.1.call-done = bf16[1536,960]{1,0:T(8,128)(2,1)} async-done(((bf16[384,960]{1,0:T(8,128)(2,1)}), bf16[1536,960]{1,0:T(8,128)(2,1)}) %all-gather.7.cloned.1.call-update) | async-done | bytes 2949136 | tf_op jit(solution)/shard_map/all_gather | solution.py:553
  659.6 2.5 slice.145
  662.2 2.9 copy.83
  665.0 2.6 slice.144
  667.7 24.4 %all-gather.9.cloned.1.call-done = bf16[1536,768]{1,0:T(8,128)(2,1)} async-done(((bf16[192,768]{1,0:T(8,128)(2,1)}), bf16[1536,768]{1,0:T(8,128)(2,1)}) %all-gather.9.cloned.1.call-update) | async-done | bytes 2359312 | tf_op jit(solution)/shard_map/all_gather | solution.py:559
  692.1 4.2 fusion.2
  696.3 0.7 copy.93
  (55 shorter events, 0.6 us)
Async XLA Ops:
  7.2 21.0 %copy-start.4 = (bf16[1536,192]{0,1:T(8,128)(2,1)S(1)}, bf16[1536,192]{0,1:T(8,128)(2,1)}, u32[]{:S(2)}) copy-start(bf16[1536,192]{0,1:T(8,128)(2,1)} %param.23) | copy-start | bytes 1769476
  7.2 95.3 %all-gather.11.cloned.1.call-start = ((), (), s32[]{:S(2)}) async-start(), calls=%async_computation.5 | async-start | bytes 9732096 | tf_op jit(solution)/shard_map/all_gather | solution.py:449
  7.3 22.1 %copy-start.7 = (bf16[384,192]{0,1:T(8,128)(2,1)S(1)}, bf16[384,192]{0,1:T(8,128)(2,1)}, u32[]{:S(2)}) copy-start(bf16[384,192]{0,1:T(8,128)(2,1)} %param.27) | copy-start | bytes 442372
  8.3 21.9 %copy-start.17 = (s32[3]{0:T(128)S(1)}, s32[3]{0:T(128)}, u32[]{:S(2)}) copy-start(s32[3]{0:T(128)} %param.24) | copy-start | bytes 40
  8.3 22.7 %copy-start.15 = (f32[4,192]{1,0:T(4,128)S(1)}, f32[4,192]{1,0:T(4,128)}, u32[]{:S(2)}) copy-start(f32[4,192]{1,0:T(4,128)} %refs_15_.1) | copy-start | bytes 9220
  8.4 23.3 %copy-start.8 = (bf16[192,192]{1,0:T(8,128)(2,1)S(1)}, bf16[192,192]{1,0:T(8,128)(2,1)}, u32[]{:S(2)}) copy-start(bf16[192,192]{1,0:T(8,128)(2,1)} %param.43) | copy-start | bytes 221188
  8.4 23.3 %copy-start.9 = (bf16[192,192]{1,0:T(8,128)(2,1)S(1)}, bf16[192,192]{1,0:T(8,128)(2,1)}, u32[]{:S(2)}) copy-start(bf16[192,192]{1,0:T(8,128)(2,1)} %param.41) | copy-start | bytes 221188
  9.1 293.1 %reduce-scatter.2.cloned.1.call-start = ((), (), s32[]{:S(2)}) async-start(), calls=%async_computation.3 | async-start | bytes 9732096 | tf_op jit(solution)/shard_map/reduce_scatter | solution.py:558
  154.9 291.2 %all-reduce.10.cloned.1.call-start = ((), (), s32[]{:S(2)}) async-start(), calls=%async_computation.6 | async-start | bytes 4718592 | tf_op jit(solution)/shard_map/psum | solution.py:567
  197.0 1.3 copy-start.3
  197.0 398.4 %all-reduce.8.cloned.1.call-start = ((), (), s32[]{:S(2)}) async-start(), calls=%async_computation.2 | async-start | bytes 9437184 | tf_op jit(solution)/shard_map/psum | solution.py:562
  202.8 1.4 copy-start.1
  202.8 456.8 %all-gather.7.cloned.1.call-start = ((), (), s32[]{:S(2)}) async-start(), calls=%async_computation.1 | async-start | bytes 3932160 | tf_op jit(solution)/shard_map/all_gather | solution.py:553
  205.4 44.1 %copy-start.2 = (f32[384,960]{1,0:T(8,128)S(1)}, f32[384,960]{1,0:T(8,128)}, u32[]{:S(2)}) copy-start(f32[384,960]{1,0:T(8,128)} %get-tuple-element.96) | copy-start | bytes 4423684
  205.4 42.4 %collective-permute-start = (bf16[384,960]{0,1:T(8,128)(2,1)}, bf16[384,960]{0,1:T(8,128)(2,1)S(1)}, u32[]{:S(2)}, u32[]{:S(2)}) collective-permute-start(bf16[384,960]{0,1:T(8,128)(2,1)} %copy.78), channel_id=1, source_target_pairs={{1,0},{2,1},{3,2},{5,4},{6,5},{7,6},{9,8},{10,9},{11,10},{13,12},{... | collective-permute-start | bytes 2211848 | tf_op jit(solution)/shard_map/ppermute | solution.py:550
  208.9 39.3 %collective-permute-start.1 = (bf16[384,960]{0,1:T(8,128)(2,1)}, bf16[384,960]{0,1:T(8,128)(2,1)}, u32[]{:S(2)}, u32[]{:S(2)}) collective-permute-start(bf16[384,960]{0,1:T(8,128)(2,1)} %copy.80), channel_id=1, source_target_pairs={{0,1},{1,2},{2,3},{4,5},{5,6},{6,7},{8,9},{9,10},{10,11},{12,13},{... | collective-permute-start | bytes 2211848 | tf_op jit(solution)/shard_map/ppermute | solution.py:551
  249.5 52.7 %copy-start.6 = (bf16[384,192]{1,0:T(8,128)(2,1)S(1)}, bf16[384,192]{1,0:T(8,128)(2,1)}, u32[]{:S(2)}) copy-start(bf16[384,192]{1,0:T(8,128)(2,1)} %get-tuple-element.179) | copy-start | bytes 442372
  249.6 53.5 %copy-start.10 = (f32[8,768]{1,0:T(8,128)S(1)}, f32[8,768]{1,0:T(8,128)}, u32[]{:S(2)}) copy-start(f32[8,768]{1,0:T(8,128)} %get-tuple-element.101) | copy-start | bytes 73732
  249.6 53.5 %copy-start.11 = (f32[4,1,768]{2,1,0:T(1,128)S(1)}, f32[4,1,768]{2,1,0:T(1,128)}, u32[]{:S(2)}) copy-start(f32[4,1,768]{2,1,0:T(1,128)} %get-tuple-element.110) | copy-start | bytes 36868
  249.6 53.5 %copy-start.12 = (f32[8,192]{1,0:T(8,128)S(1)}, f32[8,192]{1,0:T(8,128)}, u32[]{:S(2)}) copy-start(f32[8,192]{1,0:T(8,128)} %get-tuple-element.113) | copy-start | bytes 18436
  249.6 53.5 %copy-start.13 = (f32[2,768]{1,0:T(2,128)S(1)}, f32[2,768]{1,0:T(2,128)}, u32[]{:S(2)}) copy-start(f32[2,768]{1,0:T(2,128)} %get-tuple-element.100) | copy-start | bytes 18436
  249.6 53.5 %copy-start.14 = (f32[4,1,192]{2,1,0:T(1,128)S(1)}, f32[4,1,192]{2,1,0:T(1,128)}, u32[]{:S(2)}) copy-start(f32[4,1,192]{2,1,0:T(1,128)} %get-tuple-element.116) | copy-start | bytes 9220
  249.6 53.5 %copy-start.16 = (f32[2,256]{1,0:T(2,128)S(1)}, f32[2,256]{1,0:T(2,128)}, u32[]{:S(2)}) copy-start(f32[2,256]{1,0:T(2,128)} %get-tuple-element.112) | copy-start | bytes 6148
  250.9 441.2 %all-gather.9.cloned.1.call-start = ((), (), s32[]{:S(2)}) async-start(), calls=%async_computation.4 | async-start | bytes 2654208 | tf_op jit(solution)/shard_map/all_gather | solution.py:559
  659.6 5.4 copy-start
  667.7 28.6 %copy-start.5 = (f32[192,192]{1,0:T(8,128)S(1)}, f32[192,192]{1,0:T(8,128)}, u32[]{:S(2)}) copy-start(f32[192,192]{1,0:T(8,128)} %get-tuple-element.255) | copy-start | bytes 442372
Sparse Core Ops, SparseCore 0:
  11.5 90.9 all-gather.10
  155.0 147.1 reduce-scatter.1
  310.3 135.7 all-reduce.9
  452.2 143.1 all-reduce.7
  597.5 62.0 all-gather.6
  661.5 30.5 all-gather.8

commit v2 on v1

v2 whole, which is shorter than its diff:
```python
import functools
import math

import jax
import jax.numpy as jnp
from jax import lax
from jax.experimental import pallas as pl
from jax.experimental.pallas import tpu as pltpu
from jax.sharding import PartitionSpec as P

HEADS = 12
DOC = 2048
LANES = 128
epsilon = 1e-05
masked_score = -1e30
F32 = jnp.float32
BF = jnp.bfloat16

OWN, WINDOW, SHIFT, LOCAL, LIMIT, FLAGGED, PLACE, GROUP, HALF, PIECE, SLOT = 0, 1, 2, 3, 6, 9, 12, 15, 16, 18, 22
PIECES = 8
VMEM_LIMIT = 56 << 20
PER_MICROSECOND = 1e9
MICROSECONDS = {
    "pack": 2, "project": 9, "attend": 11, "first_norm": 7, "shard": 6, "turn": 24, "lower": 5, "ffn_keep": 9,
    "attend_back": 20, "sides": 7, "copied_send": 11, "own": 7, "copied_keep": 9, "input_final": 3,
    "ffn_spread": 3, "ffn_final": 4, "copied_spread": 2, "copied_final": 8,
}


def nn(a, b):
    return lax.dot_general(a, b, (((1,), (0,)), ((), ())), preferred_element_type=F32)


def nt(a, b):
    return lax.dot_general(a, b, (((1,), (1,)), ((), ())), preferred_element_type=F32)


def tn(a, b):
    return lax.dot_general(a, b, (((0,), (0,)), ((), ())), preferred_element_type=F32)


def mean(values):
    return jnp.mean(values, axis=-1, keepdims=True)


def column_sum(values):
    return jnp.sum(values.astype(F32), axis=0, keepdims=True)


def normalised(values):
    centre = values - mean(values)
    scale = lax.rsqrt(mean(centre * centre) + epsilon)
    return centre * scale, scale


def norm_back(upstream, normal, scale, gain_row):
    u = upstream * gain_row
    return scale * (u - mean(u) - normal * mean(u * normal))


def lanes_of(start):
    return pl.ds(pl.multiple_of(start, LANES), LANES)


def head_masks(pair, text_scale, layout_scale):
    lane = lax.broadcasted_iota(jnp.int32, (1, LANES), 1)
    first = 32 * pair - LANES * (pair // 4)
    text_a = jnp.where(lane < 64, text_scale, 0.0)
    text_b = jnp.where(lane < 64, 0.0, text_scale)
    layout_a = jnp.where((lane >= first) & (lane < first + 16), layout_scale, 0.0)
    layout_b = jnp.where((lane >= first + 16) & (lane < first + 32), layout_scale, 0.0)
    return text_a, layout_a, text_b, layout_b


def stack_heads(text, layout, masks):
    text_a, layout_a, text_b, layout_b = (m.astype(BF) for m in masks)
    upper = jnp.concatenate([text * text_a, layout * layout_a], axis=1)
    lower = jnp.concatenate([text * text_b, layout * layout_b], axis=1)
    return jnp.concatenate([upper, lower], axis=0)


def unstack_heads(stacked, masks):
    text_a, layout_a, text_b, layout_b = masks
    upper, lower = stacked[:LANES], stacked[LANES:]
    text = upper[:, :LANES] * text_a + lower[:, :LANES] * text_b
    layout = upper[:, LANES:] * layout_a + lower[:, LANES:] * layout_b
    return text, layout


def pair_scores(stacked, keys, limit):
    scores = nt(stacked, keys)
    key = lax.broadcasted_iota(jnp.int32, (1, scores.shape[1]), 1)
    return jnp.where(key < limit, scores, masked_score)


def pack_kernel(info, widen, narrow, widen_l, narrow_l, bias, mine, small, hidden):
    rows = piece_rows(info, 0)
    mine[0] = widen[rows, :]
    mine[1] = narrow[rows, :]
    width_l = widen_l.shape[0]
    small[:, width_l:] = jnp.zeros((small.shape[0], small.shape[1] - width_l), BF)
    small[:width_l, :width_l] = widen_l[...]
    small[width_l:, :width_l] = narrow_l[...]
    high = bias[...].astype(BF).astype(F32)
    middle = (bias[...] - high).astype(BF).astype(F32)
    low = bias[...] - high - middle
    upper = jnp.concatenate([high, middle], axis=0)
    hidden[...] = jnp.concatenate([upper, jnp.concatenate([low, jnp.zeros_like(low)], axis=0)], axis=1).astype(BF)


def biases_of(hidden):
    split = hidden[...].astype(F32)
    rows = split[:8, :LANES] + split[8:, :LANES] + split[:8, LANES:]
    text = jnp.concatenate([rows[i : i + 1] for i in range(6)], axis=1)
    layout = jnp.concatenate([rows[i : i + 1] for i in (6, 7)], axis=1)
    return text, layout


def identity(size):
    row = lax.broadcasted_iota(jnp.int32, (size, size), 0)
    column = lax.broadcasted_iota(jnp.int32, (size, size), 1)
    return jnp.where(row == column, 1.0, 0.0).astype(BF)


def project_kernel(info, xt, xlt, wt, wl, bt, bl, qt, kt, vt, ql, kl, vl, xl_own, wide_l):
    own_rows, width = qt.shape
    wide = ql.shape[1]
    width_l = wl.shape[0]
    own = pl.multiple_of(info[OWN], LANES)
    start = pl.multiple_of(info[WINDOW], LANES)
    rows = pl.ds(own, own_rows)
    for i in range(3):
        wide_l[:, i * wide : i * wide + width_l] = wl[:, i * width_l : (i + 1) * width_l]
        wide_l[:, i * wide + width_l : (i + 1) * wide] = jnp.zeros((width_l, wide - width_l), BF)
    edge = jnp.zeros((1, wide - width_l), F32)
    bias = [jnp.concatenate([bl[i : i + 1, :], edge], axis=1) for i in (0, 1)]
    qt[...] = (nn(xt[rows, :], wt[:, :width]) + bt[0:1, :]).astype(BF)
    ql[...] = (tn(xlt[:, rows], wide_l[:, :wide]) + bias[0]).astype(BF)
    xl_own[...] = tn(xlt[:, rows], identity(width_l)).astype(BF)

    def part(i, carry):
        rows = pl.ds(pl.multiple_of(i * 256, 256), 256)
        from_rows = pl.ds(pl.multiple_of(start + i * 256, 256), 256)
        x = xt[from_rows, :]
        kt[rows, :] = nn(x, wt[:, width : 2 * width]).astype(BF)
        vt[rows, :] = (nn(x, wt[:, 2 * width :]) + bt[1:2, :]).astype(BF)
        x = xlt[:, from_rows]
        kl[rows, :] = tn(x, wide_l[:, wide : 2 * wide]).astype(BF)
        vl[rows, :] = (tn(x, wide_l[:, 2 * wide :]) + bias[1]).astype(BF)
        return carry

    lax.fori_loop(0, kt.shape[0] // 256, part, 0)


def attend_kernel(info, qt, kt, vt, ql, kl, vl, ct, cl, lse, cl_acc):
    own_rows, layout_width = cl.shape
    block = kt.shape[0] // 2
    cl_acc[...] = jnp.zeros_like(cl_acc)
    lse[...] = jnp.zeros_like(lse)
    lane = lax.broadcasted_iota(jnp.int32, (1, LANES), 1)

    def one_pair(pair, carry):
        text_lanes = lanes_of(pair * LANES)
        group_lanes = lanes_of((pair // 4) * LANES)
        scaled = head_masks(pair, 0.125, 0.25)
        plain = head_masks(pair, 1.0, 1.0)
        for j in range(own_rows // LANES):
            rows = pl.ds(j * LANES, LANES)
            keys_at = pl.ds(pl.multiple_of(info[LOCAL + j] * block, block), block)
            stacked = stack_heads(qt[rows, text_lanes], ql[rows, group_lanes], scaled)
            keys = jnp.concatenate([kt[keys_at, text_lanes], kl[keys_at, group_lanes]], axis=1)
            values = jnp.concatenate([vt[keys_at, text_lanes], vl[keys_at, group_lanes]], axis=1)
            scores = pair_scores(stacked, keys, info[LIMIT + j])
            highest = jnp.max(scores, axis=-1, keepdims=True)
            exponent = jnp.exp(scores - highest)
            totals = jnp.sum(exponent, axis=-1, keepdims=True)
            probs = (exponent * (1.0 / totals)).astype(BF)
            text, layout = unstack_heads(nn(probs, values), plain)
            ct[rows, text_lanes] = text.astype(BF)
            cl_acc[rows, group_lanes] += layout
            log_total = highest + jnp.log(totals)
            lse[rows, :] = (
                lse[rows, :]
                + jnp.where(lane == 2 * pair, log_total[:LANES], 0.0)
                + jnp.where(lane == 2 * pair + 1, log_total[LANES:], 0.0)
            )
        return carry

    lax.fori_loop(0, HEADS // 2, one_pair, 0)
    cl[...] = cl_acc[:, :layout_width].astype(BF)


def gelu_both(hidden):
    below = 0.5 * (1.0 + lax.erf(hidden * math.sqrt(0.5)))
    density = jnp.exp(-0.5 * hidden * hidden) * (1.0 / math.sqrt(2.0 * math.pi))
    return hidden * below, below + hidden * density


def shard_forward(low, widen, bias, narrow, active, slope, total):
    hid = widen.shape[1]
    step = 256 if hid % 256 == 0 else hid
    for n in range(hid // step):
        cols = slice(n * step, (n + 1) * step)
        value, gradient = gelu_both(nn(low[...], widen[:, cols]) + bias[:, cols])
        active[:, cols] = value.astype(BF)
        slope[:, cols] = gradient
    total[...] += nn(active[...], narrow[...])


def shard_backward(dout, narrow, slope, widen, dhid, sums, total):
    hid = widen.shape[1]
    step = 256 if hid % 256 == 0 else hid
    for n in range(hid // step):
        cols = slice(n * step, (n + 1) * step)
        dhidden = (nt(dout[...], narrow[cols, :]) * slope[:, cols]).astype(BF)
        dhid[:, cols] = dhidden
        sums[:, cols] = column_sum(dhidden)
    total[...] += nt(dhid[...], widen[...])


def first_norm_kernel(
    info, xt, xl_own, ct, cl, dense_t, dense_l, bt, bl, gt, st, gl, sl, widen, hidden, narrow,
    first_t, first_l, low_t, low_l, normed_l, active, slope, total,
):
    own_rows, width = first_t.shape
    rows = pl.ds(pl.multiple_of(info[OWN], LANES), own_rows)
    first = xt[rows, :].astype(F32) + (nn(ct[...], dense_t[...]) + bt[2:3, :])
    first_t[...] = first
    normed = normalised(first)[0] * gt[0:1, :] + st[0:1, :]
    low_t[...] = normed.astype(BF)
    total[...] = normed + bt[3:4, :]
    first = xl_own[...].astype(F32) + (nn(cl[...], dense_l[...]) + bl[2:3, :])
    first_l[...] = first
    normed = normalised(first)[0] * gl[0:1, :] + sl[0:1, :]
    low_l[...] = normed.astype(BF)
    normed_l[...] = normed + bl[3:4, :]
    shard_forward(low_t, widen, biases_of(hidden)[0], narrow, active, slope, total)


def piece_rows(info, rel):
    return pl.ds(pl.multiple_of(info[HALF + rel // 4] + info[PIECE + rel % 4], 32), 96)


def load_shard(info, plan, refs, weights, sems, at):
    copies = []
    for i, (rel, low, high) in enumerate(plan):
        copy = pltpu.make_async_copy(
            refs[i], weights.at[at, pl.ds(low, high - low), piece_rows(info, rel), :], sems.at[at, i]
        )
        copy.start()
        copies.append(copy)
    return copies


def shard_kernel(plan, info, low, total_in, hidden, *refs):
    pieces = refs[: len(plan)]
    active, slope, total, weights, sems = refs[len(plan) :]
    copies = load_shard(info, plan, pieces, weights, sems, 0)
    total[...] = total_in[...]
    for copy in copies:
        copy.wait()
    shard_forward(low, weights.at[0, 0], biases_of(hidden)[0], weights.at[0, 1], active, slope, total)


def upper_back(total, gain, shift, cot, keep, result, dout, sums):
    normal, scale = normalised(total[...])
    result[...] = (normal * gain[1:2, :] + shift[1:2, :]).astype(BF)
    upstream = cot.astype(F32) * keep
    dsecond = norm_back(upstream, normal, scale, gain[1:2, :])
    dout[...] = dsecond.astype(BF)
    sums[0:1, :] = column_sum(upstream * normal)
    sums[1:2, :] = column_sum(upstream)
    sums[2:3, :] = column_sum(dout[...])
    sums[3:4, :] = jnp.zeros_like(sums[3:4, :])
    total[...] = dsecond


def turn_kernel(plans, info, *refs):
    refs = list(refs)
    take = lambda n: [refs.pop(0) for _ in range(n)]
    low, total_in, gain, shift, cot, widen_own, narrow_own = take(7)
    slopes_in, actives = take(3), take(3)
    low_l, normed_l, gain_l, shift_l, cot_lt = take(5)
    small, hidden = take(4), take(4)
    pieces = [take(len(plan)) for plan in plans]
    result, dout, dhid, dnormed, sums, hsums, active = take(7)
    result_lt, dnormed_l, sums_l, hsums_l = take(4)
    send_a, send_b, pack = take(3)
    weights, slope, slope_l, active_l, dhid_l, dout_l, result_l, grad, sems = take(9)
    shards = dhid.shape[0]
    copies = [load_shard(info, plan, piece, weights, sems, s) for s, (plan, piece) in enumerate(zip(plans, pieces))]
    dnormed[...] = total_in[...]
    dnormed_l[...] = normed_l[...]
    row = lax.broadcasted_iota(jnp.int32, (LANES, 1), 0)
    keep = []
    for j in range(low.shape[0] // LANES):
        place = row + info[PLACE + j]
        keep.append(jnp.where((place >= info[FLAGGED + j]) & (place < info[LIMIT + j]), 1.0, 0.0))
    keep = jnp.concatenate(keep, axis=0)

    width_l = low_l.shape[1]
    for s in range(shards):
        widen, narrow = (small[s][i * width_l : (i + 1) * width_l, :width_l] for i in (0, 1))
        shard_forward(low_l, widen, biases_of(hidden[s])[1][:, :width_l], narrow, active_l.at[s], slope_l.at[s], dnormed_l)
    cot_l = tn(cot_lt[...], identity(width_l))
    upper_back(dnormed_l, gain_l, shift_l, cot_l, keep, result_l, dout_l, sums_l)
    result_lt[...] = nt(identity(width_l), result_l[...]).astype(BF)
    for s in range(shards):
        widen, narrow = (small[s][i * width_l : (i + 1) * width_l, :width_l] for i in (0, 1))
        shard_backward(dout_l, narrow, slope_l.at[s], widen, dhid_l.at[s], hsums_l.at[s], dnormed_l)
    for s in range(shards):
        pack[s] = jnp.zeros_like(pack[s])
        g = tn(active_l[s], dout_l[...]).astype(BF)
        pack[s, :128, :width_l] = g[:128]
        pack[s, :64, 512 : 512 + width_l] = g[128:]
        g = tn(low_l[...], dhid_l[s]).astype(BF)
        pack[s, :128, 256 : 256 + width_l] = g[:128]
        pack[s, 64:, 512 : 512 + width_l] = g[128:]

    for copy in copies[1]:
        copy.wait()
    shard_forward(low, weights.at[1, 0], biases_of(hidden[2])[0], weights.at[1, 1], active, slope, dnormed)
    upper_back(dnormed, gain, shift, cot[...], keep, result, dout, sums)
    shard_backward(dout, narrow_own, slopes_in[0], widen_own, dhid.at[0], hsums.at[0], dnormed)
    for copy in copies[0] + copies[2]:
        copy.wait()
    shard_backward(dout, weights.at[0, 1], slopes_in[1], weights.at[0, 0], dhid.at[1], hsums.at[1], dnormed)
    shard_backward(dout, weights.at[1, 1], slope, weights.at[1, 0], dhid.at[2], hsums.at[2], dnormed)
    shard_backward(dout, weights.at[2, 1], slopes_in[2], weights.at[2, 0], dhid.at[3], hsums.at[3], dnormed)

    half = pl.ds(pl.multiple_of(info[HALF + 1], LANES), grad.shape[0])
    for s, act in enumerate((actives[0], actives[1], active, actives[2])):
        grad[...] = tn(act[:, half], dout[...])

        def store_a(rel, rows, s=s):
            send_a[s, rel % 2, rel // 2, :96] = rows.astype(BF)
            send_a[s, rel % 2, rel // 2, 96:] = pack[s, extra_rows(info, 1, rel), :]

        pieces_of(info, grad, store_a)
        grad[...] = tn(low[:, half], dhid[s])

        def store_b(rel, rows, s=s):
            send_b[s, rel // 2, rel % 2] = rows.astype(BF)

        pieces_of(info, grad, store_b)


def lower_back(first, dnormed, gain, dense, dfirst, dbranch, dcontext, sums):
    width = first.shape[1]
    wide = dcontext.shape[1]
    normal, scale = normalised(first[...])
    back = norm_back(dnormed[...], normal, scale, gain[0:1, :])
    sums[0:1, :] = column_sum(dnormed[...] * normal)
    sums[1:2, :] = column_sum(dnormed[...])
    dfirst[...] = back
    dbranch[...] = back.astype(BF)
    sums[2:3, :] = column_sum(dbranch[...])
    sums[3:4, :] = jnp.zeros_like(sums[3:4, :])
    dc = nt(dbranch[...], dense[...]).astype(BF)
    dcontext[:, :width] = dc
    if wide > width:
        dcontext[:, width:] = jnp.zeros((dc.shape[0], wide - width), BF)


def lower_kernel(
    info, first, dnormed, gain, dense, first_l, dnormed_l, gain_l, dense_l,
    dfirst, dbranch, dcontext, sums, dfirst_lt, dbranch_l, dcontext_l, sums_l, dfirst_l,
):
    lower_back(first, dnormed, gain, dense, dfirst, dbranch, dcontext, sums)
    lower_back(first_l, dnormed_l, gain_l, dense_l, dfirst_l, dbranch_l, dcontext_l, sums_l)
    dfirst_lt[...] = jnp.transpose(dfirst_l[...])


EXTRA = 16


def extra_rows(info, half, rel):
    return pl.ds(pl.multiple_of((info[HALF + half] + info[PIECE + rel]) // 6, EXTRA), EXTRA)


def pieces_of(info, grad, store):
    for rel in range(4):
        store(rel, grad[pl.ds(pl.multiple_of(info[PIECE + rel], 32), 96), :])


def ffn_keep_kernel(
    info, a0, a1, a2, a3, dout, low, dhid, recv_a, recv_b, pack, next_a, keep_a, next_b, keep_b, grad,
):
    half = pl.ds(pl.multiple_of(info[HALF], LANES), grad.shape[0])
    for s, active in enumerate((a0, a1, a2, a3)):
        grad[...] = tn(active[:, half], dout[...])

        def store_a(rel, rows, s=s):
            to = next_a if rel % 2 else keep_a
            recv = recv_a[s, rel % 2, rel // 2].astype(F32)
            to[rel // 2, s, :96] = (rows + recv[:96]).astype(BF)
            to[rel // 2, s, 96:] = (pack[s, extra_rows(info, 0, rel), :].astype(F32) + recv[96:]).astype(BF)

        pieces_of(info, grad, store_a)
        grad[...] = tn(low[:, half], dhid[s])

        def store_b(rel, rows, s=s):
            to = next_b if rel // 2 else keep_b
            to[rel % 2, s] = (rows + recv_b[s, rel // 2, rel % 2].astype(F32)).astype(BF)

        pieces_of(info, grad, store_b)


def add(a, b, *more):
    total = a.astype(F32) + b.astype(F32)
    for value in more:
        total = total + value.astype(F32)
    return total.astype(BF)


def add_split(keep, recv):
    return add(keep[1], recv[1]), add(keep[0], recv[0])


def ffn_spread_kernel(info, keep_a, recv_a, keep_b, recv_b, *outs):
    rows = keep_a.shape[1]
    for k, out in enumerate(outs):
        out[:rows] = (keep_a[k].astype(F32) + recv_a[k].astype(F32)).astype(out.dtype)
        out[rows:] = (keep_b[k].astype(F32) + recv_b[k].astype(F32)).astype(out.dtype)


def copied_spread_kernel(info, keep_a, recv_a, keep_b, recv_b, *outs):
    for k, out in enumerate(outs):
        keep, recv = (keep_a, recv_a) if k < 2 else (keep_b, recv_b)
        out[...] = (keep[k % 2].astype(F32) + recv[k % 2].astype(F32)).astype(out.dtype)


def ffn_final_kernel(plan, info, *refs):
    pieces, (narrow, widen, narrow_l, widen_l, pack) = refs[: len(plan)], refs[len(plan) :]
    for piece, (rel, low, high) in zip(pieces, plan):
        rows = piece_rows(info, rel)
        if low == 0:
            narrow[rows, :] = piece[:96].astype(F32)
            pack[extra_rows(info, rel // 4, rel % 4), :] = piece[96:112].astype(F32)
        if high > 112:
            widen[rows, :] = piece[112 - low :].astype(F32)
    width_l = narrow_l.shape[0]
    narrow_l[:128] = pack[:, :width_l]
    narrow_l[128:] = pack[:64, 512 : 512 + width_l]
    widen_l[:128] = pack[:, 256 : 256 + width_l]
    widen_l[128:] = pack[64:, 512 : 512 + width_l]


def copied_final_kernel(plan, info, *refs):
    pieces, refs = refs[: len(plan)], refs[len(plan) :]
    project, dense, project_l, dense_l = refs[:4]
    vectors, vectors_l, (extra,) = refs[4:8], refs[8:12], refs[12:]
    width = dense.shape[1]
    for piece, (rel, low, high) in zip(pieces, plan):
        rows = piece_rows(info, rel)
        for part in range(low, high):
            block = lax.rem(info[GROUP] + part, 4)
            at = pl.ds(pl.multiple_of(128 * block + (info[HALF + rel // 4] + info[PIECE + rel % 4]) // 6, EXTRA), EXTRA)
            extra[at, :] = piece[part - low, 96:].astype(F32)

            @pl.when(block < 3)
            def _():
                project[rows, pl.ds(pl.multiple_of(block * width, LANES), width)] = piece[part - low, :96].astype(F32)

            @pl.when(block == 3)
            def _():
                dense[rows, :] = piece[part - low, :96].astype(F32)

    width_l = dense_l.shape[0]
    for i in range(3):
        project_l[:, i * width_l : (i + 1) * width_l] = extra[:width_l, i * 256 : i * 256 + width_l]
    dense_l[...] = extra[width_l : 2 * width_l, :width_l]
    for at, (biases, gains, shifts, hidden), lanes in ((2 * width_l, vectors, width), (2 * width_l + 16, vectors_l, width_l)):
        rows = extra[at : at + 16, :lanes]
        for i, row in enumerate((8, 9, 6, 2)):
            biases[i : i + 1, :] = rows[row : row + 1]
        gains[0:1, :] = rows[4:5]
        gains[1:2, :] = rows[0:1]
        shifts[0:1, :] = rows[5:6]
        shifts[1:2, :] = rows[1:2]
        hidden[...] = extra[pl.ds(at + 12 + info[GROUP], 1), :lanes]


def attend_back_kernel(
    info, qt, kt, vt, ql, kl, vl, dct, dcl, lse,
    dq, dk, dv, dq_l, dk_l, dv_l,
    k_acc, v_acc, kl_acc, vl_acc, ql_acc,
):
    own_rows = qt.shape[0]
    window = kt.shape[0]
    block = window // 2
    pad = (dk.shape[0] - window) // 2
    for acc in (k_acc, v_acc, kl_acc, vl_acc, ql_acc):
        acc[...] = jnp.zeros_like(acc)
    for out in (dk, dv, dk_l, dv_l):
        edge = jnp.zeros((pad, out.shape[1]), BF)
        out[:pad, :] = edge
        out[pad + window :, :] = edge
    lane = lax.broadcasted_iota(jnp.int32, (1, LANES), 1)

    def one_pair(pair, carry):
        text_lanes = lanes_of(pair * LANES)
        group_lanes = lanes_of((pair // 4) * LANES)
        scaled = head_masks(pair, 0.125, 0.25)
        plain = head_masks(pair, 1.0, 1.0)
        for j in range(own_rows // LANES):
            rows = pl.ds(j * LANES, LANES)
            keys_at = pl.ds(pl.multiple_of(info[LOCAL + j] * block, block), block)
            stacked = stack_heads(qt[rows, text_lanes], ql[rows, group_lanes], scaled)
            keys = jnp.concatenate([kt[keys_at, text_lanes], kl[keys_at, group_lanes]], axis=1)
            values = jnp.concatenate([vt[keys_at, text_lanes], vl[keys_at, group_lanes]], axis=1)
            dcs = stack_heads(dct[rows, text_lanes], dcl[rows, group_lanes], plain)
            logs = lse[rows, :]
            log_total = jnp.concatenate(
                [
                    jnp.sum(jnp.where(lane == 2 * pair, logs, 0.0), axis=1, keepdims=True),
                    jnp.sum(jnp.where(lane == 2 * pair + 1, logs, 0.0), axis=1, keepdims=True),
                ],
                axis=0,
            )
            probs = jnp.exp(pair_scores(stacked, keys, info[LIMIT + j]) - log_total)
            dprobs = nt(dcs, values)
            inner = jnp.sum(probs * dprobs, axis=1, keepdims=True)
            dscores = (probs * (dprobs - inner)).astype(BF)
            text, layout = unstack_heads(nn(dscores, keys), scaled)
            dq[rows, text_lanes] = text.astype(BF)
            ql_acc[rows, group_lanes] += layout
            both = tn(dscores, stacked)
            k_acc[keys_at, text_lanes] += both[:, :LANES]
            kl_acc[keys_at, group_lanes] += both[:, LANES:]
            both = tn(probs.astype(BF), dcs)
            v_acc[keys_at, text_lanes] += both[:, :LANES]
            vl_acc[keys_at, group_lanes] += both[:, LANES:]
        return carry

    lax.fori_loop(0, HEADS // 2, one_pair, 0)
    middle = pl.ds(pad, window)
    dk[middle, :] = k_acc[...].astype(BF)
    dv[middle, :] = v_acc[...].astype(BF)
    dk_l[middle, :] = kl_acc[...].astype(BF)
    dv_l[middle, :] = vl_acc[...].astype(BF)
    dq_l[...] = ql_acc[...].astype(BF)


def key_value_grad(info, at, rows_out, wt, wl, dk, dv, dk_l, dv_l):
    width, wide = dk.shape[1], dk_l.shape[1]
    rows = pl.ds(pl.multiple_of(info[SHIFT] + at, LANES), rows_out)
    text = nt(dk[rows, :], wt[:, width : 2 * width]) + nt(dv[rows, :], wt[:, 2 * width :])
    layout = nt(wl[:, wide : 2 * wide], dk_l[rows, :]) + nt(wl[:, 2 * wide :], dv_l[rows, :])
    return text, layout


def store_packed(out, text, layout):
    own_rows = text.shape[0]
    half = layout.shape[0] // 2
    out[:own_rows, :] = text.astype(BF)
    out[own_rows:, :own_rows] = layout[:half].astype(BF)
    out[own_rows:, own_rows:] = layout[half:].astype(BF)


def sides_kernel(info, wt, wl, dk, dv, dk_l, dv_l, left, right):
    own_rows = left.shape[0] * 4 // 5
    for side, shift in ((left, 0), (right, 2 * own_rows)):
        store_packed(side, *key_value_grad(info, shift, own_rows, wt, wl, dk, dv, dk_l, dv_l))


def own_kernel(info, wt, wl, dq, dk, dv, dq_l, dk_l, dv_l, dfirst_t, dfirst_lt, left, right, out):
    own_rows, width = dq.shape
    wide = dq_l.shape[1]
    half = dfirst_lt.shape[0] // 2
    text, layout = key_value_grad(info, own_rows, own_rows, wt, wl, dk, dv, dk_l, dv_l)
    text = dfirst_t[...] + text + nt(dq[...], wt[:, :width])
    layout = dfirst_lt[...] + layout + nt(wl[:, :wide], dq_l[...])
    got = left[...].astype(F32) + right[...].astype(F32)
    text = text + got[:own_rows]
    layout = layout + jnp.concatenate([got[own_rows:, :own_rows], got[own_rows:, own_rows:]], axis=0)
    store_packed(out, text, layout)


def input_final_kernel(info, rows, text, layout):
    own_rows = rows.shape[1] * 4 // 5
    half = layout.shape[0] // 2
    for t in range(rows.shape[0]):
        at = pl.ds(t * own_rows, own_rows)
        text[at, :] = rows[t, :own_rows, :].astype(F32)
        layout[:half, at] = rows[t, own_rows:, :own_rows].astype(F32)
        layout[half:, at] = rows[t, own_rows:, own_rows:].astype(F32)


def extras(
    info, xlt, dq, dv, dq_l, dk_l, dv_l, cl, db_l, sums_a, sums_b, hsums, sums_al, sums_bl, hsums_l, extra, small,
):
    own_rows = dq.shape[0]
    wide = dq_l.shape[1]
    width_l = xlt.shape[0]
    window = dk_l.shape[0] - 2 * own_rows
    own = pl.ds(pl.multiple_of(info[OWN], LANES), own_rows)
    seen = pl.ds(pl.multiple_of(info[WINDOW], LANES), window)
    middle = pl.ds(own_rows, window)
    extra[width_l:, :] = jnp.zeros((extra.shape[0] - width_l, extra.shape[1]), BF)
    extra[:width_l, :wide] = nn(xlt[:, own], dq_l[...]).astype(BF)
    extra[:width_l, wide : 2 * wide] = nn(xlt[:, seen], dk_l[middle, :]).astype(BF)
    extra[:width_l, 2 * wide : 3 * wide] = nn(xlt[:, seen], dv_l[middle, :]).astype(BF)
    extra[width_l : 2 * width_l, :width_l] = tn(cl[...], db_l[...]).astype(BF)
    small[...] = jnp.zeros_like(small)
    small[0:4, :] = sums_a[...]
    small[4:8, :] = sums_b[...]
    small[8:9, :] = column_sum(dq[...])
    small[9:10, :] = column_sum(dv[middle, :])
    small[16:20, :width_l] = sums_al[...]
    small[20:24, :width_l] = sums_bl[...]
    small[24:25, :wide] = column_sum(dq_l[...])
    small[25:26, :wide] = column_sum(dv_l[middle, :])
    for s in range(4):
        group = lax.rem(info[GROUP] + s, 4)
        small[pl.ds(12 + group, 1), :] = hsums[s]
        small[pl.ds(28 + group, 1), :width_l] = hsums_l[s]
    extra[2 * width_l : 2 * width_l + 32, :] = small[...].astype(BF)


def copied_grads(info, xt, dq, dk, dv, ct, db, half, grad, store):
    own_rows = dq.shape[0]
    window = dk.shape[0] - 2 * own_rows
    own = pl.ds(pl.multiple_of(info[OWN], LANES), own_rows)
    seen = pl.ds(pl.multiple_of(info[WINDOW], LANES), window)
    middle = pl.ds(own_rows, window)
    for block in range(4):
        if block == 0:
            grad[...] = tn(xt[own, half], dq[...])
        elif block == 1:
            grad[...] = tn(xt[seen, half], dk[middle, :])
        elif block == 2:
            grad[...] = tn(xt[seen, half], dv[middle, :])
        else:
            grad[...] = tn(ct[:, half], db[...])
        slot = info[SLOT + block]
        for p in range(2):
            for q in range(2):
                row = jnp.where(slot < 2, info[PIECE + p + 2 * q], info[PIECE + q + 2 * p])
                store(block, slot, p, q, row, grad[pl.ds(pl.multiple_of(row, 32), 96), :])


def copied_send_kernel(
    info, xt, dq, dk, dv, ct, db, xlt, dq_l, dk_l, dv_l, cl, db_l, sums_a, sums_b, hsums, sums_al, sums_bl, hsums_l,
    send, extra, grad, small,
):
    half = pl.ds(pl.multiple_of(info[HALF + 1], LANES), grad.shape[0])
    extras(info, xlt, dq, dv, dq_l, dk_l, dv_l, cl, db_l, sums_a, sums_b, hsums, sums_al, sums_bl, hsums_l, extra, small)

    def store(block, slot, p, q, row, rows):
        at = pl.multiple_of(128 * block + (info[HALF + 1] + row) // 6, EXTRA)
        send[slot, p, q, :96] = rows.astype(BF)
        send[slot, p, q, 96:] = extra[pl.ds(at, EXTRA), :]

    copied_grads(info, xt, dq, dk, dv, ct, db, half, grad, store)


def copied_keep_kernel(info, xt, dq, dk, dv, ct, db, extra, recv, next_a, keep_a, next_b, keep_b, grad):
    half = pl.ds(pl.multiple_of(info[HALF], LANES), grad.shape[0])

    def store(block, slot, p, q, row, rows):
        at = pl.multiple_of(128 * block + (info[HALF] + row) // 6, EXTRA)
        got = recv[slot, p, q].astype(F32)
        text = (rows + got[:96]).astype(BF)
        rest = (extra[pl.ds(at, EXTRA), :].astype(F32) + got[96:]).astype(BF)

        @pl.when(slot < 2)
        def _():
            (next_a if p else keep_a)[q, slot, :96] = text
            (next_a if p else keep_a)[q, slot, 96:] = rest

        @pl.when(slot >= 2)
        def _():
            (next_b if p else keep_b)[q, slot - 2, :96] = text
            (next_b if p else keep_b)[q, slot - 2, 96:] = rest

    copied_grads(info, xt, dq, dk, dv, ct, db, half, grad, store)


SM = pl.BlockSpec(memory_space=pltpu.SMEM)
VM = pl.BlockSpec(memory_space=pltpu.VMEM)
HB = pl.BlockSpec(memory_space=pl.ANY)


def call(name, kernel, operands, outs, scratch=(), after=(), in_hbm=0):
    operands = tuple(operands)
    outs = tuple(outs) + (shape((8, LANES), F32),)
    specs = [HB] * len(after) + [SM] + [VM] * (len(operands) - 1 - in_hbm) + [HB] * in_hbm
    operands = tuple(after) + operands
    at = len(operands) + len(outs) - 1

    def with_token(*refs):
        kernel(*refs[len(after) : at], *refs[at + 1 :])
        refs[at][...] = jnp.zeros_like(refs[at])

    return pl.pallas_call(
        with_token,
        out_shape=outs,
        in_specs=specs,
        out_specs=[VM] * len(outs),
        scratch_shapes=list(scratch),
        cost_estimate=pl.CostEstimate(flops=int(MICROSECONDS[name] * PER_MICROSECOND), bytes_accessed=0, transcendentals=0),
        compiler_params=pltpu.CompilerParams(vmem_limit_bytes=VMEM_LIMIT),
        name=name,
    )(*operands)


def shape(dims, dtype=BF):
    return jax.ShapeDtypeStruct(dims, dtype)


def flip(planes, bit):
    return [(i, i ^ bit) for i in range(planes)]


def tie(value, *tokens):
    return lax.optimization_barrier((value, tokens))[0]


def spread(piece, planes, split, mid=None, second=(), third=()):
    parts = piece.shape[0]
    core, x, y = 1, 2, 4
    send = lambda v, bit: lax.ppermute(v, "dp", flip(planes, bit))
    later = lambda v, tokens: tie(v, *tokens) if tokens else v
    by_x, by_y = send(piece, x), send(piece, y)
    held = [(later(v, second), rel, 0, parts) for rel, v in enumerate((piece, by_x, by_y))]
    by_x, by_y = held[1][0], held[2][0]
    if split == "x":
        forwarded = [(send(by_x, y), 3, 0, parts)]
    elif split == "y":
        forwarded = [(send(by_y, x), 3, 0, parts)]
    else:
        mid = mid or parts // 2
        forwarded = [(send(by_x[:mid], y), 3, 0, mid), (send(by_y[mid:], x), 3, mid, parts)]
    held += [(later(v, third), rel, low, high) for v, rel, low, high in forwarded]
    held += [(send(v, core), rel + 4, low, high) for v, rel, low, high in held]
    return [h[0] for h in held], tuple(h[1:] for h in held)


def per_device(
    text_input, layout_input, block_starts, intersection_flags, text_cotangent, layout_cotangent,
    text_project, text_biases, text_dense, text_gains, text_shifts, text_widen, text_hidden_bias, text_narrow,
    layout_project, layout_biases, layout_dense, layout_gains, layout_shifts, layout_widen, layout_hidden_bias,
    layout_narrow,
):
    blocks, length = intersection_flags.shape
    total = blocks * length
    groups = lax.axis_size("tensor")
    planes = lax.axis_size("dp")
    own = total // groups
    tiles = own // LANES
    width = text_input.shape[1]
    width_l = layout_input.shape[1]
    wide = 2 * LANES
    window = 2 * length
    padded = window + 2 * own
    hid = text_narrow.shape[0]
    hid_l = layout_narrow.shape[0]
    piece = width // PIECES
    t = lax.axis_index("tensor").astype(jnp.int32)
    me = lax.axis_index("dp").astype(jnp.int32)
    core, x_bit, y_bit = me & 1, (me >> 1) & 1, (me >> 2) & 1

    def row_of(rc, rx, ry):
        return 4 * piece * (core ^ rc) + piece * ((x_bit ^ rx) + 2 * (y_bit ^ ry))

    flagged = jnp.sum(intersection_flags, axis=1, dtype=jnp.int32)
    base = jnp.minimum((t * own) // length, blocks - 2)
    tile_rows = t * own + LANES * jnp.arange(tiles, dtype=jnp.int32)
    tile_block = tile_rows // length
    pick = tile_block[:, None] == jnp.arange(blocks, dtype=jnp.int32)[None, :]
    limit = DOC - jnp.sum(jnp.where(pick, block_starts[None, :], 0), axis=1)
    flags_of = jnp.sum(jnp.where(pick, flagged[None, :], 0), axis=1)
    info = jnp.concatenate(
        [
            jnp.stack([t * own, base * length, t * own - base * length]),
            tile_block - base,
            limit,
            flags_of,
            tile_rows - tile_block * length,
            jnp.stack(
                [t, 4 * piece * core, 4 * piece * (1 - core)]
                + [row_of(0, rx, ry) - 4 * piece * core for ry in (0, 1) for rx in (0, 1)]
                + [(b - t) % groups for b in range(4)]
            ),
        ]
    ).astype(jnp.int32)

    shift_from = lambda k: [(i, (i - k) % groups) for i in range(groups)]
    shift_to = lambda k: [(i, (i + k) % groups) for i in range(groups)]
    bias = jnp.concatenate([text_hidden_bias, layout_hidden_bias, jnp.zeros((8 * LANES - hid - hid_l,), F32)])
    mine, small, hidden, packed_up = call(
        "pack", pack_kernel,
        (info, text_widen, text_narrow, layout_widen, layout_narrow, bias.reshape(8, LANES)),
        (shape((2, piece, width)), shape((2 * width_l, wide)), shape((16, wide))),
    )
    come = {k: lax.ppermute(mine, "tensor", shift_from(k)) for k in (1, 3)}
    hiddens = [hidden] + [lax.ppermute(hidden, "tensor", shift_from(k)) for k in (1, 2, 3)]

    xlt = layout_input.T
    qt, kt, vt, ql, kl, vl, xl_own, wl, projected = call(
        "project", project_kernel,
        (info, text_input, xlt, text_project, layout_project, text_biases, layout_biases),
        (shape((own, width)), shape((window, width)), shape((window, width)),
         shape((own, wide)), shape((window, wide)), shape((window, wide)),
         shape((own, width_l)), shape((width_l, 3 * wide))),
        after=(packed_up,),
    )
    come[2] = lax.ppermute(tie(mine, projected), "tensor", shift_from(2))
    ct, cl, lse, attended = call(
        "attend", attend_kernel,
        (info, qt, kt, vt, ql, kl, vl),
        (shape((own, width)), shape((own, width_l)), shape((own, LANES), F32)),
        scratch=(pltpu.VMEM((own, wide), F32),),
    )
    first_t, first_l, low_t, low_l, normed_l, active0, slope0, total_t, first_done = call(
        "first_norm", first_norm_kernel,
        (info, text_input, xl_own, ct, cl, text_dense, layout_dense, text_biases, layout_biases,
         text_gains, text_shifts, layout_gains, layout_shifts, text_widen, hidden, text_narrow),
        (shape((own, width), F32), shape((own, width_l), F32), shape((own, width)), shape((own, width_l)),
         shape((own, width_l), F32), shape((own, hid)), shape((own, hid), F32), shape((own, width), F32)),
    )
    shards = {
        k: spread(tie(come[k], projected), planes, {1: "x", 3: "y"}[k], second=(attended,), third=(first_done,)) for k in (1, 3)
    }
    smalls = [small] + [lax.ppermute(tie(small, first_done), "tensor", shift_from(k)) for k in (1, 2, 3)]
    actives, slopes, shard_done = {0: active0}, {0: slope0}, {}
    for k in (1, 3):
        arrays, plan = shards[k]
        actives[k], slopes[k], total_t, shard_done[k] = call(
            "shard", functools.partial(shard_kernel, plan),
            (info, low_t, total_t, hiddens[k], *arrays),
            (shape((own, hid)), shape((own, hid), F32), shape((own, width), F32)),
            scratch=(pltpu.VMEM((1, 2, width, hid), BF), pltpu.SemaphoreType.DMA((1, len(plan)))),
            in_hbm=len(plan),
        )
    shards[2] = spread(tie(come[2], first_done), planes, "half", second=(shard_done[1],), third=(shard_done[3],))
    plans = tuple(shards[k][1] for k in (1, 2, 3))
    arrays = sum((shards[k][0] for k in (1, 2, 3)), [])
    rows_a = piece + EXTRA
    outs = call(
        "turn", functools.partial(turn_kernel, plans),
        (info, low_t, total_t, text_gains, text_shifts, text_cotangent, text_widen, text_narrow,
         slopes[0], slopes[1], slopes[3], actives[0], actives[1], actives[3],
         low_l, normed_l, layout_gains, layout_shifts, layout_cotangent.T, *smalls, *hiddens, *arrays),
        (shape((own, width)), shape((own, width)), shape((groups, own, hid)), shape((own, width), F32),
         shape((4, width), F32), shape((groups, 1, hid), F32), shape((own, hid)),
         shape((width_l, own)), shape((own, width_l), F32), shape((4, width_l), F32), shape((groups, 1, hid_l), F32),
         shape((groups, 2, 2, rows_a, width)), shape((groups, 2, 2, piece, width)), shape((groups, 128, width))),
        scratch=(pltpu.VMEM((3, 2, width, hid), BF), pltpu.VMEM((own, hid), F32),
                 pltpu.VMEM((groups, own, hid_l), F32), pltpu.VMEM((groups, own, hid_l), BF),
                 pltpu.VMEM((groups, own, hid_l), BF), pltpu.VMEM((own, width_l), BF), pltpu.VMEM((own, width_l), BF),
                 pltpu.VMEM((4 * piece, width), F32), pltpu.SemaphoreType.DMA((3, max(map(len, plans))))),
        in_hbm=len(arrays),
    )
    result_t, dout_t, dhid_t, dnormed_t, sums_t, hsums_t, actives[2] = outs[:7]
    result_lt, dnormed_l, sums_l, hsums_l, send_a, send_b, pack, turned = outs[7:]

    in_order = [actives[k] for k in range(4)]
    across = lambda v, bit: lax.ppermute(v, "dp", flip(planes, bit))
    recv_a, recv_b = across(send_a, 1), across(send_b, 1)
    dfirst_t, db_t, dc_t, low_sums_t, dfirst_lt, db_l, dc_l, low_sums_l, lowered = call(
        "lower", lower_kernel,
        (info, first_t, dnormed_t, text_gains, text_dense, first_l, dnormed_l, layout_gains, layout_dense),
        (shape((own, width), F32), shape((own, width)), shape((own, width)), shape((4, width), F32),
         shape((width_l, own), F32), shape((own, width_l)), shape((own, wide)), shape((4, width_l), F32)),
        scratch=(pltpu.VMEM((own, width_l), F32),),
    )
    next_a, keep_a, next_b, keep_b, kept = call(
        "ffn_keep", ffn_keep_kernel,
        (info, *in_order, dout_t, low_t, dhid_t, recv_a, recv_b, pack),
        (shape((2, groups, rows_a, width)),) * 2 + (shape((2, groups, piece, width)),) * 2,
        scratch=(pltpu.VMEM((4 * piece, width), F32),), after=(lowered,),
    )
    recv_a, recv_b = across(next_a, 2), across(next_b, 4)

    dq, dk, dv, dq_l, dk_l, dv_l, attended_back = call(
        "attend_back", attend_back_kernel,
        (info, qt, kt, vt, ql, kl, vl, dc_t, dc_l, lse),
        (shape((own, width)), shape((padded, width)), shape((padded, width)),
         shape((own, wide)), shape((padded, wide)), shape((padded, wide))),
        scratch=(pltpu.VMEM((window, width), F32), pltpu.VMEM((window, width), F32),
                 pltpu.VMEM((window, wide), F32), pltpu.VMEM((window, wide), F32), pltpu.VMEM((own, wide), F32)),
        after=(kept,),
    )
    packed = shape((own + own // 4, width))
    left, right, sided = call("sides", sides_kernel, (info, text_project, wl, dk, dv, dk_l, dv_l), (packed, packed))
    from_right = lax.ppermute(left, "tensor", [(i + 1, i) for i in range(groups - 1)])
    from_left = lax.ppermute(right, "tensor", [(i, i + 1) for i in range(groups - 1)])

    next_a, keep_a = add_split(keep_a, recv_a)
    next_b, keep_b = add_split(keep_b, recv_b)
    copied_in = (text_input, dq, dk, dv, ct, db_t)
    send, extra, sent = call(
        "copied_send", copied_send_kernel,
        (info,) + copied_in + (xlt, dq_l, dk_l, dv_l, cl, db_l, sums_t, low_sums_t, hsums_t, sums_l, low_sums_l, hsums_l),
        (shape((groups, 2, 2, rows_a, width)), shape((4 * 128, width))),
        scratch=(pltpu.VMEM((4 * piece, width), F32), pltpu.VMEM((32, width), F32)), after=(sided, next_a, next_b),
    )
    recv = across(send, 1)
    recv_a, recv_b = across(next_a, 4), across(next_b, 2)
    copied_next_a, copied_keep_a, copied_next_b, copied_keep_b, copied_kept = call(
        "copied_keep", copied_keep_kernel, (info,) + copied_in + (extra, recv),
        (shape((2, 2, rows_a, width)),) * 4,
        scratch=(pltpu.VMEM((4 * piece, width), F32),),
    )
    own_sum, owned = call(
        "own", own_kernel,
        (info, text_project, wl, dq, dk, dv, dq_l, dk_l, dv_l, dfirst_t, dfirst_lt, from_right, from_left),
        (packed,), after=(copied_kept,),
    )
    all_rows = lax.all_gather(own_sum, "tensor", axis=0, tiled=False)
    copied_recv_a, copied_recv_b = across(copied_next_a, 2), across(copied_next_b, 4)
    *ffn_parts, ffn_spreaded = call(
        "ffn_spread", ffn_spread_kernel, (info, keep_a, recv_a, keep_b, recv_b),
        (shape((rows_a + piece, width)),) * 4, after=(owned,),
    )
    ffn_parts = [ffn_parts[0]] + [lax.ppermute(ffn_parts[k], "tensor", shift_to(k)) for k in (1, 2, 3)]

    def across_planes(value):
        bit = PIECES
        while bit < planes:
            value = add(value, across(value, bit))
            bit *= 2
        return value

    next_a, keep_a = add_split(copied_keep_a, tie(copied_recv_a, ffn_spreaded))
    next_b, keep_b = add_split(copied_keep_b, tie(copied_recv_b, ffn_spreaded))
    recv_a, recv_b = across(next_a, 4), across(next_b, 2)
    ffn_arrays, ffn_plan = spread(across_planes(add(*ffn_parts)), planes, "half", rows_a)
    *parts, _ = call(
        "copied_spread", copied_spread_kernel, (info, keep_a, recv_a, keep_b, recv_b), (shape((rows_a, width)),) * 4,
    )
    parts = [parts[0]] + [lax.ppermute(parts[k], "tensor", shift_to(k)) for k in (1, 2, 3)]
    summed = across_planes(add(*parts))
    g_narrow, g_widen, g_narrow_l, g_widen_l, _ = call(
        "ffn_final", functools.partial(ffn_final_kernel, ffn_plan), (info, *ffn_arrays),
        (shape((hid, width), F32), shape((width, hid), F32), shape((hid_l, width_l), F32), shape((width_l, hid_l), F32)),
        scratch=(pltpu.VMEM((128, width), F32),),
    )
    every = jnp.stack([summed] + [lax.ppermute(summed, "tensor", shift_from(k)) for k in (1, 2, 3)])
    text_grad, layout_grad_t, given = call(
        "input_final", input_final_kernel, (info, all_rows),
        (shape((total, width), F32), shape((width_l, total), F32)),
    )
    arrays, plan = spread(tie(every, given), planes, "half")
    vectors = lambda w, h: (shape((4, w), F32), shape((2, w), F32), shape((2, w), F32), shape((1, h), F32))
    outs = call(
        "copied_final", functools.partial(copied_final_kernel, plan), (info, *arrays),
        (shape((width, 3 * width), F32), shape((width, width), F32),
         shape((width_l, 3 * width_l), F32), shape((width_l, width_l), F32)) + vectors(width, hid) + vectors(width_l, hid_l),
        scratch=(pltpu.VMEM((4 * 128, width), F32),),
    )
    g_project, g_dense, g_project_l, g_dense_l = outs[:4]
    bias_t, gain_t, shift_t, hb_t, bias_l, gain_l, shift_l, hb_l = outs[4:12]
    return (
        result_t, result_lt.T, text_grad, layout_grad_t.T,
        g_project, bias_t, g_dense, gain_t, shift_t, g_widen, hb_t[0], g_narrow,
        g_project_l, bias_l, g_dense_l, gain_l, shift_l, g_widen_l, hb_l[0], g_narrow_l,
    )


def solution(mesh):
    rows = P(("dp", "tensor"), None)
    weights = (P(), P(), P(), P(), P(), P(None, "tensor"), P("tensor"), P("tensor", None))
    return jax.shard_map(
        per_device,
        mesh=mesh,
        in_specs=(P("dp", None), P("dp", None), P("dp"), P("dp", None), rows, rows) + weights + weights,
        out_specs=(rows, rows, P("dp", None), P("dp", None)) + weights + weights,
        check_vma=False,
    )
```

time: 706 us -> 415 us (0.59)
  waiting for transfers between devices: 434 us -> 150 us
  blocking collectives: 79.1 us -> 0 us
  starting transfers between devices: 5.99 us -> 69.9 us
  Pallas kernels: 97.5 us -> 154 us
  local copies, waits for them, and re-layouts: 48.3 us -> 9.25 us
  other arithmetic: 23.7 us -> 10.2 us
    psum x2 -> x0, waiting for transfers between devices: 241 us -> none  [the longest x1 144 us: per_device(): copied = lax.psum(copied, both).astype(F32)]
    ppermute x2 -> x72, waiting for transfers between devices: 35.7 us -> 150 us  [the longest x3 53.2 us: per_device(): lax.ppermute(summed, 'tensor', shift_from(k))]
    all_gather x3 -> x1, waiting for transfers between devices: 106 us -> 0.01 us  [per_device(): all_rows = lax.all_gather(own_sum, 'tensor', axis=0, tiled=False)]
    ppermute x2 -> x72, starting transfers between devices: 5.52 us -> 69.9 us  [the longest x41 41.6 us: spread(): send = lambda v, bit: lax.ppermute(v, 'dp', flip(planes, bit))]
    pallas_call x5 -> x19, Pallas kernels: 97.5 us -> 154 us  [call(): pl.pallas_call(with_token, out_shape=outs, in_specs=specs, out_specs=[VM]...]
    reduce_scatter x1 -> x0, waiting for transfers between devices: 51.3 us -> none  [per_device(): sharded = lax.psum_scatter(sharded, both, scatter_dimension=0, tiled=True)]
    psum x1 -> x0, blocking collectives: 41.6 us -> none  [per_device(): lax.psum((gn_l, gw_l, gp_l[:, :, :w], gd_l, sums_t, hsum_t, sums_l, hsum_...]
    all_gather x1 -> x0, blocking collectives: 25.3 us -> none  [per_device(): lax.all_gather(jnp.concatenate([layout_widen, layout_narrow], axis=0), 't...]
  transfers between devices with their start and end apart: 8 -> 73, of which waited for: 7 -> 26; matrix products, arithmetic and copies ran while one was open for 7% -> 1% of each run, Pallas kernels for 9% -> 26%
where the time goes in v2:
time: 415 us; the launch traced here: 408 us
  Pallas kernels  154 us (37%)
  waiting for transfers between devices  150 us (36%)
  starting transfers between devices  69.9 us (17%)
  between operations  15.1 us (4%)
  other arithmetic  10.2 us (2%)
  local copies, waits for them, and re-layouts  9.25 us (2%)
    pallas_call x19, Pallas kernels, call(): pl.pallas_call(with_token, out_shape=outs, in_specs=specs, out_specs=[VM]...  154 us
    ppermute x3, waiting for transfers between devices, per_device(): lax.ppermute(summed, 'tensor', shift_from(k))  53.2 us
    ppermute x41, starting transfers between devices, spread(): send = lambda v, bit: lax.ppermute(v, 'dp', flip(planes, bit))  41.6 us
    ppermute x3, waiting for transfers between devices, per_device(): lax.ppermute(parts[k], 'tensor', shift_to(k))  35.1 us
    ppermute x41, waiting for transfers between devices, spread(): send = lambda v, bit: lax.ppermute(v, 'dp', flip(planes, bit))  31.8 us
    ppermute x11, waiting for transfers between devices, per_device(): across = lambda v, bit: lax.ppermute(v, 'dp', flip(planes, bit))  16.7 us
    unnamed x146, local copies, waits for them, and re-layouts  8.48 us
  transfers between devices with their start and end apart: 73, of which 26 were waited for; matrix products, arithmetic and copies ran while one was open for 1% of the time, Pallas kernels for 26%

profile of v2, /device:TPU:9, one launch (start us, length us, event | category | flops | bytes accessed | tf_op | source)
XLA Modules:
  0.0 408.3 jit_solution(2066678343207284820)
XLA Ops:
  9.1 1.4 maximum_bitcast_fusion.refs_5_
  11.2 2.5 pack.1
  13.6 1.3 collective-permute-start.10
  15.1 9.0 %project.1 = (bf16[384,768]{1,0:T(8,128)(2,1)}, bf16[1024,768]{1,0:T(8,128)(2,1)}, bf16[1024,768]{1,0:T(8,128)(2,1)}, bf16[384,256]{1,0:T(8,128)(2,1)}, bf16[102...) custom-call(f32[8,128]{1,0:T(8,128)} %get-tuple-element.147.refs_0_,, ...), custom_call_target="tpu_custom_call" | custom-call | flops 8999999488 | tf_op jit(solution)/shard_map/project/pallas_call | solution.py:696
  24.2 2.4 collective-permute-start.22
  26.6 4.1 %collective-permute-done.1.refs_4_.refs_27_ = bf16[2,96,768]{2,1,0:T(8,128)(2,1)S(1)} collective-permute-done((bf16[2,96,768]{2,1,0:T(8,128)(2,1)}, bf16[2,96,768]{2,1,0:T(8,128)(2,1)S(1)}, u32[]{:S(2)}, u32[]{:S(2)}) %collective-permute-start.1) | collective-permute-done | bytes 294944 | tf_op jit(solution)/shard_map/ppermute | solution.py:797
  30.6 1.5 collective-permute-start.2
  33.3 10.8 %attend.1 = (bf16[384,768]{1,0:T(8,128)(2,1)}, bf16[384,192]{1,0:T(8,128)(2,1)}, f32[384,128]{1,0:T(8,128)}, f32[8,128]{1,0:T(8,128)}) custom-call(s32[26]{0:T(128)} %concatenate.6.refs_0_.refs_1_.refs_3_, bf16[384,768]{1,0:T(8,128)(2,1)} %get-tuple-element.149.refs_1_.refs_2_, bf16[1024,768]{1,0:T(8,128)(2,1)} %get-tuple-element.150.refs_2_.refs_3_, ...), custom_call_target="tpu_custom_call" | custom-call | flops 11000000512 | tf_op jit(solution)/shard_map/attend/pallas_call | solution.py:696
  45.9 3.1 collective-permute-done.21.refs_25_
  49.4 2.0 collective-permute-done.3.refs_6_.refs_29_
  51.4 5.8 %collective-permute-start.5 = (bf16[2,96,768]{2,1,0:T(8,128)(2,1)S(1)}, bf16[2,96,768]{2,1,0:T(8,128)(2,1)S(1)}, u32[]{:S(2)}, u32[]{:S(2)}) collective-permute-start(bf16[2,96,768]{2,1,0:T(8,128)(2,1)S(1)} %collective-permute-done.1.refs_4_.refs_27_), channel_id=1, source_target_pairs={{0,4},{4,0},{8,12},{12,8},{16,20},{20,16},{24,28},{28,24},{1,5},{5... | collective-permute-start | bytes 884744 | tf_op jit(solution)/shard_map/ppermute | solution.py:723
  58.4 7.2 %first_norm.1 = (f32[384,768]{1,0:T(8,128)}, f32[384,192]{1,0:T(8,128)}, bf16[384,768]{1,0:T(8,128)(2,1)}, bf16[384,192]{1,0:T(8,128)(2,1)}, f32[384,192]{1,0:T(...) custom-call(s32[26]{0:T(128)} %concatenate.6.refs_0_.refs_1_.refs_3_, ...), custom_call_target="tpu_custom_call" | custom-call | flops 7000000000 | tf_op jit(solution)/shard_map/first_norm/pallas_call | solution.py:696
  66.7 3.1 collective-permute-start.6
  70.5 1.6 collective-permute-done.24.refs_37_
  72.1 1.4 collective-permute-start.20
  73.5 3.2 collective-permute-start.14
  78.0 5.8 %shard.2 = (bf16[384,768]{1,0:T(8,128)(2,1)}, f32[384,768]{1,0:T(8,128)}, f32[384,768]{1,0:T(8,128)}, f32[8,128]{1,0:T(8,128)}) custom-call(s32[26]{0:T(128)} %concatenate.6.refs_0_.refs_1_.refs_3_, bf16[384,768]{1,0:T(8,128)(2,1)} %get-tuple-element.158.refs_1_.refs_7_, f32[384,768]{1,0:T(8,128)} %get-tuple-element.159.refs_2_, bf16[16,256]{1,0:T(8,128)(2,1)} %copy-done.72, ...), custom_call_target="tpu_custom_call" | custom-call | flops 6000000000 | tf_op jit(solution)/shard_map/shard/pallas_call | solution.py:696
  84.7 2.5 collective-permute-start.19
  87.8 1.3 collective-permute-start.28
  90.7 5.9 %shard.3 = (bf16[384,768]{1,0:T(8,128)(2,1)}, f32[384,768]{1,0:T(8,128)}, f32[384,768]{1,0:T(8,128)}, f32[8,128]{1,0:T(8,128)}) custom-call(s32[26]{0:T(128)} %concatenate.6.refs_0_.refs_1_.refs_3_, bf16[384,768]{1,0:T(8,128)(2,1)} %get-tuple-element.158.refs_1_.refs_7_, f32[384,768]{1,0:T(8,128)} %get-tuple-element.169.refs_2_, bf16[16,256]{1,0:T(8,128)(2,1)} %copy-done.71, ...), custom_call_target="tpu_custom_call" | custom-call | flops 6000000000 | tf_op jit(solution)/shard_map/shard/pallas_call | solution.py:696
  96.6 3.5 collective-permute-done.19.refs_21_
  103.5 21.6 %turn.1 = (bf16[384,768]{1,0:T(8,128)(2,1)}, bf16[384,768]{1,0:T(8,128)(2,1)}, bf16[4,384,768]{2,1,0:T(8,128)(2,1)}, f32[384,768]{1,0:T(8,128)}, f32[4,768]{1,0:...) custom-call(s32[26]{0:T(128)} %concatenate.6.refs_0_.refs_1_.refs_3_, ...), custom_call_target="tpu_custom_call" | custom-call | flops 24000000000 | tf_op jit(solution)/shard_map/turn/pallas_call | solution.py:696
  125.7 4.9 %lower.1 = (f32[384,768]{1,0:T(8,128)}, bf16[384,768]{1,0:T(8,128)(2,1)}, bf16[384,768]{1,0:T(8,128)(2,1)}, f32[4,768]{1,0:T(4,128)}, f32[192,384]{1,0:T(8,128)}...) custom-call(s32[26]{0:T(128)} %concatenate.6.refs_0_.refs_1_.refs_3_, ...), custom_call_target="tpu_custom_call" | custom-call | flops 5000000000 | tf_op jit(solution)/shard_map/lower/pallas_call | solution.py:696
  130.7 3.2 collective-permute-done.33.refs_10_
  133.9 1.4 copy-done.17
  136.2 10.2 %ffn_keep.1 = (bf16[2,4,112,768]{3,2,1,0:T(8,128)(2,1)}, bf16[2,4,112,768]{3,2,1,0:T(8,128)(2,1)}, bf16[2,4,96,768]{3,2,1,0:T(8,128)(2,1)}, bf16[2,4,96,768]{3,2,1,0:T(8,128)(2,1)}, f32[8,128]{1,0:T(8,128)}) custom-call(f32[8,128]{1,0:T(8,128)} %get-tuple-element.201.refs_0_, s32[26]{0:T(128)} %concatenate.6.refs_0_.refs_1_.refs_3_, ...), custom_call_target="tpu_custom_call" | custom-call | flops 8999999488 | tf_op jit(solution)/shard_map/ffn_keep/pallas_call | solution.py:696
  148.5 19.4 %attend_back.1 = (bf16[384,768]{1,0:T(8,128)(2,1)}, bf16[1792,768]{1,0:T(8,128)(2,1)}, bf16[1792,768]{1,0:T(8,128)(2,1)}, bf16[384,256]{1,0:T(8,128)(2,1)}, bf16...) custom-call(f32[8,128]{1,0:T(8,128)} %get-tuple-element.208.refs_0_, ...), custom_call_target="tpu_custom_call" | custom-call | flops 20000000000 | tf_op jit(solution)/shard_map/attend_back/pallas_call | solution.py:696
  167.9 7.4 %sides.1 = (bf16[480,768]{1,0:T(8,128)(2,1)}, bf16[480,768]{1,0:T(8,128)(2,1)}, f32[8,128]{1,0:T(8,128)}) custom-call(s32[26]{0:T(128)} %concatenate.6.refs_0_.refs_1_.refs_3_, bf16[768,2304]{1,0:T(8,128)(2,1)} %refs_2_.5, bf16[192,768]{1,0:T(8,128)(2,1)} %get-tuple-element.216.refs_2_.refs_3_, bf16[1792,768]{1,0:T(8,128)(2,1)} %get-tuple-element.213.refs_3_.refs_6_.refs_5_, ...), custom_call_target="tpu_custom_call" | custom-call | flops 7000000000 | tf_op jit(solution)/shard_map/sides/pallas_call | solution.py:696
  175.3 1.3 fusion.3
  176.6 2.0 collective-permute-done.34
  178.6 1.5 fusion.1
  180.1 9.2 %copied_send.1 = (bf16[4,2,2,112,768]{4,3,2,1,0:T(8,128)(2,1)}, bf16[512,768]{1,0:T(8,128)(2,1)}, f32[8,128]{1,0:T(8,128)}) custom-call(f32[8,128]{1,0:T(8,128)} %get-tuple-element.219.refs_0_, bf16[4,112,768]{2,1,0:T(8,128)(2,1)} %get-tuple-element.277.refs_1_, bf16[4,96,768]{2,1,0:T(8,128)(2,1)} %get-tuple-element.279.refs_2_, ...), custom_call_target="tpu_custom_call" | custom-call | flops 11000000512 | tf_op jit(solution)/shard_map/copied_send/pallas_call | solution.py:696
  189.3 1.5 collective-permute-start.36
  190.8 1.9 collective-permute-start.37
  192.7 3.4 collective-permute-start.38
  198.0 1.5 copy-done.16
  199.6 10.5 %copied_keep.1 = (bf16[2,2,112,768]{3,2,1,0:T(8,128)(2,1)}, bf16[2,2,112,768]{3,2,1,0:T(8,128)(2,1)}, bf16[2,2,112,768]{3,2,1,0:T(8,128)(2,1)}, bf16[2,2,112,768]{3,2,1,0:T(8,128)(2,1)}, f32[8,128]{1,0:T(8,128)}) custom-call(s32[26]{0:T(128)} %concatenate.6.refs_0_.refs_1_.refs_3_, bf16[1536,768]{1,0:T(8,128)(2,1)} %refs_1_.7, ...), custom_call_target="tpu_custom_call" | custom-call | flops 8999999488 | tf_op jit(solution)/shard_map/copied_keep/pallas_call | solution.py:696
  211.5 1.3 collective-permute-done.38.refs_13_
  212.8 7.9 %own.1 = (bf16[480,768]{1,0:T(8,128)(2,1)}, f32[8,128]{1,0:T(8,128)}) custom-call(f32[8,128]{1,0:T(8,128)} %get-tuple-element.234.refs_0_, s32[26]{0:T(128)} %concatenate.6.refs_0_.refs_1_.refs_3_, bf16[768,2304]{1,0:T(8,128)(2,1)} %refs_2_.5, bf16[192,768]{1,0:T(8,128)(2,1)} %get-tuple-element.216.refs_2_.refs_3_, ...), custom_call_target="tpu_custom_call" | custom-call | flops 7000000000 | tf_op jit(solution)/shard_map/own/pallas_call | solution.py:696
  220.8 2.8 ffn_spread.1
  223.6 2.6 collective-permute-done.39
  229.5 5.2 %collective-permute-done.42.refs_2_ = bf16[2,112,768]{2,1,0:T(8,128)(2,1)S(1)} collective-permute-done((bf16[2,112,768]{2,1,0:T(8,128)(2,1)S(1)}, bf16[2,112,768]{2,1,0:T(8,128)(2,1)S(1)}, u32[]{:S(2)}, u32[]{:S(2)}) %collective-permute-start.42) | collective-permute-done | bytes 344096 | tf_op jit(solution)/shard_map/ppermute | solution.py:860
  234.7 2.9 collective-permute-done.44.refs_4_
  238.3 2.3 copied_spread.1
  240.6 1.4 collective-permute-start.45
  242.0 1.3 collective-permute-start.46
  243.4 10.4 %collective-permute-done.45 = bf16[112,768]{1,0:T(8,128)(2,1)S(1)} collective-permute-done((bf16[112,768]{1,0:T(8,128)(2,1)}, bf16[112,768]{1,0:T(8,128)(2,1)S(1)}, u32[]{:S(2)}, u32[]{:S(2)}) %collective-permute-start.45) | collective-permute-done | bytes 172064 | tf_op jit(solution)/shard_map/ppermute | solution.py:934
  253.8 19.4 %collective-permute-done.46 = bf16[112,768]{1,0:T(8,128)(2,1)S(1)} collective-permute-done((bf16[112,768]{1,0:T(8,128)(2,1)}, bf16[112,768]{1,0:T(8,128)(2,1)S(1)}, u32[]{:S(2)}, u32[]{:S(2)}) %collective-permute-start.46) | collective-permute-done | bytes 172064 | tf_op jit(solution)/shard_map/ppermute | solution.py:934
  273.2 5.3 %collective-permute-done.47 = bf16[112,768]{1,0:T(8,128)(2,1)S(1)} collective-permute-done((bf16[112,768]{1,0:T(8,128)(2,1)}, bf16[112,768]{1,0:T(8,128)(2,1)S(1)}, u32[]{:S(2)}, u32[]{:S(2)}) %collective-permute-start.47) | collective-permute-done | bytes 172064 | tf_op jit(solution)/shard_map/ppermute | solution.py:934
  280.1 3.0 collective-permute-start.61
  283.5 5.8 %collective-permute-done.50 = bf16[112,768]{1,0:T(8,128)(2,1)S(1)} collective-permute-done((bf16[112,768]{1,0:T(8,128)(2,1)S(1)}, bf16[112,768]{1,0:T(8,128)(2,1)S(1)}, u32[]{:S(2)}, u32[]{:S(2)}) %collective-permute-start.50) | collective-permute-done | bytes 172064 | tf_op jit(solution)/shard_map/ppermute | solution.py:941
  289.3 45.0 %collective-permute-done.49 = bf16[112,768]{1,0:T(8,128)(2,1)S(1)} collective-permute-done((bf16[112,768]{1,0:T(8,128)(2,1)S(1)}, bf16[112,768]{1,0:T(8,128)(2,1)S(1)}, u32[]{:S(2)}, u32[]{:S(2)}) %collective-permute-start.49) | collective-permute-done | bytes 172064 | tf_op jit(solution)/shard_map/ppermute | solution.py:941
  334.3 2.4 collective-permute-done.48
  336.8 1.3 collective-permute-start.52
  340.1 20.8 %collective-permute-done.63.refs_2_ = bf16[208,768]{1,0:T(8,128)(2,1)S(1)} collective-permute-done((bf16[208,768]{1,0:T(8,128)(2,1)S(1)}, bf16[208,768]{1,0:T(8,128)(2,1)S(1)}, u32[]{:S(2)}, u32[]{:S(2)}) %collective-permute-start.63) | collective-permute-done | bytes 319520 | tf_op jit(solution)/shard_map/ppermute | solution.py:723
  361.1 1.3 collective-permute-start.66
  362.4 2.5 collective-permute-start.67
  365.2 3.4 collective-permute-start.69
  369.3 1.3 collective-permute-start.54
  373.2 5.3 %collective-permute-done.54.refs_5_ = bf16[2,112,768]{2,1,0:T(8,128)(2,1)S(1)} collective-permute-done((bf16[2,112,768]{2,1,0:T(8,128)(2,1)S(1)}, bf16[2,112,768]{2,1,0:T(8,128)(2,1)S(1)}, u32[]{:S(2)}, u32[]{:S(2)}) %collective-permute-start.54) | collective-permute-done | bytes 344096 | tf_op jit(solution)/shard_map/ppermute | solution.py:723
  381.1 4.2 %ffn_final.1 = (f32[768,768]{1,0:T(8,128)}, f32[768,768]{1,0:T(8,128)}, f32[192,192]{1,0:T(8,128)}, f32[192,192]{1,0:T(8,128)}, f32[8,128]{1,0:T(8,128)}) custom-call(s32[26]{0:T(128)} %concatenate.6.refs_0_.refs_1_.refs_3_, bf16[208,768]{1,0:T(8,128)(2,1)} %copy-done.8, bf16[208,768]{1,0:T(8,128)(2,1)} %copy-done.11, bf16[208,768]{1,0:T(8,128)(2,1)} %copy-done.14, ...), custom_call_target="tpu_custom_call" | custom-call | flops 4000000000 | tf_op jit(solution)/shard_map/ffn_final/pallas_call | solution.py:696
  387.6 7.9 %copied_final.1 = (f32[768,2304]{1,0:T(8,128)}, f32[768,768]{1,0:T(8,128)}, f32[192,576]{1,0:T(8,128)}, f32[192,192]{1,0:T(8,128)}, f32[4,768]{1,0:T(4,128)}, /*...) custom-call(s32[26]{0:T(128)} %concatenate.6.refs_0_.refs_1_.refs_3_, ...), custom_call_target="tpu_custom_call" | custom-call | flops 8000000000 | tf_op jit(solution)/shard_map/copied_final/pallas_call | solution.py:696
  395.4 1.3 reduce
  396.7 4.5 %input_final.1 = (f32[1536,768]{1,0:T(8,128)}, f32[192,1536]{1,0:T(8,128)}, f32[8,128]{1,0:T(8,128)}) custom-call(s32[26]{0:T(128)} %concatenate.6.refs_0_.refs_1_.refs_3_, bf16[4,480,768]{2,1,0:T(8,128)(2,1)} %bitcast.46), custom_call_target="tpu_custom_call" | custom-call | flops 3000000000 | tf_op jit(solution)/shard_map/input_final/pallas_call | solution.py:696
  (270 shorter events, 40.1 us)
Async XLA Ops:
  7.2 389.5 %all-gather.3.cloned.1.call-start = ((), (), s32[]{:S(2)}) async-start(), calls=%async_computation | async-start | bytes 3686400 | tf_op jit(solution)/shard_map/all_gather | solution.py:912
  13.6 12.9 %collective-permute-start.10 = (bf16[2,96,768]{2,1,0:T(8,128)(2,1)}, bf16[2,96,768]{2,1,0:T(8,128)(2,1)S(1)}, u32[]{:S(2)}, u32[]{:S(2)}) collective-permute-start(bf16[2,96,768]{2,1,0:T(8,128)(2,1)} %get-tuple-element.186), channel_id=1, source_target_pairs={{0,1},{1,2},{2,3},{3,0},{4,5},{5,6},{6,7},{7,4},{8,9},{9,10},{10,1... | collective-permute-start | bytes 884744 | tf_op jit(solution)/shard_map/ppermute | solution.py:797
  14.9 15.7 %collective-permute-start.1 = (bf16[2,96,768]{2,1,0:T(8,128)(2,1)}, bf16[2,96,768]{2,1,0:T(8,128)(2,1)S(1)}, u32[]{:S(2)}, u32[]{:S(2)}) collective-permute-start(bf16[2,96,768]{2,1,0:T(8,128)(2,1)} %get-tuple-element.186), channel_id=1, source_target_pairs={{0,3},{1,0},{2,1},{3,2},{4,7},{5,4},{6,5},{7,6},{8,11},{9,8},{10,9... | collective-permute-start | bytes 884744 | tf_op jit(solution)/shard_map/ppermute | solution.py:797
  24.2 24.9 %collective-permute-start.22 = (bf16[2,96,768]{2,1,0:T(8,128)(2,1)S(1)}, bf16[2,96,768]{2,1,0:T(8,128)(2,1)S(1)}, u32[]{:S(2)}, u32[]{:S(2)}) collective-permute-start(bf16[2,96,768]{2,1,0:T(8,128)(2,1)S(1)} %copy-done.56), channel_id=1, source_target_pairs={{0,2},{1,3},{2,0},{3,1},{4,6},{5,7},{6,4},{7,5},{8,10},{9,11},{10,... | collective-permute-start | bytes 884744 | tf_op jit(solution)/shard_map/ppermute | solution.py:809
  30.6 13.7 %collective-permute-start.2 = (bf16[2,96,768]{2,1,0:T(8,128)(2,1)S(1)}, bf16[2,96,768]{2,1,0:T(8,128)(2,1)S(1)}, u32[]{:S(2)}, u32[]{:S(2)}) collective-permute-start(bf16[2,96,768]{2,1,0:T(8,128)(2,1)S(1)} %collective-permute-done.1.refs_4_.refs_27_), channel_id=1, source_target_pairs={{0,8},{4,12},{8,0},{12,4},{16,24},{20,28},{24,16},{28,20},{1,9},{5... | collective-permute-start | bytes 884744 | tf_op jit(solution)/shard_map/ppermute | solution.py:723
  32.1 13.5 %collective-permute-start.12 = (bf16[2,96,768]{2,1,0:T(8,128)(2,1)S(1)}, bf16[2,96,768]{2,1,0:T(8,128)(2,1)S(1)}, u32[]{:S(2)}, u32[]{:S(2)}) collective-permute-start(bf16[2,96,768]{2,1,0:T(8,128)(2,1)S(1)} %collective-permute-done.10.refs_4_.refs_45_), channel_id=1, source_target_pairs={{0,16},{4,20},{8,24},{12,28},{16,0},{20,4},{24,8},{28,12},{1,17},{... | collective-permute-start | bytes 884744 | tf_op jit(solution)/shard_map/ppermute | solution.py:723
  44.2 7.2 %collective-permute-start.3 = (bf16[2,96,768]{2,1,0:T(8,128)(2,1)S(1)}, bf16[2,96,768]{2,1,0:T(8,128)(2,1)S(1)}, u32[]{:S(2)}, u32[]{:S(2)}) collective-permute-start(bf16[2,96,768]{2,1,0:T(8,128)(2,1)S(1)} %collective-permute-done.1.refs_4_.refs_27_), channel_id=1, source_target_pairs={{0,16},{4,20},{8,24},{12,28},{16,0},{20,4},{24,8},{28,12},{1,17},{... | collective-permute-start | bytes 884744 | tf_op jit(solution)/shard_map/ppermute | solution.py:723
  44.4 13.3 %collective-permute-start.4 = (bf16[2,96,768]{2,1,0:T(8,128)(2,1)S(1)}, bf16[2,96,768]{2,1,0:T(8,128)(2,1)S(1)}, u32[]{:S(2)}, u32[]{:S(2)}) collective-permute-start(bf16[2,96,768]{2,1,0:T(8,128)(2,1)S(1)} %collective-permute-done.2.refs_5_.refs_28_), channel_id=1, source_target_pairs={{0,16},{4,20},{8,24},{12,28},{16,0},{20,4},{24,8},{28,12},{1,17},{... | collective-permute-start | bytes 884744 | tf_op jit(solution)/shard_map/ppermute | solution.py:723
  45.7 19.9 %collective-permute-start.9 = (bf16[16,256]{1,0:T(8,128)(2,1)S(1)}, bf16[16,256]{1,0:T(8,128)(2,1)S(1)}, u32[]{:S(2)}, u32[]{:S(2)}) collective-permute-start(bf16[16,256]{1,0:T(8,128)(2,1)S(1)} %copy-done.69), channel_id=1, source_target_pairs={{0,1},{1,2},{2,3},{3,0},{4,5},{5,6},{6,7},{7,4},{8,9},{9,10},{10,1... | collective-permute-start | bytes 24584 | tf_op jit(solution)/shard_map/ppermute | solution.py:798
  49.0 16.8 %collective-permute-start = (bf16[16,256]{1,0:T(8,128)(2,1)S(1)}, bf16[16,256]{1,0:T(8,128)(2,1)S(1)}, u32[]{:S(2)}, u32[]{:S(2)}) collective-permute-start(bf16[16,256]{1,0:T(8,128)(2,1)S(1)} %copy-done.69), channel_id=1, source_target_pairs={{0,3},{1,0},{2,1},{3,2},{4,7},{5,4},{6,5},{7,6},{8,11},{9,8},{10,9... | collective-permute-start | bytes 24584 | tf_op jit(solution)/shard_map/ppermute | solution.py:798
  49.1 17.6 %collective-permute-start.11 = (bf16[2,96,768]{2,1,0:T(8,128)(2,1)S(1)}, bf16[2,96,768]{2,1,0:T(8,128)(2,1)S(1)}, u32[]{:S(2)}, u32[]{:S(2)}) collective-permute-start(bf16[2,96,768]{2,1,0:T(8,128)(2,1)S(1)} %collective-permute-done.10.refs_4_.refs_45_), channel_id=1, source_target_pairs={{0,8},{4,12},{8,0},{12,4},{16,24},{20,28},{24,16},{28,20},{1,9},{5... | collective-permute-start | bytes 884744 | tf_op jit(solution)/shard_map/ppermute | solution.py:723
  51.4 18.4 %collective-permute-start.5 = (bf16[2,96,768]{2,1,0:T(8,128)(2,1)S(1)}, bf16[2,96,768]{2,1,0:T(8,128)(2,1)S(1)}, u32[]{:S(2)}, u32[]{:S(2)}) collective-permute-start(bf16[2,96,768]{2,1,0:T(8,128)(2,1)S(1)} %collective-permute-done.1.refs_4_.refs_27_), channel_id=1, source_target_pairs={{0,4},{4,0},{8,12},{12,8},{16,20},{20,16},{24,28},{28,24},{1,5},{5... | collective-permute-start | bytes 884744 | tf_op jit(solution)/shard_map/ppermute | solution.py:723
  57.7 12.2 %collective-permute-start.13 = (bf16[2,96,768]{2,1,0:T(8,128)(2,1)S(1)}, bf16[2,96,768]{2,1,0:T(8,128)(2,1)S(1)}, u32[]{:S(2)}, u32[]{:S(2)}) collective-permute-start(bf16[2,96,768]{2,1,0:T(8,128)(2,1)S(1)} %collective-permute-done.12.refs_6_.refs_47_), channel_id=1, source_target_pairs={{0,8},{4,12},{8,0},{12,4},{16,24},{20,28},{24,16},{28,20},{1,9},{5... | collective-permute-start | bytes 884744 | tf_op jit(solution)/shard_map/ppermute | solution.py:723
  65.6 6.5 %collective-permute-start.24 = (bf16[2,96,768]{2,1,0:T(8,128)(2,1)S(1)}, bf16[2,96,768]{2,1,0:T(8,128)(2,1)S(1)}, u32[]{:S(2)}, u32[]{:S(2)}) collective-permute-start(bf16[2,96,768]{2,1,0:T(8,128)(2,1)S(1)} %collective-permute-done.22.refs_35_), channel_id=1, source_target_pairs={{0,16},{4,20},{8,24},{12,28},{16,0},{20,4},{24,8},{28,12},{1,17},{... | collective-permute-start | bytes 884744 | tf_op jit(solution)/shard_map/ppermute | solution.py:723
  65.9 7.6 %collective-permute-start.23 = (bf16[2,96,768]{2,1,0:T(8,128)(2,1)S(1)}, bf16[2,96,768]{2,1,0:T(8,128)(2,1)S(1)}, u32[]{:S(2)}, u32[]{:S(2)}) collective-permute-start(bf16[2,96,768]{2,1,0:T(8,128)(2,1)S(1)} %collective-permute-done.22.refs_35_), channel_id=1, source_target_pairs={{0,8},{4,12},{8,0},{12,4},{16,24},{20,28},{24,16},{28,20},{1,9},{5... | collective-permute-start | bytes 884744 | tf_op jit(solution)/shard_map/ppermute | solution.py:723
  66.7 10.0 %collective-permute-start.6 = (bf16[2,96,768]{2,1,0:T(8,128)(2,1)S(1)}, bf16[2,96,768]{2,1,0:T(8,128)(2,1)S(1)}, u32[]{:S(2)}, u32[]{:S(2)}) collective-permute-start(bf16[2,96,768]{2,1,0:T(8,128)(2,1)S(1)} %collective-permute-done.2.refs_5_.refs_28_), channel_id=1, source_target_pairs={{0,4},{4,0},{8,12},{12,8},{16,20},{20,16},{24,28},{28,24},{1,5},{5... | collective-permute-start | bytes 884744 | tf_op jit(solution)/shard_map/ppermute | solution.py:723
  69.8 7.0 %collective-permute-start.7 = (bf16[2,96,768]{2,1,0:T(8,128)(2,1)S(1)}, bf16[2,96,768]{2,1,0:T(8,128)(2,1)S(1)}, u32[]{:S(2)}, u32[]{:S(2)}) collective-permute-start(bf16[2,96,768]{2,1,0:T(8,128)(2,1)S(1)} %collective-permute-done.3.refs_6_.refs_29_), channel_id=1, source_target_pairs={{0,4},{4,0},{8,12},{12,8},{16,20},{20,16},{24,28},{28,24},{1,5},{5... | collective-permute-start | bytes 884744 | tf_op jit(solution)/shard_map/ppermute | solution.py:723
  69.9 7.3 %collective-permute-start.8 = (bf16[2,96,768]{2,1,0:T(8,128)(2,1)S(1)}, bf16[2,96,768]{2,1,0:T(8,128)(2,1)S(1)}, u32[]{:S(2)}, u32[]{:S(2)}) collective-permute-start(bf16[2,96,768]{2,1,0:T(8,128)(2,1)S(1)} %collective-permute-done.4.refs_7_.refs_30_), channel_id=1, source_target_pairs={{0,4},{4,0},{8,12},{12,8},{16,20},{20,16},{24,28},{28,24},{1,5},{5... | collective-permute-start | bytes 884744 | tf_op jit(solution)/shard_map/ppermute | solution.py:723
  72.1 11.8 %collective-permute-start.20 = (bf16[384,256]{1,0:T(8,128)(2,1)S(1)}, bf16[384,256]{1,0:T(8,128)(2,1)S(1)}, u32[]{:S(2)}, u32[]{:S(2)}) collective-permute-start(bf16[384,256]{1,0:T(8,128)(2,1)S(1)} %copy-done.57), channel_id=1, source_target_pairs={{0,1},{1,2},{2,3},{3,0},{4,5},{5,6},{6,7},{7,4},{8,9},{9,10},{10,1... | collective-permute-start | bytes 589832 | tf_op jit(solution)/shard_map/ppermute | solution.py:826
  73.5 10.9 %collective-permute-start.14 = (bf16[2,96,768]{2,1,0:T(8,128)(2,1)S(1)}, bf16[2,96,768]{2,1,0:T(8,128)(2,1)S(1)}, u32[]{:S(2)}, u32[]{:S(2)}) collective-permute-start(bf16[2,96,768]{2,1,0:T(8,128)(2,1)S(1)} %collective-permute-done.10.refs_4_.refs_45_), channel_id=1, source_target_pairs={{0,4},{4,0},{8,12},{12,8},{16,20},{20,16},{24,28},{28,24},{1,5},{5... | collective-permute-start | bytes 884744 | tf_op jit(solution)/shard_map/ppermute | solution.py:723
  76.7 10.5 %collective-permute-start.16 = (bf16[2,96,768]{2,1,0:T(8,128)(2,1)S(1)}, bf16[2,96,768]{2,1,0:T(8,128)(2,1)S(1)}, u32[]{:S(2)}, u32[]{:S(2)}) collective-permute-start(bf16[2,96,768]{2,1,0:T(8,128)(2,1)S(1)} %collective-permute-done.12.refs_6_.refs_47_), channel_id=1, source_target_pairs={{0,4},{4,0},{8,12},{12,8},{16,20},{20,16},{24,28},{28,24},{1,5},{5... | collective-permute-start | bytes 884744 | tf_op jit(solution)/shard_map/ppermute | solution.py:723
  76.8 7.9 %collective-permute-start.15 = (bf16[2,96,768]{2,1,0:T(8,128)(2,1)S(1)}, bf16[2,96,768]{2,1,0:T(8,128)(2,1)S(1)}, u32[]{:S(2)}, u32[]{:S(2)}) collective-permute-start(bf16[2,96,768]{2,1,0:T(8,128)(2,1)S(1)} %collective-permute-done.11.refs_5_.refs_46_), channel_id=1, source_target_pairs={{0,4},{4,0},{8,12},{12,8},{16,20},{20,16},{24,28},{28,24},{1,5},{5... | collective-permute-start | bytes 884744 | tf_op jit(solution)/shard_map/ppermute | solution.py:723
  77.3 10.5 %collective-permute-start.17 = (bf16[2,96,768]{2,1,0:T(8,128)(2,1)S(1)}, bf16[2,96,768]{2,1,0:T(8,128)(2,1)S(1)}, u32[]{:S(2)}, u32[]{:S(2)}) collective-permute-start(bf16[2,96,768]{2,1,0:T(8,128)(2,1)S(1)} %collective-permute-done.13.refs_7_.refs_48_), channel_id=1, source_target_pairs={{0,4},{4,0},{8,12},{12,8},{16,20},{20,16},{24,28},{28,24},{1,5},{5... | collective-permute-start | bytes 884744 | tf_op jit(solution)/shard_map/ppermute | solution.py:723
  84.4 5.8 %collective-permute-start.25 = (bf16[1,96,768]{2,1,0:T(8,128)(2,1)S(1)}, bf16[1,96,768]{2,1,0:T(8,128)(2,1)S(1)}, u32[]{:S(2)}, u32[]{:S(2)}) collective-permute-start(bf16[1,96,768]{2,1,0:T(8,128)(2,1)S(1)} %slice.66), channel_id=1, source_target_pairs={{0,16},{4,20},{8,24},{12,28},{16,0},{20,4},{24,8},{28,12},{1,17},{... | collective-permute-start | bytes 442376 | tf_op jit(solution)/shard_map/ppermute | solution.py:723
  84.7 15.4 %collective-permute-start.19 = (bf16[384,256]{1,0:T(8,128)(2,1)S(1)}, bf16[384,256]{1,0:T(8,128)(2,1)S(1)}, u32[]{:S(2)}, u32[]{:S(2)}) collective-permute-start(bf16[384,256]{1,0:T(8,128)(2,1)S(1)} %copy-done.57), channel_id=1, source_target_pairs={{0,2},{1,3},{2,0},{3,1},{4,6},{5,7},{6,4},{7,5},{8,10},{9,11},{10,... | collective-permute-start | bytes 589832 | tf_op jit(solution)/shard_map/ppermute | solution.py:826
  87.2 13.8 %collective-permute-start.18 = (bf16[384,256]{1,0:T(8,128)(2,1)S(1)}, bf16[384,256]{1,0:T(8,128)(2,1)S(1)}, u32[]{:S(2)}, u32[]{:S(2)}) collective-permute-start(bf16[384,256]{1,0:T(8,128)(2,1)S(1)} %copy-done.57), channel_id=1, source_target_pairs={{0,3},{1,0},{2,1},{3,2},{4,7},{5,4},{6,5},{7,6},{8,11},{9,8},{10,9... | collective-permute-start | bytes 589832 | tf_op jit(solution)/shard_map/ppermute | solution.py:826
  87.8 14.8 %collective-permute-start.28 = (bf16[2,96,768]{2,1,0:T(8,128)(2,1)S(1)}, bf16[2,96,768]{2,1,0:T(8,128)(2,1)S(1)}, u32[]{:S(2)}, u32[]{:S(2)}) collective-permute-start(bf16[2,96,768]{2,1,0:T(8,128)(2,1)S(1)} %collective-permute-done.23.refs_36_), channel_id=1, source_target_pairs={{0,4},{4,0},{8,12},{12,8},{16,20},{20,16},{24,28},{28,24},{1,5},{5... | collective-permute-start | bytes 884744 | tf_op jit(solution)/shard_map/ppermute | solution.py:723
  89.3 13.2 %collective-permute-start.29 = (bf16[2,96,768]{2,1,0:T(8,128)(2,1)S(1)}, bf16[2,96,768]{2,1,0:T(8,128)(2,1)S(1)}, u32[]{:S(2)}, u32[]{:S(2)}) collective-permute-start(bf16[2,96,768]{2,1,0:T(8,128)(2,1)S(1)} %collective-permute-done.24.refs_37_), channel_id=1, source_target_pairs={{0,4},{4,0},{8,12},{12,8},{16,20},{20,16},{24,28},{28,24},{1,5},{5... | collective-permute-start | bytes 884744 | tf_op jit(solution)/shard_map/ppermute | solution.py:723
  90.2 12.3 %collective-permute-start.27 = (bf16[2,96,768]{2,1,0:T(8,128)(2,1)S(1)}, bf16[2,96,768]{2,1,0:T(8,128)(2,1)S(1)}, u32[]{:S(2)}, u32[]{:S(2)}) collective-permute-start(bf16[2,96,768]{2,1,0:T(8,128)(2,1)S(1)} %collective-permute-done.22.refs_35_), channel_id=1, source_target_pairs={{0,4},{4,0},{8,12},{12,8},{16,20},{20,16},{24,28},{28,24},{1,5},{5... | collective-permute-start | bytes 884744 | tf_op jit(solution)/shard_map/ppermute | solution.py:723
  125.2 8.8 %collective-permute-start.32 = (bf16[4,2,2,112,768]{4,3,2,1,0:T(8,128)(2,1)}, bf16[4,2,2,112,768]{4,3,2,1,0:T(8,128)(2,1)S(1)}, u32[]{:S(2)}, u32[]{:S(2)}) collective-permute-start(bf16[4,2,2,112,768]{4,3,2,1,0:T(8,128)(2,1)} %get-tuple-element.205), channel_id=1, source_target_pairs={{0,4},{4,0},{8,12},{12,8},{16,20},{20,16},{24,28},{28,24},{1,5},{5... | collective-permute-start | bytes 8257544 | tf_op jit(solution)/shard_map/ppermute | solution.py:860
  125.6 8.3 %collective-permute-start.33 = (bf16[4,2,2,96,768]{4,3,2,1,0:T(8,128)(2,1)}, bf16[4,2,2,96,768]{4,3,2,1,0:T(8,128)(2,1)S(1)}, u32[]{:S(2)}, u32[]{:S(2)}) collective-permute-start(bf16[4,2,2,96,768]{4,3,2,1,0:T(8,128)(2,1)} %get-tuple-element.206), channel_id=1, source_target_pairs={{0,4},{4,0},{8,12},{12,8},{16,20},{20,16},{24,28},{28,24},{1,5},{5... | collective-permute-start | bytes 7077896 | tf_op jit(solution)/shard_map/ppermute | solution.py:860
  146.5 28.8 %collective-permute-start.35 = (bf16[2,4,96,768]{3,2,1,0:T(8,128)(2,1)}, bf16[2,4,96,768]{3,2,1,0:T(8,128)(2,1)S(1)}, u32[]{:S(2)}, u32[]{:S(2)}) collective-permute-start(bf16[2,4,96,768]{3,2,1,0:T(8,128)(2,1)} %get-tuple-element.223), channel_id=1, source_target_pairs={{0,16},{4,20},{8,24},{12,28},{16,0},{20,4},{24,8},{28,12},{1,17},{... | collective-permute-start | bytes 3538952 | tf_op jit(solution)/shard_map/ppermute | solution.py:860
  147.3 31.4 %collective-permute-start.34 = (bf16[2,4,112,768]{3,2,1,0:T(8,128)(2,1)}, bf16[2,4,112,768]{3,2,1,0:T(8,128)(2,1)S(1)}, u32[]{:S(2)}, u32[]{:S(2)}) collective-permute-start(bf16[2,4,112,768]{3,2,1,0:T(8,128)(2,1)} %get-tuple-element.221), channel_id=1, source_target_pairs={{0,8},{4,12},{8,0},{12,4},{16,24},{20,28},{24,16},{28,20},{1,9},{5... | collective-permute-start | bytes 4128776 | tf_op jit(solution)/shard_map/ppermute | solution.py:860
  189.3 8.8 %collective-permute-start.36 = (bf16[4,2,2,112,768]{4,3,2,1,0:T(8,128)(2,1)}, bf16[4,2,2,112,768]{4,3,2,1,0:T(8,128)(2,1)S(1)}, u32[]{:S(2)}, u32[]{:S(2)}) collective-permute-start(bf16[4,2,2,112,768]{4,3,2,1,0:T(8,128)(2,1)} %get-tuple-element.233), channel_id=1, source_target_pairs={{0,4},{4,0},{8,12},{12,8},{16,20},{20,16},{24,28},{28,24},{1,5},{5... | collective-permute-start | bytes 8257544 | tf_op jit(solution)/shard_map/ppermute | solution.py:860
  190.8 20.1 %collective-permute-start.37 = (bf16[480,768]{1,0:T(8,128)(2,1)S(1)}, bf16[480,768]{1,0:T(8,128)(2,1)S(1)}, u32[]{:S(2)}, u32[]{:S(2)}) collective-permute-start(bf16[480,768]{1,0:T(8,128)(2,1)S(1)} %copy-done.19), channel_id=1, source_target_pairs={{1,0},{2,1},{3,2},{5,4},{6,5},{7,6},{9,8},{10,9},{11,10},{13,12},{... | collective-permute-start | bytes 2211848 | tf_op jit(solution)/shard_map/ppermute | solution.py:888
  192.7 20.1 %collective-permute-start.38 = (bf16[480,768]{1,0:T(8,128)(2,1)S(1)}, bf16[480,768]{1,0:T(8,128)(2,1)}, u32[]{:S(2)}, u32[]{:S(2)}) collective-permute-start(bf16[480,768]{1,0:T(8,128)(2,1)S(1)} %copy-done.18), channel_id=1, source_target_pairs={{0,1},{1,2},{2,3},{4,5},{5,6},{6,7},{8,9},{9,10},{10,11},{12,13},{... | collective-permute-start | bytes 2211848 | tf_op jit(solution)/shard_map/ppermute | solution.py:889
  196.1 24.6 %collective-permute-start.41 = (bf16[4,96,768]{2,1,0:T(8,128)(2,1)S(1)}, bf16[4,96,768]{2,1,0:T(8,128)(2,1)}, u32[]{:S(2)}, u32[]{:S(2)}) collective-permute-start(bf16[4,96,768]{2,1,0:T(8,128)(2,1)S(1)} %copy-done.6), channel_id=1, source_target_pairs={{0,8},{4,12},{8,0},{12,4},{16,24},{20,28},{24,16},{28,20},{1,9},{5... | collective-permute-start | bytes 1769480 | tf_op jit(solution)/shard_map/ppermute | solution.py:860
  197.3 23.4 %collective-permute-start.40 = (bf16[4,112,768]{2,1,0:T(8,128)(2,1)S(1)}, bf16[4,112,768]{2,1,0:T(8,128)(2,1)}, u32[]{:S(2)}, u32[]{:S(2)}) collective-permute-start(bf16[4,112,768]{2,1,0:T(8,128)(2,1)S(1)} %copy-done.5), channel_id=1, source_target_pairs={{0,16},{4,20},{8,24},{12,28},{16,0},{20,4},{24,8},{28,12},{1,17},{... | collective-permute-start | bytes 2064392 | tf_op jit(solution)/shard_map/ppermute | solution.py:860
  210.1 16.0 %collective-permute-start.39 = (bf16[2,2,112,768]{3,2,1,0:T(8,128)(2,1)}, bf16[2,2,112,768]{3,2,1,0:T(8,128)(2,1)S(1)}, u32[]{:S(2)}, u32[]{:S(2)}) collective-permute-start(bf16[2,2,112,768]{3,2,1,0:T(8,128)(2,1)} %get-tuple-element.243), channel_id=1, source_target_pairs={{0,8},{4,12},{8,0},{12,4},{16,24},{20,28},{24,16},{28,20},{1,9},{5... | collective-permute-start | bytes 2064392 | tf_op jit(solution)/shard_map/ppermute | solution.py:860
  210.9 17.7 %collective-permute-start.43 = (bf16[2,2,112,768]{3,2,1,0:T(8,128)(2,1)}, bf16[2,2,112,768]{3,2,1,0:T(8,128)(2,1)S(1)}, u32[]{:S(2)}, u32[]{:S(2)}) collective-permute-start(bf16[2,2,112,768]{3,2,1,0:T(8,128)(2,1)} %get-tuple-element.248), channel_id=1, source_target_pairs={{0,16},{4,20},{8,24},{12,28},{16,0},{20,4},{24,8},{28,12},{1,17},{... | collective-permute-start | bytes 2064392 | tf_op jit(solution)/shard_map/ppermute | solution.py:860
  227.0 7.6 %collective-permute-start.42 = (bf16[2,112,768]{2,1,0:T(8,128)(2,1)S(1)}, bf16[2,112,768]{2,1,0:T(8,128)(2,1)S(1)}, u32[]{:S(2)}, u32[]{:S(2)}) collective-permute-start(bf16[2,112,768]{2,1,0:T(8,128)(2,1)S(1)} %get-tuple-element.282), channel_id=1, source_target_pairs={{0,16},{4,20},{8,24},{12,28},{16,0},{20,4},{24,8},{28,12},{1,17},{... | collective-permute-start | bytes 1032200 | tf_op jit(solution)/shard_map/ppermute | solution.py:860
  229.5 8.1 %collective-permute-start.44 = (bf16[2,112,768]{2,1,0:T(8,128)(2,1)S(1)}, bf16[2,112,768]{2,1,0:T(8,128)(2,1)S(1)}, u32[]{:S(2)}, u32[]{:S(2)}) collective-permute-start(bf16[2,112,768]{2,1,0:T(8,128)(2,1)S(1)} %get-tuple-element.280), channel_id=1, source_target_pairs={{0,8},{4,12},{8,0},{12,4},{16,24},{20,28},{24,16},{28,20},{1,9},{5... | collective-permute-start | bytes 1032200 | tf_op jit(solution)/shard_map/ppermute | solution.py:860
  240.6 13.2 %collective-permute-start.45 = (bf16[112,768]{1,0:T(8,128)(2,1)}, bf16[112,768]{1,0:T(8,128)(2,1)S(1)}, u32[]{:S(2)}, u32[]{:S(2)}) collective-permute-start(bf16[112,768]{1,0:T(8,128)(2,1)} %get-tuple-element.251), channel_id=1, source_target_pairs={{0,1},{1,2},{2,3},{3,0},{4,5},{5,6},{6,7},{7,4},{8,9},{9,10},{10,1... | collective-permute-start | bytes 516104 | tf_op jit(solution)/shard_map/ppermute | solution.py:934
  242.0 31.2 %collective-permute-start.46 = (bf16[112,768]{1,0:T(8,128)(2,1)}, bf16[112,768]{1,0:T(8,128)(2,1)S(1)}, u32[]{:S(2)}, u32[]{:S(2)}) collective-permute-start(bf16[112,768]{1,0:T(8,128)(2,1)} %get-tuple-element.252), channel_id=1, source_target_pairs={{0,2},{1,3},{2,0},{3,1},{4,6},{5,7},{6,4},{7,5},{8,10},{9,11},{10,... | collective-permute-start | bytes 516104 | tf_op jit(solution)/shard_map/ppermute | solution.py:934
  243.4 35.1 %collective-permute-start.47 = (bf16[112,768]{1,0:T(8,128)(2,1)}, bf16[112,768]{1,0:T(8,128)(2,1)S(1)}, u32[]{:S(2)}, u32[]{:S(2)}) collective-permute-start(bf16[112,768]{1,0:T(8,128)(2,1)} %get-tuple-element.253), channel_id=1, source_target_pairs={{0,3},{1,0},{2,1},{3,2},{4,7},{5,4},{6,5},{7,6},{8,11},{9,8},{10,9... | collective-permute-start | bytes 516104 | tf_op jit(solution)/shard_map/ppermute | solution.py:934
  279.5 9.8 %collective-permute-start.50 = (bf16[112,768]{1,0:T(8,128)(2,1)S(1)}, bf16[112,768]{1,0:T(8,128)(2,1)S(1)}, u32[]{:S(2)}, u32[]{:S(2)}) collective-permute-start(bf16[112,768]{1,0:T(8,128)(2,1)S(1)} %add_convert_fusion.9), channel_id=1, source_target_pairs={{0,1},{1,2},{2,3},{3,0},{4,5},{5,6},{6,7},{7,4},{8,9},{9,10},{10,1... | collective-permute-start | bytes 516104 | tf_op jit(solution)/shard_map/ppermute | solution.py:941
  279.6 59.6 %collective-permute-start.60 = (bf16[208,768]{1,0:T(8,128)(2,1)S(1)}, bf16[208,768]{1,0:T(8,128)(2,1)S(1)}, u32[]{:S(2)}, u32[]{:S(2)}) collective-permute-start(bf16[208,768]{1,0:T(8,128)(2,1)S(1)} %copy-done.32), channel_id=1, source_target_pairs={{0,1},{1,2},{2,3},{3,0},{4,5},{5,6},{6,7},{7,4},{8,9},{9,10},{10,1... | collective-permute-start | bytes 958472 | tf_op jit(solution)/shard_map/ppermute | solution.py:918
  280.1 59.0 %collective-permute-start.61 = (bf16[208,768]{1,0:T(8,128)(2,1)S(1)}, bf16[208,768]{1,0:T(8,128)(2,1)S(1)}, u32[]{:S(2)}, u32[]{:S(2)}) collective-permute-start(bf16[208,768]{1,0:T(8,128)(2,1)S(1)} %copy-done.31), channel_id=1, source_target_pairs={{0,2},{1,3},{2,0},{3,1},{4,6},{5,7},{6,4},{7,5},{8,10},{9,11},{10,... | collective-permute-start | bytes 958472 | tf_op jit(solution)/shard_map/ppermute | solution.py:918
  283.1 56.0 %collective-permute-start.62 = (bf16[208,768]{1,0:T(8,128)(2,1)S(1)}, bf16[208,768]{1,0:T(8,128)(2,1)S(1)}, u32[]{:S(2)}, u32[]{:S(2)}) collective-permute-start(bf16[208,768]{1,0:T(8,128)(2,1)S(1)} %copy-done.30), channel_id=1, source_target_pairs={{0,3},{1,0},{2,1},{3,2},{4,7},{5,4},{6,5},{7,6},{8,11},{9,8},{10,9... | collective-permute-start | bytes 958472 | tf_op jit(solution)/shard_map/ppermute | solution.py:918
  283.1 51.2 %collective-permute-start.49 = (bf16[112,768]{1,0:T(8,128)(2,1)S(1)}, bf16[112,768]{1,0:T(8,128)(2,1)S(1)}, u32[]{:S(2)}, u32[]{:S(2)}) collective-permute-start(bf16[112,768]{1,0:T(8,128)(2,1)S(1)} %add_convert_fusion.9), channel_id=1, source_target_pairs={{0,2},{1,3},{2,0},{3,1},{4,6},{5,7},{6,4},{7,5},{8,10},{9,11},{10,... | collective-permute-start | bytes 516104 | tf_op jit(solution)/shard_map/ppermute | solution.py:941
  289.3 47.4 %collective-permute-start.48 = (bf16[112,768]{1,0:T(8,128)(2,1)S(1)}, bf16[112,768]{1,0:T(8,128)(2,1)S(1)}, u32[]{:S(2)}, u32[]{:S(2)}) collective-permute-start(bf16[112,768]{1,0:T(8,128)(2,1)S(1)} %add_convert_fusion.9), channel_id=1, source_target_pairs={{0,3},{1,0},{2,1},{3,2},{4,7},{5,4},{6,5},{7,6},{8,11},{9,8},{10,9... | collective-permute-start | bytes 516104 | tf_op jit(solution)/shard_map/ppermute | solution.py:941
  336.8 31.9 %collective-permute-start.52 = (bf16[4,112,768]{2,1,0:T(8,128)(2,1)S(1)}, bf16[4,112,768]{2,1,0:T(8,128)(2,1)S(1)}, u32[]{:S(2)}, u32[]{:S(2)}) collective-permute-start(bf16[4,112,768]{2,1,0:T(8,128)(2,1)S(1)} %pad_maximum_fusion.refs_1_), channel_id=1, source_target_pairs={{0,16},{4,20},{8,24},{12,28},{16,0},{20,4},{24,8},{28,12},{1,17},{... | collective-permute-start | bytes 2064392 | tf_op jit(solution)/shard_map/ppermute | solution.py:723
  338.1 31.0 %collective-permute-start.51 = (bf16[4,112,768]{2,1,0:T(8,128)(2,1)S(1)}, bf16[4,112,768]{2,1,0:T(8,128)(2,1)S(1)}, u32[]{:S(2)}, u32[]{:S(2)}) collective-permute-start(bf16[4,112,768]{2,1,0:T(8,128)(2,1)S(1)} %pad_maximum_fusion.refs_1_), channel_id=1, source_target_pairs={{0,8},{4,12},{8,0},{12,4},{16,24},{20,28},{24,16},{28,20},{1,9},{5... | collective-permute-start | bytes 2064392 | tf_op jit(solution)/shard_map/ppermute | solution.py:723
  339.4 21.5 %collective-permute-start.63 = (bf16[208,768]{1,0:T(8,128)(2,1)S(1)}, bf16[208,768]{1,0:T(8,128)(2,1)S(1)}, u32[]{:S(2)}, u32[]{:S(2)}) collective-permute-start(bf16[208,768]{1,0:T(8,128)(2,1)S(1)} %add_convert_fusion.8.refs_1_), channel_id=1, source_target_pairs={{0,8},{4,12},{8,0},{12,4},{16,24},{20,28},{24,16},{28,20},{1,9},{5... | collective-permute-start | bytes 958472 | tf_op jit(solution)/shard_map/ppermute | solution.py:723
  339.8 21.2 %collective-permute-start.64 = (bf16[208,768]{1,0:T(8,128)(2,1)S(1)}, bf16[208,768]{1,0:T(8,128)(2,1)S(1)}, u32[]{:S(2)}, u32[]{:S(2)}) collective-permute-start(bf16[208,768]{1,0:T(8,128)(2,1)S(1)} %add_convert_fusion.8.refs_1_), channel_id=1, source_target_pairs={{0,16},{4,20},{8,24},{12,28},{16,0},{20,4},{24,8},{28,12},{1,17},{... | collective-permute-start | bytes 958472 | tf_op jit(solution)/shard_map/ppermute | solution.py:723
  360.8 7.8 %collective-permute-start.65 = (bf16[112,768]{1,0:T(8,128)(2,1)S(1)}, bf16[112,768]{1,0:T(8,128)(2,1)S(1)}, u32[]{:S(2)}, u32[]{:S(2)}) collective-permute-start(bf16[112,768]{1,0:T(8,128)(2,1)S(1)} %slice.94), channel_id=1, source_target_pairs={{0,16},{4,20},{8,24},{12,28},{16,0},{20,4},{24,8},{28,12},{1,17},{... | collective-permute-start | bytes 516104 | tf_op jit(solution)/shard_map/ppermute | solution.py:723
  362.4 6.9 %collective-permute-start.67 = (bf16[208,768]{1,0:T(8,128)(2,1)S(1)}, bf16[208,768]{1,0:T(8,128)(2,1)S(1)}, u32[]{:S(2)}, u32[]{:S(2)}) collective-permute-start(bf16[208,768]{1,0:T(8,128)(2,1)S(1)} %add_convert_fusion.8.refs_1_), channel_id=1, source_target_pairs={{0,4},{4,0},{8,12},{12,8},{16,20},{20,16},{24,28},{28,24},{1,5},{5... | collective-permute-start | bytes 958472 | tf_op jit(solution)/shard_map/ppermute | solution.py:723
  365.2 6.6 %collective-permute-start.69 = (bf16[208,768]{1,0:T(8,128)(2,1)S(1)}, bf16[208,768]{1,0:T(8,128)(2,1)S(1)}, u32[]{:S(2)}, u32[]{:S(2)}) collective-permute-start(bf16[208,768]{1,0:T(8,128)(2,1)S(1)} %collective-permute-done.64.refs_3_), channel_id=1, source_target_pairs={{0,4},{4,0},{8,12},{12,8},{16,20},{20,16},{24,28},{28,24},{1,5},{5... | collective-permute-start | bytes 958472 | tf_op jit(solution)/shard_map/ppermute | solution.py:723
  369.3 9.3 %collective-permute-start.54 = (bf16[2,112,768]{2,1,0:T(8,128)(2,1)S(1)}, bf16[2,112,768]{2,1,0:T(8,128)(2,1)S(1)}, u32[]{:S(2)}, u32[]{:S(2)}) collective-permute-start(bf16[2,112,768]{2,1,0:T(8,128)(2,1)S(1)} %slice.93), channel_id=1, source_target_pairs={{0,8},{4,12},{8,0},{12,4},{16,24},{20,28},{24,16},{28,20},{1,9},{5... | collective-permute-start | bytes 1032200 | tf_op jit(solution)/shard_map/ppermute | solution.py:723
  370.6 9.3 %collective-permute-start.53 = (bf16[2,112,768]{2,1,0:T(8,128)(2,1)S(1)}, bf16[2,112,768]{2,1,0:T(8,128)(2,1)S(1)}, u32[]{:S(2)}, u32[]{:S(2)}) collective-permute-start(bf16[2,112,768]{2,1,0:T(8,128)(2,1)S(1)} %slice.92), channel_id=1, source_target_pairs={{0,16},{4,20},{8,24},{12,28},{16,0},{20,4},{24,8},{28,12},{1,17},{... | collective-permute-start | bytes 1032200 | tf_op jit(solution)/shard_map/ppermute | solution.py:723
  371.8 13.5 %collective-permute-start.55 = (bf16[4,112,768]{2,1,0:T(8,128)(2,1)S(1)}, bf16[4,112,768]{2,1,0:T(8,128)(2,1)S(1)}, u32[]{:S(2)}, u32[]{:S(2)}) collective-permute-start(bf16[4,112,768]{2,1,0:T(8,128)(2,1)S(1)} %pad_maximum_fusion.refs_1_), channel_id=1, source_target_pairs={{0,4},{4,0},{8,12},{12,8},{16,20},{20,16},{24,28},{28,24},{1,5},{5... | collective-permute-start | bytes 2064392 | tf_op jit(solution)/shard_map/ppermute | solution.py:723
  372.7 12.6 %collective-permute-start.57 = (bf16[4,112,768]{2,1,0:T(8,128)(2,1)S(1)}, bf16[4,112,768]{2,1,0:T(8,128)(2,1)S(1)}, u32[]{:S(2)}, u32[]{:S(2)}) collective-permute-start(bf16[4,112,768]{2,1,0:T(8,128)(2,1)S(1)} %collective-permute-done.52.refs_3_), channel_id=1, source_target_pairs={{0,4},{4,0},{8,12},{12,8},{16,20},{20,16},{24,28},{28,24},{1,5},{5... | collective-permute-start | bytes 2064392 | tf_op jit(solution)/shard_map/ppermute | solution.py:723
  372.8 12.6 %collective-permute-start.56 = (bf16[4,112,768]{2,1,0:T(8,128)(2,1)S(1)}, bf16[4,112,768]{2,1,0:T(8,128)(2,1)S(1)}, u32[]{:S(2)}, u32[]{:S(2)}) collective-permute-start(bf16[4,112,768]{2,1,0:T(8,128)(2,1)S(1)} %collective-permute-done.51.refs_2_), channel_id=1, source_target_pairs={{0,4},{4,0},{8,12},{12,8},{16,20},{20,16},{24,28},{28,24},{1,5},{5... | collective-permute-start | bytes 2064392 | tf_op jit(solution)/shard_map/ppermute | solution.py:723
  378.6 6.8 %collective-permute-start.59 = (bf16[2,112,768]{2,1,0:T(8,128)(2,1)S(1)}, bf16[2,112,768]{2,1,0:T(8,128)(2,1)S(1)}, u32[]{:S(2)}, u32[]{:S(2)}) collective-permute-start(bf16[2,112,768]{2,1,0:T(8,128)(2,1)S(1)} %collective-permute-done.54.refs_5_), channel_id=1, source_target_pairs={{0,4},{4,0},{8,12},{12,8},{16,20},{20,16},{24,28},{28,24},{1,5},{5... | collective-permute-start | bytes 1032200 | tf_op jit(solution)/shard_map/ppermute | solution.py:723
  (82 other events, 997.5 us)
Sparse Core Ops, SparseCore 0:
  220.8 100.8 all-gather.2

commit v3 on v2

--- a/solution.py
+++ b/solution.py
@@ -18,12 +18,12 @@
 
 OWN, WINDOW, SHIFT, LOCAL, LIMIT, FLAGGED, PLACE, GROUP, HALF, PIECE, SLOT = 0, 1, 2, 3, 6, 9, 12, 15, 16, 18, 22
 PIECES = 8
-VMEM_LIMIT = 56 << 20
+CORE, X, Y = 1, 2, 4
 PER_MICROSECOND = 1e9
 MICROSECONDS = {
-    "pack": 2, "project": 9, "attend": 11, "first_norm": 7, "shard": 6, "turn": 24, "lower": 5, "ffn_keep": 9,
-    "attend_back": 20, "sides": 7, "copied_send": 11, "own": 7, "copied_keep": 9, "input_final": 3,
-    "ffn_spread": 3, "ffn_final": 4, "copied_spread": 2, "copied_final": 8,
+    "pack": 1, "project": 5, "attend": 9, "first_norm": 4, "shard": 3, "turn": 21, "lower": 2, "ffn_keep": 4,
+    "attend_back": 15, "sides": 3, "copied_send": 4, "own": 3, "copied_keep": 5, "input_final": 3,
+    "ffn_spread": 1, "ffn_final": 3, "copied_spread": 1, "copied_final": 6,
 }
 
 
@@ -93,24 +93,24 @@
     return jnp.where(key < limit, scores, masked_score)
 
 
-def pack_kernel(info, widen, narrow, widen_l, narrow_l, bias, mine, small, hidden):
-    rows = piece_rows(info, 0)
-    mine[0] = widen[rows, :]
-    mine[1] = narrow[rows, :]
-    width_l = widen_l.shape[0]
-    small[:, width_l:] = jnp.zeros((small.shape[0], small.shape[1] - width_l), BF)
-    small[:width_l, :width_l] = widen_l[...]
-    small[width_l:, :width_l] = narrow_l[...]
+def pack_kernel(place, weights, layout, bias, mine):
+    mine[:192] = weights[...]
+    width_l = layout.shape[1]
     high = bias[...].astype(BF).astype(F32)
     middle = (bias[...] - high).astype(BF).astype(F32)
     low = bias[...] - high - middle
-    upper = jnp.concatenate([high, middle], axis=0)
-    hidden[...] = jnp.concatenate([upper, jnp.concatenate([low, jnp.zeros_like(low)], axis=0)], axis=1).astype(BF)
-
-
-def biases_of(hidden):
-    split = hidden[...].astype(F32)
-    rows = split[:8, :LANES] + split[8:, :LANES] + split[:8, LANES:]
+    biases = jnp.concatenate([high, middle, low, jnp.zeros_like(low)], axis=0)
+    mine[192:, :] = jnp.zeros((32, mine.shape[1]), BF)
+    empty = jnp.zeros((8, width_l), F32)
+    both = layout[...].astype(F32)
+    mine[192:, :width_l] = jnp.concatenate([both[:24], empty], axis=0).astype(BF)
+    mine[192:, 256 : 256 + width_l] = jnp.concatenate([both[24:], empty], axis=0).astype(BF)
+    mine[192:, 512:640] = biases.astype(BF)
+
+
+def biases_of(rest):
+    split = rest[:, 512:640].astype(F32)
+    rows = split[:8] + split[8:16] + split[16:24]
     text = jnp.concatenate([rows[i : i + 1] for i in range(6)], axis=1)
     layout = jnp.concatenate([rows[i : i + 1] for i in (6, 7)], axis=1)
     return text, layout
@@ -234,32 +234,36 @@
     normed = normalised(first)[0] * gl[0:1, :] + sl[0:1, :]
     low_l[...] = normed.astype(BF)
     normed_l[...] = normed + bl[3:4, :]
-    shard_forward(low_t, widen, biases_of(hidden)[0], narrow, active, slope, total)
+    shard_forward(low_t, widen, biases_of(hidden[192:, :])[0], narrow, active, slope, total)
 
 
 def piece_rows(info, rel):
     return pl.ds(pl.multiple_of(info[HALF + rel // 4] + info[PIECE + rel % 4], 32), 96)
 
 
-def load_shard(info, plan, refs, weights, sems, at):
-    copies = []
-    for i, (rel, low, high) in enumerate(plan):
-        copy = pltpu.make_async_copy(
-            refs[i], weights.at[at, pl.ds(low, high - low), piece_rows(info, rel), :], sems.at[at, i]
-        )
-        copy.start()
-        copies.append(copy)
-    return copies
-
-
-def shard_kernel(plan, info, low, total_in, hidden, *refs):
+def place_shard(info, plan, refs, weights):
+    for ref, (rel, low, high) in zip(refs, plan):
+        for part in (0, 1):
+            if low <= 96 * part and high >= 96 * (part + 1):
+                weights[part, piece_rows(info, rel), :] = ref[96 * part - low : 96 * (part + 1) - low, :]
+
+
+def place_layout(info, plan, refs, both):
+    for ref, (rel, low, high) in zip(refs, plan):
+        if high == 224:
+            at = pl.multiple_of((info[HALF + rel // 4] + info[PIECE + rel % 4]) // 4, 8)
+            both[pl.ds(at, 24), :] = ref[192 - low :, :512].astype(F32)[:24]
+
+
+def shard_kernel(plan, info, low, total_in, *refs):
     pieces = refs[: len(plan)]
-    active, slope, total, weights, sems = refs[len(plan) :]
-    copies = load_shard(info, plan, pieces, weights, sems, 0)
+    active, slope, total, weights, layout, both = refs[len(plan) :]
+    place_shard(info, plan, pieces, weights)
+    place_layout(info, plan, pieces, both)
+    layout[...] = both[...].astype(BF)
     total[...] = total_in[...]
-    for copy in copies:
-        copy.wait()
-    shard_forward(low, weights.at[0, 0], biases_of(hidden)[0], weights.at[0, 1], active, slope, total)
+    bias = biases_of(pieces[0][192:, :])[0]
+    shard_forward(low, weights.at[0], bias, weights.at[1], active, slope, total)
 
 
 def upper_back(total, gain, shift, cot, keep, result, dout, sums):
@@ -275,20 +279,21 @@
     total[...] = dsecond
 
 
-def turn_kernel(plans, info, *refs):
+def turn_kernel(plan, info, *refs):
     refs = list(refs)
     take = lambda n: [refs.pop(0) for _ in range(n)]
     low, total_in, gain, shift, cot, widen_own, narrow_own = take(7)
     slopes_in, actives = take(3), take(3)
     low_l, normed_l, gain_l, shift_l, cot_lt = take(5)
-    small, hidden = take(4), take(4)
-    pieces = [take(len(plan)) for plan in plans]
+    widen_own_l, narrow_own_l, layout_one, layout_three, mine, first_piece, third_piece = take(7)
+    weights_one, weights_three = take(2)
+    pieces = take(len(plan))
     result, dout, dhid, dnormed, sums, hsums, active = take(7)
     result_lt, dnormed_l, sums_l, hsums_l = take(4)
     send_a, send_b, pack = take(3)
-    weights, slope, slope_l, active_l, dhid_l, dout_l, result_l, grad, sems = take(9)
+    weights, slope, slope_l, active_l, dhid_l, dout_l, result_l, both = take(8)
     shards = dhid.shape[0]
-    copies = [load_shard(info, plan, piece, weights, sems, s) for s, (plan, piece) in enumerate(zip(plans, pieces))]
+    width = low.shape[1]
     dnormed[...] = total_in[...]
     dnormed_l[...] = normed_l[...]
     row = lax.broadcasted_iota(jnp.int32, (LANES, 1), 0)
@@ -299,14 +304,19 @@
     keep = jnp.concatenate(keep, axis=0)
 
     width_l = low_l.shape[1]
+    hidden_bias = [biases_of(ref[192:, :]) for ref in (mine, first_piece, pieces[0], third_piece)]
+    place_layout(info, plan, pieces, both)
+    last_l = both[...].astype(BF)
+    layouts = [(widen_own_l[...], narrow_own_l[...])]
+    layouts += [(v[:, :width_l], v[:, 256 : 256 + width_l]) for v in (layout_one[...], last_l, layout_three[...])]
     for s in range(shards):
-        widen, narrow = (small[s][i * width_l : (i + 1) * width_l, :width_l] for i in (0, 1))
-        shard_forward(low_l, widen, biases_of(hidden[s])[1][:, :width_l], narrow, active_l.at[s], slope_l.at[s], dnormed_l)
+        widen, narrow = layouts[s]
+        shard_forward(low_l, widen, hidden_bias[s][1][:, :width_l], narrow, active_l.at[s], slope_l.at[s], dnormed_l)
     cot_l = tn(cot_lt[...], identity(width_l))
     upper_back(dnormed_l, gain_l, shift_l, cot_l, keep, result_l, dout_l, sums_l)
     result_lt[...] = nt(identity(width_l), result_l[...]).astype(BF)
     for s in range(shards):
-        widen, narrow = (small[s][i * width_l : (i + 1) * width_l, :width_l] for i in (0, 1))
+        widen, narrow = layouts[s]
         shard_backward(dout_l, narrow, slope_l.at[s], widen, dhid_l.at[s], hsums_l.at[s], dnormed_l)
     for s in range(shards):
         pack[s] = jnp.zeros_like(pack[s])
@@ -317,32 +327,20 @@
         pack[s, :128, 256 : 256 + width_l] = g[:128]
         pack[s, 64:, 512 : 512 + width_l] = g[128:]
 
-    for copy in copies[1]:
-        copy.wait()
-    shard_forward(low, weights.at[1, 0], biases_of(hidden[2])[0], weights.at[1, 1], active, slope, dnormed)
+    place_shard(info, plan, pieces, weights)
+    shard_forward(low, weights.at[0], hidden_bias[2][0], weights.at[1], active, slope, dnormed)
     upper_back(dnormed, gain, shift, cot[...], keep, result, dout, sums)
     shard_backward(dout, narrow_own, slopes_in[0], widen_own, dhid.at[0], hsums.at[0], dnormed)
-    for copy in copies[0] + copies[2]:
-        copy.wait()
-    shard_backward(dout, weights.at[0, 1], slopes_in[1], weights.at[0, 0], dhid.at[1], hsums.at[1], dnormed)
-    shard_backward(dout, weights.at[1, 1], slope, weights.at[1, 0], dhid.at[2], hsums.at[2], dnormed)
-    shard_backward(dout, weights.at[2, 1], slopes_in[2], weights.at[2, 0], dhid.at[3], hsums.at[3], dnormed)
-
-    half = pl.ds(pl.multiple_of(info[HALF + 1], LANES), grad.shape[0])
+    shard_backward(dout, weights_one.at[1], slopes_in[1], weights_one.at[0], dhid.at[1], hsums.at[1], dnormed)
+    shard_backward(dout, weights.at[1], slope, weights.at[0], dhid.at[2], hsums.at[2], dnormed)
+    shard_backward(dout, weights_three.at[1], slopes_in[2], weights_three.at[0], dhid.at[3], hsums.at[3], dnormed)
+
+    half = pl.ds(pl.multiple_of(info[HALF + 1], LANES), send_b.shape[1])
+    more = pl.ds(pl.multiple_of(info[HALF + 1] // 6, 64), 64)
     for s, act in enumerate((actives[0], actives[1], active, actives[2])):
-        grad[...] = tn(act[:, half], dout[...])
-
-        def store_a(rel, rows, s=s):
-            send_a[s, rel % 2, rel // 2, :96] = rows.astype(BF)
-            send_a[s, rel % 2, rel // 2, 96:] = pack[s, extra_rows(info, 1, rel), :]
-
-        pieces_of(info, grad, store_a)
-        grad[...] = tn(low[:, half], dhid[s])
-
-        def store_b(rel, rows, s=s):
-            send_b[s, rel // 2, rel % 2] = rows.astype(BF)
-
-        pieces_of(info, grad, store_b)
+        send_a[s, :384] = tn(act[:, half], dout[...]).astype(BF)
+        send_a[s, 384:] = pack[s, more, :]
+        send_b[s] = tn(low[:, half], dhid[s]).astype(BF)
 
 
 def lower_back(first, dnormed, gain, dense, dfirst, dbranch, dcontext, sums):
@@ -378,32 +376,24 @@
     return pl.ds(pl.multiple_of((info[HALF + half] + info[PIECE + rel]) // 6, EXTRA), EXTRA)
 
 
-def pieces_of(info, grad, store):
-    for rel in range(4):
-        store(rel, grad[pl.ds(pl.multiple_of(info[PIECE + rel], 32), 96), :])
-
-
 def ffn_keep_kernel(
-    info, a0, a1, a2, a3, dout, low, dhid, recv_a, recv_b, pack, next_a, keep_a, next_b, keep_b, grad,
+    info, a0, a1, a2, a3, dout, low, dhid, recv_a, recv_b, pack, next_a1, next_a2, next_b1, next_b2, keep_a, keep_b, sum_a, sum_b,
 ):
-    half = pl.ds(pl.multiple_of(info[HALF], LANES), grad.shape[0])
+    half = pl.ds(pl.multiple_of(info[HALF], LANES), 384)
+    more = pl.ds(pl.multiple_of(info[HALF] // 6, 64), 64)
     for s, active in enumerate((a0, a1, a2, a3)):
-        grad[...] = tn(active[:, half], dout[...])
-
-        def store_a(rel, rows, s=s):
-            to = next_a if rel % 2 else keep_a
-            recv = recv_a[s, rel % 2, rel // 2].astype(F32)
-            to[rel // 2, s, :96] = (rows + recv[:96]).astype(BF)
-            to[rel // 2, s, 96:] = (pack[s, extra_rows(info, 0, rel), :].astype(F32) + recv[96:]).astype(BF)
-
-        pieces_of(info, grad, store_a)
-        grad[...] = tn(low[:, half], dhid[s])
-
-        def store_b(rel, rows, s=s):
-            to = next_b if rel // 2 else keep_b
-            to[rel % 2, s] = (rows + recv_b[s, rel // 2, rel % 2].astype(F32)).astype(BF)
-
-        pieces_of(info, grad, store_b)
+        sum_a[:384] = (tn(active[:, half], dout[...]) + recv_a[s, :384].astype(F32)).astype(BF)
+        sum_a[384:] = (pack[s, more, :].astype(F32) + recv_a[s, 384:].astype(F32)).astype(BF)
+        sum_b[...] = (tn(low[:, half], dhid[s]) + recv_b[s].astype(F32)).astype(BF)
+        next_a, next_b = ((next_a1, next_b1), (next_a2, next_b2))[s // 2]
+        for rel in range(4):
+            rows = pl.ds(pl.multiple_of(info[PIECE + rel], 32), 96)
+            rest = pl.ds(pl.multiple_of(384 + info[PIECE + rel] // 6, EXTRA), EXTRA)
+            to = next_a.at[rel // 2, s % 2] if rel % 2 else keep_a.at[rel // 2, s]
+            to[:96] = sum_a[rows, :]
+            to[96:] = sum_a[rest, :]
+            to = next_b.at[rel % 2, s % 2] if rel // 2 else keep_b.at[rel % 2, s]
+            to[...] = sum_b[rows, :]
 
 
 def add(a, b, *more):
@@ -413,15 +403,17 @@
     return total.astype(BF)
 
 
-def add_split(keep, recv):
-    return add(keep[1], recv[1]), add(keep[0], recv[0])
-
-
-def ffn_spread_kernel(info, keep_a, recv_a, keep_b, recv_b, *outs):
+def add_split(keep, recv, token=None):
+    later = () if token is None else (token[0, 0],)
+    return add(keep[1], recv[1], *later), add(keep[0], recv[0], *later)
+
+
+def ffn_spread_kernel(info, keep_a, recv_a, keep_b, recv_b, out):
     rows = keep_a.shape[1]
-    for k, out in enumerate(outs):
-        out[:rows] = (keep_a[k].astype(F32) + recv_a[k].astype(F32)).astype(out.dtype)
-        out[rows:] = (keep_b[k].astype(F32) + recv_b[k].astype(F32)).astype(out.dtype)
+    for s in range(4):
+        group = lax.rem(info[GROUP] + s, 4)
+        out[group, :rows] = (keep_a[s].astype(F32) + recv_a[s].astype(F32)).astype(BF)
+        out[group, rows:] = (keep_b[s].astype(F32) + recv_b[s].astype(F32)).astype(BF)
 
 
 def copied_spread_kernel(info, keep_a, recv_a, keep_b, recv_b, *outs):
@@ -577,14 +569,17 @@
     store_packed(out, text, layout)
 
 
-def input_final_kernel(info, rows, text, layout):
-    own_rows = rows.shape[1] * 4 // 5
-    half = layout.shape[0] // 2
-    for t in range(rows.shape[0]):
-        at = pl.ds(t * own_rows, own_rows)
-        text[at, :] = rows[t, :own_rows, :].astype(F32)
-        layout[:half, at] = rows[t, own_rows:, :own_rows].astype(F32)
-        layout[half:, at] = rows[t, own_rows:, own_rows:].astype(F32)
+def input_final_kernel(info, own, l1, l2, l3, r1, r2, r3, text, layout):
+    own_rows, half = own.shape[0] * 4 // 5, layout.shape[0] // 2
+    for distance, rows in ((0, own), (-1, l1), (-2, l2), (-3, l3), (1, r1), (2, r2), (3, r3)):
+        group = info[GROUP] + distance
+
+        @pl.when((group >= 0) & (group < 4))
+        def _():
+            at = pl.ds(pl.multiple_of(group * own_rows, LANES), own_rows)
+            text[at, :] = rows[:own_rows, :].astype(F32)
+            layout[:half, at] = rows[own_rows:, :own_rows].astype(F32)
+            layout[half:, at] = rows[own_rows:, own_rows:].astype(F32)
 
 
 def extras(
@@ -618,7 +613,7 @@
     extra[2 * width_l : 2 * width_l + 32, :] = small[...].astype(BF)
 
 
-def copied_grads(info, xt, dq, dk, dv, ct, db, half, grad, store):
+def copied_grads(info, xt, dq, dk, dv, ct, db, half, store):
     own_rows = dq.shape[0]
     window = dk.shape[0] - 2 * own_rows
     own = pl.ds(pl.multiple_of(info[OWN], LANES), own_rows)
@@ -626,55 +621,46 @@
     middle = pl.ds(own_rows, window)
     for block in range(4):
         if block == 0:
-            grad[...] = tn(xt[own, half], dq[...])
+            grad = tn(xt[own, half], dq[...])
         elif block == 1:
-            grad[...] = tn(xt[seen, half], dk[middle, :])
+            grad = tn(xt[seen, half], dk[middle, :])
         elif block == 2:
-            grad[...] = tn(xt[seen, half], dv[middle, :])
+            grad = tn(xt[seen, half], dv[middle, :])
         else:
-            grad[...] = tn(ct[:, half], db[...])
-        slot = info[SLOT + block]
-        for p in range(2):
-            for q in range(2):
-                row = jnp.where(slot < 2, info[PIECE + p + 2 * q], info[PIECE + q + 2 * p])
-                store(block, slot, p, q, row, grad[pl.ds(pl.multiple_of(row, 32), 96), :])
+            grad = tn(ct[:, half], db[...])
+        store(block, info[SLOT + block], grad)
 
 
 def copied_send_kernel(
     info, xt, dq, dk, dv, ct, db, xlt, dq_l, dk_l, dv_l, cl, db_l, sums_a, sums_b, hsums, sums_al, sums_bl, hsums_l,
-    send, extra, grad, small,
+    send, extra, small,
 ):
-    half = pl.ds(pl.multiple_of(info[HALF + 1], LANES), grad.shape[0])
+    half = pl.ds(pl.multiple_of(info[HALF + 1], LANES), 384)
     extras(info, xlt, dq, dv, dq_l, dk_l, dv_l, cl, db_l, sums_a, sums_b, hsums, sums_al, sums_bl, hsums_l, extra, small)
 
-    def store(block, slot, p, q, row, rows):
-        at = pl.multiple_of(128 * block + (info[HALF + 1] + row) // 6, EXTRA)
-        send[slot, p, q, :96] = rows.astype(BF)
-        send[slot, p, q, 96:] = extra[pl.ds(at, EXTRA), :]
-
-    copied_grads(info, xt, dq, dk, dv, ct, db, half, grad, store)
-
-
-def copied_keep_kernel(info, xt, dq, dk, dv, ct, db, extra, recv, next_a, keep_a, next_b, keep_b, grad):
-    half = pl.ds(pl.multiple_of(info[HALF], LANES), grad.shape[0])
-
-    def store(block, slot, p, q, row, rows):
-        at = pl.multiple_of(128 * block + (info[HALF] + row) // 6, EXTRA)
-        got = recv[slot, p, q].astype(F32)
-        text = (rows + got[:96]).astype(BF)
-        rest = (extra[pl.ds(at, EXTRA), :].astype(F32) + got[96:]).astype(BF)
-
-        @pl.when(slot < 2)
-        def _():
-            (next_a if p else keep_a)[q, slot, :96] = text
-            (next_a if p else keep_a)[q, slot, 96:] = rest
-
-        @pl.when(slot >= 2)
-        def _():
-            (next_b if p else keep_b)[q, slot - 2, :96] = text
-            (next_b if p else keep_b)[q, slot - 2, 96:] = rest
-
-    copied_grads(info, xt, dq, dk, dv, ct, db, half, grad, store)
+    def store(block, slot, grad):
+        send[slot, :384] = grad.astype(BF)
+        send[slot, 384:] = extra[pl.ds(pl.multiple_of(128 * block + info[HALF + 1] // 6, 64), 64), :]
+
+    copied_grads(info, xt, dq, dk, dv, ct, db, half, store)
+
+
+def copied_keep_kernel(info, xt, dq, dk, dv, ct, db, extra, recv, next_a, keep_a, next_b, keep_b, total):
+    half = pl.ds(pl.multiple_of(info[HALF], LANES), 384)
+
+    def store(block, slot, grad):
+        more = pl.ds(pl.multiple_of(128 * block + info[HALF] // 6, 64), 64)
+        total[slot, :384] = (grad + recv[slot, :384].astype(F32)).astype(BF)
+        total[slot, 384:] = (extra[more, :].astype(F32) + recv[slot, 384:].astype(F32)).astype(BF)
+
+    copied_grads(info, xt, dq, dk, dv, ct, db, half, store)
+    for slot in range(4):
+        for rel in range(4):
+            x_part, y_part = rel % 2, rel // 2
+            first, second = (x_part, y_part) if slot < 2 else (y_part, x_part)
+            out = ((keep_a, next_a), (keep_b, next_b))[slot // 2][first].at[second, slot % 2]
+            out[:96] = total[slot, pl.ds(pl.multiple_of(info[PIECE + rel], 32), 96), :]
+            out[96:] = total[slot, pl.ds(pl.multiple_of(384 + info[PIECE + rel] // 6, EXTRA), EXTRA), :]
 
 
 SM = pl.BlockSpec(memory_space=pltpu.SMEM)
@@ -682,10 +668,16 @@
 HB = pl.BlockSpec(memory_space=pl.ANY)
 
 
+def vmem_of(operands, outs, scratch):
+    held = list(operands) + list(outs) + [v for v in scratch if str(v.memory_space) == "vmem"]
+    return int(1.1 * sum(math.prod(v.shape) * jnp.dtype(v.dtype).itemsize for v in held)) + (8 << 20)
+
+
 def call(name, kernel, operands, outs, scratch=(), after=(), in_hbm=0):
     operands = tuple(operands)
     outs = tuple(outs) + (shape((8, LANES), F32),)
-    specs = [HB] * len(after) + [SM] + [VM] * (len(operands) - 1 - in_hbm) + [HB] * in_hbm
+    specs = [HB] * len(after) + [SM] + [VM] * (len(operands) - 1 - in_hbm) + [pl.BlockSpec(memory_space=pltpu.HBM)] * in_hbm
+    limit = vmem_of(operands[1 : len(operands) - in_hbm], outs, scratch)
     operands = tuple(after) + operands
     at = len(operands) + len(outs) - 1
 
@@ -700,7 +692,7 @@
         out_specs=[VM] * len(outs),
         scratch_shapes=list(scratch),
         cost_estimate=pl.CostEstimate(flops=int(MICROSECONDS[name] * PER_MICROSECOND), bytes_accessed=0, transcendentals=0),
-        compiler_params=pltpu.CompilerParams(vmem_limit_bytes=VMEM_LIMIT),
+        compiler_params=pltpu.CompilerParams(vmem_limit_bytes=limit),
         name=name,
     )(*operands)
 
@@ -713,28 +705,45 @@
     return [(i, i ^ bit) for i in range(planes)]
 
 
-def tie(value, *tokens):
-    return lax.optimization_barrier((value, tokens))[0]
-
-
-def spread(piece, planes, split, mid=None, second=(), third=()):
-    parts = piece.shape[0]
-    core, x, y = 1, 2, 4
-    send = lambda v, bit: lax.ppermute(v, "dp", flip(planes, bit))
-    later = lambda v, tokens: tie(v, *tokens) if tokens else v
-    by_x, by_y = send(piece, x), send(piece, y)
-    held = [(later(v, second), rel, 0, parts) for rel, v in enumerate((piece, by_x, by_y))]
-    by_x, by_y = held[1][0], held[2][0]
+def gate(values, *tokens):
+    outs = pl.pallas_call(
+        lambda *refs: None,
+        out_shape=tuple(shape(v.shape, v.dtype) for v in values),
+        in_specs=[HB] * (len(values) + len(tokens)),
+        out_specs=[HB] * len(values),
+        input_output_aliases={i: i for i in range(len(values))},
+        cost_estimate=pl.CostEstimate(flops=0, bytes_accessed=0, transcendentals=0),
+        compiler_params=pltpu.CompilerParams(vmem_limit_bytes=1 << 20),
+        name="gate",
+    )(*values, *tokens)
+    return list(outs)
+
+
+def around(planes):
+    return lambda v, bit: lax.ppermute(v, "dp", flip(planes, bit))
+
+
+def forward(piece, by_x, by_y, planes, split, mid=None):
+    across, parts = around(planes), piece.shape[0]
     if split == "x":
-        forwarded = [(send(by_x, y), 3, 0, parts)]
-    elif split == "y":
-        forwarded = [(send(by_y, x), 3, 0, parts)]
-    else:
-        mid = mid or parts // 2
-        forwarded = [(send(by_x[:mid], y), 3, 0, mid), (send(by_y[mid:], x), 3, mid, parts)]
-    held += [(later(v, third), rel, low, high) for v, rel, low, high in forwarded]
-    held += [(send(v, core), rel + 4, low, high) for v, rel, low, high in held]
+        return [(across(by_x, Y), 3, 0, parts)]
+    if split == "y":
+        return [(across(by_y, X), 3, 0, parts)]
+    mid = mid or parts // 2
+    return [(across(by_x[:mid], Y), 3, 0, mid), (across(by_y[mid:], X), 3, mid, parts)]
+
+
+def to_core(held, planes):
+    across = around(planes)
+    held = held + [(across(v, CORE), rel + 4, low, high) for v, rel, low, high in held]
     return [h[0] for h in held], tuple(h[1:] for h in held)
+
+
+def spread(piece, planes, mid=None):
+    across, parts = around(planes), piece.shape[0]
+    by_x, by_y = across(piece, X), across(piece, Y)
+    held = [(piece, 0, 0, parts), (by_x, 1, 0, parts), (by_y, 2, 0, parts)]
+    return to_core(held + forward(piece, by_x, by_y, planes, "half", mid), planes)
 
 
 def per_device(
@@ -789,13 +798,18 @@
     shift_from = lambda k: [(i, (i - k) % groups) for i in range(groups)]
     shift_to = lambda k: [(i, (i + k) % groups) for i in range(groups)]
     bias = jnp.concatenate([text_hidden_bias, layout_hidden_bias, jnp.zeros((8 * LANES - hid - hid_l,), F32)])
-    mine, small, hidden, packed_up = call(
+    across = around(planes)
+    row = row_of(0, 0, 0)
+    mine, packed_up = call(
         "pack", pack_kernel,
-        (info, text_widen, text_narrow, layout_widen, layout_narrow, bias.reshape(8, LANES)),
-        (shape((2, piece, width)), shape((2 * width_l, wide)), shape((16, wide))),
-    )
-    come = {k: lax.ppermute(mine, "tensor", shift_from(k)) for k in (1, 3)}
-    hiddens = [hidden] + [lax.ppermute(hidden, "tensor", shift_from(k)) for k in (1, 2, 3)]
+        (jnp.zeros((1,), jnp.int32),
+         jnp.concatenate([lax.dynamic_slice_in_dim(v, row, piece, 0) for v in (text_widen, text_narrow)], axis=0),
+         jnp.concatenate([lax.dynamic_slice_in_dim(v, row // 4, piece // 4, 0) for v in (layout_widen, layout_narrow)], axis=0),
+         bias.reshape(8, LANES)),
+        (shape((2 * piece + 32, width)),),
+    )
+    from_group = lambda v, k: lax.ppermute(v, "tensor", shift_from(k))
+    come = {k: from_group(mine, k) for k in (1, 3)}
 
     xlt = layout_input.T
     qt, kt, vt, ql, kl, vl, xl_own, wl, projected = call(
@@ -806,59 +820,71 @@
          shape((own, width_l)), shape((width_l, 3 * wide))),
         after=(packed_up,),
     )
-    come[2] = lax.ppermute(tie(mine, projected), "tensor", shift_from(2))
+    mine_again, come[1], come[3] = gate((mine, come[1], come[3]), projected)
+    come[2] = from_group(mine_again, 2)
+    by_x, by_y = {}, {}
+    for k in (1, 3):
+        by_x[k], by_y[k] = across(come[k], X), across(come[k], Y)
     ct, cl, lse, attended = call(
         "attend", attend_kernel,
         (info, qt, kt, vt, ql, kl, vl),
         (shape((own, width)), shape((own, width_l)), shape((own, LANES), F32)),
         scratch=(pltpu.VMEM((own, wide), F32),),
     )
+    by_x[1], by_y[3] = gate((by_x[1], by_y[3]), attended)
+    forwarded = {k: forward(come[k], by_x[k], by_y[k], planes, {1: "x", 3: "y"}[k]) for k in (1, 3)}
     first_t, first_l, low_t, low_l, normed_l, active0, slope0, total_t, first_done = call(
         "first_norm", first_norm_kernel,
         (info, text_input, xl_own, ct, cl, text_dense, layout_dense, text_biases, layout_biases,
-         text_gains, text_shifts, layout_gains, layout_shifts, text_widen, hidden, text_narrow),
+         text_gains, text_shifts, layout_gains, layout_shifts, text_widen, mine, text_narrow),
         (shape((own, width), F32), shape((own, width_l), F32), shape((own, width)), shape((own, width_l)),
          shape((own, width_l), F32), shape((own, hid)), shape((own, hid), F32), shape((own, width), F32)),
-    )
-    shards = {
-        k: spread(tie(come[k], projected), planes, {1: "x", 3: "y"}[k], second=(attended,), third=(first_done,)) for k in (1, 3)
-    }
-    smalls = [small] + [lax.ppermute(tie(small, first_done), "tensor", shift_from(k)) for k in (1, 2, 3)]
-    actives, slopes, shard_done = {0: active0}, {0: slope0}, {}
+        after=(by_y[1], by_x[3]),
+    )
+    both = gate((forwarded[1][0][0], forwarded[3][0][0]), first_done)
+    shards = {}
+    for k, array in zip((1, 3), both):
+        parts = come[k].shape[0]
+        held = [(come[k], 0, 0, parts), (by_x[k], 1, 0, parts), (by_y[k], 2, 0, parts), (array, 3, 0, parts)]
+        shards[k] = to_core(held, planes)
+    by_x[2], by_y[2] = across(come[2], X), across(come[2], Y)
+    actives, slopes, shard_weights, layouts, shard_done = {0: active0}, {0: slope0}, {}, {}, {}
     for k in (1, 3):
         arrays, plan = shards[k]
-        actives[k], slopes[k], total_t, shard_done[k] = call(
+        actives[k], slopes[k], total_t, shard_weights[k], layouts[k], shard_done[k] = call(
             "shard", functools.partial(shard_kernel, plan),
-            (info, low_t, total_t, hiddens[k], *arrays),
-            (shape((own, hid)), shape((own, hid), F32), shape((own, width), F32)),
-            scratch=(pltpu.VMEM((1, 2, width, hid), BF), pltpu.SemaphoreType.DMA((1, len(plan)))),
-            in_hbm=len(plan),
+            (info, low_t, total_t, *arrays),
+            (shape((own, hid)), shape((own, hid), F32), shape((own, width), F32), shape((2, width, hid)),
+             shape((width_l, 2 * wide))),
+            scratch=(pltpu.VMEM((width_l, 2 * wide), F32),),
+            after=(by_x[2], by_y[2]) if k == 3 else (),
         )
-    shards[2] = spread(tie(come[2], first_done), planes, "half", second=(shard_done[1],), third=(shard_done[3],))
-    plans = tuple(shards[k][1] for k in (1, 2, 3))
-    arrays = sum((shards[k][0] for k in (1, 2, 3)), [])
+    last = forward(come[2], by_x[2], by_y[2], planes, "half", 96)
+    last = [(v,) + f[1:] for v, f in zip(gate([f[0] for f in last], shard_done[3]), last)]
+    parts = come[2].shape[0]
+    shards[2] = to_core([(come[2], 0, 0, parts), (by_x[2], 1, 0, parts), (by_y[2], 2, 0, parts)] + last, planes)
+    arrays, plan = shards[2]
     rows_a = piece + EXTRA
     outs = call(
-        "turn", functools.partial(turn_kernel, plans),
+        "turn", functools.partial(turn_kernel, plan),
         (info, low_t, total_t, text_gains, text_shifts, text_cotangent, text_widen, text_narrow,
          slopes[0], slopes[1], slopes[3], actives[0], actives[1], actives[3],
-         low_l, normed_l, layout_gains, layout_shifts, layout_cotangent.T, *smalls, *hiddens, *arrays),
+         low_l, normed_l, layout_gains, layout_shifts, layout_cotangent.T, layout_widen, layout_narrow, layouts[1], layouts[3],
+         mine, come[1], come[3],         shard_weights[1], shard_weights[3], *arrays),
         (shape((own, width)), shape((own, width)), shape((groups, own, hid)), shape((own, width), F32),
          shape((4, width), F32), shape((groups, 1, hid), F32), shape((own, hid)),
          shape((width_l, own)), shape((own, width_l), F32), shape((4, width_l), F32), shape((groups, 1, hid_l), F32),
-         shape((groups, 2, 2, rows_a, width)), shape((groups, 2, 2, piece, width)), shape((groups, 128, width))),
-        scratch=(pltpu.VMEM((3, 2, width, hid), BF), pltpu.VMEM((own, hid), F32),
+         shape((groups, 4 * rows_a, width)), shape((groups, 4 * piece, width)), shape((groups, 128, width))),
+        scratch=(pltpu.VMEM((2, width, hid), BF), pltpu.VMEM((own, hid), F32),
                  pltpu.VMEM((groups, own, hid_l), F32), pltpu.VMEM((groups, own, hid_l), BF),
                  pltpu.VMEM((groups, own, hid_l), BF), pltpu.VMEM((own, width_l), BF), pltpu.VMEM((own, width_l), BF),
-                 pltpu.VMEM((4 * piece, width), F32), pltpu.SemaphoreType.DMA((3, max(map(len, plans))))),
-        in_hbm=len(arrays),
+                 pltpu.VMEM((width_l, 2 * wide), F32)),
     )
     result_t, dout_t, dhid_t, dnormed_t, sums_t, hsums_t, actives[2] = outs[:7]
     result_lt, dnormed_l, sums_l, hsums_l, send_a, send_b, pack, turned = outs[7:]
 
     in_order = [actives[k] for k in range(4)]
-    across = lambda v, bit: lax.ppermute(v, "dp", flip(planes, bit))
-    recv_a, recv_b = across(send_a, 1), across(send_b, 1)
+    recv_a, recv_b = across(send_a, CORE), across(send_b, CORE)
     dfirst_t, db_t, dc_t, low_sums_t, dfirst_lt, db_l, dc_l, low_sums_l, lowered = call(
         "lower", lower_kernel,
         (info, first_t, dnormed_t, text_gains, text_dense, first_l, dnormed_l, layout_gains, layout_dense),
@@ -866,13 +892,14 @@
          shape((width_l, own), F32), shape((own, width_l)), shape((own, wide)), shape((4, width_l), F32)),
         scratch=(pltpu.VMEM((own, width_l), F32),),
     )
-    next_a, keep_a, next_b, keep_b, kept = call(
+    next_a1, next_a2, next_b1, next_b2, keep_a, keep_b, kept = call(
         "ffn_keep", ffn_keep_kernel,
         (info, *in_order, dout_t, low_t, dhid_t, recv_a, recv_b, pack),
-        (shape((2, groups, rows_a, width)),) * 2 + (shape((2, groups, piece, width)),) * 2,
-        scratch=(pltpu.VMEM((4 * piece, width), F32),), after=(lowered,),
-    )
-    recv_a, recv_b = across(next_a, 2), across(next_b, 4)
+        (shape((2, 2, rows_a, width)),) * 2 + (shape((2, 2, piece, width)),) * 2
+        + (shape((2, groups, rows_a, width)), shape((2, groups, piece, width))),
+        scratch=(pltpu.VMEM((4 * rows_a, width), BF), pltpu.VMEM((4 * piece, width), BF)), after=(lowered,),
+    )
+    recv_a1, recv_b1 = across(next_a1, X), across(next_b1, Y)
 
     dq, dk, dv, dq_l, dk_l, dv_l, attended_back = call(
         "attend_back", attend_back_kernel,
@@ -883,39 +910,37 @@
                  pltpu.VMEM((window, wide), F32), pltpu.VMEM((window, wide), F32), pltpu.VMEM((own, wide), F32)),
         after=(kept,),
     )
-    packed = shape((own + own // 4, width))
-    left, right, sided = call("sides", sides_kernel, (info, text_project, wl, dk, dv, dk_l, dv_l), (packed, packed))
-    from_right = lax.ppermute(left, "tensor", [(i + 1, i) for i in range(groups - 1)])
-    from_left = lax.ppermute(right, "tensor", [(i, i + 1) for i in range(groups - 1)])
-
-    next_a, keep_a = add_split(keep_a, recv_a)
-    next_b, keep_b = add_split(keep_b, recv_b)
     copied_in = (text_input, dq, dk, dv, ct, db_t)
     send, extra, sent = call(
         "copied_send", copied_send_kernel,
         (info,) + copied_in + (xlt, dq_l, dk_l, dv_l, cl, db_l, sums_t, low_sums_t, hsums_t, sums_l, low_sums_l, hsums_l),
-        (shape((groups, 2, 2, rows_a, width)), shape((4 * 128, width))),
-        scratch=(pltpu.VMEM((4 * piece, width), F32), pltpu.VMEM((32, width), F32)), after=(sided, next_a, next_b),
-    )
-    recv = across(send, 1)
-    recv_a, recv_b = across(next_a, 4), across(next_b, 2)
+        (shape((groups, 4 * rows_a, width)), shape((4 * 128, width))),
+        scratch=(pltpu.VMEM((32, width), F32),), after=(recv_a1, recv_b1),
+    )
+    packed = shape((own + own // 4, width))
+    left, right, sided = call(
+        "sides", sides_kernel, (info, text_project, wl, dk, dv, dk_l, dv_l), (packed, packed), after=(sent,)
+    )
+    recv_a2, recv_b2 = across(next_a2, X), across(next_b2, Y)
+    from_right = lax.ppermute(left, "tensor", [(i + 1, i) for i in range(groups - 1)])
+    from_left = lax.ppermute(right, "tensor", [(i, i + 1) for i in range(groups - 1)])
+
+    recv = across(send, CORE)
     copied_next_a, copied_keep_a, copied_next_b, copied_keep_b, copied_kept = call(
         "copied_keep", copied_keep_kernel, (info,) + copied_in + (extra, recv),
         (shape((2, 2, rows_a, width)),) * 4,
-        scratch=(pltpu.VMEM((4 * piece, width), F32),),
-    )
+        scratch=(pltpu.VMEM((groups, 4 * rows_a, width), BF),),
+    )
+    copied_recv_a, copied_recv_b = across(copied_next_a, X), across(copied_next_b, Y)
     own_sum, owned = call(
         "own", own_kernel,
         (info, text_project, wl, dq, dk, dv, dq_l, dk_l, dv_l, dfirst_t, dfirst_lt, from_right, from_left),
-        (packed,), after=(copied_kept,),
-    )
-    all_rows = lax.all_gather(own_sum, "tensor", axis=0, tiled=False)
-    copied_recv_a, copied_recv_b = across(copied_next_a, 2), across(copied_next_b, 4)
-    *ffn_parts, ffn_spreaded = call(
-        "ffn_spread", ffn_spread_kernel, (info, keep_a, recv_a, keep_b, recv_b),
-        (shape((rows_a + piece, width)),) * 4, after=(owned,),
-    )
-    ffn_parts = [ffn_parts[0]] + [lax.ppermute(ffn_parts[k], "tensor", shift_to(k)) for k in (1, 2, 3)]
+        (packed,), after=(copied_kept, recv_a2, recv_b2),
+    )
+    step_right = lambda v, far: lax.ppermute(v, "tensor", [(i, i + 1) for i in range(far, groups - 1)])
+    step_left = lambda v, far: lax.ppermute(v, "tensor", [(i, i - 1) for i in range(groups - 1 - far, 0, -1)])
+    lefts, rights = [step_right(own_sum, 0)], [step_left(own_sum, 0)]
+    to_group = lambda v, k: lax.ppermute(v, "tensor", shift_to(k))
 
     def across_planes(value):
         bit = PIECES
@@ -924,32 +949,48 @@
             bit *= 2
         return value
 
-    next_a, keep_a = add_split(copied_keep_a, tie(copied_recv_a, ffn_spreaded))
-    next_b, keep_b = add_split(copied_keep_b, tie(copied_recv_b, ffn_spreaded))
-    recv_a, recv_b = across(next_a, 4), across(next_b, 2)
-    ffn_arrays, ffn_plan = spread(across_planes(add(*ffn_parts)), planes, "half", rows_a)
-    *parts, _ = call(
-        "copied_spread", copied_spread_kernel, (info, keep_a, recv_a, keep_b, recv_b), (shape((rows_a, width)),) * 4,
-    )
-    parts = [parts[0]] + [lax.ppermute(parts[k], "tensor", shift_to(k)) for k in (1, 2, 3)]
+    copied_next_a, copied_keep_a = add_split(copied_keep_a, copied_recv_a)
+    copied_next_b, copied_keep_b = add_split(copied_keep_b, copied_recv_b)
+    copied_recv_a, copied_recv_b = across(copied_next_a, Y), across(copied_next_b, X)
+    *parts, copied_spreaded = call(
+        "copied_spread", copied_spread_kernel, (info, copied_keep_a, copied_recv_a, copied_keep_b, copied_recv_b),
+        (shape((rows_a, width)),) * 4,
+        after=(lefts[0], rights[0]),
+    )
+    parts = [parts[0]] + [to_group(parts[k], k) for k in (1, 2, 3)]
     summed = across_planes(add(*parts))
-    g_narrow, g_widen, g_narrow_l, g_widen_l, _ = call(
+    next_a, keep_a = add_split(keep_a, jnp.concatenate([recv_a1, recv_a2], axis=1), copied_spreaded)
+    next_b, keep_b = add_split(keep_b, jnp.concatenate([recv_b1, recv_b2], axis=1), copied_spreaded)
+    recv_a, recv_b = across(next_a, Y), across(next_b, X)
+    ffn_parts, ffn_spreaded = call(
+        "ffn_spread", ffn_spread_kernel, (info, keep_a, recv_a, keep_b, recv_b),
+        (shape((groups, rows_a + piece, width)),), after=(summed,),
+    )
+    ffn_summed = lax.psum_scatter(ffn_parts, "tensor", scatter_dimension=0, tiled=False)
+    ffn_arrays, ffn_plan = spread(across_planes(ffn_summed), planes, rows_a)
+    every = [summed] + [from_group(summed, k) for k in (1, 2, 3)]
+    left, right = gate((lefts[0], rights[0]), every[1], every[2], every[3])
+    lefts, rights = [left], [right]
+    for far in (1, 2):
+        lefts.append(step_right(lefts[-1], far))
+        rights.append(step_left(rights[-1], far))
+    g_narrow, g_widen, g_narrow_l, g_widen_l, ffn_done = call(
         "ffn_final", functools.partial(ffn_final_kernel, ffn_plan), (info, *ffn_arrays),
         (shape((hid, width), F32), shape((width, hid), F32), shape((hid_l, width_l), F32), shape((width_l, hid_l), F32)),
         scratch=(pltpu.VMEM((128, width), F32),),
     )
-    every = jnp.stack([summed] + [lax.ppermute(summed, "tensor", shift_from(k)) for k in (1, 2, 3)])
-    text_grad, layout_grad_t, given = call(
-        "input_final", input_final_kernel, (info, all_rows),
-        (shape((total, width), F32), shape((width_l, total), F32)),
-    )
-    arrays, plan = spread(tie(every, given), planes, "half")
+    arrays, plan = spread(jnp.stack(every), planes)
     vectors = lambda w, h: (shape((4, w), F32), shape((2, w), F32), shape((2, w), F32), shape((1, h), F32))
     outs = call(
         "copied_final", functools.partial(copied_final_kernel, plan), (info, *arrays),
         (shape((width, 3 * width), F32), shape((width, width), F32),
          shape((width_l, 3 * width_l), F32), shape((width_l, width_l), F32)) + vectors(width, hid) + vectors(width_l, hid_l),
         scratch=(pltpu.VMEM((4 * 128, width), F32),),
+    )
+    text_grad, layout_grad_t, given = call(
+        "input_final", input_final_kernel, (info, own_sum, *lefts, *rights),
+        (shape((total, width), F32), shape((width_l, total), F32)),
+        after=(ffn_done, outs[-1]),
     )
     g_project, g_dense, g_project_l, g_dense_l = outs[:4]
     bias_t, gain_t, shift_t, hb_t, bias_l, gain_l, shift_l, hb_l = outs[4:12]

time: 415 us -> 338 us (0.81)
  Pallas kernels: 154 us -> 95 us
  waiting for transfers between devices: 150 us -> 110 us
  local copies, waits for them, and re-layouts: 9.25 us -> 39.1 us
    pallas_call x19, Pallas kernels: 154 us -> 95 us  [call(): pl.pallas_call(with_token, out_shape=outs, in_specs=specs, out_specs=[VM]...]
    ppermute x70 -> x69, waiting for transfers between devices: 148 us -> 100 us  [the longest x6 44.5 us: per_device(): from_group = lambda v, k: lax.ppermute(v, 'tensor', shift_from(k))]
    unnamed x146 -> x151, local copies, waits for them, and re-layouts: 8.48 us -> 33.3 us
    ppermute x1, waiting for transfers between devices: 0.5 us -> 5.39 us  [per_device(): lax.ppermute(left, 'tensor', [(i + 1, i) for i in range(groups - 1)])]
    ppermute x70 -> x69, starting transfers between devices: 64.6 us -> 60.1 us  [the longest x54 39.9 us: around(): return lambda v, bit: lax.ppermute(v, 'dp', flip(planes, bit))]
  transfers between devices with their start and end apart: 73 -> 72, of which waited for: 26 -> 19; matrix products, arithmetic and copies ran while one was open for 1% -> 3% of each run, Pallas kernels for 26% -> 18%
where the time goes in v3:
time: 338 us; the launch traced here: 333 us
  waiting for transfers between devices  110 us (33%)
  Pallas kernels  95 us (28%)
  starting transfers between devices  66.9 us (20%)
  local copies, waits for them, and re-layouts  39.1 us (12%)
  between operations  15.2 us (4%)
  other arithmetic  7.79 us (2%)
    pallas_call x19, Pallas kernels, call(): pl.pallas_call(with_token, out_shape=outs, in_specs=specs, out_specs=[VM]...  95 us
    ppermute x6, waiting for transfers between devices, per_device(): from_group = lambda v, k: lax.ppermute(v, 'tensor', shift_from(k))  44.5 us
    ppermute x54, starting transfers between devices, around(): return lambda v, bit: lax.ppermute(v, 'dp', flip(planes, bit))  39.9 us
    unnamed x151, local copies, waits for them, and re-layouts  33.3 us
    ppermute x54, waiting for transfers between devices, around(): return lambda v, bit: lax.ppermute(v, 'dp', flip(planes, bit))  29.5 us
    ppermute x3, waiting for transfers between devices, per_device(): to_group = lambda v, k: lax.ppermute(v, 'tensor', shift_to(k))  13.8 us
    ppermute x3, waiting for transfers between devices, per_device(): lax.ppermute(v, 'tensor', [(i, i - 1) for i in range(groups - 1 - far, 0,...  10.5 us
  transfers between devices with their start and end apart: 72, of which 19 were waited for; matrix products, arithmetic and copies ran while one was open for 3% of the time, Pallas kernels for 18%

profile of v3, /device:TPU:9, one launch (start us, length us, event | category | flops | bytes accessed | tf_op | source)
XLA Modules:
  0.0 333.4 jit_solution(1182431295805002909)
XLA Ops:
  11.2 1.3 collective-permute-start.1
  13.2 1.7 copy.53.refs_0_
  16.3 1.4 select_reduce_fusion
  19.0 1.7 copy-done.8
  24.0 4.7 %project.1 = (bf16[384,768]{1,0:T(8,128)(2,1)S(1)}, bf16[1024,768]{1,0:T(8,128)(2,1)S(1)}, bf16[1024,768]{1,0:T(8,128)(2,1)S(1)}, bf16[384,256]{1,0:T(8,128)(2,1...) custom-call(f32[8,128]{1,0:T(8,128)S(1)} %copy-done.71, ...), custom_call_target="tpu_custom_call" | custom-call | flops 5000000000 | tf_op jit(solution)/shard_map/project/pallas_call | solution.py:688
  32.3 8.4 %attend.1 = (bf16[384,768]{1,0:T(8,128)(2,1)S(1)}, bf16[384,192]{1,0:T(8,128)(2,1)S(1)}, f32[384,128]{1,0:T(8,128)S(1)}, f32[8,128]{1,0:T(8,128)S(1)}) custom-call(s32[26]{0:T(128)S(1)} %concatenate.18.refs_1_.refs_0_.refs_2_.refs_3_, bf16[384,768]{1,0:T(8,128)(2,1)S(1)} %get-tuple-element.145.refs_1_.refs_2_, ...), custom_call_target="tpu_custom_call" | custom-call | flops 8999999488 | tf_op jit(solution)/shard_map/attend/pallas_call | solution.py:688
  41.3 1.5 collective-permute-start.4
  45.3 12.6 %collective-permute-done.4.refs_28_ = bf16[224,768]{1,0:T(8,128)(2,1)S(1)} collective-permute-done((bf16[224,768]{1,0:T(8,128)(2,1)S(1)}, bf16[224,768]{1,0:T(8,128)(2,1)S(1)}, u32[]{:S(2)}, u32[]{:S(2)}) %collective-permute-start.4) | collective-permute-done | bytes 344096 | tf_op jit(solution)/shard_map/ppermute | solution.py:811
  58.4 1.3 collective-permute-start.6
  62.0 3.5 %first_norm.1 = (f32[384,768]{1,0:T(8,128)S(1)}, f32[384,192]{1,0:T(8,128)S(1)}, bf16[384,768]{1,0:T(8,128)(2,1)S(1)}, bf16[384,192]{1,0:T(8,128)(2,1)S(1)}, f32...) custom-call(bf16[224,768]{1,0:T(8,128)(2,1)S(1)} %collective-permute, ...), custom_call_target="tpu_custom_call" | custom-call | flops 4000000000 | tf_op jit(solution)/shard_map/first_norm/pallas_call | solution.py:688
  67.6 1.3 collective-permute-start.15
  70.9 3.2 shard.2
  74.1 1.4 copy-done.51
  79.0 2.8 shard.3
  81.8 1.4 copy-done.41
  86.7 1.3 collective-permute-done.24.refs_36_
  88.0 19.7 %turn.1 = (bf16[384,768]{1,0:T(8,128)(2,1)}, bf16[384,768]{1,0:T(8,128)(2,1)S(1)}, bf16[4,384,768]{2,1,0:T(8,128)(2,1)}, f32[384,768]{1,0:T(8,128)}, f32[4,768]{...) custom-call(s32[26]{0:T(128)S(1)} %concatenate.18.refs_1_.refs_0_.re, ...), custom_call_target="tpu_custom_call" | custom-call | flops 20999999488 | tf_op jit(solution)/shard_map/turn/pallas_call | solution.py:688
  109.0 1.3 copy-done.39
  111.3 2.2 lower.1
  113.5 3.6 %collective-permute-done.27.refs_10_ = bf16[4,384,768]{2,1,0:T(8,128)(2,1)S(1)} collective-permute-done((bf16[4,384,768]{2,1,0:T(8,128)(2,1)}, bf16[4,384,768]{2,1,0:T(8,128)(2,1)S(1)}, u32[]{:S(2)}, u32[]{:S(2)}) %collective-permute-start.27) | collective-permute-done | bytes 2359328 | tf_op jit(solution)/shard_map/ppermute | solution.py:723
  117.2 3.6 %ffn_keep.1 = (bf16[2,2,112,768]{3,2,1,0:T(8,128)(2,1)S(1)}, bf16[2,2,112,768]{3,2,1,0:T(8,128)(2,1)S(1)}, bf16[2,2,96,768]{3,2,1,0:T(8,128)(2,1)S(1)}, bf16[2,2...) custom-call(f32[8,128]{1,0:T(8,128)S(1)} %get-tuple-element.185.refs, ...), custom_call_target="tpu_custom_call" | custom-call | flops 4000000000 | tf_op jit(solution)/shard_map/ffn_keep/pallas_call | solution.py:688
  120.8 1.3 collective-permute-start.29
  122.4 1.4 copy-done.59
  123.8 1.4 copy-done.61
  125.2 15.6 %attend_back.1 = (bf16[384,768]{1,0:T(8,128)(2,1)S(1)}, bf16[1792,768]{1,0:T(8,128)(2,1)S(1)}, bf16[1792,768]{1,0:T(8,128)(2,1)S(1)}, bf16[384,256]{1,0:T(8,128)...) custom-call(f32[8,128]{1,0:T(8,128)S(1)} %get-tuple-element.192.refs_0_, ...), custom_call_target="tpu_custom_call" | custom-call | flops 15000000512 | tf_op jit(solution)/shard_map/attend_back/pallas_call | solution.py:688
  140.9 3.3 %copied_send.1 = (bf16[4,448,768]{2,1,0:T(8,128)(2,1)S(1)}, bf16[512,768]{1,0:T(8,128)(2,1)S(1)}, f32[8,128]{1,0:T(8,128)S(1)}) custom-call(bf16[2,2,112,768]{3,2,1,0:T(8,128)(2,1)S(1)} %collective-permute-done.28.refs_0_, bf16[2,2,96,768]{3,2,1,0:T(8,128)(2,1)S(1)} %collective-permute-done.29.refs_1_, s32[26]{0:T(128)S(1)} %concatenate.18.refs_1_.refs_0_.refs_2_.refs_3_, ...), custom_call_target="tpu_custom_call" | custom-call | flops 4000000000 | tf_op jit(solution)/shard_map/copied_send/pallas_call | solution.py:688
  146.6 3.3 sides.1
  149.9 4.8 %collective-permute-start.33 = (bf16[480,768]{1,0:T(8,128)(2,1)S(1)}, bf16[480,768]{1,0:T(8,128)(2,1)S(1)}, u32[]{:S(2)}, u32[]{:S(2)}) collective-permute-start(bf16[480,768]{1,0:T(8,128)(2,1)S(1)} %get-tuple-element.221), channel_id=1, source_target_pairs={{1,0},{2,1},{3,2},{5,4},{6,5},{7,6},{9,8},{10,9},{11,10},{13,12},{... | collective-permute-start | bytes 2211848 | tf_op jit(solution)/shard_map/ppermute | solution.py:925
  154.7 1.9 collective-permute-start.34
  156.7 1.5 copy-done.6
  158.2 1.8 copy-done.7
  160.0 2.9 copied_keep.1
  164.5 5.4 %collective-permute-done.33.refs_14_ = bf16[480,768]{1,0:T(8,128)(2,1)S(1)} collective-permute-done((bf16[480,768]{1,0:T(8,128)(2,1)S(1)}, bf16[480,768]{1,0:T(8,128)(2,1)S(1)}, u32[]{:S(2)}, u32[]{:S(2)}) %collective-permute-start.33) | collective-permute-done | bytes 737312 | tf_op jit(solution)/shard_map/ppermute | solution.py:925
  169.9 3.8 %collective-permute-done.34.refs_15_ = bf16[480,768]{1,0:T(8,128)(2,1)S(1)} collective-permute-done((bf16[480,768]{1,0:T(8,128)(2,1)S(1)}, bf16[480,768]{1,0:T(8,128)(2,1)S(1)}, u32[]{:S(2)}, u32[]{:S(2)}) %collective-permute-start.34) | collective-permute-done | bytes 737312 | tf_op jit(solution)/shard_map/ppermute | solution.py:926
  173.7 3.0 own.1
  176.7 1.9 collective-permute-start.36
  178.6 3.5 %collective-permute-start.35 = (bf16[480,768]{1,0:T(8,128)(2,1)S(1)}, bf16[480,768]{1,0:T(8,128)(2,1)S(1)}, u32[]{:S(2)}, u32[]{:S(2)}) collective-permute-start(bf16[480,768]{1,0:T(8,128)(2,1)S(1)} %get-tuple-element.223.refs_3_), channel_id=1, source_target_pairs={{0,1},{1,2},{2,3},{4,5},{5,6},{6,7},{8,9},{9,10},{10,11},{12,13},{... | collective-permute-start | bytes 2211848 | tf_op jit(solution)/shard_map/ppermute | solution.py:940
  182.4 1.3 collective-permute-start.38
  184.3 10.5 %collective-permute-done.36.refs_1_ = bf16[480,768]{1,0:T(8,128)(2,1)S(1)} collective-permute-done((bf16[480,768]{1,0:T(8,128)(2,1)S(1)}, bf16[480,768]{1,0:T(8,128)(2,1)S(1)}, u32[]{:S(2)}, u32[]{:S(2)}) %collective-permute-start.36) | collective-permute-done | bytes 737312 | tf_op jit(solution)/shard_map/ppermute | solution.py:941
  194.8 1.9 collective-permute-done.35.refs_0_
  199.0 1.3 collective-permute-start.44
  203.2 1.5 collective-permute-start.43
  204.7 1.5 collective-permute-done.41
  206.2 9.8 %collective-permute-done.42 = bf16[112,768]{1,0:T(8,128)(2,1)S(1)} collective-permute-done((bf16[112,768]{1,0:T(8,128)(2,1)S(1)}, bf16[112,768]{1,0:T(8,128)(2,1)S(1)}, u32[]{:S(2)}, u32[]{:S(2)}) %collective-permute-start.42) | collective-permute-done | bytes 172064 | tf_op jit(solution)/shard_map/ppermute | solution.py:943
  216.0 2.5 collective-permute-done.43
  218.6 1.9 ffn_spread.1
  220.9 1.4 collective-permute-start.55
  222.3 3.0 collective-permute-done.57.refs_4_
  225.3 7.1 %collective-permute-done.56.refs_3_ = bf16[112,768]{1,0:T(8,128)(2,1)S(1)} collective-permute-done((bf16[112,768]{1,0:T(8,128)(2,1)S(1)}, bf16[112,768]{1,0:T(8,128)(2,1)S(1)}, u32[]{:S(2)}, u32[]{:S(2)}) %collective-permute-start.56) | collective-permute-done | bytes 172064 | tf_op jit(solution)/shard_map/ppermute | solution.py:811
  232.4 21.0 %collective-permute-done.55.refs_2_ = bf16[112,768]{1,0:T(8,128)(2,1)S(1)} collective-permute-done((bf16[112,768]{1,0:T(8,128)(2,1)S(1)}, bf16[112,768]{1,0:T(8,128)(2,1)S(1)}, u32[]{:S(2)}, u32[]{:S(2)}) %collective-permute-start.55) | collective-permute-done | bytes 172064 | tf_op jit(solution)/shard_map/ppermute | solution.py:811
  255.9 1.3 collective-permute-start.67
  257.2 1.9 collective-permute-start.69
  259.1 10.8 %collective-permute-done.59.refs_3_ = bf16[4,112,768]{2,1,0:T(8,128)(2,1)S(1)} collective-permute-done((bf16[4,112,768]{2,1,0:T(8,128)(2,1)S(1)}, bf16[4,112,768]{2,1,0:T(8,128)(2,1)S(1)}, u32[]{:S(2)}, u32[]{:S(2)}) %collective-permute-start.59) | collective-permute-done | bytes 688160 | tf_op jit(solution)/shard_map/ppermute | solution.py:723
  273.1 1.8 collective-permute-start.64
  274.9 3.3 collective-permute-done.61.refs_5_
  278.1 2.4 collective-permute-start.66
  284.0 6.5 %collective-permute-done.47.refs_3_ = bf16[208,768]{1,0:T(8,128)(2,1)} collective-permute-done((bf16[208,768]{1,0:T(8,128)(2,1)}, bf16[208,768]{1,0:T(8,128)(2,1)}, u32[]{:S(2)}, u32[]{:S(2)}) %collective-permute-start.47) | collective-permute-done | bytes 319520 | tf_op jit(solution)/shard_map/ppermute | solution.py:723
  290.5 1.3 collective-permute-start.50
  295.3 3.0 collective-permute-done.49.refs_5_
  299.7 1.5 collective-permute-start.68
  301.3 2.2 collective-permute-start.70
  306.4 7.0 %copied_final.1 = (f32[768,2304]{1,0:T(8,128)}, f32[768,768]{1,0:T(8,128)}, f32[192,576]{1,0:T(8,128)}, f32[192,192]{1,0:T(8,128)}, f32[4,768]{1,0:T(4,128)}, /*...) custom-call(s32[26]{0:T(128)S(1)} %concatenate.18.refs_1_.refs_0_.re, ...), custom_call_target="tpu_custom_call" | custom-call | flops 6000000000 | tf_op jit(solution)/shard_map/copied_final/pallas_call | solution.py:688
  317.9 3.8 %ffn_final.1 = (f32[768,768]{1,0:T(8,128)}, f32[768,768]{1,0:T(8,128)}, f32[192,192]{1,0:T(8,128)}, f32[192,192]{1,0:T(8,128)}, f32[8,128]{1,0:T(8,128)S(1)}) custom-call(s32[26]{0:T(128)S(1)} %concatenate.18.refs_1_.refs_0_.refs_2_.refs_3_, bf16[208,768]{1,0:T(8,128)(2,1)S(1)} %bitcast.52, bf16[208,768]{1,0:T(8,128)(2,1)} %collective-permute-done.46.refs_2_, ...), custom_call_target="tpu_custom_call" | custom-call | flops 3000000000 | tf_op jit(solution)/shard_map/ffn_final/pallas_call | solution.py:688
  321.8 4.6 %input_final.1 = (f32[1536,768]{1,0:T(8,128)}, f32[192,1536]{1,0:T(8,128)}, f32[8,128]{1,0:T(8,128)}) custom-call(f32[8,128]{1,0:T(8,128)S(1)} %get-tuple-element.236.refs_0_, f32[8,128]{1,0:T(8,128)S(1)} %get-tuple-element.237.refs_1_, s32[26]{0:T(128)S(1)} %concatenate.18.refs_1_.refs_0_.refs_2_.refs_3_, bf16[480,768]{1,0:T(8,128)(2,1)S(1)} %copy-done.14, ...), custom_call_target="tpu_custom_call" | custom-call | flops 3000000000 | tf_op jit(solution)/shard_map/input_final/pallas_call | solution.py:688
  (284 shorter events, 65.6 us)
Async XLA Ops:
  7.2 274.3 %reduce-scatter.2.cloned.1.call-start = ((), (), s32[]{:S(2)}) async-start(), calls=%async_computation.1 | async-start | bytes 1597440 | tf_op jit(solution)/shard_map/reduce_scatter | solution.py:969
  11.2 17.6 %collective-permute-start.1 = (bf16[224,768]{1,0:T(8,128)(2,1)}, bf16[224,768]{1,0:T(8,128)(2,1)}, u32[]{:S(2)}, u32[]{:S(2)}) collective-permute-start(bf16[224,768]{1,0:T(8,128)(2,1)} %get-tuple-element.139.refs_16_.refs_23_), channel_id=1, source_target_pairs={{0,1},{1,2},{2,3},{3,0},{4,5},{5,6},{6,7},{7,4},{8,9},{9,10},{10,1... | collective-permute-start | bytes 1032200 | tf_op jit(solution)/shard_map/ppermute | solution.py:811
  12.5 17.2 %collective-permute-start = (bf16[224,768]{1,0:T(8,128)(2,1)}, bf16[224,768]{1,0:T(8,128)(2,1)}, u32[]{:S(2)}, u32[]{:S(2)}) collective-permute-start(bf16[224,768]{1,0:T(8,128)(2,1)} %get-tuple-element.139.refs_16_.refs_23_), channel_id=1, source_target_pairs={{0,3},{1,0},{2,1},{3,2},{4,7},{5,4},{6,5},{7,6},{8,11},{9,8},{10,9... | collective-permute-start | bytes 1032200 | tf_op jit(solution)/shard_map/ppermute | solution.py:811
  29.8 13.1 %collective-permute-start.7 = (bf16[224,768]{1,0:T(8,128)(2,1)}, bf16[224,768]{1,0:T(8,128)(2,1)S(1)}, u32[]{:S(2)}, u32[]{:S(2)}) collective-permute-start(bf16[224,768]{1,0:T(8,128)(2,1)} %get-tuple-element.142.refs_3_.refs_24_), channel_id=1, source_target_pairs={{0,8},{4,12},{8,0},{12,4},{16,24},{20,28},{24,16},{28,20},{1,9},{5... | collective-permute-start | bytes 1032200 | tf_op jit(solution)/shard_map/ppermute | solution.py:723
  31.0 11.9 %collective-permute-start.8 = (bf16[224,768]{1,0:T(8,128)(2,1)}, bf16[224,768]{1,0:T(8,128)(2,1)S(1)}, u32[]{:S(2)}, u32[]{:S(2)}) collective-permute-start(bf16[224,768]{1,0:T(8,128)(2,1)} %get-tuple-element.143.refs_5_.refs_25_), channel_id=1, source_target_pairs={{0,16},{4,20},{8,24},{12,28},{16,0},{20,4},{24,8},{28,12},{1,17},{... | collective-permute-start | bytes 1032200 | tf_op jit(solution)/shard_map/ppermute | solution.py:723
  40.8 17.6 %collective-permute-start.2 = (bf16[224,768]{1,0:T(8,128)(2,1)}, bf16[224,768]{1,0:T(8,128)(2,1)S(1)}, u32[]{:S(2)}, u32[]{:S(2)}) collective-permute-start(bf16[224,768]{1,0:T(8,128)(2,1)} %get-tuple-element.142.refs_3_.refs_24_), channel_id=1, source_target_pairs={{0,16},{4,20},{8,24},{12,28},{16,0},{20,4},{24,8},{28,12},{1,17},{... | collective-permute-start | bytes 1032200 | tf_op jit(solution)/shard_map/ppermute | solution.py:723
  41.1 17.3 %collective-permute-start.3 = (bf16[224,768]{1,0:T(8,128)(2,1)}, bf16[224,768]{1,0:T(8,128)(2,1)S(1)}, u32[]{:S(2)}, u32[]{:S(2)}) collective-permute-start(bf16[224,768]{1,0:T(8,128)(2,1)} %get-tuple-element.143.refs_5_.refs_25_), channel_id=1, source_target_pairs={{0,8},{4,12},{8,0},{12,4},{16,24},{20,28},{24,16},{28,20},{1,9},{5... | collective-permute-start | bytes 1032200 | tf_op jit(solution)/shard_map/ppermute | solution.py:723
  41.3 16.5 %collective-permute-start.4 = (bf16[224,768]{1,0:T(8,128)(2,1)S(1)}, bf16[224,768]{1,0:T(8,128)(2,1)S(1)}, u32[]{:S(2)}, u32[]{:S(2)}) collective-permute-start(bf16[224,768]{1,0:T(8,128)(2,1)S(1)} %get-tuple-element.154), channel_id=1, source_target_pairs={{0,2},{1,3},{2,0},{3,1},{4,6},{5,7},{6,4},{7,5},{8,10},{9,11},{10,... | collective-permute-start | bytes 1032200 | tf_op jit(solution)/shard_map/ppermute | solution.py:811
  42.9 16.8 %collective-permute-start.9 = (bf16[224,768]{1,0:T(8,128)(2,1)S(1)}, bf16[224,768]{1,0:T(8,128)(2,1)S(1)}, u32[]{:S(2)}, u32[]{:S(2)}) collective-permute-start(bf16[224,768]{1,0:T(8,128)(2,1)S(1)} %get-tuple-element.157.refs_4_), channel_id=1, source_target_pairs={{0,16},{4,20},{8,24},{12,28},{16,0},{20,4},{24,8},{28,12},{1,17},{... | collective-permute-start | bytes 1032200 | tf_op jit(solution)/shard_map/ppermute | solution.py:723
  44.1 16.8 %collective-permute-start.10 = (bf16[224,768]{1,0:T(8,128)(2,1)S(1)}, bf16[224,768]{1,0:T(8,128)(2,1)S(1)}, u32[]{:S(2)}, u32[]{:S(2)}) collective-permute-start(bf16[224,768]{1,0:T(8,128)(2,1)S(1)} %get-tuple-element.158.refs_7_), channel_id=1, source_target_pairs={{0,8},{4,12},{8,0},{12,4},{16,24},{20,28},{24,16},{28,20},{1,9},{5... | collective-permute-start | bytes 1032200 | tf_op jit(solution)/shard_map/ppermute | solution.py:723
  57.9 8.6 %collective-permute-start.11 = (bf16[224,768]{1,0:T(8,128)(2,1)}, bf16[224,768]{1,0:T(8,128)(2,1)S(1)}, u32[]{:S(2)}, u32[]{:S(2)}) collective-permute-start(bf16[224,768]{1,0:T(8,128)(2,1)} %get-tuple-element.142.refs_3_.refs_24_), channel_id=1, source_target_pairs={{0,4},{4,0},{8,12},{12,8},{16,20},{20,16},{24,28},{28,24},{1,5},{5... | collective-permute-start | bytes 1032200 | tf_op jit(solution)/shard_map/ppermute | solution.py:723
  58.4 11.8 %collective-permute-start.12 = (bf16[224,768]{1,0:T(8,128)(2,1)S(1)}, bf16[224,768]{1,0:T(8,128)(2,1)S(1)}, u32[]{:S(2)}, u32[]{:S(2)}) collective-permute-start(bf16[224,768]{1,0:T(8,128)(2,1)S(1)} %get-tuple-element.157.refs_4_), channel_id=1, source_target_pairs={{0,4},{4,0},{8,12},{12,8},{16,20},{20,16},{24,28},{28,24},{1,5},{5... | collective-permute-start | bytes 1032200 | tf_op jit(solution)/shard_map/ppermute | solution.py:723
  58.4 9.2 %collective-permute-start.6 = (bf16[224,768]{1,0:T(8,128)(2,1)S(1)}, bf16[224,768]{1,0:T(8,128)(2,1)S(1)}, u32[]{:S(2)}, u32[]{:S(2)}) collective-permute-start(bf16[224,768]{1,0:T(8,128)(2,1)S(1)} %collective-permute-done.4.refs_28_), channel_id=1, source_target_pairs={{0,16},{4,20},{8,24},{12,28},{16,0},{20,4},{24,8},{28,12},{1,17},{... | collective-permute-start | bytes 1032200 | tf_op jit(solution)/shard_map/ppermute | solution.py:723
  59.7 9.2 %collective-permute-start.5 = (bf16[224,768]{1,0:T(8,128)(2,1)S(1)}, bf16[224,768]{1,0:T(8,128)(2,1)S(1)}, u32[]{:S(2)}, u32[]{:S(2)}) collective-permute-start(bf16[224,768]{1,0:T(8,128)(2,1)S(1)} %collective-permute-done.4.refs_28_), channel_id=1, source_target_pairs={{0,8},{4,12},{8,0},{12,4},{16,24},{20,28},{24,16},{28,20},{1,9},{5... | collective-permute-start | bytes 1032200 | tf_op jit(solution)/shard_map/ppermute | solution.py:723
  60.9 9.3 %collective-permute-start.13 = (bf16[224,768]{1,0:T(8,128)(2,1)S(1)}, bf16[224,768]{1,0:T(8,128)(2,1)S(1)}, u32[]{:S(2)}, u32[]{:S(2)}) collective-permute-start(bf16[224,768]{1,0:T(8,128)(2,1)S(1)} %collective-permute-done.2.refs_0_.refs_5_), channel_id=1, source_target_pairs={{0,4},{4,0},{8,12},{12,8},{16,20},{20,16},{24,28},{28,24},{1,5},{5... | collective-permute-start | bytes 1032200 | tf_op jit(solution)/shard_map/ppermute | solution.py:723
  67.6 8.9 %collective-permute-start.15 = (bf16[224,768]{1,0:T(8,128)(2,1)}, bf16[224,768]{1,0:T(8,128)(2,1)S(1)}, u32[]{:S(2)}, u32[]{:S(2)}) collective-permute-start(bf16[224,768]{1,0:T(8,128)(2,1)} %get-tuple-element.143.refs_5_.refs_25_), channel_id=1, source_target_pairs={{0,4},{4,0},{8,12},{12,8},{16,20},{20,16},{24,28},{28,24},{1,5},{5... | collective-permute-start | bytes 1032200 | tf_op jit(solution)/shard_map/ppermute | solution.py:723
  68.9 8.8 %collective-permute-start.16 = (bf16[224,768]{1,0:T(8,128)(2,1)S(1)}, bf16[224,768]{1,0:T(8,128)(2,1)S(1)}, u32[]{:S(2)}, u32[]{:S(2)}) collective-permute-start(bf16[224,768]{1,0:T(8,128)(2,1)S(1)} %collective-permute-done.3.refs_1_.refs_6_), channel_id=1, source_target_pairs={{0,4},{4,0},{8,12},{12,8},{16,20},{20,16},{24,28},{28,24},{1,5},{5... | collective-permute-start | bytes 1032200 | tf_op jit(solution)/shard_map/ppermute | solution.py:723
  70.2 8.0 %collective-permute-start.17 = (bf16[224,768]{1,0:T(8,128)(2,1)S(1)}, bf16[224,768]{1,0:T(8,128)(2,1)S(1)}, u32[]{:S(2)}, u32[]{:S(2)}) collective-permute-start(bf16[224,768]{1,0:T(8,128)(2,1)S(1)} %get-tuple-element.158.refs_7_), channel_id=1, source_target_pairs={{0,4},{4,0},{8,12},{12,8},{16,20},{20,16},{24,28},{28,24},{1,5},{5... | collective-permute-start | bytes 1032200 | tf_op jit(solution)/shard_map/ppermute | solution.py:723
  70.2 8.8 %collective-permute-start.18 = (bf16[224,768]{1,0:T(8,128)(2,1)S(1)}, bf16[224,768]{1,0:T(8,128)(2,1)S(1)}, u32[]{:S(2)}, u32[]{:S(2)}) collective-permute-start(bf16[224,768]{1,0:T(8,128)(2,1)S(1)} %get-tuple-element.162.refs_8_), channel_id=1, source_target_pairs={{0,4},{4,0},{8,12},{12,8},{16,20},{20,16},{24,28},{28,24},{1,5},{5... | collective-permute-start | bytes 1032200 | tf_op jit(solution)/shard_map/ppermute | solution.py:723
  70.7 15.9 %collective-permute-start.21 = (bf16[224,768]{1,0:T(8,128)(2,1)S(1)}, bf16[224,768]{1,0:T(8,128)(2,1)S(1)}, u32[]{:S(2)}, u32[]{:S(2)}) collective-permute-start(bf16[224,768]{1,0:T(8,128)(2,1)S(1)} %collective-permute-done.4.refs_28_), channel_id=1, source_target_pairs={{0,4},{4,0},{8,12},{12,8},{16,20},{20,16},{24,28},{28,24},{1,5},{5... | collective-permute-start | bytes 1032200 | tf_op jit(solution)/shard_map/ppermute | solution.py:723
  76.5 9.7 %collective-permute-start.20 = (bf16[128,768]{1,0:T(8,128)(2,1)S(1)}, bf16[128,768]{1,0:T(8,128)(2,1)S(1)}, u32[]{:S(2)}, u32[]{:S(2)}) collective-permute-start(bf16[128,768]{1,0:T(8,128)(2,1)S(1)} %slice.94), channel_id=1, source_target_pairs={{0,8},{4,12},{8,0},{12,4},{16,24},{20,28},{24,16},{28,20},{1,9},{5... | collective-permute-start | bytes 589832 | tf_op jit(solution)/shard_map/ppermute | solution.py:723
  77.7 8.4 %collective-permute-start.19 = (bf16[96,768]{1,0:T(8,128)(2,1)S(1)}, bf16[96,768]{1,0:T(8,128)(2,1)S(1)}, u32[]{:S(2)}, u32[]{:S(2)}) collective-permute-start(bf16[96,768]{1,0:T(8,128)(2,1)S(1)} %slice.93), channel_id=1, source_target_pairs={{0,16},{4,20},{8,24},{12,28},{16,0},{20,4},{24,8},{28,12},{1,17},{... | collective-permute-start | bytes 442376 | tf_op jit(solution)/shard_map/ppermute | solution.py:723
  78.2 8.5 %collective-permute-start.23 = (bf16[224,768]{1,0:T(8,128)(2,1)S(1)}, bf16[224,768]{1,0:T(8,128)(2,1)S(1)}, u32[]{:S(2)}, u32[]{:S(2)}) collective-permute-start(bf16[224,768]{1,0:T(8,128)(2,1)S(1)} %collective-permute-done.6.refs_1_.refs_30_), channel_id=1, source_target_pairs={{0,4},{4,0},{8,12},{12,8},{16,20},{20,16},{24,28},{28,24},{1,5},{5... | collective-permute-start | bytes 1032200 | tf_op jit(solution)/shard_map/ppermute | solution.py:723
  79.0 7.7 %collective-permute-start.22 = (bf16[224,768]{1,0:T(8,128)(2,1)S(1)}, bf16[224,768]{1,0:T(8,128)(2,1)S(1)}, u32[]{:S(2)}, u32[]{:S(2)}) collective-permute-start(bf16[224,768]{1,0:T(8,128)(2,1)S(1)} %collective-permute-done.5.refs_0_.refs_29_), channel_id=1, source_target_pairs={{0,4},{4,0},{8,12},{12,8},{16,20},{20,16},{24,28},{28,24},{1,5},{5... | collective-permute-start | bytes 1032200 | tf_op jit(solution)/shard_map/ppermute | solution.py:723
  108.4 8.7 %collective-permute-start.26 = (bf16[4,448,768]{2,1,0:T(8,128)(2,1)}, bf16[4,448,768]{2,1,0:T(8,128)(2,1)S(1)}, u32[]{:S(2)}, u32[]{:S(2)}) collective-permute-start(bf16[4,448,768]{2,1,0:T(8,128)(2,1)} %get-tuple-element.189), channel_id=1, source_target_pairs={{0,4},{4,0},{8,12},{12,8},{16,20},{20,16},{24,28},{28,24},{1,5},{5... | collective-permute-start | bytes 8257544 | tf_op jit(solution)/shard_map/ppermute | solution.py:723
  108.8 8.4 %collective-permute-start.27 = (bf16[4,384,768]{2,1,0:T(8,128)(2,1)}, bf16[4,384,768]{2,1,0:T(8,128)(2,1)S(1)}, u32[]{:S(2)}, u32[]{:S(2)}) collective-permute-start(bf16[4,384,768]{2,1,0:T(8,128)(2,1)} %get-tuple-element.190), channel_id=1, source_target_pairs={{0,4},{4,0},{8,12},{12,8},{16,20},{20,16},{24,28},{28,24},{1,5},{5... | collective-permute-start | bytes 7077896 | tf_op jit(solution)/shard_map/ppermute | solution.py:723
  120.8 20.0 %collective-permute-start.29 = (bf16[2,2,96,768]{3,2,1,0:T(8,128)(2,1)S(1)}, bf16[2,2,96,768]{3,2,1,0:T(8,128)(2,1)S(1)}, u32[]{:S(2)}, u32[]{:S(2)}) collective-permute-start(bf16[2,2,96,768]{3,2,1,0:T(8,128)(2,1)S(1)} %get-tuple-element.201), channel_id=1, source_target_pairs={{0,16},{4,20},{8,24},{12,28},{16,0},{20,4},{24,8},{28,12},{1,17},{... | collective-permute-start | bytes 1769480 | tf_op jit(solution)/shard_map/ppermute | solution.py:723
  122.1 18.7 %collective-permute-start.28 = (bf16[2,2,112,768]{3,2,1,0:T(8,128)(2,1)S(1)}, bf16[2,2,112,768]{3,2,1,0:T(8,128)(2,1)S(1)}, u32[]{:S(2)}, u32[]{:S(2)}) collective-permute-start(bf16[2,2,112,768]{3,2,1,0:T(8,128)(2,1)S(1)} %get-tuple-element.200), channel_id=1, source_target_pairs={{0,8},{4,12},{8,0},{12,4},{16,24},{20,28},{24,16},{28,20},{1,9},{5... | collective-permute-start | bytes 2064392 | tf_op jit(solution)/shard_map/ppermute | solution.py:723
  144.2 12.5 %collective-permute-start.30 = (bf16[4,448,768]{2,1,0:T(8,128)(2,1)S(1)}, bf16[4,448,768]{2,1,0:T(8,128)(2,1)S(1)}, u32[]{:S(2)}, u32[]{:S(2)}) collective-permute-start(bf16[4,448,768]{2,1,0:T(8,128)(2,1)S(1)} %get-tuple-element.213), channel_id=1, source_target_pairs={{0,4},{4,0},{8,12},{12,8},{16,20},{20,16},{24,28},{28,24},{1,5},{5... | collective-permute-start | bytes 8257544 | tf_op jit(solution)/shard_map/ppermute | solution.py:723
  145.2 18.1 %collective-permute-start.32 = (bf16[2,2,96,768]{3,2,1,0:T(8,128)(2,1)S(1)}, bf16[2,2,96,768]{3,2,1,0:T(8,128)(2,1)S(1)}, u32[]{:S(2)}, u32[]{:S(2)}) collective-permute-start(bf16[2,2,96,768]{3,2,1,0:T(8,128)(2,1)S(1)} %get-tuple-element.216), channel_id=1, source_target_pairs={{0,16},{4,20},{8,24},{12,28},{16,0},{20,4},{24,8},{28,12},{1,17},{... | collective-permute-start | bytes 1769480 | tf_op jit(solution)/shard_map/ppermute | solution.py:723
  145.4 19.1 %collective-permute-start.31 = (bf16[2,2,112,768]{3,2,1,0:T(8,128)(2,1)S(1)}, bf16[2,2,112,768]{3,2,1,0:T(8,128)(2,1)S(1)}, u32[]{:S(2)}, u32[]{:S(2)}) collective-permute-start(bf16[2,2,112,768]{3,2,1,0:T(8,128)(2,1)S(1)} %get-tuple-element.215), channel_id=1, source_target_pairs={{0,8},{4,12},{8,0},{12,4},{16,24},{20,28},{24,16},{28,20},{1,9},{5... | collective-permute-start | bytes 2064392 | tf_op jit(solution)/shard_map/ppermute | solution.py:723
  149.9 20.0 %collective-permute-start.33 = (bf16[480,768]{1,0:T(8,128)(2,1)S(1)}, bf16[480,768]{1,0:T(8,128)(2,1)S(1)}, u32[]{:S(2)}, u32[]{:S(2)}) collective-permute-start(bf16[480,768]{1,0:T(8,128)(2,1)S(1)} %get-tuple-element.221), channel_id=1, source_target_pairs={{1,0},{2,1},{3,2},{5,4},{6,5},{7,6},{9,8},{10,9},{11,10},{13,12},{... | collective-permute-start | bytes 2211848 | tf_op jit(solution)/shard_map/ppermute | solution.py:925
  154.7 19.0 %collective-permute-start.34 = (bf16[480,768]{1,0:T(8,128)(2,1)S(1)}, bf16[480,768]{1,0:T(8,128)(2,1)S(1)}, u32[]{:S(2)}, u32[]{:S(2)}) collective-permute-start(bf16[480,768]{1,0:T(8,128)(2,1)S(1)} %get-tuple-element.222), channel_id=1, source_target_pairs={{0,1},{1,2},{2,3},{4,5},{5,6},{6,7},{8,9},{9,10},{10,11},{12,13},{... | collective-permute-start | bytes 2211848 | tf_op jit(solution)/shard_map/ppermute | solution.py:926
  162.9 19.2 %collective-permute-start.37 = (bf16[2,2,112,768]{3,2,1,0:T(8,128)(2,1)S(1)}, bf16[2,2,112,768]{3,2,1,0:T(8,128)(2,1)S(1)}, u32[]{:S(2)}, u32[]{:S(2)}) collective-permute-start(bf16[2,2,112,768]{3,2,1,0:T(8,128)(2,1)S(1)} %get-tuple-element.225), channel_id=1, source_target_pairs={{0,8},{4,12},{8,0},{12,4},{16,24},{20,28},{24,16},{28,20},{1,9},{5... | collective-permute-start | bytes 2064392 | tf_op jit(solution)/shard_map/ppermute | solution.py:723
  163.2 20.4 %collective-permute-start.39 = (bf16[2,2,112,768]{3,2,1,0:T(8,128)(2,1)S(1)}, bf16[2,2,112,768]{3,2,1,0:T(8,128)(2,1)S(1)}, u32[]{:S(2)}, u32[]{:S(2)}) collective-permute-start(bf16[2,2,112,768]{3,2,1,0:T(8,128)(2,1)S(1)} %get-tuple-element.227), channel_id=1, source_target_pairs={{0,16},{4,20},{8,24},{12,28},{16,0},{20,4},{24,8},{28,12},{1,17},{... | collective-permute-start | bytes 2064392 | tf_op jit(solution)/shard_map/ppermute | solution.py:723
  176.7 18.1 %collective-permute-start.36 = (bf16[480,768]{1,0:T(8,128)(2,1)S(1)}, bf16[480,768]{1,0:T(8,128)(2,1)S(1)}, u32[]{:S(2)}, u32[]{:S(2)}) collective-permute-start(bf16[480,768]{1,0:T(8,128)(2,1)S(1)} %get-tuple-element.223.refs_3_), channel_id=1, source_target_pairs={{3,2},{2,1},{1,0},{7,6},{6,5},{5,4},{11,10},{10,9},{9,8},{15,14},{... | collective-permute-start | bytes 2211848 | tf_op jit(solution)/shard_map/ppermute | solution.py:941
  178.6 18.1 %collective-permute-start.35 = (bf16[480,768]{1,0:T(8,128)(2,1)S(1)}, bf16[480,768]{1,0:T(8,128)(2,1)S(1)}, u32[]{:S(2)}, u32[]{:S(2)}) collective-permute-start(bf16[480,768]{1,0:T(8,128)(2,1)S(1)} %get-tuple-element.223.refs_3_), channel_id=1, source_target_pairs={{0,1},{1,2},{2,3},{4,5},{5,6},{6,7},{8,9},{9,10},{10,11},{12,13},{... | collective-permute-start | bytes 2211848 | tf_op jit(solution)/shard_map/ppermute | solution.py:940
  182.4 14.3 %collective-permute-start.38 = (bf16[2,112,768]{2,1,0:T(8,128)(2,1)S(1)}, bf16[2,112,768]{2,1,0:T(8,128)(2,1)S(1)}, u32[]{:S(2)}, u32[]{:S(2)}) collective-permute-start(bf16[2,112,768]{2,1,0:T(8,128)(2,1)S(1)} %get-tuple-element.266), channel_id=1, source_target_pairs={{0,16},{4,20},{8,24},{12,28},{16,0},{20,4},{24,8},{28,12},{1,17},{... | collective-permute-start | bytes 1032200 | tf_op jit(solution)/shard_map/ppermute | solution.py:723
  183.8 12.9 %collective-permute-start.40 = (bf16[2,112,768]{2,1,0:T(8,128)(2,1)S(1)}, bf16[2,112,768]{2,1,0:T(8,128)(2,1)S(1)}, u32[]{:S(2)}, u32[]{:S(2)}) collective-permute-start(bf16[2,112,768]{2,1,0:T(8,128)(2,1)S(1)} %get-tuple-element.264), channel_id=1, source_target_pairs={{0,8},{4,12},{8,0},{12,4},{16,24},{20,28},{24,16},{28,20},{1,9},{5... | collective-permute-start | bytes 1032200 | tf_op jit(solution)/shard_map/ppermute | solution.py:723
  199.0 19.6 %collective-permute-start.44 = (bf16[4,112,768]{2,1,0:T(8,128)(2,1)S(1)}, bf16[4,112,768]{2,1,0:T(8,128)(2,1)S(1)}, u32[]{:S(2)}, u32[]{:S(2)}) collective-permute-start(bf16[4,112,768]{2,1,0:T(8,128)(2,1)S(1)} %get-tuple-element.260), channel_id=1, source_target_pairs={{0,16},{4,20},{8,24},{12,28},{16,0},{20,4},{24,8},{28,12},{1,17},{... | collective-permute-start | bytes 2064392 | tf_op jit(solution)/shard_map/ppermute | solution.py:723
  201.3 17.3 %collective-permute-start.45 = (bf16[4,96,768]{2,1,0:T(8,128)(2,1)S(1)}, bf16[4,96,768]{2,1,0:T(8,128)(2,1)S(1)}, u32[]{:S(2)}, u32[]{:S(2)}) collective-permute-start(bf16[4,96,768]{2,1,0:T(8,128)(2,1)S(1)} %get-tuple-element.262), channel_id=1, source_target_pairs={{0,8},{4,12},{8,0},{12,4},{16,24},{20,28},{24,16},{28,20},{1,9},{5... | collective-permute-start | bytes 1769480 | tf_op jit(solution)/shard_map/ppermute | solution.py:723
  202.8 13.2 %collective-permute-start.42 = (bf16[112,768]{1,0:T(8,128)(2,1)S(1)}, bf16[112,768]{1,0:T(8,128)(2,1)S(1)}, u32[]{:S(2)}, u32[]{:S(2)}) collective-permute-start(bf16[112,768]{1,0:T(8,128)(2,1)S(1)} %get-tuple-element.230), channel_id=1, source_target_pairs={{0,2},{1,3},{2,0},{3,1},{4,6},{5,7},{6,4},{7,5},{8,10},{9,11},{10,... | collective-permute-start | bytes 516104 | tf_op jit(solution)/shard_map/ppermute | solution.py:943
  203.2 15.3 %collective-permute-start.43 = (bf16[112,768]{1,0:T(8,128)(2,1)S(1)}, bf16[112,768]{1,0:T(8,128)(2,1)S(1)}, u32[]{:S(2)}, u32[]{:S(2)}) collective-permute-start(bf16[112,768]{1,0:T(8,128)(2,1)S(1)} %get-tuple-element.231), channel_id=1, source_target_pairs={{0,3},{1,0},{2,1},{3,2},{4,7},{5,4},{6,5},{7,6},{8,11},{9,8},{10,9... | collective-permute-start | bytes 516104 | tf_op jit(solution)/shard_map/ppermute | solution.py:943
  220.6 11.8 %collective-permute-start.56 = (bf16[112,768]{1,0:T(8,128)(2,1)S(1)}, bf16[112,768]{1,0:T(8,128)(2,1)S(1)}, u32[]{:S(2)}, u32[]{:S(2)}) collective-permute-start(bf16[112,768]{1,0:T(8,128)(2,1)S(1)} %add_convert_fusion.8.refs_0_), channel_id=1, source_target_pairs={{0,2},{1,3},{2,0},{3,1},{4,6},{5,7},{6,4},{7,5},{8,10},{9,11},{10,... | collective-permute-start | bytes 516104 | tf_op jit(solution)/shard_map/ppermute | solution.py:811
  220.9 32.5 %collective-permute-start.55 = (bf16[112,768]{1,0:T(8,128)(2,1)S(1)}, bf16[112,768]{1,0:T(8,128)(2,1)S(1)}, u32[]{:S(2)}, u32[]{:S(2)}) collective-permute-start(bf16[112,768]{1,0:T(8,128)(2,1)S(1)} %add_convert_fusion.8.refs_0_), channel_id=1, source_target_pairs={{0,3},{1,0},{2,1},{3,2},{4,7},{5,4},{6,5},{7,6},{8,11},{9,8},{10,9... | collective-permute-start | bytes 516104 | tf_op jit(solution)/shard_map/ppermute | solution.py:811
  253.5 16.4 %collective-permute-start.59 = (bf16[4,112,768]{2,1,0:T(8,128)(2,1)S(1)}, bf16[4,112,768]{2,1,0:T(8,128)(2,1)S(1)}, u32[]{:S(2)}, u32[]{:S(2)}) collective-permute-start(bf16[4,112,768]{2,1,0:T(8,128)(2,1)S(1)} %pad_maximum_fusion.refs_1_), channel_id=1, source_target_pairs={{0,16},{4,20},{8,24},{12,28},{16,0},{20,4},{24,8},{28,12},{1,17},{... | collective-permute-start | bytes 2064392 | tf_op jit(solution)/shard_map/ppermute | solution.py:723
  253.6 17.6 %collective-permute-start.58 = (bf16[4,112,768]{2,1,0:T(8,128)(2,1)S(1)}, bf16[4,112,768]{2,1,0:T(8,128)(2,1)S(1)}, u32[]{:S(2)}, u32[]{:S(2)}) collective-permute-start(bf16[4,112,768]{2,1,0:T(8,128)(2,1)S(1)} %pad_maximum_fusion.refs_1_), channel_id=1, source_target_pairs={{0,8},{4,12},{8,0},{12,4},{16,24},{20,28},{24,16},{28,20},{1,9},{5... | collective-permute-start | bytes 2064392 | tf_op jit(solution)/shard_map/ppermute | solution.py:723
  254.8 17.4 %collective-permute-start.62 = (bf16[4,112,768]{2,1,0:T(8,128)(2,1)S(1)}, bf16[4,112,768]{2,1,0:T(8,128)(2,1)S(1)}, u32[]{:S(2)}, u32[]{:S(2)}) collective-permute-start(bf16[4,112,768]{2,1,0:T(8,128)(2,1)S(1)} %pad_maximum_fusion.refs_1_), channel_id=1, source_target_pairs={{0,4},{4,0},{8,12},{12,8},{16,20},{20,16},{24,28},{28,24},{1,5},{5... | collective-permute-start | bytes 2064392 | tf_op jit(solution)/shard_map/ppermute | solution.py:723
  255.9 24.7 %collective-permute-start.67 = (bf16[480,768]{1,0:T(8,128)(2,1)S(1)}, bf16[480,768]{1,0:T(8,128)(2,1)S(1)}, u32[]{:S(2)}, u32[]{:S(2)}) collective-permute-start(bf16[480,768]{1,0:T(8,128)(2,1)S(1)} %get-tuple-element.238.refs_4_), channel_id=1, source_target_pairs={{1,2},{2,3},{5,6},{6,7},{9,10},{10,11},{13,14},{14,15},{17,18},{18... | collective-permute-start | bytes 2211848 | tf_op jit(solution)/shard_map/ppermute | solution.py:940
  257.2 24.2 %collective-permute-start.69 = (bf16[480,768]{1,0:T(8,128)(2,1)S(1)}, bf16[480,768]{1,0:T(8,128)(2,1)}, u32[]{:S(2)}, u32[]{:S(2)}) collective-permute-start(bf16[480,768]{1,0:T(8,128)(2,1)S(1)} %get-tuple-element.239.refs_7_), channel_id=1, source_target_pairs={{2,1},{1,0},{6,5},{5,4},{10,9},{9,8},{14,13},{13,12},{18,17},{17,1... | collective-permute-start | bytes 2211848 | tf_op jit(solution)/shard_map/ppermute | solution.py:941
  269.9 8.2 %collective-permute-start.61 = (bf16[2,112,768]{2,1,0:T(8,128)(2,1)S(1)}, bf16[2,112,768]{2,1,0:T(8,128)(2,1)}, u32[]{:S(2)}, u32[]{:S(2)}) collective-permute-start(bf16[2,112,768]{2,1,0:T(8,128)(2,1)S(1)} %slice.106), channel_id=1, source_target_pairs={{0,8},{4,12},{8,0},{12,4},{16,24},{20,28},{24,16},{28,20},{1,9},{5... | collective-permute-start | bytes 1032200 | tf_op jit(solution)/shard_map/ppermute | solution.py:723
  271.9 9.9 %collective-permute-start.60 = (bf16[2,112,768]{2,1,0:T(8,128)(2,1)}, bf16[2,112,768]{2,1,0:T(8,128)(2,1)}, u32[]{:S(2)}, u32[]{:S(2)}) collective-permute-start(bf16[2,112,768]{2,1,0:T(8,128)(2,1)} %slice.105), channel_id=1, source_target_pairs={{0,16},{4,20},{8,24},{12,28},{16,0},{20,4},{24,8},{28,12},{1,17},{... | collective-permute-start | bytes 1032200 | tf_op jit(solution)/shard_map/ppermute | solution.py:723
  273.1 21.8 %collective-permute-start.64 = (bf16[4,112,768]{2,1,0:T(8,128)(2,1)S(1)}, bf16[4,112,768]{2,1,0:T(8,128)(2,1)}, u32[]{:S(2)}, u32[]{:S(2)}) collective-permute-start(bf16[4,112,768]{2,1,0:T(8,128)(2,1)S(1)} %collective-permute-done.59.refs_3_), channel_id=1, source_target_pairs={{0,4},{4,0},{8,12},{12,8},{16,20},{20,16},{24,28},{28,24},{1,5},{5... | collective-permute-start | bytes 2064392 | tf_op jit(solution)/shard_map/ppermute | solution.py:723
  281.4 19.8 %collective-permute-start.63 = (bf16[4,112,768]{2,1,0:T(8,128)(2,1)S(1)}, bf16[4,112,768]{2,1,0:T(8,128)(2,1)}, u32[]{:S(2)}, u32[]{:S(2)}) collective-permute-start(bf16[4,112,768]{2,1,0:T(8,128)(2,1)S(1)} %collective-permute-done.58.refs_2_), channel_id=1, source_target_pairs={{0,4},{4,0},{8,12},{12,8},{16,20},{20,16},{24,28},{28,24},{1,5},{5... | collective-permute-start | bytes 2064392 | tf_op jit(solution)/shard_map/ppermute | solution.py:723
  281.5 9.0 %collective-permute-start.47 = (bf16[208,768]{1,0:T(8,128)(2,1)}, bf16[208,768]{1,0:T(8,128)(2,1)}, u32[]{:S(2)}, u32[]{:S(2)}) collective-permute-start(bf16[208,768]{1,0:T(8,128)(2,1)} %bitcast.49), channel_id=1, source_target_pairs={{0,16},{4,20},{8,24},{12,28},{16,0},{20,4},{24,8},{28,12},{1,17},{... | collective-permute-start | bytes 958472 | tf_op jit(solution)/shard_map/ppermute | solution.py:723
  281.8 10.9 %collective-permute-start.46 = (bf16[208,768]{1,0:T(8,128)(2,1)}, bf16[208,768]{1,0:T(8,128)(2,1)}, u32[]{:S(2)}, u32[]{:S(2)}) collective-permute-start(bf16[208,768]{1,0:T(8,128)(2,1)} %bitcast.50), channel_id=1, source_target_pairs={{0,8},{4,12},{8,0},{12,4},{16,24},{20,28},{24,16},{28,20},{1,9},{5... | collective-permute-start | bytes 958472 | tf_op jit(solution)/shard_map/ppermute | solution.py:723
  283.0 16.7 %collective-permute-start.65 = (bf16[2,112,768]{2,1,0:T(8,128)(2,1)}, bf16[2,112,768]{2,1,0:T(8,128)(2,1)S(1)}, u32[]{:S(2)}, u32[]{:S(2)}) collective-permute-start(bf16[2,112,768]{2,1,0:T(8,128)(2,1)} %collective-permute-done.60.refs_4_), channel_id=1, source_target_pairs={{0,4},{4,0},{8,12},{12,8},{16,20},{20,16},{24,28},{28,24},{1,5},{5... | collective-permute-start | bytes 1032200 | tf_op jit(solution)/shard_map/ppermute | solution.py:723
  290.5 12.9 %collective-permute-start.50 = (bf16[208,768]{1,0:T(8,128)(2,1)}, bf16[208,768]{1,0:T(8,128)(2,1)S(1)}, u32[]{:S(2)}, u32[]{:S(2)}) collective-permute-start(bf16[208,768]{1,0:T(8,128)(2,1)} %bitcast.51), channel_id=1, source_target_pairs={{0,4},{4,0},{8,12},{12,8},{16,20},{20,16},{24,28},{28,24},{1,5},{5... | collective-permute-start | bytes 958472 | tf_op jit(solution)/shard_map/ppermute | solution.py:723
  294.9 9.2 %collective-permute-start.48 = (bf16[112,768]{1,0:T(8,128)(2,1)S(1)}, bf16[112,768]{1,0:T(8,128)(2,1)}, u32[]{:S(2)}, u32[]{:S(2)}) collective-permute-start(bf16[112,768]{1,0:T(8,128)(2,1)S(1)} %slice.103), channel_id=1, source_target_pairs={{0,16},{4,20},{8,24},{12,28},{16,0},{20,4},{24,8},{28,12},{1,17},{... | collective-permute-start | bytes 516104 | tf_op jit(solution)/shard_map/ppermute | solution.py:723
  299.7 22.0 %collective-permute-start.68 = (bf16[480,768]{1,0:T(8,128)(2,1)}, bf16[480,768]{1,0:T(8,128)(2,1)}, u32[]{:S(2)}, u32[]{:S(2)}) collective-permute-start(bf16[480,768]{1,0:T(8,128)(2,1)} %copy-done.15), channel_id=1, source_target_pairs={{2,3},{6,7},{10,11},{14,15},{18,19},{22,23},{26,27},{30,31}} | collective-permute-start | bytes 2211848 | tf_op jit(solution)/shard_map/ppermute | solution.py:940
  301.3 20.5 %collective-permute-start.70 = (bf16[480,768]{1,0:T(8,128)(2,1)}, bf16[480,768]{1,0:T(8,128)(2,1)}, u32[]{:S(2)}, u32[]{:S(2)}) collective-permute-start(bf16[480,768]{1,0:T(8,128)(2,1)} %collective-permute-done.69.refs_8_), channel_id=1, source_target_pairs={{1,0},{5,4},{9,8},{13,12},{17,16},{21,20},{25,24},{29,28}} | collective-permute-start | bytes 2211848 | tf_op jit(solution)/shard_map/ppermute | solution.py:941
  304.1 9.9 %collective-permute-start.52 = (bf16[208,768]{1,0:T(8,128)(2,1)}, bf16[208,768]{1,0:T(8,128)(2,1)}, u32[]{:S(2)}, u32[]{:S(2)}) collective-permute-start(bf16[208,768]{1,0:T(8,128)(2,1)} %collective-permute-done.47.refs_3_), channel_id=1, source_target_pairs={{0,4},{4,0},{8,12},{12,8},{16,20},{20,16},{24,28},{28,24},{1,5},{5... | collective-permute-start | bytes 958472 | tf_op jit(solution)/shard_map/ppermute | solution.py:723
  304.1 9.9 %collective-permute-start.51 = (bf16[208,768]{1,0:T(8,128)(2,1)}, bf16[208,768]{1,0:T(8,128)(2,1)}, u32[]{:S(2)}, u32[]{:S(2)}) collective-permute-start(bf16[208,768]{1,0:T(8,128)(2,1)} %collective-permute-done.46.refs_2_), channel_id=1, source_target_pairs={{0,4},{4,0},{8,12},{12,8},{16,20},{20,16},{24,28},{28,24},{1,5},{5... | collective-permute-start | bytes 958472 | tf_op jit(solution)/shard_map/ppermute | solution.py:723
  305.3 8.7 %collective-permute-start.53 = (bf16[112,768]{1,0:T(8,128)(2,1)}, bf16[112,768]{1,0:T(8,128)(2,1)}, u32[]{:S(2)}, u32[]{:S(2)}) collective-permute-start(bf16[112,768]{1,0:T(8,128)(2,1)} %collective-permute-done.48.refs_4_), channel_id=1, source_target_pairs={{0,4},{4,0},{8,12},{12,8},{16,20},{20,16},{24,28},{28,24},{1,5},{5... | collective-permute-start | bytes 516104 | tf_op jit(solution)/shard_map/ppermute | solution.py:723
  (82 other events, 663.6 us)
Sparse Core Ops, SparseCore 0:
  220.7 37.9 reduce-scatter.1

commit v4 on v3

--- a/solution.py
+++ b/solution.py
@@ -18,12 +18,13 @@
 
 OWN, WINDOW, SHIFT, LOCAL, LIMIT, FLAGGED, PLACE, GROUP, HALF, PIECE, SLOT = 0, 1, 2, 3, 6, 9, 12, 15, 16, 18, 22
 PIECES = 8
+MARGIN = 8
 CORE, X, Y = 1, 2, 4
-PER_MICROSECOND = 1e9
+PER_MICROSECOND = 0.2e9
 MICROSECONDS = {
-    "pack": 1, "project": 5, "attend": 9, "first_norm": 4, "shard": 3, "turn": 21, "lower": 2, "ffn_keep": 4,
-    "attend_back": 15, "sides": 3, "copied_send": 4, "own": 3, "copied_keep": 5, "input_final": 3,
-    "ffn_spread": 1, "ffn_final": 3, "copied_spread": 1, "copied_final": 6,
+    "pack": 1, "project": 5, "attend": 9, "first_norm": 3, "shard": 3, "turn": 12, "ffn_send": 4, "ffn_keep": 4, "ffn_spread": 1,
+    "attend_back": 15, "copied_send": 4, "sides": 3, "copied_keep": 3, "own": 3, "input_final": 4,
+    "ffn_final": 3, "copied_spread": 1, "copied_final": 6,
 }
 
 
@@ -285,13 +286,14 @@
     low, total_in, gain, shift, cot, widen_own, narrow_own = take(7)
     slopes_in, actives = take(3), take(3)
     low_l, normed_l, gain_l, shift_l, cot_lt = take(5)
+    first, first_l, dense, dense_l = take(4)
     widen_own_l, narrow_own_l, layout_one, layout_three, mine, first_piece, third_piece = take(7)
     weights_one, weights_three = take(2)
     pieces = take(len(plan))
-    result, dout, dhid, dnormed, sums, hsums, active = take(7)
-    result_lt, dnormed_l, sums_l, hsums_l = take(4)
-    send_a, send_b, pack = take(3)
-    weights, slope, slope_l, active_l, dhid_l, dout_l, result_l, both = take(8)
+    result, dout, dhid, sums, hsums, active = take(6)
+    result_lt, sums_l, hsums_l, pack = take(4)
+    lower, lower_l = take(4), take(4)
+    weights, slope, dnormed, slope_l, active_l, dhid_l, dout_l, result_l, dnormed_l, dfirst_l, both = take(11)
     shards = dhid.shape[0]
     width = low.shape[1]
     dnormed[...] = total_in[...]
@@ -335,12 +337,10 @@
     shard_backward(dout, weights.at[1], slope, weights.at[0], dhid.at[2], hsums.at[2], dnormed)
     shard_backward(dout, weights_three.at[1], slopes_in[2], weights_three.at[0], dhid.at[3], hsums.at[3], dnormed)
 
-    half = pl.ds(pl.multiple_of(info[HALF + 1], LANES), send_b.shape[1])
-    more = pl.ds(pl.multiple_of(info[HALF + 1] // 6, 64), 64)
-    for s, act in enumerate((actives[0], actives[1], active, actives[2])):
-        send_a[s, :384] = tn(act[:, half], dout[...]).astype(BF)
-        send_a[s, 384:] = pack[s, more, :]
-        send_b[s] = tn(low[:, half], dhid[s]).astype(BF)
+    lower_back(first, dnormed, gain, dense, *lower)
+    dfirst_lt = lower_l[0]
+    lower_back(first_l, dnormed_l, gain_l, dense_l, dfirst_l, *lower_l[1:])
+    dfirst_lt[...] = jnp.transpose(dfirst_l[...])
 
 
 def lower_back(first, dnormed, gain, dense, dfirst, dbranch, dcontext, sums):
@@ -360,24 +360,20 @@
         dcontext[:, width:] = jnp.zeros((dc.shape[0], wide - width), BF)
 
 
-def lower_kernel(
-    info, first, dnormed, gain, dense, first_l, dnormed_l, gain_l, dense_l,
-    dfirst, dbranch, dcontext, sums, dfirst_lt, dbranch_l, dcontext_l, sums_l, dfirst_l,
-):
-    lower_back(first, dnormed, gain, dense, dfirst, dbranch, dcontext, sums)
-    lower_back(first_l, dnormed_l, gain_l, dense_l, dfirst_l, dbranch_l, dcontext_l, sums_l)
-    dfirst_lt[...] = jnp.transpose(dfirst_l[...])
-
-
 EXTRA = 16
 
 
-def extra_rows(info, half, rel):
-    return pl.ds(pl.multiple_of((info[HALF + half] + info[PIECE + rel]) // 6, EXTRA), EXTRA)
+def ffn_send_kernel(info, a0, a1, a2, a3, dout, low, dhid, pack, send_a, send_b):
+    half = pl.ds(pl.multiple_of(info[HALF + 1], LANES), 384)
+    more = pl.ds(pl.multiple_of(info[HALF + 1] // 6, 64), 64)
+    for s, active in enumerate((a0, a1, a2, a3)):
+        send_a[s, :384] = tn(active[:, half], dout[...]).astype(BF)
+        send_a[s, 384:] = pack[s, more, :]
+        send_b[s] = tn(low[:, half], dhid[s]).astype(BF)
 
 
 def ffn_keep_kernel(
-    info, a0, a1, a2, a3, dout, low, dhid, recv_a, recv_b, pack, next_a1, next_a2, next_b1, next_b2, keep_a, keep_b, sum_a, sum_b,
+    info, a0, a1, a2, a3, dout, low, dhid, recv_a, recv_b, pack, next_a, next_b, keep_a, keep_b, sum_a, sum_b,
 ):
     half = pl.ds(pl.multiple_of(info[HALF], LANES), 384)
     more = pl.ds(pl.multiple_of(info[HALF] // 6, 64), 64)
@@ -385,27 +381,13 @@
         sum_a[:384] = (tn(active[:, half], dout[...]) + recv_a[s, :384].astype(F32)).astype(BF)
         sum_a[384:] = (pack[s, more, :].astype(F32) + recv_a[s, 384:].astype(F32)).astype(BF)
         sum_b[...] = (tn(low[:, half], dhid[s]) + recv_b[s].astype(F32)).astype(BF)
-        next_a, next_b = ((next_a1, next_b1), (next_a2, next_b2))[s // 2]
         for rel in range(4):
             rows = pl.ds(pl.multiple_of(info[PIECE + rel], 32), 96)
             rest = pl.ds(pl.multiple_of(384 + info[PIECE + rel] // 6, EXTRA), EXTRA)
-            to = next_a.at[rel // 2, s % 2] if rel % 2 else keep_a.at[rel // 2, s]
+            to = (next_a if rel % 2 else keep_a).at[rel // 2, s]
             to[:96] = sum_a[rows, :]
             to[96:] = sum_a[rest, :]
-            to = next_b.at[rel % 2, s % 2] if rel // 2 else keep_b.at[rel % 2, s]
-            to[...] = sum_b[rows, :]
-
-
-def add(a, b, *more):
-    total = a.astype(F32) + b.astype(F32)
-    for value in more:
-        total = total + value.astype(F32)
-    return total.astype(BF)
-
-
-def add_split(keep, recv, token=None):
-    later = () if token is None else (token[0, 0],)
-    return add(keep[1], recv[1], *later), add(keep[0], recv[0], *later)
+            (next_b if rel // 2 else keep_b)[rel % 2, s] = sum_b[rows, :]
 
 
 def ffn_spread_kernel(info, keep_a, recv_a, keep_b, recv_b, out):
@@ -416,6 +398,21 @@
         out[group, rows:] = (keep_b[s].astype(F32) + recv_b[s].astype(F32)).astype(BF)
 
 
+def add(a, b, *more):
+    total = a.astype(F32) + b.astype(F32)
+    for value in more:
+        total = total + value.astype(F32)
+    return total.astype(BF)
+
+
+def add_split(keep, recv, *zeros):
+    return add(keep[1], recv[1], *zeros), add(keep[0], recv[0], *zeros)
+
+
+def zero_of(value):
+    return value[(0,) * value.ndim].astype(F32) * 0.0
+
+
 def copied_spread_kernel(info, keep_a, recv_a, keep_b, recv_b, *outs):
     for k, out in enumerate(outs):
         keep, recv = (keep_a, recv_a) if k < 2 else (keep_b, recv_b)
@@ -428,7 +425,8 @@
         rows = piece_rows(info, rel)
         if low == 0:
             narrow[rows, :] = piece[:96].astype(F32)
-            pack[extra_rows(info, rel // 4, rel % 4), :] = piece[96:112].astype(F32)
+            rest = pl.ds(pl.multiple_of((info[HALF + rel // 4] + info[PIECE + rel % 4]) // 6, EXTRA), EXTRA)
+            pack[rest, :] = piece[96:112].astype(F32)
         if high > 112:
             widen[rows, :] = piece[112 - low :].astype(F32)
     width_l = narrow_l.shape[0]
@@ -668,16 +666,21 @@
 HB = pl.BlockSpec(memory_space=pl.ANY)
 
 
-def vmem_of(operands, outs, scratch):
-    held = list(operands) + list(outs) + [v for v in scratch if str(v.memory_space) == "vmem"]
-    return int(1.1 * sum(math.prod(v.shape) * jnp.dtype(v.dtype).itemsize for v in held)) + (8 << 20)
-
-
-def call(name, kernel, operands, outs, scratch=(), after=(), in_hbm=0):
+class InHbm:
+    def __init__(self, dims, dtype=BF):
+        self.shape, self.dtype = dims, dtype
+
+
+def vmem_of(outs, scratch):
+    held = list(outs) + [v for v in scratch if str(v.memory_space) == "vmem"]
+    return int(1.1 * sum(math.prod(v.shape) * jnp.dtype(v.dtype).itemsize for v in held)) + (MARGIN << 20)
+
+
+def call(name, kernel, operands, outs, scratch=(), after=(), in_hbm=0, final=False):
     operands = tuple(operands)
     outs = tuple(outs) + (shape((8, LANES), F32),)
     specs = [HB] * len(after) + [SM] + [VM] * (len(operands) - 1 - in_hbm) + [pl.BlockSpec(memory_space=pltpu.HBM)] * in_hbm
-    limit = vmem_of(operands[1 : len(operands) - in_hbm], outs, scratch)
+    limit = vmem_of(outs if final else (), scratch)
     operands = tuple(after) + operands
     at = len(operands) + len(outs) - 1
 
@@ -687,9 +690,9 @@
 
     return pl.pallas_call(
         with_token,
-        out_shape=outs,
+        out_shape=tuple(shape(o.shape, o.dtype) for o in outs),
         in_specs=specs,
-        out_specs=[VM] * len(outs),
+        out_specs=[HB if isinstance(o, InHbm) else VM for o in outs],
         scratch_shapes=list(scratch),
         cost_estimate=pl.CostEstimate(flops=int(MICROSECONDS[name] * PER_MICROSECOND), bytes_accessed=0, transcendentals=0),
         compiler_params=pltpu.CompilerParams(vmem_limit_bytes=limit),
@@ -723,14 +726,17 @@
     return lambda v, bit: lax.ppermute(v, "dp", flip(planes, bit))
 
 
-def forward(piece, by_x, by_y, planes, split, mid=None):
+def forward(piece, by_x, by_y, planes, split, mid=None, zero=None):
     across, parts = around(planes), piece.shape[0]
     if split == "x":
         return [(across(by_x, Y), 3, 0, parts)]
     if split == "y":
         return [(across(by_y, X), 3, 0, parts)]
     mid = mid or parts // 2
-    return [(across(by_x[:mid], Y), 3, 0, mid), (across(by_y[mid:], X), 3, mid, parts)]
+    low, high = by_x[:mid], by_y[mid:]
+    if zero is not None:
+        low, high = add(low, zero), add(high, zero)
+    return [(across(low, Y), 3, 0, mid), (across(high, X), 3, mid, parts)]
 
 
 def to_core(held, planes):
@@ -739,11 +745,11 @@
     return [h[0] for h in held], tuple(h[1:] for h in held)
 
 
-def spread(piece, planes, mid=None):
+def spread(piece, planes, mid=None, zero=None):
     across, parts = around(planes), piece.shape[0]
     by_x, by_y = across(piece, X), across(piece, Y)
     held = [(piece, 0, 0, parts), (by_x, 1, 0, parts), (by_y, 2, 0, parts)]
-    return to_core(held + forward(piece, by_x, by_y, planes, "half", mid), planes)
+    return to_core(held + forward(piece, by_x, by_y, planes, "half", mid, zero), planes)
 
 
 def per_device(
@@ -831,7 +837,10 @@
         (shape((own, width)), shape((own, width_l)), shape((own, LANES), F32)),
         scratch=(pltpu.VMEM((own, wide), F32),),
     )
-    by_x[1], by_y[3] = gate((by_x[1], by_y[3]), attended)
+    by_x[1], by_y[1], by_x[3], by_y[3], *came = gate(
+        (by_x[1], by_y[1], by_x[3], by_y[3], come[1], come[2], come[3]), attended
+    )
+    come = dict(zip((1, 2, 3), came))
     forwarded = {k: forward(come[k], by_x[k], by_y[k], planes, {1: "x", 3: "y"}[k]) for k in (1, 3)}
     first_t, first_l, low_t, low_l, normed_l, active0, slope0, total_t, first_done = call(
         "first_norm", first_norm_kernel,
@@ -839,7 +848,6 @@
          text_gains, text_shifts, layout_gains, layout_shifts, text_widen, mine, text_narrow),
         (shape((own, width), F32), shape((own, width_l), F32), shape((own, width)), shape((own, width_l)),
          shape((own, width_l), F32), shape((own, hid)), shape((own, hid), F32), shape((own, width), F32)),
-        after=(by_y[1], by_x[3]),
     )
     both = gate((forwarded[1][0][0], forwarded[3][0][0]), first_done)
     shards = {}
@@ -848,6 +856,7 @@
         held = [(come[k], 0, 0, parts), (by_x[k], 1, 0, parts), (by_y[k], 2, 0, parts), (array, 3, 0, parts)]
         shards[k] = to_core(held, planes)
     by_x[2], by_y[2] = across(come[2], X), across(come[2], Y)
+    last = forward(come[2], by_x[2], by_y[2], planes, "half", 96)
     actives, slopes, shard_weights, layouts, shard_done = {0: active0}, {0: slope0}, {}, {}, {}
     for k in (1, 3):
         arrays, plan = shards[k]
@@ -857,10 +866,8 @@
             (shape((own, hid)), shape((own, hid), F32), shape((own, width), F32), shape((2, width, hid)),
              shape((width_l, 2 * wide))),
             scratch=(pltpu.VMEM((width_l, 2 * wide), F32),),
-            after=(by_x[2], by_y[2]) if k == 3 else (),
+            after=tuple(f[0] for f in last) if k == 3 else (),
         )
-    last = forward(come[2], by_x[2], by_y[2], planes, "half", 96)
-    last = [(v,) + f[1:] for v, f in zip(gate([f[0] for f in last], shard_done[3]), last)]
     parts = come[2].shape[0]
     shards[2] = to_core([(come[2], 0, 0, parts), (by_x[2], 1, 0, parts), (by_y[2], 2, 0, parts)] + last, planes)
     arrays, plan = shards[2]
@@ -869,38 +876,36 @@
         "turn", functools.partial(turn_kernel, plan),
         (info, low_t, total_t, text_gains, text_shifts, text_cotangent, text_widen, text_narrow,
          slopes[0], slopes[1], slopes[3], actives[0], actives[1], actives[3],
-         low_l, normed_l, layout_gains, layout_shifts, layout_cotangent.T, layout_widen, layout_narrow, layouts[1], layouts[3],
-         mine, come[1], come[3],         shard_weights[1], shard_weights[3], *arrays),
-        (shape((own, width)), shape((own, width)), shape((groups, own, hid)), shape((own, width), F32),
+         low_l, normed_l, layout_gains, layout_shifts, layout_cotangent.T, first_t, first_l, text_dense, layout_dense,
+         layout_widen, layout_narrow, layouts[1], layouts[3],
+         mine, come[1], come[3], shard_weights[1], shard_weights[3], *arrays),
+        (shape((own, width)), shape((own, width)), shape((groups, own, hid)),
          shape((4, width), F32), shape((groups, 1, hid), F32), shape((own, hid)),
-         shape((width_l, own)), shape((own, width_l), F32), shape((4, width_l), F32), shape((groups, 1, hid_l), F32),
-         shape((groups, 4 * rows_a, width)), shape((groups, 4 * piece, width)), shape((groups, 128, width))),
-        scratch=(pltpu.VMEM((2, width, hid), BF), pltpu.VMEM((own, hid), F32),
+         shape((width_l, own)), shape((4, width_l), F32), shape((groups, 1, hid_l), F32), shape((groups, 128, width)),
+         shape((own, width), F32), shape((own, width)), shape((own, width)), shape((4, width), F32),
+         shape((width_l, own), F32), shape((own, width_l)), shape((own, wide)), shape((4, width_l), F32)),
+        scratch=(pltpu.VMEM((2, width, hid), BF), pltpu.VMEM((own, hid), F32), pltpu.VMEM((own, width), F32),
                  pltpu.VMEM((groups, own, hid_l), F32), pltpu.VMEM((groups, own, hid_l), BF),
                  pltpu.VMEM((groups, own, hid_l), BF), pltpu.VMEM((own, width_l), BF), pltpu.VMEM((own, width_l), BF),
-                 pltpu.VMEM((width_l, 2 * wide), F32)),
-    )
-    result_t, dout_t, dhid_t, dnormed_t, sums_t, hsums_t, actives[2] = outs[:7]
-    result_lt, dnormed_l, sums_l, hsums_l, send_a, send_b, pack, turned = outs[7:]
-
-    in_order = [actives[k] for k in range(4)]
+                 pltpu.VMEM((own, width_l), F32), pltpu.VMEM((own, width_l), F32), pltpu.VMEM((width_l, 2 * wide), F32)),
+    )
+    result_t, dout_t, dhid_t, sums_t, hsums_t, actives[2] = outs[:6]
+    result_lt, sums_l, hsums_l, pack = outs[6:10]
+    dfirst_t, db_t, dc_t, low_sums_t, dfirst_lt, db_l, dc_l, low_sums_l, turned = outs[10:]
+
+    def across_planes(value):
+        bit = PIECES
+        while bit < planes:
+            value = add(value, across(value, bit))
+            bit *= 2
+        return value
+
+    ffn_in = (*(actives[k] for k in range(4)), dout_t, low_t, dhid_t)
+    send_a, send_b, ffn_sent = call(
+        "ffn_send", ffn_send_kernel, (info, *ffn_in, pack),
+        (shape((groups, 4 * rows_a, width)), shape((groups, 4 * piece, width))),
+    )
     recv_a, recv_b = across(send_a, CORE), across(send_b, CORE)
-    dfirst_t, db_t, dc_t, low_sums_t, dfirst_lt, db_l, dc_l, low_sums_l, lowered = call(
-        "lower", lower_kernel,
-        (info, first_t, dnormed_t, text_gains, text_dense, first_l, dnormed_l, layout_gains, layout_dense),
-        (shape((own, width), F32), shape((own, width)), shape((own, width)), shape((4, width), F32),
-         shape((width_l, own), F32), shape((own, width_l)), shape((own, wide)), shape((4, width_l), F32)),
-        scratch=(pltpu.VMEM((own, width_l), F32),),
-    )
-    next_a1, next_a2, next_b1, next_b2, keep_a, keep_b, kept = call(
-        "ffn_keep", ffn_keep_kernel,
-        (info, *in_order, dout_t, low_t, dhid_t, recv_a, recv_b, pack),
-        (shape((2, 2, rows_a, width)),) * 2 + (shape((2, 2, piece, width)),) * 2
-        + (shape((2, groups, rows_a, width)), shape((2, groups, piece, width))),
-        scratch=(pltpu.VMEM((4 * rows_a, width), BF), pltpu.VMEM((4 * piece, width), BF)), after=(lowered,),
-    )
-    recv_a1, recv_b1 = across(next_a1, X), across(next_b1, Y)
-
     dq, dk, dv, dq_l, dk_l, dv_l, attended_back = call(
         "attend_back", attend_back_kernel,
         (info, qt, kt, vt, ql, kl, vl, dc_t, dc_l, lse),
@@ -908,20 +913,25 @@
          shape((own, wide)), shape((padded, wide)), shape((padded, wide))),
         scratch=(pltpu.VMEM((window, width), F32), pltpu.VMEM((window, width), F32),
                  pltpu.VMEM((window, wide), F32), pltpu.VMEM((window, wide), F32), pltpu.VMEM((own, wide), F32)),
-        after=(kept,),
-    )
+        after=(ffn_sent,),
+    )
+    next_a, next_b, keep_a, keep_b, kept = call(
+        "ffn_keep", ffn_keep_kernel, (info, *ffn_in, recv_a, recv_b, pack),
+        (shape((2, groups, rows_a, width)), shape((2, groups, piece, width))) * 2,
+        scratch=(pltpu.VMEM((4 * rows_a, width), BF), pltpu.VMEM((4 * piece, width), BF)), after=(attended_back,),
+    )
+    recv_a, recv_b = across(next_a, X), across(next_b, Y)
     copied_in = (text_input, dq, dk, dv, ct, db_t)
     send, extra, sent = call(
         "copied_send", copied_send_kernel,
         (info,) + copied_in + (xlt, dq_l, dk_l, dv_l, cl, db_l, sums_t, low_sums_t, hsums_t, sums_l, low_sums_l, hsums_l),
         (shape((groups, 4 * rows_a, width)), shape((4 * 128, width))),
-        scratch=(pltpu.VMEM((32, width), F32),), after=(recv_a1, recv_b1),
+        scratch=(pltpu.VMEM((32, width), F32),), after=(kept,),
     )
     packed = shape((own + own // 4, width))
     left, right, sided = call(
         "sides", sides_kernel, (info, text_project, wl, dk, dv, dk_l, dv_l), (packed, packed), after=(sent,)
     )
-    recv_a2, recv_b2 = across(next_a2, X), across(next_b2, Y)
     from_right = lax.ppermute(left, "tensor", [(i + 1, i) for i in range(groups - 1)])
     from_left = lax.ppermute(right, "tensor", [(i, i + 1) for i in range(groups - 1)])
 
@@ -929,26 +939,21 @@
     copied_next_a, copied_keep_a, copied_next_b, copied_keep_b, copied_kept = call(
         "copied_keep", copied_keep_kernel, (info,) + copied_in + (extra, recv),
         (shape((2, 2, rows_a, width)),) * 4,
-        scratch=(pltpu.VMEM((groups, 4 * rows_a, width), BF),),
+        scratch=(pltpu.VMEM((groups, 4 * rows_a, width), BF),), after=(sided,),
     )
     copied_recv_a, copied_recv_b = across(copied_next_a, X), across(copied_next_b, Y)
     own_sum, owned = call(
         "own", own_kernel,
         (info, text_project, wl, dq, dk, dv, dq_l, dk_l, dv_l, dfirst_t, dfirst_lt, from_right, from_left),
-        (packed,), after=(copied_kept, recv_a2, recv_b2),
+        (packed,), after=(copied_kept, recv_a, recv_b),
     )
     step_right = lambda v, far: lax.ppermute(v, "tensor", [(i, i + 1) for i in range(far, groups - 1)])
     step_left = lambda v, far: lax.ppermute(v, "tensor", [(i, i - 1) for i in range(groups - 1 - far, 0, -1)])
     lefts, rights = [step_right(own_sum, 0)], [step_left(own_sum, 0)]
+    for far in (1, 2):
+        lefts.append(step_right(lefts[-1], far))
+        rights.append(step_left(rights[-1], far))
     to_group = lambda v, k: lax.ppermute(v, "tensor", shift_to(k))
-
-    def across_planes(value):
-        bit = PIECES
-        while bit < planes:
-            value = add(value, across(value, bit))
-            bit *= 2
-        return value
-
     copied_next_a, copied_keep_a = add_split(copied_keep_a, copied_recv_a)
     copied_next_b, copied_keep_b = add_split(copied_keep_b, copied_recv_b)
     copied_recv_a, copied_recv_b = across(copied_next_a, Y), across(copied_next_b, X)
@@ -958,39 +963,35 @@
         after=(lefts[0], rights[0]),
     )
     parts = [parts[0]] + [to_group(parts[k], k) for k in (1, 2, 3)]
-    summed = across_planes(add(*parts))
-    next_a, keep_a = add_split(keep_a, jnp.concatenate([recv_a1, recv_a2], axis=1), copied_spreaded)
-    next_b, keep_b = add_split(keep_b, jnp.concatenate([recv_b1, recv_b2], axis=1), copied_spreaded)
+    summed = across_planes(add(*parts, zero_of(lefts[1]), zero_of(rights[1])))
+    next_a, keep_a = add_split(keep_a, recv_a, zero_of(summed))
+    next_b, keep_b = add_split(keep_b, recv_b, zero_of(summed))
     recv_a, recv_b = across(next_a, Y), across(next_b, X)
-    ffn_parts, ffn_spreaded = call(
+    every = [summed] + [from_group(summed, k) for k in (1, 2, 3)]
+    ffn_parts, _ = call(
         "ffn_spread", ffn_spread_kernel, (info, keep_a, recv_a, keep_b, recv_b),
-        (shape((groups, rows_a + piece, width)),), after=(summed,),
-    )
-    ffn_summed = lax.psum_scatter(ffn_parts, "tensor", scatter_dimension=0, tiled=False)
-    ffn_arrays, ffn_plan = spread(across_planes(ffn_summed), planes, rows_a)
-    every = [summed] + [from_group(summed, k) for k in (1, 2, 3)]
-    left, right = gate((lefts[0], rights[0]), every[1], every[2], every[3])
-    lefts, rights = [left], [right]
-    for far in (1, 2):
-        lefts.append(step_right(lefts[-1], far))
-        rights.append(step_left(rights[-1], far))
-    g_narrow, g_widen, g_narrow_l, g_widen_l, ffn_done = call(
-        "ffn_final", functools.partial(ffn_final_kernel, ffn_plan), (info, *ffn_arrays),
-        (shape((hid, width), F32), shape((width, hid), F32), shape((hid_l, width_l), F32), shape((width_l, hid_l), F32)),
-        scratch=(pltpu.VMEM((128, width), F32),),
-    )
-    arrays, plan = spread(jnp.stack(every), planes)
+        (shape((groups, rows_a + piece, width)),), after=tuple(every[1:]),
+    )
+    ffn_grads = lax.psum_scatter(ffn_parts, "tensor", scatter_dimension=0, tiled=False)
+    every = jnp.stack(every)
+    arrays, plan = spread(every, planes)
     vectors = lambda w, h: (shape((4, w), F32), shape((2, w), F32), shape((2, w), F32), shape((1, h), F32))
     outs = call(
         "copied_final", functools.partial(copied_final_kernel, plan), (info, *arrays),
         (shape((width, 3 * width), F32), shape((width, width), F32),
          shape((width_l, 3 * width_l), F32), shape((width_l, width_l), F32)) + vectors(width, hid) + vectors(width_l, hid_l),
-        scratch=(pltpu.VMEM((4 * 128, width), F32),),
+        scratch=(pltpu.VMEM((4 * 128, width), F32),), final=True,
     )
     text_grad, layout_grad_t, given = call(
         "input_final", input_final_kernel, (info, own_sum, *lefts, *rights),
-        (shape((total, width), F32), shape((width_l, total), F32)),
-        after=(ffn_done, outs[-1]),
+        (shape((total, width), F32), shape((width_l, total), F32)), after=(outs[-1],), final=True,
+    )
+    ffn_grads = add(across_planes(ffn_grads), zero_of(outs[-1]))
+    ffn_arrays, ffn_plan = spread(ffn_grads, planes, rows_a, zero_of(given))
+    g_narrow, g_widen, g_narrow_l, g_widen_l, _ = call(
+        "ffn_final", functools.partial(ffn_final_kernel, ffn_plan), (info, *ffn_arrays),
+        (shape((hid, width), F32), shape((width, hid), F32), shape((hid_l, width_l), F32), shape((width_l, hid_l), F32)),
+        scratch=(pltpu.VMEM((128, width), F32),), final=True,
     )
     g_project, g_dense, g_project_l, g_dense_l = outs[:4]
     bias_t, gain_t, shift_t, hb_t, bias_l, gain_l, shift_l, hb_l = outs[4:12]

time: 338 us -> 310 us (0.917)
  the two profiles are of different devices: /device:TPU:9 before, /device:TPU:0 now
where the time goes in v4:
time: 310 us; the launch traced here: 307 us
  waiting for transfers between devices  120 us (39%)
  Pallas kernels  83.5 us (27%)
  starting transfers between devices  70.2 us (23%)
  between operations  18.4 us (6%)
  local copies, waits for them, and re-layouts  10.8 us (3%)
  other arithmetic  4.15 us (1%)
    pallas_call x19, Pallas kernels, call(): pl.pallas_call(with_token, out_shape=tuple((shape(o.shape, o.dtype) for o...  83.5 us
    ppermute x52, waiting for transfers between devices, around(): return lambda v, bit: lax.ppermute(v, 'dp', flip(planes, bit))  66.7 us
    ppermute x52, starting transfers between devices, around(): return lambda v, bit: lax.ppermute(v, 'dp', flip(planes, bit))  31.1 us
    ppermute x3, waiting for transfers between devices, per_device(): lax.ppermute(v, 'tensor', [(i, i - 1) for i in range(groups - 1 - far, 0,...  21.1 us
    ppermute x6, waiting for transfers between devices, per_device(): from_group = lambda v, k: lax.ppermute(v, 'tensor', shift_from(k))  17.1 us
    ppermute x6, starting transfers between devices, per_device(): from_group = lambda v, k: lax.ppermute(v, 'tensor', shift_from(k))  14.3 us
    ppermute x1, waiting for transfers between devices, per_device(): lax.ppermute(left, 'tensor', [(i + 1, i) for i in range(groups - 1)])  9.76 us
    ppermute x3, starting transfers between devices, per_device(): lax.ppermute(v, 'tensor', [(i, i + 1) for i in range(far, groups - 1)])  7.9 us
  transfers between devices with their start and end apart: 70, of which 28 were waited for; matrix products, arithmetic and copies ran while one was open for 2% of the time, Pallas kernels for 19%

profile of v4, /device:TPU:0, one launch (start us, length us, event | category | flops | bytes accessed | tf_op | source)
XLA Modules:
  0.0 306.6 jit_solution(14157177509305000456)
XLA Ops:
  10.1 3.1 %collective-permute-start.1 = (bf16[224,768]{1,0:T(8,128)(2,1)S(1)}, bf16[224,768]{1,0:T(8,128)(2,1)S(1)}, u32[]{:S(2)}, u32[]{:S(2)}) collective-permute-start(bf16[224,768]{1,0:T(8,128)(2,1)S(1)} %get-tuple-element.146.refs_14_.refs_27_), channel_id=1, source_target_pairs={{0,1},{1,2},{2,3},{3,0},{4,5},{5,6},{6,7},{7,4},{8,9},{9,10},{10,1... | collective-permute-start | bytes 1032200 | tf_op jit(solution)/shard_map/ppermute | solution.py:817
  13.2 2.1 collective-permute-start
  16.6 2.0 copy-done.1
  20.6 4.7 %project.1 = (bf16[384,768]{1,0:T(8,128)(2,1)S(1)}, bf16[1024,768]{1,0:T(8,128)(2,1)S(1)}, bf16[1024,768]{1,0:T(8,128)(2,1)S(1)}, bf16[384,256]{1,0:T(8,128)(2,1...) custom-call(f32[8,128]{1,0:T(8,128)S(1)} %get-tuple-element.136.refs, ...), custom_call_target="tpu_custom_call" | custom-call | flops 1000000000 | tf_op jit(solution)/shard_map/project/pallas_call | solution.py:691
  25.3 4.7 %collective-permute-done.refs_1_ = bf16[224,768]{1,0:T(8,128)(2,1)S(1)} collective-permute-done((bf16[224,768]{1,0:T(8,128)(2,1)S(1)}, bf16[224,768]{1,0:T(8,128)(2,1)S(1)}, u32[]{:S(2)}, u32[]{:S(2)}) %collective-permute-start) | collective-permute-done | bytes 344096 | tf_op jit(solution)/shard_map/ppermute | solution.py:817
  30.1 1.3 collective-permute-start.6
  31.4 1.5 collective-permute-start.3
  32.9 1.5 collective-permute-start.2
  35.4 8.6 %attend.1 = (bf16[384,768]{1,0:T(8,128)(2,1)S(1)}, bf16[384,192]{1,0:T(8,128)(2,1)S(1)}, f32[384,128]{1,0:T(8,128)S(1)}, f32[8,128]{1,0:T(8,128)S(1)}) custom-call(s32[26]{0:T(128)S(1)} %concatenate.12.refs_1_.refs_0_.refs_2_.refs_3_, bf16[384,768]{1,0:T(8,128)(2,1)S(1)} %get-tuple-element.138.refs_1_.refs_2_, ...), custom_call_target="tpu_custom_call" | custom-call | flops 1800000000 | tf_op jit(solution)/shard_map/attend/pallas_call | solution.py:691
  44.1 3.6 %collective-permute-done.6.refs_5_ = bf16[224,768]{1,0:T(8,128)(2,1)S(1)} collective-permute-done((bf16[224,768]{1,0:T(8,128)(2,1)S(1)}, bf16[224,768]{1,0:T(8,128)(2,1)S(1)}, u32[]{:S(2)}, u32[]{:S(2)}) %collective-permute-start.6) | collective-permute-done | bytes 344096 | tf_op jit(solution)/shard_map/ppermute | solution.py:817
  49.9 1.5 collective-permute-start.12
  53.2 6.8 %collective-permute-done.11.refs_0_ = bf16[224,768]{1,0:T(8,128)(2,1)S(1)} collective-permute-done((bf16[224,768]{1,0:T(8,128)(2,1)S(1)}, bf16[224,768]{1,0:T(8,128)(2,1)S(1)}, u32[]{:S(2)}, u32[]{:S(2)}) %collective-permute-start.11) | collective-permute-done | bytes 344096 | tf_op jit(solution)/shard_map/ppermute | solution.py:726
  60.8 5.6 %collective-permute-done.9.refs_34_ = bf16[224,768]{1,0:T(8,128)(2,1)S(1)} collective-permute-done((bf16[224,768]{1,0:T(8,128)(2,1)S(1)}, bf16[224,768]{1,0:T(8,128)(2,1)S(1)}, u32[]{:S(2)}, u32[]{:S(2)}) %collective-permute-start.9) | collective-permute-done | bytes 344096 | tf_op jit(solution)/shard_map/ppermute | solution.py:726
  66.5 3.0 first_norm.1
  69.5 1.5 collective-permute-start.10
  72.7 4.7 %collective-permute-done.8.refs_0_.refs_35_ = bf16[96,768]{1,0:T(8,128)(2,1)S(1)} collective-permute-done((bf16[96,768]{1,0:T(8,128)(2,1)S(1)}, bf16[96,768]{1,0:T(8,128)(2,1)S(1)}, u32[]{:S(2)}, u32[]{:S(2)}) %collective-permute-start.8) | collective-permute-done | bytes 147488 | tf_op jit(solution)/shard_map/ppermute | solution.py:726
  78.5 2.8 shard.2
  81.2 2.8 shard.3
  84.1 11.3 %turn.1 = (bf16[384,768]{1,0:T(8,128)(2,1)}, bf16[384,768]{1,0:T(8,128)(2,1)S(1)}, bf16[4,384,768]{2,1,0:T(8,128)(2,1)S(1)}, f32[4,768]{1,0:T(4,128)S(1)}, f32[4...) custom-call(s32[26]{0:T(128)S(1)} %concatenate.12.refs_1_.refs_0_.re, ...), custom_call_target="tpu_custom_call" | custom-call | flops 2400000000 | tf_op jit(solution)/shard_map/turn/pallas_call | solution.py:691
  95.4 3.2 %ffn_send.1 = (bf16[4,448,768]{2,1,0:T(8,128)(2,1)S(1)}, bf16[4,384,768]{2,1,0:T(8,128)(2,1)S(1)}, f32[8,128]{1,0:T(8,128)S(1)}) custom-call(s32[26]{0:T(128)S(1)} %concatenate.12.refs_1_.refs_0_.refs_2_.refs_3_, bf16[384,768]{1,0:T(8,128)(2,1)S(1)} %get-tuple-element.169.refs_11_.refs_1_.refs_2_, ...), custom_call_target="tpu_custom_call" | custom-call | flops 800000000 | tf_op jit(solution)/shard_map/ffn_send/pallas_call | solution.py:691
  99.2 14.7 %attend_back.1 = (bf16[384,768]{1,0:T(8,128)(2,1)S(1)}, bf16[1792,768]{1,0:T(8,128)(2,1)S(1)}, bf16[1792,768]{1,0:T(8,128)(2,1)S(1)}, bf16[384,256]{1,0:T(8,128)...) custom-call(f32[8,128]{1,0:T(8,128)S(1)} %get-tuple-element.186.refs_0_, ...), custom_call_target="tpu_custom_call" | custom-call | flops 3000000000 | tf_op jit(solution)/shard_map/attend_back/pallas_call | solution.py:691
  114.0 3.5 %ffn_keep.1 = (bf16[2,4,112,768]{3,2,1,0:T(8,128)(2,1)S(1)}, bf16[2,4,96,768]{3,2,1,0:T(8,128)(2,1)S(1)}, bf16[2,4,112,768]{3,2,1,0:T(8,128)(2,1)S(1)}, bf16[2,4,96,768]{3,2,1,0:T(8,128)(2,1)S(1)}, f32[8,128]{1,0:T(8,128)S(1)}) custom-call(f32[8,128]{1,0:T(8,128)S(1)} %get-tuple-element.190.refs_0_, s32[26]{0:T(128)S(1)} %concatenate.12.refs_1_.refs_0_.refs_2_.refs_3_, ...), custom_call_target="tpu_custom_call" | custom-call | flops 800000000 | tf_op jit(solution)/shard_map/ffn_keep/pallas_call | solution.py:691
  117.5 3.4 %copied_send.1 = (bf16[4,448,768]{2,1,0:T(8,128)(2,1)S(1)}, bf16[512,768]{1,0:T(8,128)(2,1)S(1)}, f32[8,128]{1,0:T(8,128)S(1)}) custom-call(f32[8,128]{1,0:T(8,128)S(1)} %get-tuple-element.193.refs_0_, s32[26]{0:T(128)S(1)} %concatenate.12.refs_1_.refs_0_.refs_2_.refs_3_, bf16[1536,768]{1,0:T(8,128)(2,1)S(1)} %copy-done, ...), custom_call_target="tpu_custom_call" | custom-call | flops 800000000 | tf_op jit(solution)/shard_map/copied_send/pallas_call | solution.py:691
  122.7 2.8 sides.1
  125.6 1.3 collective-permute-start.31
  126.9 4.6 %collective-permute-start.32 = (bf16[480,768]{1,0:T(8,128)(2,1)S(1)}, bf16[480,768]{1,0:T(8,128)(2,1)S(1)}, u32[]{:S(2)}, u32[]{:S(2)}) collective-permute-start(bf16[480,768]{1,0:T(8,128)(2,1)S(1)} %get-tuple-element.219), channel_id=1, source_target_pairs={{0,1},{1,2},{2,3},{4,5},{5,6},{6,7},{8,9},{9,10},{10,11},{12,13},{... | collective-permute-start | bytes 2211848 | tf_op jit(solution)/shard_map/ppermute | solution.py:936
  131.5 2.9 copied_keep.1
  135.6 9.8 %collective-permute-done.31.refs_14_ = bf16[480,768]{1,0:T(8,128)(2,1)S(1)} collective-permute-done((bf16[480,768]{1,0:T(8,128)(2,1)S(1)}, bf16[480,768]{1,0:T(8,128)(2,1)S(1)}, u32[]{:S(2)}, u32[]{:S(2)}) %collective-permute-start.31) | collective-permute-done | bytes 737312 | tf_op jit(solution)/shard_map/ppermute | solution.py:935
  146.6 3.0 collective-permute-done.30.refs_2_
  149.6 4.4 %collective-permute-done.29.refs_1_ = bf16[2,4,112,768]{3,2,1,0:T(8,128)(2,1)S(1)} collective-permute-done((bf16[2,4,112,768]{3,2,1,0:T(8,128)(2,1)S(1)}, bf16[2,4,112,768]{3,2,1,0:T(8,128)(2,1)S(1)}, u32[]{:S(2)}, u32[]{:S(2)}) %collective-permute-start.29) | collective-permute-done | bytes 1376288 | tf_op jit(solution)/shard_map/ppermute | solution.py:726
  154.0 3.0 own.1
  158.3 4.6 %collective-permute-start.33 = (bf16[480,768]{1,0:T(8,128)(2,1)S(1)}, bf16[480,768]{1,0:T(8,128)(2,1)S(1)}, u32[]{:S(2)}, u32[]{:S(2)}) collective-permute-start(bf16[480,768]{1,0:T(8,128)(2,1)S(1)} %get-tuple-element.220.refs_2_), channel_id=1, source_target_pairs={{0,1},{1,2},{2,3},{4,5},{5,6},{6,7},{8,9},{9,10},{10,11},{12,13},{... | collective-permute-start | bytes 2211848 | tf_op jit(solution)/shard_map/ppermute | solution.py:950
  163.8 4.5 %collective-permute-done.35 = bf16[2,2,112,768]{3,2,1,0:T(8,128)(2,1)S(1)} collective-permute-done((bf16[2,2,112,768]{3,2,1,0:T(8,128)(2,1)S(1)}, bf16[2,2,112,768]{3,2,1,0:T(8,128)(2,1)S(1)}, u32[]{:S(2)}, u32[]{:S(2)}) %collective-permute-start.35) | collective-permute-done | bytes 688160 | tf_op jit(solution)/shard_map/ppermute | solution.py:726
  169.4 7.1 %collective-permute-done.34.refs_1_.refs_6_ = bf16[480,768]{1,0:T(8,128)(2,1)S(1)} collective-permute-done((bf16[480,768]{1,0:T(8,128)(2,1)S(1)}, bf16[480,768]{1,0:T(8,128)(2,1)S(1)}, u32[]{:S(2)}, u32[]{:S(2)}) %collective-permute-start.34) | collective-permute-done | bytes 737312 | tf_op jit(solution)/shard_map/ppermute | solution.py:951
  176.5 1.3 collective-permute-start.43
  177.8 1.8 collective-permute-start.42
  179.5 1.8 collective-permute-done.37
  182.4 3.8 %collective-permute-done.36.refs_4_ = bf16[2,112,768]{2,1,0:T(8,128)(2,1)S(1)} collective-permute-done((bf16[2,112,768]{2,1,0:T(8,128)(2,1)S(1)}, bf16[2,112,768]{2,1,0:T(8,128)(2,1)S(1)}, u32[]{:S(2)}, u32[]{:S(2)}) %collective-permute-start.36) | collective-permute-done | bytes 344096 | tf_op jit(solution)/shard_map/ppermute | solution.py:726
  186.3 2.5 collective-permute-done.38.refs_6_
  189.9 4.8 %collective-permute-start.39 = (bf16[112,768]{1,0:T(8,128)(2,1)S(1)}, bf16[112,768]{1,0:T(8,128)(2,1)S(1)}, u32[]{:S(2)}, u32[]{:S(2)}) collective-permute-start(bf16[112,768]{1,0:T(8,128)(2,1)S(1)} %get-tuple-element.226), channel_id=1, source_target_pairs={{0,1},{1,2},{2,3},{3,0},{4,5},{5,6},{6,7},{7,4},{8,9},{9,10},{10,1... | collective-permute-start | bytes 516104 | tf_op jit(solution)/shard_map/ppermute | solution.py:956
  194.7 2.4 collective-permute-start.41
  197.1 4.3 %collective-permute-done.43.refs_7_ = bf16[480,768]{1,0:T(8,128)(2,1)} collective-permute-done((bf16[480,768]{1,0:T(8,128)(2,1)S(1)}, bf16[480,768]{1,0:T(8,128)(2,1)}, u32[]{:S(2)}, u32[]{:S(2)}) %collective-permute-start.43) | collective-permute-done | bytes 737312 | tf_op jit(solution)/shard_map/ppermute | solution.py:951
  205.1 3.7 %collective-permute-done.40 = bf16[112,768]{1,0:T(8,128)(2,1)S(1)} collective-permute-done((bf16[112,768]{1,0:T(8,128)(2,1)S(1)}, bf16[112,768]{1,0:T(8,128)(2,1)S(1)}, u32[]{:S(2)}, u32[]{:S(2)}) %collective-permute-start.40) | collective-permute-done | bytes 172064 | tf_op jit(solution)/shard_map/ppermute | solution.py:956
  211.5 4.5 %collective-permute-start.46 = (bf16[112,768]{1,0:T(8,128)(2,1)S(1)}, bf16[112,768]{1,0:T(8,128)(2,1)S(1)}, u32[]{:S(2)}, u32[]{:S(2)}) collective-permute-start(bf16[112,768]{1,0:T(8,128)(2,1)S(1)} %add_convert_fusion.10), channel_id=1, source_target_pairs={{0,1},{1,2},{2,3},{3,0},{4,5},{5,6},{6,7},{7,4},{8,9},{9,10},{10,1... | collective-permute-start | bytes 516104 | tf_op jit(solution)/shard_map/ppermute | solution.py:817
  216.0 3.4 %collective-permute-start.45 = (bf16[112,768]{1,0:T(8,128)(2,1)S(1)}, bf16[112,768]{1,0:T(8,128)(2,1)S(1)}, u32[]{:S(2)}, u32[]{:S(2)}) collective-permute-start(bf16[112,768]{1,0:T(8,128)(2,1)S(1)} %add_convert_fusion.10), channel_id=1, source_target_pairs={{0,2},{1,3},{2,0},{3,1},{4,6},{5,7},{6,4},{7,5},{8,10},{9,11},{10,... | collective-permute-start | bytes 516104 | tf_op jit(solution)/shard_map/ppermute | solution.py:817
  219.4 4.3 %collective-permute-done.46.refs_2_ = bf16[112,768]{1,0:T(8,128)(2,1)S(1)} collective-permute-done((bf16[112,768]{1,0:T(8,128)(2,1)S(1)}, bf16[112,768]{1,0:T(8,128)(2,1)S(1)}, u32[]{:S(2)}, u32[]{:S(2)}) %collective-permute-start.46) | collective-permute-done | bytes 172064 | tf_op jit(solution)/shard_map/ppermute | solution.py:817
  223.7 4.4 %collective-permute-done.45.refs_1_ = bf16[112,768]{1,0:T(8,128)(2,1)S(1)} collective-permute-done((bf16[112,768]{1,0:T(8,128)(2,1)S(1)}, bf16[112,768]{1,0:T(8,128)(2,1)S(1)}, u32[]{:S(2)}, u32[]{:S(2)}) %collective-permute-start.45) | collective-permute-done | bytes 172064 | tf_op jit(solution)/shard_map/ppermute | solution.py:817
  228.1 1.9 ffn_spread.1
  230.2 1.6 collective-permute-start.48
  231.7 2.0 collective-permute-start.47
  233.7 12.1 %collective-permute-done.48.refs_3_ = bf16[4,112,768]{2,1,0:T(8,128)(2,1)S(1)} collective-permute-done((bf16[4,112,768]{2,1,0:T(8,128)(2,1)S(1)}, bf16[4,112,768]{2,1,0:T(8,128)(2,1)S(1)}, u32[]{:S(2)}, u32[]{:S(2)}) %collective-permute-start.48) | collective-permute-done | bytes 688160 | tf_op jit(solution)/shard_map/ppermute | solution.py:726
  245.9 1.5 collective-permute-start.50
  249.2 5.3 %collective-permute-done.50.refs_5_ = bf16[2,112,768]{2,1,0:T(8,128)(2,1)S(1)} collective-permute-done((bf16[2,112,768]{2,1,0:T(8,128)(2,1)S(1)}, bf16[2,112,768]{2,1,0:T(8,128)(2,1)S(1)}, u32[]{:S(2)}, u32[]{:S(2)}) %collective-permute-start.50) | collective-permute-done | bytes 344096 | tf_op jit(solution)/shard_map/ppermute | solution.py:726
  254.4 3.5 %collective-permute-done.49.refs_4_ = bf16[2,112,768]{2,1,0:T(8,128)(2,1)S(1)} collective-permute-done((bf16[2,112,768]{2,1,0:T(8,128)(2,1)S(1)}, bf16[2,112,768]{2,1,0:T(8,128)(2,1)S(1)}, u32[]{:S(2)}, u32[]{:S(2)}) %collective-permute-start.49) | collective-permute-done | bytes 344096 | tf_op jit(solution)/shard_map/ppermute | solution.py:726
  257.9 1.3 collective-permute-start.57
  259.2 1.5 collective-permute-start.56
  260.7 6.0 %copied_final.1 = (f32[768,2304]{1,0:T(8,128)}, f32[768,768]{1,0:T(8,128)}, f32[192,576]{1,0:T(8,128)}, f32[192,192]{1,0:T(8,128)}, f32[4,768]{1,0:T(4,128)}, /*...) custom-call(s32[26]{0:T(128)S(1)} %concatenate.12.refs_1_.refs_0_.re, ...), custom_call_target="tpu_custom_call" | custom-call | flops 1200000000 | tf_op jit(solution)/shard_map/copied_final/pallas_call | solution.py:691
  269.6 1.5 collective-permute-start.61
  271.2 9.7 %collective-permute-done.57.refs_8_ = bf16[480,768]{1,0:T(8,128)(2,1)} collective-permute-done((bf16[480,768]{1,0:T(8,128)(2,1)}, bf16[480,768]{1,0:T(8,128)(2,1)}, u32[]{:S(2)}, u32[]{:S(2)}) %collective-permute-start.57) | collective-permute-done | bytes 737312 | tf_op jit(solution)/shard_map/ppermute | solution.py:951
  280.9 4.8 %input_final.1 = (f32[1536,768]{1,0:T(8,128)}, f32[192,1536]{1,0:T(8,128)}, f32[8,128]{1,0:T(8,128)S(1)}) custom-call(f32[8,128]{1,0:T(8,128)S(1)} %get-tuple-element.229.refs_0_, s32[26]{0:T(128)S(1)} %concatenate.12.refs_1_.refs_0_.refs_2_.refs_3_, bf16[480,768]{1,0:T(8,128)(2,1)S(1)} %get-tuple-element.220.refs_2_, ...), custom_call_target="tpu_custom_call" | custom-call | flops 800000000 | tf_op jit(solution)/shard_map/input_final/pallas_call | solution.py:691
  287.0 1.6 collective-permute-start.62
  289.8 4.0 %collective-permute-done.62.refs_4_ = bf16[112,768]{1,0:T(8,128)(2,1)S(1)} collective-permute-done((bf16[112,768]{1,0:T(8,128)(2,1)S(1)}, bf16[112,768]{1,0:T(8,128)(2,1)S(1)}, u32[]{:S(2)}, u32[]{:S(2)}) %collective-permute-start.62) | collective-permute-done | bytes 172064 | tf_op jit(solution)/shard_map/ppermute | solution.py:726
  293.8 1.3 collective-permute-done.63.refs_5_
  296.5 3.0 ffn_final.1
  (181 shorter events, 37.0 us)
Async XLA Ops:
  7.2 260.7 %reduce-scatter.2.cloned.1.call-start = ((), (), s32[]{:S(2)}) async-start(), calls=%async_computation.1 | async-start | bytes 1597440 | tf_op jit(solution)/shard_map/reduce_scatter | solution.py:975
  10.1 15.2 %collective-permute-start.1 = (bf16[224,768]{1,0:T(8,128)(2,1)S(1)}, bf16[224,768]{1,0:T(8,128)(2,1)S(1)}, u32[]{:S(2)}, u32[]{:S(2)}) collective-permute-start(bf16[224,768]{1,0:T(8,128)(2,1)S(1)} %get-tuple-element.146.refs_14_.refs_27_), channel_id=1, source_target_pairs={{0,1},{1,2},{2,3},{3,0},{4,5},{5,6},{6,7},{7,4},{8,9},{9,10},{10,1... | collective-permute-start | bytes 1032200 | tf_op jit(solution)/shard_map/ppermute | solution.py:817
  13.2 16.9 %collective-permute-start = (bf16[224,768]{1,0:T(8,128)(2,1)S(1)}, bf16[224,768]{1,0:T(8,128)(2,1)S(1)}, u32[]{:S(2)}, u32[]{:S(2)}) collective-permute-start(bf16[224,768]{1,0:T(8,128)(2,1)S(1)} %get-tuple-element.146.refs_14_.refs_27_), channel_id=1, source_target_pairs={{0,3},{1,0},{2,1},{3,2},{4,7},{5,4},{6,5},{7,6},{8,11},{9,8},{10,9... | collective-permute-start | bytes 1032200 | tf_op jit(solution)/shard_map/ppermute | solution.py:817
  30.1 17.6 %collective-permute-start.6 = (bf16[224,768]{1,0:T(8,128)(2,1)S(1)}, bf16[224,768]{1,0:T(8,128)(2,1)S(1)}, u32[]{:S(2)}, u32[]{:S(2)}) collective-permute-start(bf16[224,768]{1,0:T(8,128)(2,1)S(1)} %get-tuple-element.151), channel_id=1, source_target_pairs={{0,2},{1,3},{2,0},{3,1},{4,6},{5,7},{6,4},{7,5},{8,10},{9,11},{10,... | collective-permute-start | bytes 1032200 | tf_op jit(solution)/shard_map/ppermute | solution.py:817
  31.4 16.3 %collective-permute-start.3 = (bf16[224,768]{1,0:T(8,128)(2,1)S(1)}, bf16[224,768]{1,0:T(8,128)(2,1)S(1)}, u32[]{:S(2)}, u32[]{:S(2)}) collective-permute-start(bf16[224,768]{1,0:T(8,128)(2,1)S(1)} %get-tuple-element.149.refs_4_), channel_id=1, source_target_pairs={{0,16},{4,20},{8,24},{12,28},{16,0},{20,4},{24,8},{28,12},{1,17},{... | collective-permute-start | bytes 1032200 | tf_op jit(solution)/shard_map/ppermute | solution.py:726
  32.9 14.8 %collective-permute-start.2 = (bf16[224,768]{1,0:T(8,128)(2,1)S(1)}, bf16[224,768]{1,0:T(8,128)(2,1)S(1)}, u32[]{:S(2)}, u32[]{:S(2)}) collective-permute-start(bf16[224,768]{1,0:T(8,128)(2,1)S(1)} %get-tuple-element.149.refs_4_), channel_id=1, source_target_pairs={{0,8},{4,12},{8,0},{12,4},{16,24},{20,28},{24,16},{28,20},{1,9},{5... | collective-permute-start | bytes 1032200 | tf_op jit(solution)/shard_map/ppermute | solution.py:726
  34.4 13.3 %collective-permute-start.5 = (bf16[224,768]{1,0:T(8,128)(2,1)S(1)}, bf16[224,768]{1,0:T(8,128)(2,1)S(1)}, u32[]{:S(2)}, u32[]{:S(2)}) collective-permute-start(bf16[224,768]{1,0:T(8,128)(2,1)S(1)} %get-tuple-element.150.refs_6_), channel_id=1, source_target_pairs={{0,16},{4,20},{8,24},{12,28},{16,0},{20,4},{24,8},{28,12},{1,17},{... | collective-permute-start | bytes 1032200 | tf_op jit(solution)/shard_map/ppermute | solution.py:726
  34.9 13.7 %collective-permute-start.4 = (bf16[224,768]{1,0:T(8,128)(2,1)S(1)}, bf16[224,768]{1,0:T(8,128)(2,1)S(1)}, u32[]{:S(2)}, u32[]{:S(2)}) collective-permute-start(bf16[224,768]{1,0:T(8,128)(2,1)S(1)} %get-tuple-element.150.refs_6_), channel_id=1, source_target_pairs={{0,8},{4,12},{8,0},{12,4},{16,24},{20,28},{24,16},{28,20},{1,9},{5... | collective-permute-start | bytes 1032200 | tf_op jit(solution)/shard_map/ppermute | solution.py:726
  49.1 10.9 %collective-permute-start.11 = (bf16[224,768]{1,0:T(8,128)(2,1)S(1)}, bf16[224,768]{1,0:T(8,128)(2,1)S(1)}, u32[]{:S(2)}, u32[]{:S(2)}) collective-permute-start(bf16[224,768]{1,0:T(8,128)(2,1)S(1)} %get-tuple-element.156.refs_4_), channel_id=1, source_target_pairs={{0,16},{4,20},{8,24},{12,28},{16,0},{20,4},{24,8},{28,12},{1,17},{... | collective-permute-start | bytes 1032200 | tf_op jit(solution)/shard_map/ppermute | solution.py:726
  49.9 11.0 %collective-permute-start.12 = (bf16[224,768]{1,0:T(8,128)(2,1)S(1)}, bf16[224,768]{1,0:T(8,128)(2,1)S(1)}, u32[]{:S(2)}, u32[]{:S(2)}) collective-permute-start(bf16[224,768]{1,0:T(8,128)(2,1)S(1)} %get-tuple-element.158.refs_7_), channel_id=1, source_target_pairs={{0,8},{4,12},{8,0},{12,4},{16,24},{20,28},{24,16},{28,20},{1,9},{5... | collective-permute-start | bytes 1032200 | tf_op jit(solution)/shard_map/ppermute | solution.py:726
  51.3 15.1 %collective-permute-start.9 = (bf16[224,768]{1,0:T(8,128)(2,1)S(1)}, bf16[224,768]{1,0:T(8,128)(2,1)S(1)}, u32[]{:S(2)}, u32[]{:S(2)}) collective-permute-start(bf16[224,768]{1,0:T(8,128)(2,1)S(1)} %get-tuple-element.153.refs_32_), channel_id=1, source_target_pairs={{0,16},{4,20},{8,24},{12,28},{16,0},{20,4},{24,8},{28,12},{1,17},{... | collective-permute-start | bytes 1032200 | tf_op jit(solution)/shard_map/ppermute | solution.py:726
  52.6 16.9 %collective-permute-start.13 = (bf16[224,768]{1,0:T(8,128)(2,1)S(1)}, bf16[224,768]{1,0:T(8,128)(2,1)S(1)}, u32[]{:S(2)}, u32[]{:S(2)}) collective-permute-start(bf16[224,768]{1,0:T(8,128)(2,1)S(1)} %get-tuple-element.155.refs_3_.refs_28_), channel_id=1, source_target_pairs={{0,4},{4,0},{8,12},{12,8},{16,20},{20,16},{24,28},{28,24},{1,5},{5... | collective-permute-start | bytes 1032200 | tf_op jit(solution)/shard_map/ppermute | solution.py:726
  52.6 18.5 %collective-permute-start.7 = (bf16[224,768]{1,0:T(8,128)(2,1)S(1)}, bf16[224,768]{1,0:T(8,128)(2,1)S(1)}, u32[]{:S(2)}, u32[]{:S(2)}) collective-permute-start(bf16[224,768]{1,0:T(8,128)(2,1)S(1)} %get-tuple-element.153.refs_32_), channel_id=1, source_target_pairs={{0,8},{4,12},{8,0},{12,4},{16,24},{20,28},{24,16},{28,20},{1,9},{5... | collective-permute-start | bytes 1032200 | tf_op jit(solution)/shard_map/ppermute | solution.py:726
  60.0 11.3 %collective-permute-start.14 = (bf16[224,768]{1,0:T(8,128)(2,1)S(1)}, bf16[224,768]{1,0:T(8,128)(2,1)S(1)}, u32[]{:S(2)}, u32[]{:S(2)}) collective-permute-start(bf16[224,768]{1,0:T(8,128)(2,1)S(1)} %get-tuple-element.156.refs_4_), channel_id=1, source_target_pairs={{0,4},{4,0},{8,12},{12,8},{16,20},{20,16},{24,28},{28,24},{1,5},{5... | collective-permute-start | bytes 1032200 | tf_op jit(solution)/shard_map/ppermute | solution.py:726
  60.8 11.4 %collective-permute-start.19 = (bf16[224,768]{1,0:T(8,128)(2,1)S(1)}, bf16[224,768]{1,0:T(8,128)(2,1)S(1)}, u32[]{:S(2)}, u32[]{:S(2)}) collective-permute-start(bf16[224,768]{1,0:T(8,128)(2,1)S(1)} %get-tuple-element.158.refs_7_), channel_id=1, source_target_pairs={{0,4},{4,0},{8,12},{12,8},{16,20},{20,16},{24,28},{28,24},{1,5},{5... | collective-permute-start | bytes 1032200 | tf_op jit(solution)/shard_map/ppermute | solution.py:726
  66.5 5.8 %collective-permute-start.17 = (bf16[224,768]{1,0:T(8,128)(2,1)S(1)}, bf16[224,768]{1,0:T(8,128)(2,1)S(1)}, u32[]{:S(2)}, u32[]{:S(2)}) collective-permute-start(bf16[224,768]{1,0:T(8,128)(2,1)S(1)} %get-tuple-element.162.refs_5_.refs_29_), channel_id=1, source_target_pairs={{0,4},{4,0},{8,12},{12,8},{16,20},{20,16},{24,28},{28,24},{1,5},{5... | collective-permute-start | bytes 1032200 | tf_op jit(solution)/shard_map/ppermute | solution.py:726
  69.5 7.9 %collective-permute-start.10 = (bf16[128,768]{1,0:T(8,128)(2,1)S(1)}, bf16[128,768]{1,0:T(8,128)(2,1)S(1)}, u32[]{:S(2)}, u32[]{:S(2)}) collective-permute-start(bf16[128,768]{1,0:T(8,128)(2,1)S(1)} %slice.110), channel_id=1, source_target_pairs={{0,8},{4,12},{8,0},{12,4},{16,24},{20,28},{24,16},{28,20},{1,9},{5... | collective-permute-start | bytes 589832 | tf_op jit(solution)/shard_map/ppermute | solution.py:726
  71.1 6.9 %collective-permute-start.16 = (bf16[224,768]{1,0:T(8,128)(2,1)S(1)}, bf16[224,768]{1,0:T(8,128)(2,1)S(1)}, u32[]{:S(2)}, u32[]{:S(2)}) collective-permute-start(bf16[224,768]{1,0:T(8,128)(2,1)S(1)} %get-tuple-element.160.refs_6_), channel_id=1, source_target_pairs={{0,4},{4,0},{8,12},{12,8},{16,20},{20,16},{24,28},{28,24},{1,5},{5... | collective-permute-start | bytes 1032200 | tf_op jit(solution)/shard_map/ppermute | solution.py:726
  71.3 6.1 %collective-permute-start.8 = (bf16[96,768]{1,0:T(8,128)(2,1)S(1)}, bf16[96,768]{1,0:T(8,128)(2,1)S(1)}, u32[]{:S(2)}, u32[]{:S(2)}) collective-permute-start(bf16[96,768]{1,0:T(8,128)(2,1)S(1)} %slice.109), channel_id=1, source_target_pairs={{0,16},{4,20},{8,24},{12,28},{16,0},{20,4},{24,8},{28,12},{1,17},{... | collective-permute-start | bytes 442376 | tf_op jit(solution)/shard_map/ppermute | solution.py:726
  72.2 5.8 %collective-permute-start.20 = (bf16[224,768]{1,0:T(8,128)(2,1)S(1)}, bf16[224,768]{1,0:T(8,128)(2,1)S(1)}, u32[]{:S(2)}, u32[]{:S(2)}) collective-permute-start(bf16[224,768]{1,0:T(8,128)(2,1)S(1)} %get-tuple-element.164.refs_8_), channel_id=1, source_target_pairs={{0,4},{4,0},{8,12},{12,8},{16,20},{20,16},{24,28},{28,24},{1,5},{5... | collective-permute-start | bytes 1032200 | tf_op jit(solution)/shard_map/ppermute | solution.py:726
  72.3 11.8 %collective-permute-start.21 = (bf16[224,768]{1,0:T(8,128)(2,1)S(1)}, bf16[224,768]{1,0:T(8,128)(2,1)S(1)}, u32[]{:S(2)}, u32[]{:S(2)}) collective-permute-start(bf16[224,768]{1,0:T(8,128)(2,1)S(1)} %get-tuple-element.153.refs_32_), channel_id=1, source_target_pairs={{0,4},{4,0},{8,12},{12,8},{16,20},{20,16},{24,28},{28,24},{1,5},{5... | collective-permute-start | bytes 1032200 | tf_op jit(solution)/shard_map/ppermute | solution.py:726
  77.4 6.6 %collective-permute-start.23 = (bf16[224,768]{1,0:T(8,128)(2,1)S(1)}, bf16[224,768]{1,0:T(8,128)(2,1)S(1)}, u32[]{:S(2)}, u32[]{:S(2)}) collective-permute-start(bf16[224,768]{1,0:T(8,128)(2,1)S(1)} %collective-permute-done.9.refs_34_), channel_id=1, source_target_pairs={{0,4},{4,0},{8,12},{12,8},{16,20},{20,16},{24,28},{28,24},{1,5},{5... | collective-permute-start | bytes 1032200 | tf_op jit(solution)/shard_map/ppermute | solution.py:726
  77.4 6.6 %collective-permute-start.22 = (bf16[224,768]{1,0:T(8,128)(2,1)S(1)}, bf16[224,768]{1,0:T(8,128)(2,1)S(1)}, u32[]{:S(2)}, u32[]{:S(2)}) collective-permute-start(bf16[224,768]{1,0:T(8,128)(2,1)S(1)} %collective-permute-done.7.refs_33_), channel_id=1, source_target_pairs={{0,4},{4,0},{8,12},{12,8},{16,20},{20,16},{24,28},{28,24},{1,5},{5... | collective-permute-start | bytes 1032200 | tf_op jit(solution)/shard_map/ppermute | solution.py:726
  78.0 6.1 %collective-permute-start.25 = (bf16[128,768]{1,0:T(8,128)(2,1)S(1)}, bf16[128,768]{1,0:T(8,128)(2,1)S(1)}, u32[]{:S(2)}, u32[]{:S(2)}) collective-permute-start(bf16[128,768]{1,0:T(8,128)(2,1)S(1)} %collective-permute-done.10.refs_1_.refs_36_), channel_id=1, source_target_pairs={{0,4},{4,0},{8,12},{12,8},{16,20},{20,16},{24,28},{28,24},{1,5},{5... | collective-permute-start | bytes 589832 | tf_op jit(solution)/shard_map/ppermute | solution.py:726
  78.0 6.0 %collective-permute-start.24 = (bf16[96,768]{1,0:T(8,128)(2,1)S(1)}, bf16[96,768]{1,0:T(8,128)(2,1)S(1)}, u32[]{:S(2)}, u32[]{:S(2)}) collective-permute-start(bf16[96,768]{1,0:T(8,128)(2,1)S(1)} %collective-permute-done.8.refs_0_.refs_35_), channel_id=1, source_target_pairs={{0,4},{4,0},{8,12},{12,8},{16,20},{20,16},{24,28},{28,24},{1,5},{5... | collective-permute-start | bytes 442376 | tf_op jit(solution)/shard_map/ppermute | solution.py:726
  98.6 15.3 %collective-permute-start.26 = (bf16[4,448,768]{2,1,0:T(8,128)(2,1)S(1)}, bf16[4,448,768]{2,1,0:T(8,128)(2,1)S(1)}, u32[]{:S(2)}, u32[]{:S(2)}) collective-permute-start(bf16[4,448,768]{2,1,0:T(8,128)(2,1)S(1)} %get-tuple-element.191), channel_id=1, source_target_pairs={{0,4},{4,0},{8,12},{12,8},{16,20},{20,16},{24,28},{28,24},{1,5},{5... | collective-permute-start | bytes 8257544 | tf_op jit(solution)/shard_map/ppermute | solution.py:726
  98.7 15.2 %collective-permute-start.27 = (bf16[4,384,768]{2,1,0:T(8,128)(2,1)S(1)}, bf16[4,384,768]{2,1,0:T(8,128)(2,1)S(1)}, u32[]{:S(2)}, u32[]{:S(2)}) collective-permute-start(bf16[4,384,768]{2,1,0:T(8,128)(2,1)S(1)} %get-tuple-element.192), channel_id=1, source_target_pairs={{0,4},{4,0},{8,12},{12,8},{16,20},{20,16},{24,28},{28,24},{1,5},{5... | collective-permute-start | bytes 7077896 | tf_op jit(solution)/shard_map/ppermute | solution.py:726
  120.9 10.6 %collective-permute-start.28 = (bf16[4,448,768]{2,1,0:T(8,128)(2,1)S(1)}, bf16[4,448,768]{2,1,0:T(8,128)(2,1)S(1)}, u32[]{:S(2)}, u32[]{:S(2)}) collective-permute-start(bf16[4,448,768]{2,1,0:T(8,128)(2,1)S(1)} %get-tuple-element.212), channel_id=1, source_target_pairs={{0,4},{4,0},{8,12},{12,8},{16,20},{20,16},{24,28},{28,24},{1,5},{5... | collective-permute-start | bytes 8257544 | tf_op jit(solution)/shard_map/ppermute | solution.py:726
  121.0 33.0 %collective-permute-start.29 = (bf16[2,4,112,768]{3,2,1,0:T(8,128)(2,1)S(1)}, bf16[2,4,112,768]{3,2,1,0:T(8,128)(2,1)S(1)}, u32[]{:S(2)}, u32[]{:S(2)}) collective-permute-start(bf16[2,4,112,768]{3,2,1,0:T(8,128)(2,1)S(1)} %get-tuple-element.214), channel_id=1, source_target_pairs={{0,8},{4,12},{8,0},{12,4},{16,24},{20,28},{24,16},{28,20},{1,9},{5... | collective-permute-start | bytes 4128776 | tf_op jit(solution)/shard_map/ppermute | solution.py:726
  121.9 27.7 %collective-permute-start.30 = (bf16[2,4,96,768]{3,2,1,0:T(8,128)(2,1)S(1)}, bf16[2,4,96,768]{3,2,1,0:T(8,128)(2,1)S(1)}, u32[]{:S(2)}, u32[]{:S(2)}) collective-permute-start(bf16[2,4,96,768]{3,2,1,0:T(8,128)(2,1)S(1)} %get-tuple-element.215), channel_id=1, source_target_pairs={{0,16},{4,20},{8,24},{12,28},{16,0},{20,4},{24,8},{28,12},{1,17},{... | collective-permute-start | bytes 3538952 | tf_op jit(solution)/shard_map/ppermute | solution.py:726
  125.6 19.8 %collective-permute-start.31 = (bf16[480,768]{1,0:T(8,128)(2,1)S(1)}, bf16[480,768]{1,0:T(8,128)(2,1)S(1)}, u32[]{:S(2)}, u32[]{:S(2)}) collective-permute-start(bf16[480,768]{1,0:T(8,128)(2,1)S(1)} %get-tuple-element.218), channel_id=1, source_target_pairs={{1,0},{2,1},{3,2},{5,4},{6,5},{7,6},{9,8},{10,9},{11,10},{13,12},{... | collective-permute-start | bytes 2211848 | tf_op jit(solution)/shard_map/ppermute | solution.py:935
  126.9 19.7 %collective-permute-start.32 = (bf16[480,768]{1,0:T(8,128)(2,1)S(1)}, bf16[480,768]{1,0:T(8,128)(2,1)S(1)}, u32[]{:S(2)}, u32[]{:S(2)}) collective-permute-start(bf16[480,768]{1,0:T(8,128)(2,1)S(1)} %get-tuple-element.219), channel_id=1, source_target_pairs={{0,1},{1,2},{2,3},{4,5},{5,6},{6,7},{8,9},{9,10},{10,11},{12,13},{... | collective-permute-start | bytes 2211848 | tf_op jit(solution)/shard_map/ppermute | solution.py:936
  134.4 33.9 %collective-permute-start.35 = (bf16[2,2,112,768]{3,2,1,0:T(8,128)(2,1)S(1)}, bf16[2,2,112,768]{3,2,1,0:T(8,128)(2,1)S(1)}, u32[]{:S(2)}, u32[]{:S(2)}) collective-permute-start(bf16[2,2,112,768]{3,2,1,0:T(8,128)(2,1)S(1)} %get-tuple-element.222), channel_id=1, source_target_pairs={{0,8},{4,12},{8,0},{12,4},{16,24},{20,28},{24,16},{28,20},{1,9},{5... | collective-permute-start | bytes 2064392 | tf_op jit(solution)/shard_map/ppermute | solution.py:726
  157.0 19.4 %collective-permute-start.34 = (bf16[480,768]{1,0:T(8,128)(2,1)S(1)}, bf16[480,768]{1,0:T(8,128)(2,1)S(1)}, u32[]{:S(2)}, u32[]{:S(2)}) collective-permute-start(bf16[480,768]{1,0:T(8,128)(2,1)S(1)} %get-tuple-element.220.refs_2_), channel_id=1, source_target_pairs={{3,2},{2,1},{1,0},{7,6},{6,5},{5,4},{11,10},{10,9},{9,8},{15,14},{... | collective-permute-start | bytes 2211848 | tf_op jit(solution)/shard_map/ppermute | solution.py:951
  158.3 19.5 %collective-permute-start.33 = (bf16[480,768]{1,0:T(8,128)(2,1)S(1)}, bf16[480,768]{1,0:T(8,128)(2,1)S(1)}, u32[]{:S(2)}, u32[]{:S(2)}) collective-permute-start(bf16[480,768]{1,0:T(8,128)(2,1)S(1)} %get-tuple-element.220.refs_2_), channel_id=1, source_target_pairs={{0,1},{1,2},{2,3},{4,5},{5,6},{6,7},{8,9},{9,10},{10,11},{12,13},{... | collective-permute-start | bytes 2211848 | tf_op jit(solution)/shard_map/ppermute | solution.py:950
  162.9 18.4 %collective-permute-start.37 = (bf16[2,2,112,768]{3,2,1,0:T(8,128)(2,1)S(1)}, bf16[2,2,112,768]{3,2,1,0:T(8,128)(2,1)S(1)}, u32[]{:S(2)}, u32[]{:S(2)}) collective-permute-start(bf16[2,2,112,768]{3,2,1,0:T(8,128)(2,1)S(1)} %get-tuple-element.224), channel_id=1, source_target_pairs={{0,16},{4,20},{8,24},{12,28},{16,0},{20,4},{24,8},{28,12},{1,17},{... | collective-permute-start | bytes 2064392 | tf_op jit(solution)/shard_map/ppermute | solution.py:726
  168.5 17.8 %collective-permute-start.36 = (bf16[2,112,768]{2,1,0:T(8,128)(2,1)S(1)}, bf16[2,112,768]{2,1,0:T(8,128)(2,1)S(1)}, u32[]{:S(2)}, u32[]{:S(2)}) collective-permute-start(bf16[2,112,768]{2,1,0:T(8,128)(2,1)S(1)} %get-tuple-element.260), channel_id=1, source_target_pairs={{0,16},{4,20},{8,24},{12,28},{16,0},{20,4},{24,8},{28,12},{1,17},{... | collective-permute-start | bytes 1032200 | tf_op jit(solution)/shard_map/ppermute | solution.py:726
  176.5 24.9 %collective-permute-start.43 = (bf16[480,768]{1,0:T(8,128)(2,1)S(1)}, bf16[480,768]{1,0:T(8,128)(2,1)}, u32[]{:S(2)}, u32[]{:S(2)}) collective-permute-start(bf16[480,768]{1,0:T(8,128)(2,1)S(1)} %collective-permute-done.34.refs_1_.refs_6_), channel_id=1, source_target_pairs={{2,1},{1,0},{6,5},{5,4},{10,9},{9,8},{14,13},{13,12},{18,17},{17,1... | collective-permute-start | bytes 2211848 | tf_op jit(solution)/shard_map/ppermute | solution.py:951
  177.8 25.5 %collective-permute-start.42 = (bf16[480,768]{1,0:T(8,128)(2,1)S(1)}, bf16[480,768]{1,0:T(8,128)(2,1)}, u32[]{:S(2)}, u32[]{:S(2)}) collective-permute-start(bf16[480,768]{1,0:T(8,128)(2,1)S(1)} %collective-permute-done.33.refs_0_.refs_3_), channel_id=1, source_target_pairs={{1,2},{2,3},{5,6},{6,7},{9,10},{10,11},{13,14},{14,15},{17,18},{18... | collective-permute-start | bytes 2211848 | tf_op jit(solution)/shard_map/ppermute | solution.py:950
  181.5 7.3 %collective-permute-start.38 = (bf16[2,112,768]{2,1,0:T(8,128)(2,1)S(1)}, bf16[2,112,768]{2,1,0:T(8,128)(2,1)S(1)}, u32[]{:S(2)}, u32[]{:S(2)}) collective-permute-start(bf16[2,112,768]{2,1,0:T(8,128)(2,1)S(1)} %get-tuple-element.258), channel_id=1, source_target_pairs={{0,8},{4,12},{8,0},{12,4},{16,24},{20,28},{24,16},{28,20},{1,9},{5... | collective-permute-start | bytes 1032200 | tf_op jit(solution)/shard_map/ppermute | solution.py:726
  189.9 15.1 %collective-permute-start.39 = (bf16[112,768]{1,0:T(8,128)(2,1)S(1)}, bf16[112,768]{1,0:T(8,128)(2,1)S(1)}, u32[]{:S(2)}, u32[]{:S(2)}) collective-permute-start(bf16[112,768]{1,0:T(8,128)(2,1)S(1)} %get-tuple-element.226), channel_id=1, source_target_pairs={{0,1},{1,2},{2,3},{3,0},{4,5},{5,6},{6,7},{7,4},{8,9},{9,10},{10,1... | collective-permute-start | bytes 516104 | tf_op jit(solution)/shard_map/ppermute | solution.py:956
  194.7 14.0 %collective-permute-start.40 = (bf16[112,768]{1,0:T(8,128)(2,1)S(1)}, bf16[112,768]{1,0:T(8,128)(2,1)S(1)}, u32[]{:S(2)}, u32[]{:S(2)}) collective-permute-start(bf16[112,768]{1,0:T(8,128)(2,1)S(1)} %get-tuple-element.227), channel_id=1, source_target_pairs={{0,2},{1,3},{2,0},{3,1},{4,6},{5,7},{6,4},{7,5},{8,10},{9,11},{10,... | collective-permute-start | bytes 516104 | tf_op jit(solution)/shard_map/ppermute | solution.py:956
  194.7 14.0 %collective-permute-start.41 = (bf16[112,768]{1,0:T(8,128)(2,1)S(1)}, bf16[112,768]{1,0:T(8,128)(2,1)S(1)}, u32[]{:S(2)}, u32[]{:S(2)}) collective-permute-start(bf16[112,768]{1,0:T(8,128)(2,1)S(1)} %get-tuple-element.228), channel_id=1, source_target_pairs={{0,3},{1,0},{2,1},{3,2},{4,7},{5,4},{6,5},{7,6},{8,11},{9,8},{10,9... | collective-permute-start | bytes 516104 | tf_op jit(solution)/shard_map/ppermute | solution.py:956
  210.5 17.7 %collective-permute-start.58 = (bf16[4,112,768]{2,1,0:T(8,128)(2,1)S(1)}, bf16[4,112,768]{2,1,0:T(8,128)(2,1)S(1)}, u32[]{:S(2)}, u32[]{:S(2)}) collective-permute-start(bf16[4,112,768]{2,1,0:T(8,128)(2,1)S(1)} %get-tuple-element.254), channel_id=1, source_target_pairs={{0,16},{4,20},{8,24},{12,28},{16,0},{20,4},{24,8},{28,12},{1,17},{... | collective-permute-start | bytes 2064392 | tf_op jit(solution)/shard_map/ppermute | solution.py:726
  211.4 16.7 %collective-permute-start.59 = (bf16[4,96,768]{2,1,0:T(8,128)(2,1)S(1)}, bf16[4,96,768]{2,1,0:T(8,128)(2,1)S(1)}, u32[]{:S(2)}, u32[]{:S(2)}) collective-permute-start(bf16[4,96,768]{2,1,0:T(8,128)(2,1)S(1)} %get-tuple-element.256), channel_id=1, source_target_pairs={{0,8},{4,12},{8,0},{12,4},{16,24},{20,28},{24,16},{28,20},{1,9},{5... | collective-permute-start | bytes 1769480 | tf_op jit(solution)/shard_map/ppermute | solution.py:726
  211.5 12.2 %collective-permute-start.46 = (bf16[112,768]{1,0:T(8,128)(2,1)S(1)}, bf16[112,768]{1,0:T(8,128)(2,1)S(1)}, u32[]{:S(2)}, u32[]{:S(2)}) collective-permute-start(bf16[112,768]{1,0:T(8,128)(2,1)S(1)} %add_convert_fusion.10), channel_id=1, source_target_pairs={{0,1},{1,2},{2,3},{3,0},{4,5},{5,6},{6,7},{7,4},{8,9},{9,10},{10,1... | collective-permute-start | bytes 516104 | tf_op jit(solution)/shard_map/ppermute | solution.py:817
  216.0 12.1 %collective-permute-start.45 = (bf16[112,768]{1,0:T(8,128)(2,1)S(1)}, bf16[112,768]{1,0:T(8,128)(2,1)S(1)}, u32[]{:S(2)}, u32[]{:S(2)}) collective-permute-start(bf16[112,768]{1,0:T(8,128)(2,1)S(1)} %add_convert_fusion.10), channel_id=1, source_target_pairs={{0,2},{1,3},{2,0},{3,1},{4,6},{5,7},{6,4},{7,5},{8,10},{9,11},{10,... | collective-permute-start | bytes 516104 | tf_op jit(solution)/shard_map/ppermute | solution.py:817
  219.4 8.7 %collective-permute-start.44 = (bf16[112,768]{1,0:T(8,128)(2,1)S(1)}, bf16[112,768]{1,0:T(8,128)(2,1)S(1)}, u32[]{:S(2)}, u32[]{:S(2)}) collective-permute-start(bf16[112,768]{1,0:T(8,128)(2,1)S(1)} %add_convert_fusion.10), channel_id=1, source_target_pairs={{0,3},{1,0},{2,1},{3,2},{4,7},{5,4},{6,5},{7,6},{8,11},{9,8},{10,9... | collective-permute-start | bytes 516104 | tf_op jit(solution)/shard_map/ppermute | solution.py:817
  230.2 15.7 %collective-permute-start.48 = (bf16[4,112,768]{2,1,0:T(8,128)(2,1)S(1)}, bf16[4,112,768]{2,1,0:T(8,128)(2,1)S(1)}, u32[]{:S(2)}, u32[]{:S(2)}) collective-permute-start(bf16[4,112,768]{2,1,0:T(8,128)(2,1)S(1)} %pad_maximum_fusion.refs_1_), channel_id=1, source_target_pairs={{0,16},{4,20},{8,24},{12,28},{16,0},{20,4},{24,8},{28,12},{1,17},{... | collective-permute-start | bytes 2064392 | tf_op jit(solution)/shard_map/ppermute | solution.py:726
  231.7 16.3 %collective-permute-start.47 = (bf16[4,112,768]{2,1,0:T(8,128)(2,1)S(1)}, bf16[4,112,768]{2,1,0:T(8,128)(2,1)S(1)}, u32[]{:S(2)}, u32[]{:S(2)}) collective-permute-start(bf16[4,112,768]{2,1,0:T(8,128)(2,1)S(1)} %pad_maximum_fusion.refs_1_), channel_id=1, source_target_pairs={{0,8},{4,12},{8,0},{12,4},{16,24},{20,28},{24,16},{28,20},{1,9},{5... | collective-permute-start | bytes 2064392 | tf_op jit(solution)/shard_map/ppermute | solution.py:726
  233.7 24.2 %collective-permute-start.51 = (bf16[4,112,768]{2,1,0:T(8,128)(2,1)S(1)}, bf16[4,112,768]{2,1,0:T(8,128)(2,1)S(1)}, u32[]{:S(2)}, u32[]{:S(2)}) collective-permute-start(bf16[4,112,768]{2,1,0:T(8,128)(2,1)S(1)} %pad_maximum_fusion.refs_1_), channel_id=1, source_target_pairs={{0,4},{4,0},{8,12},{12,8},{16,20},{20,16},{24,28},{28,24},{1,5},{5... | collective-permute-start | bytes 2064392 | tf_op jit(solution)/shard_map/ppermute | solution.py:726
  245.9 8.6 %collective-permute-start.50 = (bf16[2,112,768]{2,1,0:T(8,128)(2,1)S(1)}, bf16[2,112,768]{2,1,0:T(8,128)(2,1)S(1)}, u32[]{:S(2)}, u32[]{:S(2)}) collective-permute-start(bf16[2,112,768]{2,1,0:T(8,128)(2,1)S(1)} %slice.118), channel_id=1, source_target_pairs={{0,8},{4,12},{8,0},{12,4},{16,24},{20,28},{24,16},{28,20},{1,9},{5... | collective-permute-start | bytes 1032200 | tf_op jit(solution)/shard_map/ppermute | solution.py:726
  247.3 13.4 %collective-permute-start.53 = (bf16[4,112,768]{2,1,0:T(8,128)(2,1)S(1)}, bf16[4,112,768]{2,1,0:T(8,128)(2,1)S(1)}, u32[]{:S(2)}, u32[]{:S(2)}) collective-permute-start(bf16[4,112,768]{2,1,0:T(8,128)(2,1)S(1)} %collective-permute-done.48.refs_3_), channel_id=1, source_target_pairs={{0,4},{4,0},{8,12},{12,8},{16,20},{20,16},{24,28},{28,24},{1,5},{5... | collective-permute-start | bytes 2064392 | tf_op jit(solution)/shard_map/ppermute | solution.py:726
  248.1 9.8 %collective-permute-start.49 = (bf16[2,112,768]{2,1,0:T(8,128)(2,1)S(1)}, bf16[2,112,768]{2,1,0:T(8,128)(2,1)S(1)}, u32[]{:S(2)}, u32[]{:S(2)}) collective-permute-start(bf16[2,112,768]{2,1,0:T(8,128)(2,1)S(1)} %slice.117), channel_id=1, source_target_pairs={{0,16},{4,20},{8,24},{12,28},{16,0},{20,4},{24,8},{28,12},{1,17},{... | collective-permute-start | bytes 1032200 | tf_op jit(solution)/shard_map/ppermute | solution.py:726
  248.9 11.8 %collective-permute-start.52 = (bf16[4,112,768]{2,1,0:T(8,128)(2,1)S(1)}, bf16[4,112,768]{2,1,0:T(8,128)(2,1)S(1)}, u32[]{:S(2)}, u32[]{:S(2)}) collective-permute-start(bf16[4,112,768]{2,1,0:T(8,128)(2,1)S(1)} %collective-permute-done.47.refs_2_), channel_id=1, source_target_pairs={{0,4},{4,0},{8,12},{12,8},{16,20},{20,16},{24,28},{28,24},{1,5},{5... | collective-permute-start | bytes 2064392 | tf_op jit(solution)/shard_map/ppermute | solution.py:726
  257.9 23.0 %collective-permute-start.57 = (bf16[480,768]{1,0:T(8,128)(2,1)}, bf16[480,768]{1,0:T(8,128)(2,1)}, u32[]{:S(2)}, u32[]{:S(2)}) collective-permute-start(bf16[480,768]{1,0:T(8,128)(2,1)} %collective-permute-done.43.refs_7_), channel_id=1, source_target_pairs={{1,0},{5,4},{9,8},{13,12},{17,16},{21,20},{25,24},{29,28}} | collective-permute-start | bytes 2211848 | tf_op jit(solution)/shard_map/ppermute | solution.py:951
  259.2 21.7 %collective-permute-start.56 = (bf16[480,768]{1,0:T(8,128)(2,1)}, bf16[480,768]{1,0:T(8,128)(2,1)}, u32[]{:S(2)}, u32[]{:S(2)}) collective-permute-start(bf16[480,768]{1,0:T(8,128)(2,1)} %collective-permute-done.42.refs_4_), channel_id=1, source_target_pairs={{2,3},{6,7},{10,11},{14,15},{18,19},{22,23},{26,27},{30,31}} | collective-permute-start | bytes 2211848 | tf_op jit(solution)/shard_map/ppermute | solution.py:950
  269.0 18.0 %collective-permute-start.60 = (bf16[208,768]{1,0:T(8,128)(2,1)S(1)}, bf16[208,768]{1,0:T(8,128)(2,1)S(1)}, u32[]{:S(2)}, u32[]{:S(2)}) collective-permute-start(bf16[208,768]{1,0:T(8,128)(2,1)S(1)} %fusion.8.refs_1_), channel_id=1, source_target_pairs={{0,8},{4,12},{8,0},{12,4},{16,24},{20,28},{24,16},{28,20},{1,9},{5... | collective-permute-start | bytes 958472 | tf_op jit(solution)/shard_map/ppermute | solution.py:726
  269.6 19.1 %collective-permute-start.61 = (bf16[208,768]{1,0:T(8,128)(2,1)S(1)}, bf16[208,768]{1,0:T(8,128)(2,1)S(1)}, u32[]{:S(2)}, u32[]{:S(2)}) collective-permute-start(bf16[208,768]{1,0:T(8,128)(2,1)S(1)} %fusion.8.refs_1_), channel_id=1, source_target_pairs={{0,16},{4,20},{8,24},{12,28},{16,0},{20,4},{24,8},{28,12},{1,17},{... | collective-permute-start | bytes 958472 | tf_op jit(solution)/shard_map/ppermute | solution.py:726
  286.9 8.9 %collective-permute-start.64 = (bf16[208,768]{1,0:T(8,128)(2,1)S(1)}, bf16[208,768]{1,0:T(8,128)(2,1)S(1)}, u32[]{:S(2)}, u32[]{:S(2)}) collective-permute-start(bf16[208,768]{1,0:T(8,128)(2,1)S(1)} %fusion.8.refs_1_), channel_id=1, source_target_pairs={{0,4},{4,0},{8,12},{12,8},{16,20},{20,16},{24,28},{28,24},{1,5},{5... | collective-permute-start | bytes 958472 | tf_op jit(solution)/shard_map/ppermute | solution.py:726
  287.0 6.8 %collective-permute-start.62 = (bf16[112,768]{1,0:T(8,128)(2,1)S(1)}, bf16[112,768]{1,0:T(8,128)(2,1)S(1)}, u32[]{:S(2)}, u32[]{:S(2)}) collective-permute-start(bf16[112,768]{1,0:T(8,128)(2,1)S(1)} %add_convert_fusion.9), channel_id=1, source_target_pairs={{0,16},{4,20},{8,24},{12,28},{16,0},{20,4},{24,8},{28,12},{1,17},{... | collective-permute-start | bytes 516104 | tf_op jit(solution)/shard_map/ppermute | solution.py:726
  288.6 7.9 %collective-permute-start.65 = (bf16[208,768]{1,0:T(8,128)(2,1)S(1)}, bf16[208,768]{1,0:T(8,128)(2,1)S(1)}, u32[]{:S(2)}, u32[]{:S(2)}) collective-permute-start(bf16[208,768]{1,0:T(8,128)(2,1)S(1)} %collective-permute-done.60.refs_2_), channel_id=1, source_target_pairs={{0,4},{4,0},{8,12},{12,8},{16,20},{20,16},{24,28},{28,24},{1,5},{5... | collective-permute-start | bytes 958472 | tf_op jit(solution)/shard_map/ppermute | solution.py:726
  288.8 7.7 %collective-permute-start.66 = (bf16[208,768]{1,0:T(8,128)(2,1)S(1)}, bf16[208,768]{1,0:T(8,128)(2,1)S(1)}, u32[]{:S(2)}, u32[]{:S(2)}) collective-permute-start(bf16[208,768]{1,0:T(8,128)(2,1)S(1)} %collective-permute-done.61.refs_3_), channel_id=1, source_target_pairs={{0,4},{4,0},{8,12},{12,8},{16,20},{20,16},{24,28},{28,24},{1,5},{5... | collective-permute-start | bytes 958472 | tf_op jit(solution)/shard_map/ppermute | solution.py:726
  289.1 6.0 %collective-permute-start.63 = (bf16[96,768]{1,0:T(8,128)(2,1)S(1)}, bf16[96,768]{1,0:T(8,128)(2,1)S(1)}, u32[]{:S(2)}, u32[]{:S(2)}) collective-permute-start(bf16[96,768]{1,0:T(8,128)(2,1)S(1)} %add_convert_fusion.11), channel_id=1, source_target_pairs={{0,8},{4,12},{8,0},{12,4},{16,24},{20,28},{24,16},{28,20},{1,9},{5... | collective-permute-start | bytes 442376 | tf_op jit(solution)/shard_map/ppermute | solution.py:726
  (31 other events, 314.3 us)
Sparse Core Ops, SparseCore 0:
  230.2 32.1 reduce-scatter.1

commit v5 on v4

--- a/solution.py
+++ b/solution.py
@@ -726,17 +726,17 @@
     return lambda v, bit: lax.ppermute(v, "dp", flip(planes, bit))
 
 
-def forward(piece, by_x, by_y, planes, split, mid=None, zero=None):
+def forward(piece, by_x, by_y, planes, split, mid=None, token=None):
     across, parts = around(planes), piece.shape[0]
     if split == "x":
         return [(across(by_x, Y), 3, 0, parts)]
     if split == "y":
         return [(across(by_y, X), 3, 0, parts)]
     mid = mid or parts // 2
-    low, high = by_x[:mid], by_y[mid:]
-    if zero is not None:
-        low, high = add(low, zero), add(high, zero)
-    return [(across(low, Y), 3, 0, mid), (across(high, X), 3, mid, parts)]
+    low, high = across(by_x[:mid], Y), across(by_y[mid:], X)
+    if token is not None:
+        low, high = gate((low, high), token)
+    return [(low, 3, 0, mid), (high, 3, mid, parts)]
 
 
 def to_core(held, planes):
@@ -745,11 +745,11 @@
     return [h[0] for h in held], tuple(h[1:] for h in held)
 
 
-def spread(piece, planes, mid=None, zero=None):
+def spread(piece, planes, mid=None, token=None):
     across, parts = around(planes), piece.shape[0]
     by_x, by_y = across(piece, X), across(piece, Y)
     held = [(piece, 0, 0, parts), (by_x, 1, 0, parts), (by_y, 2, 0, parts)]
-    return to_core(held + forward(piece, by_x, by_y, planes, "half", mid, zero), planes)
+    return to_core(held + forward(piece, by_x, by_y, planes, "half", mid, token), planes)
 
 
 def per_device(
@@ -849,13 +849,16 @@
         (shape((own, width), F32), shape((own, width_l), F32), shape((own, width)), shape((own, width_l)),
          shape((own, width_l), F32), shape((own, hid)), shape((own, hid), F32), shape((own, width), F32)),
     )
-    both = gate((forwarded[1][0][0], forwarded[3][0][0]), first_done)
+    last_x, last_y = across(come[2], X), across(come[2], Y)
+    *both, come[1], come[3], by_x[1], by_y[1], by_x[3], by_y[3] = gate(
+        (forwarded[1][0][0], forwarded[3][0][0], come[1], come[3], by_x[1], by_y[1], by_x[3], by_y[3]), first_done
+    )
     shards = {}
     for k, array in zip((1, 3), both):
         parts = come[k].shape[0]
         held = [(come[k], 0, 0, parts), (by_x[k], 1, 0, parts), (by_y[k], 2, 0, parts), (array, 3, 0, parts)]
         shards[k] = to_core(held, planes)
-    by_x[2], by_y[2] = across(come[2], X), across(come[2], Y)
+    by_x[2], by_y[2] = last_x, last_y
     last = forward(come[2], by_x[2], by_y[2], planes, "half", 96)
     actives, slopes, shard_weights, layouts, shard_done = {0: active0}, {0: slope0}, {}, {}, {}
     for k in (1, 3):
@@ -866,8 +869,8 @@
             (shape((own, hid)), shape((own, hid), F32), shape((own, width), F32), shape((2, width, hid)),
              shape((width_l, 2 * wide))),
             scratch=(pltpu.VMEM((width_l, 2 * wide), F32),),
-            after=tuple(f[0] for f in last) if k == 3 else (),
         )
+    last = [(v,) + f[1:] for v, f in zip(gate([f[0] for f in last], shard_done[3]), last)]
     parts = come[2].shape[0]
     shards[2] = to_core([(come[2], 0, 0, parts), (by_x[2], 1, 0, parts), (by_y[2], 2, 0, parts)] + last, planes)
     arrays, plan = shards[2]
@@ -945,7 +948,7 @@
     own_sum, owned = call(
         "own", own_kernel,
         (info, text_project, wl, dq, dk, dv, dq_l, dk_l, dv_l, dfirst_t, dfirst_lt, from_right, from_left),
-        (packed,), after=(copied_kept, recv_a, recv_b),
+        (packed,), after=(copied_kept,),
     )
     step_right = lambda v, far: lax.ppermute(v, "tensor", [(i, i + 1) for i in range(far, groups - 1)])
     step_left = lambda v, far: lax.ppermute(v, "tensor", [(i, i - 1) for i in range(groups - 1 - far, 0, -1)])
@@ -954,8 +957,8 @@
         lefts.append(step_right(lefts[-1], far))
         rights.append(step_left(rights[-1], far))
     to_group = lambda v, k: lax.ppermute(v, "tensor", shift_to(k))
-    copied_next_a, copied_keep_a = add_split(copied_keep_a, copied_recv_a)
-    copied_next_b, copied_keep_b = add_split(copied_keep_b, copied_recv_b)
+    copied_next_a, copied_keep_a = add_split(copied_keep_a, copied_recv_a, zero_of(recv_a))
+    copied_next_b, copied_keep_b = add_split(copied_keep_b, copied_recv_b, zero_of(recv_b))
     copied_recv_a, copied_recv_b = across(copied_next_a, Y), across(copied_next_b, X)
     *parts, copied_spreaded = call(
         "copied_spread", copied_spread_kernel, (info, copied_keep_a, copied_recv_a, copied_keep_b, copied_recv_b),
@@ -964,8 +967,8 @@
     )
     parts = [parts[0]] + [to_group(parts[k], k) for k in (1, 2, 3)]
     summed = across_planes(add(*parts, zero_of(lefts[1]), zero_of(rights[1])))
-    next_a, keep_a = add_split(keep_a, recv_a, zero_of(summed))
-    next_b, keep_b = add_split(keep_b, recv_b, zero_of(summed))
+    next_a, keep_a = add_split(keep_a, recv_a, zero_of(lefts[1]), zero_of(rights[1]))
+    next_b, keep_b = add_split(keep_b, recv_b, zero_of(lefts[1]), zero_of(rights[1]))
     recv_a, recv_b = across(next_a, Y), across(next_b, X)
     every = [summed] + [from_group(summed, k) for k in (1, 2, 3)]
     ffn_parts, _ = call(
@@ -987,7 +990,7 @@
         (shape((total, width), F32), shape((width_l, total), F32)), after=(outs[-1],), final=True,
     )
     ffn_grads = add(across_planes(ffn_grads), zero_of(outs[-1]))
-    ffn_arrays, ffn_plan = spread(ffn_grads, planes, rows_a, zero_of(given))
+    ffn_arrays, ffn_plan = spread(ffn_grads, planes, rows_a, given)
     g_narrow, g_widen, g_narrow_l, g_widen_l, _ = call(
         "ffn_final", functools.partial(ffn_final_kernel, ffn_plan), (info, *ffn_arrays),
         (shape((hid, width), F32), shape((width, hid), F32), shape((hid_l, width_l), F32), shape((width_l, hid_l), F32)),

time: 310 us -> 287 us (0.926)
  the two profiles are of different devices: /device:TPU:0 before, /device:TPU:9 now
where the time goes in v5:
time: 287 us; the launch traced here: 281 us
  starting transfers between devices  92.2 us (32%)
  Pallas kernels  83.7 us (29%)
  waiting for transfers between devices  72.1 us (25%)
  between operations  18.3 us (6%)
  local copies, waits for them, and re-layouts  10.8 us (4%)
  other arithmetic  4.32 us (2%)
    pallas_call x19, Pallas kernels, call(): pl.pallas_call(with_token, out_shape=tuple((shape(o.shape, o.dtype) for o...  83.7 us
    ppermute x52, starting transfers between devices, around(): return lambda v, bit: lax.ppermute(v, 'dp', flip(planes, bit))  60.8 us
    ppermute x52, waiting for transfers between devices, around(): return lambda v, bit: lax.ppermute(v, 'dp', flip(planes, bit))  27.4 us
    ppermute x6, waiting for transfers between devices, per_device(): from_group = lambda v, k: lax.ppermute(v, 'tensor', shift_from(k))  17.1 us
    ppermute x1, waiting for transfers between devices, per_device(): lax.ppermute(left, 'tensor', [(i + 1, i) for i in range(groups - 1)])  10.4 us
    ppermute x3, starting transfers between devices, per_device(): lax.ppermute(v, 'tensor', [(i, i + 1) for i in range(far, groups - 1)])  9.91 us
    ppermute x3, waiting for transfers between devices, per_device(): to_group = lambda v, k: lax.ppermute(v, 'tensor', shift_to(k))  7.75 us
    ppermute x3, starting transfers between devices, per_device(): lax.ppermute(v, 'tensor', [(i, i - 1) for i in range(groups - 1 - far, 0,...  6.27 us
  transfers between devices with their start and end apart: 70, of which 25 were waited for; matrix products, arithmetic and copies ran while one was open for 3% of the time, Pallas kernels for 20%

profile of v5, /device:TPU:9, one launch (start us, length us, event | category | flops | bytes accessed | tf_op | source)
XLA Modules:
  0.0 281.5 jit_solution(12697281315735961437)
XLA Ops:
  8.1 1.2 constant_dynamic-slice_fusion.1
  10.1 1.3 collective-permute-start.1
  12.9 2.0 copy-done.1
  14.9 1.1 copy-done.6
  16.9 4.7 %project.1 = (bf16[384,768]{1,0:T(8,128)(2,1)S(1)}, bf16[1024,768]{1,0:T(8,128)(2,1)S(1)}, bf16[1024,768]{1,0:T(8,128)(2,1)S(1)}, bf16[384,256]{1,0:T(8,128)(2,1...) custom-call(f32[8,128]{1,0:T(8,128)S(1)} %get-tuple-element.147.refs, ...), custom_call_target="tpu_custom_call" | custom-call | flops 1000000000 | tf_op jit(solution)/shard_map/project/pallas_call | solution.py:691
  21.7 6.7 %collective-permute-done.refs_1_ = bf16[224,768]{1,0:T(8,128)(2,1)S(1)} collective-permute-done((bf16[224,768]{1,0:T(8,128)(2,1)S(1)}, bf16[224,768]{1,0:T(8,128)(2,1)S(1)}, u32[]{:S(2)}, u32[]{:S(2)}) %collective-permute-start) | collective-permute-done | bytes 344096 | tf_op jit(solution)/shard_map/ppermute | solution.py:817
  28.6 1.2 collective-permute-start.3
  29.8 1.2 collective-permute-start.2
  31.5 8.6 %attend.1 = (bf16[384,768]{1,0:T(8,128)(2,1)S(1)}, bf16[384,192]{1,0:T(8,128)(2,1)S(1)}, f32[384,128]{1,0:T(8,128)S(1)}, f32[8,128]{1,0:T(8,128)S(1)}) custom-call(s32[26]{0:T(128)S(1)} %concatenate.12.refs_1_.refs_0_.refs_2_.refs_3_, bf16[384,768]{1,0:T(8,128)(2,1)S(1)} %get-tuple-element.149.refs_1_.refs_2_, ...), custom_call_target="tpu_custom_call" | custom-call | flops 1800000000 | tf_op jit(solution)/shard_map/attend/pallas_call | solution.py:691
  40.2 3.2 %collective-permute-done.6.refs_5_ = bf16[224,768]{1,0:T(8,128)(2,1)S(1)} collective-permute-done((bf16[224,768]{1,0:T(8,128)(2,1)S(1)}, bf16[224,768]{1,0:T(8,128)(2,1)S(1)}, u32[]{:S(2)}, u32[]{:S(2)}) %collective-permute-start.6) | collective-permute-done | bytes 344096 | tf_op jit(solution)/shard_map/ppermute | solution.py:817
  45.1 1.2 collective-permute-start.8
  47.2 3.0 %first_norm.1 = (f32[384,768]{1,0:T(8,128)S(1)}, f32[384,192]{1,0:T(8,128)S(1)}, bf16[384,768]{1,0:T(8,128)(2,1)S(1)}, bf16[384,192]{1,0:T(8,128)(2,1)S(1)}, f32...) custom-call(s32[26]{0:T(128)S(1)} %concatenate.12.refs_1_.refs_0_.re, ...), custom_call_target="tpu_custom_call" | custom-call | flops 600000000 | tf_op jit(solution)/shard_map/first_norm/pallas_call | solution.py:691
  51.5 7.1 %collective-permute-start.10 = (bf16[224,768]{1,0:T(8,128)(2,1)S(1)}, bf16[224,768]{1,0:T(8,128)(2,1)S(1)}, u32[]{:S(2)}, u32[]{:S(2)}) collective-permute-start(bf16[224,768]{1,0:T(8,128)(2,1)S(1)} %get-tuple-element.173.refs_4_), channel_id=1, source_target_pairs={{0,4},{4,0},{8,12},{12,8},{16,20},{20,16},{24,28},{28,24},{1,5},{5... | collective-permute-start | bytes 1032200 | tf_op jit(solution)/shard_map/ppermute | solution.py:726
  59.2 3.2 %collective-permute-start.14 = (bf16[224,768]{1,0:T(8,128)(2,1)S(1)}, bf16[224,768]{1,0:T(8,128)(2,1)S(1)}, u32[]{:S(2)}, u32[]{:S(2)}) collective-permute-start(bf16[224,768]{1,0:T(8,128)(2,1)S(1)} %get-tuple-element.178.refs_4_), channel_id=1, source_target_pairs={{0,4},{4,0},{8,12},{12,8},{16,20},{20,16},{24,28},{28,24},{1,5},{5... | collective-permute-start | bytes 1032200 | tf_op jit(solution)/shard_map/ppermute | solution.py:726
  63.6 1.2 collective-permute-start.20
  65.6 1.1 collective-permute-start.19
  67.3 2.8 shard.2
  70.1 2.3 shard.3
  72.9 1.2 collective-permute-done.24.refs_40_
  74.2 11.4 %turn.1 = (bf16[384,768]{1,0:T(8,128)(2,1)}, bf16[384,768]{1,0:T(8,128)(2,1)S(1)}, bf16[4,384,768]{2,1,0:T(8,128)(2,1)S(1)}, f32[4,768]{1,0:T(4,128)S(1)}, f32[4...) custom-call(s32[26]{0:T(128)S(1)} %concatenate.12.refs_1_.refs_0_.re, ...), custom_call_target="tpu_custom_call" | custom-call | flops 2400000000 | tf_op jit(solution)/shard_map/turn/pallas_call | solution.py:691
  85.5 3.2 %ffn_send.1 = (bf16[4,448,768]{2,1,0:T(8,128)(2,1)S(1)}, bf16[4,384,768]{2,1,0:T(8,128)(2,1)S(1)}, f32[8,128]{1,0:T(8,128)S(1)}) custom-call(s32[26]{0:T(128)S(1)} %concatenate.12.refs_1_.refs_0_.refs_2_.refs_3_, bf16[384,768]{1,0:T(8,128)(2,1)S(1)} %get-tuple-element.185.refs_11_.refs_1_.refs_2_, ...), custom_call_target="tpu_custom_call" | custom-call | flops 800000000 | tf_op jit(solution)/shard_map/ffn_send/pallas_call | solution.py:691
  89.3 14.8 %attend_back.1 = (bf16[384,768]{1,0:T(8,128)(2,1)S(1)}, bf16[1792,768]{1,0:T(8,128)(2,1)S(1)}, bf16[1792,768]{1,0:T(8,128)(2,1)S(1)}, bf16[384,256]{1,0:T(8,128)...) custom-call(f32[8,128]{1,0:T(8,128)S(1)} %get-tuple-element.206.refs_0_, ...), custom_call_target="tpu_custom_call" | custom-call | flops 3000000000 | tf_op jit(solution)/shard_map/attend_back/pallas_call | solution.py:691
  104.1 3.6 %ffn_keep.1 = (bf16[2,4,112,768]{3,2,1,0:T(8,128)(2,1)S(1)}, bf16[2,4,96,768]{3,2,1,0:T(8,128)(2,1)S(1)}, bf16[2,4,112,768]{3,2,1,0:T(8,128)(2,1)S(1)}, bf16[2,4,96,768]{3,2,1,0:T(8,128)(2,1)S(1)}, f32[8,128]{1,0:T(8,128)S(1)}) custom-call(f32[8,128]{1,0:T(8,128)S(1)} %get-tuple-element.210.refs_0_, s32[26]{0:T(128)S(1)} %concatenate.12.refs_1_.refs_0_.refs_2_.refs_3_, ...), custom_call_target="tpu_custom_call" | custom-call | flops 800000000 | tf_op jit(solution)/shard_map/ffn_keep/pallas_call | solution.py:691
  107.7 3.3 %copied_send.1 = (bf16[4,448,768]{2,1,0:T(8,128)(2,1)S(1)}, bf16[512,768]{1,0:T(8,128)(2,1)S(1)}, f32[8,128]{1,0:T(8,128)S(1)}) custom-call(f32[8,128]{1,0:T(8,128)S(1)} %get-tuple-element.213.refs_0_, s32[26]{0:T(128)S(1)} %concatenate.12.refs_1_.refs_0_.refs_2_.refs_3_, bf16[1536,768]{1,0:T(8,128)(2,1)S(1)} %copy-done, ...), custom_call_target="tpu_custom_call" | custom-call | flops 800000000 | tf_op jit(solution)/shard_map/copied_send/pallas_call | solution.py:691
  111.7 2.8 %sides.1 = (bf16[480,768]{1,0:T(8,128)(2,1)S(1)}, bf16[480,768]{1,0:T(8,128)(2,1)S(1)}, f32[8,128]{1,0:T(8,128)S(1)}) custom-call(f32[8,128]{1,0:T(8,128)S(1)} %get-tuple-element.228.refs_0_, s32[26]{0:T(128)S(1)} %concatenate.12.refs_1_.refs_0_.refs_2_.refs_3_, bf16[768,2304]{1,0:T(8,128)(2,1)S(1)} %copy-done.2, ...), custom_call_target="tpu_custom_call" | custom-call | flops 600000000 | tf_op jit(solution)/shard_map/sides/pallas_call | solution.py:691
  114.5 3.6 %collective-permute-start.29 = (bf16[480,768]{1,0:T(8,128)(2,1)S(1)}, bf16[480,768]{1,0:T(8,128)(2,1)S(1)}, u32[]{:S(2)}, u32[]{:S(2)}) collective-permute-start(bf16[480,768]{1,0:T(8,128)(2,1)S(1)} %get-tuple-element.236), channel_id=1, source_target_pairs={{1,0},{2,1},{3,2},{5,4},{6,5},{7,6},{9,8},{10,9},{11,10},{13,12},{... | collective-permute-start | bytes 2211848 | tf_op jit(solution)/shard_map/ppermute | solution.py:938
  118.1 1.9 collective-permute-start.30
  120.6 2.9 %copied_keep.1 = (bf16[2,2,112,768]{3,2,1,0:T(8,128)(2,1)S(1)}, bf16[2,2,112,768]{3,2,1,0:T(8,128)(2,1)S(1)}, bf16[2,2,112,768]{3,2,1,0:T(8,128)(2,1)S(1)}, bf16...) custom-call(f32[8,128]{1,0:T(8,128)S(1)} %get-tuple-element.230.refs_0_, s32[26]{0:T(128)S(1)} %concatenate.12.refs_1_.refs_0_.refs_2_.refs_3_, ...), custom_call_target="tpu_custom_call" | custom-call | flops 600000000 | tf_op jit(solution)/shard_map/copied_keep/pallas_call | solution.py:691
  123.6 10.4 %collective-permute-done.29.refs_12_ = bf16[480,768]{1,0:T(8,128)(2,1)S(1)} collective-permute-done((bf16[480,768]{1,0:T(8,128)(2,1)S(1)}, bf16[480,768]{1,0:T(8,128)(2,1)S(1)}, u32[]{:S(2)}, u32[]{:S(2)}) %collective-permute-start.29) | collective-permute-done | bytes 737312 | tf_op jit(solution)/shard_map/ppermute | solution.py:938
  134.0 3.2 %collective-permute-done.30.refs_13_ = bf16[480,768]{1,0:T(8,128)(2,1)S(1)} collective-permute-done((bf16[480,768]{1,0:T(8,128)(2,1)S(1)}, bf16[480,768]{1,0:T(8,128)(2,1)S(1)}, u32[]{:S(2)}, u32[]{:S(2)}) %collective-permute-start.30) | collective-permute-done | bytes 737312 | tf_op jit(solution)/shard_map/ppermute | solution.py:939
  137.2 3.0 %own.1 = (bf16[480,768]{1,0:T(8,128)(2,1)S(1)}, f32[8,128]{1,0:T(8,128)}) custom-call(f32[8,128]{1,0:T(8,128)S(1)} %get-tuple-element.233.refs_0_, s32[26]{0:T(128)S(1)} %concatenate.12.refs_1_.refs_0_.refs_2_.refs_3_, bf16[768,2304]{1,0:T(8,128)(2,1)S(1)} %copy-done.2, bf16[192,768]{1,0:T(8,128)(2,1)S(1)} %get-tuple-element.229.refs_3_, ...), custom_call_target="tpu_custom_call" | custom-call | flops 600000000 | tf_op jit(solution)/shard_map/own/pallas_call | solution.py:691
  140.1 1.9 collective-permute-start.32
  142.1 3.4 %collective-permute-start.31 = (bf16[480,768]{1,0:T(8,128)(2,1)S(1)}, bf16[480,768]{1,0:T(8,128)(2,1)S(1)}, u32[]{:S(2)}, u32[]{:S(2)}) collective-permute-start(bf16[480,768]{1,0:T(8,128)(2,1)S(1)} %get-tuple-element.238.refs_2_), channel_id=1, source_target_pairs={{0,1},{1,2},{2,3},{4,5},{5,6},{6,7},{8,9},{9,10},{10,11},{12,13},{... | collective-permute-start | bytes 2211848 | tf_op jit(solution)/shard_map/ppermute | solution.py:953
  147.7 3.1 %collective-permute-done.34 = bf16[2,4,112,768]{3,2,1,0:T(8,128)(2,1)S(1)} collective-permute-done((bf16[2,4,112,768]{3,2,1,0:T(8,128)(2,1)S(1)}, bf16[2,4,112,768]{3,2,1,0:T(8,128)(2,1)S(1)}, u32[]{:S(2)}, u32[]{:S(2)}) %collective-permute-start.34) | collective-permute-done | bytes 1376288 | tf_op jit(solution)/shard_map/ppermute | solution.py:726
  152.0 6.3 %collective-permute-done.32.refs_1_.refs_6_ = bf16[480,768]{1,0:T(8,128)(2,1)S(1)} collective-permute-done((bf16[480,768]{1,0:T(8,128)(2,1)S(1)}, bf16[480,768]{1,0:T(8,128)(2,1)S(1)}, u32[]{:S(2)}, u32[]{:S(2)}) %collective-permute-start.32) | collective-permute-done | bytes 737312 | tf_op jit(solution)/shard_map/ppermute | solution.py:954
  158.3 2.2 collective-permute-start.43
  160.5 5.0 %collective-permute-start.42 = (bf16[480,768]{1,0:T(8,128)(2,1)S(1)}, bf16[480,768]{1,0:T(8,128)(2,1)}, u32[]{:S(2)}, u32[]{:S(2)}) collective-permute-start(bf16[480,768]{1,0:T(8,128)(2,1)S(1)} %collective-permute-done.31.refs_0_.refs_3_), channel_id=1, source_target_pairs={{1,2},{2,3},{5,6},{6,7},{9,10},{10,11},{13,14},{14,15},{17,18},{18... | collective-permute-start | bytes 2211848 | tf_op jit(solution)/shard_map/ppermute | solution.py:953
  167.5 4.9 %collective-permute-done.35.refs_4_ = bf16[2,112,768]{2,1,0:T(8,128)(2,1)S(1)} collective-permute-done((bf16[2,112,768]{2,1,0:T(8,128)(2,1)S(1)}, bf16[2,112,768]{2,1,0:T(8,128)(2,1)S(1)}, u32[]{:S(2)}, u32[]{:S(2)}) %collective-permute-start.35) | collective-permute-done | bytes 344096 | tf_op jit(solution)/shard_map/ppermute | solution.py:726
  173.3 1.1 copied_spread.1
  174.5 2.3 collective-permute-start.39
  176.8 1.9 collective-permute-start.40
  178.7 1.2 slice.121
  180.5 1.2 slice.120
  185.0 3.3 %collective-permute-done.39 = bf16[112,768]{1,0:T(8,128)(2,1)S(1)} collective-permute-done((bf16[112,768]{1,0:T(8,128)(2,1)S(1)}, bf16[112,768]{1,0:T(8,128)(2,1)S(1)}, u32[]{:S(2)}, u32[]{:S(2)}) %collective-permute-start.39) | collective-permute-done | bytes 172064 | tf_op jit(solution)/shard_map/ppermute | solution.py:959
  188.3 3.8 %collective-permute-done.40 = bf16[112,768]{1,0:T(8,128)(2,1)S(1)} collective-permute-done((bf16[112,768]{1,0:T(8,128)(2,1)S(1)}, bf16[112,768]{1,0:T(8,128)(2,1)S(1)}, u32[]{:S(2)}, u32[]{:S(2)}) %collective-permute-start.40) | collective-permute-done | bytes 172064 | tf_op jit(solution)/shard_map/ppermute | solution.py:959
  193.0 2.2 collective-permute-start.45
  195.2 1.4 collective-permute-start.44
  197.5 5.9 %collective-permute-done.45.refs_1_ = bf16[112,768]{1,0:T(8,128)(2,1)S(1)} collective-permute-done((bf16[112,768]{1,0:T(8,128)(2,1)S(1)}, bf16[112,768]{1,0:T(8,128)(2,1)S(1)}, u32[]{:S(2)}, u32[]{:S(2)}) %collective-permute-start.45) | collective-permute-done | bytes 172064 | tf_op jit(solution)/shard_map/ppermute | solution.py:817
  203.7 1.9 ffn_spread.1
  205.8 5.5 %collective-permute-start.48 = (bf16[4,112,768]{2,1,0:T(8,128)(2,1)S(1)}, bf16[4,112,768]{2,1,0:T(8,128)(2,1)S(1)}, u32[]{:S(2)}, u32[]{:S(2)}) collective-permute-start(bf16[4,112,768]{2,1,0:T(8,128)(2,1)S(1)} %pad_maximum_fusion.refs_1_), channel_id=1, source_target_pairs={{0,16},{4,20},{8,24},{12,28},{16,0},{20,4},{24,8},{28,12},{1,17},{... | collective-permute-start | bytes 2064392 | tf_op jit(solution)/shard_map/ppermute | solution.py:726
  211.9 5.1 %collective-permute-start.51 = (bf16[4,112,768]{2,1,0:T(8,128)(2,1)S(1)}, bf16[4,112,768]{2,1,0:T(8,128)(2,1)S(1)}, u32[]{:S(2)}, u32[]{:S(2)}) collective-permute-start(bf16[4,112,768]{2,1,0:T(8,128)(2,1)S(1)} %pad_maximum_fusion.refs_1_), channel_id=1, source_target_pairs={{0,4},{4,0},{8,12},{12,8},{16,20},{20,16},{24,28},{28,24},{1,5},{5... | collective-permute-start | bytes 2064392 | tf_op jit(solution)/shard_map/ppermute | solution.py:726
  217.0 4.6 %collective-permute-done.48.refs_3_ = bf16[4,112,768]{2,1,0:T(8,128)(2,1)S(1)} collective-permute-done((bf16[4,112,768]{2,1,0:T(8,128)(2,1)S(1)}, bf16[4,112,768]{2,1,0:T(8,128)(2,1)S(1)}, u32[]{:S(2)}, u32[]{:S(2)}) %collective-permute-start.48) | collective-permute-done | bytes 688160 | tf_op jit(solution)/shard_map/ppermute | solution.py:726
  222.3 1.2 collective-permute-done.47.refs_2_
  223.5 1.1 collective-permute-start.49
  224.6 8.4 %collective-permute-start.53 = (bf16[4,112,768]{2,1,0:T(8,128)(2,1)S(1)}, bf16[4,112,768]{2,1,0:T(8,128)(2,1)S(1)}, u32[]{:S(2)}, u32[]{:S(2)}) collective-permute-start(bf16[4,112,768]{2,1,0:T(8,128)(2,1)S(1)} %collective-permute-done.48.refs_3_), channel_id=1, source_target_pairs={{0,4},{4,0},{8,12},{12,8},{16,20},{20,16},{24,28},{28,24},{1,5},{5... | collective-permute-start | bytes 2064392 | tf_op jit(solution)/shard_map/ppermute | solution.py:726
  233.1 3.4 %collective-permute-start.55 = (bf16[2,112,768]{2,1,0:T(8,128)(2,1)S(1)}, bf16[2,112,768]{2,1,0:T(8,128)(2,1)S(1)}, u32[]{:S(2)}, u32[]{:S(2)}) collective-permute-start(bf16[2,112,768]{2,1,0:T(8,128)(2,1)S(1)} %collective-permute-done.50.refs_5_), channel_id=1, source_target_pairs={{0,4},{4,0},{8,12},{12,8},{16,20},{20,16},{24,28},{28,24},{1,5},{5... | collective-permute-start | bytes 1032200 | tf_op jit(solution)/shard_map/ppermute | solution.py:726
  236.5 3.7 %collective-permute-start.54 = (bf16[2,112,768]{2,1,0:T(8,128)(2,1)S(1)}, bf16[2,112,768]{2,1,0:T(8,128)(2,1)S(1)}, u32[]{:S(2)}, u32[]{:S(2)}) collective-permute-start(bf16[2,112,768]{2,1,0:T(8,128)(2,1)S(1)} %collective-permute-done.49.refs_4_), channel_id=1, source_target_pairs={{0,4},{4,0},{8,12},{12,8},{16,20},{20,16},{24,28},{28,24},{1,5},{5... | collective-permute-start | bytes 1032200 | tf_op jit(solution)/shard_map/ppermute | solution.py:726
  240.2 2.2 collective-permute-start.57
  242.4 1.5 collective-permute-start.56
  243.9 6.0 %copied_final.1 = (f32[768,2304]{1,0:T(8,128)}, f32[768,768]{1,0:T(8,128)}, f32[192,576]{1,0:T(8,128)}, f32[192,192]{1,0:T(8,128)}, f32[4,768]{1,0:T(4,128)}, /*...) custom-call(s32[26]{0:T(128)S(1)} %concatenate.12.refs_1_.refs_0_.re, ...), custom_call_target="tpu_custom_call" | custom-call | flops 1200000000 | tf_op jit(solution)/shard_map/copied_final/pallas_call | solution.py:691
  252.9 8.5 %collective-permute-done.60.refs_2_ = bf16[208,768]{1,0:T(8,128)(2,1)S(1)} collective-permute-done((bf16[208,768]{1,0:T(8,128)(2,1)S(1)}, bf16[208,768]{1,0:T(8,128)(2,1)S(1)}, u32[]{:S(2)}, u32[]{:S(2)}) %collective-permute-start.60) | collective-permute-done | bytes 319520 | tf_op jit(solution)/shard_map/ppermute | solution.py:726
  261.4 1.2 collective-permute-start.64
  264.0 4.8 %input_final.1 = (f32[1536,768]{1,0:T(8,128)}, f32[192,1536]{1,0:T(8,128)}, f32[8,128]{1,0:T(8,128)S(1)}) custom-call(f32[8,128]{1,0:T(8,128)S(1)} %get-tuple-element.249.refs_0_, s32[26]{0:T(128)S(1)} %concatenate.12.refs_1_.refs_0_.refs_2_.refs_3_, bf16[480,768]{1,0:T(8,128)(2,1)S(1)} %get-tuple-element.238.refs_2_, ...), custom_call_target="tpu_custom_call" | custom-call | flops 800000000 | tf_op jit(solution)/shard_map/input_final/pallas_call | solution.py:691
  270.7 3.6 %ffn_final.1 = (f32[768,768]{1,0:T(8,128)}, f32[768,768]{1,0:T(8,128)}, f32[192,192]{1,0:T(8,128)}, f32[192,192]{1,0:T(8,128)}, f32[8,128]{1,0:T(8,128)}) custom-call(s32[26]{0:T(128)S(1)} %concatenate.12.refs_1_.refs_0_.refs_2_.refs_3_, bf16[208,768]{1,0:T(8,128)(2,1)S(1)} %fusion.8.refs_1_, bf16[208,768]{1,0:T(8,128)(2,1)S(1)} %collective-permute-done.60.refs_2_, ...), custom_call_target="tpu_custom_call" | custom-call | flops 600000000 | tf_op jit(solution)/shard_map/ffn_final/pallas_call | solution.py:691
  (179 shorter events, 31.2 us)
Async XLA Ops:
  7.2 243.9 %reduce-scatter.2.cloned.1.call-start = ((), (), s32[]{:S(2)}) async-start(), calls=%async_computation.1 | async-start | bytes 1597440 | tf_op jit(solution)/shard_map/reduce_scatter | solution.py:978
  10.1 11.6 %collective-permute-start.1 = (bf16[224,768]{1,0:T(8,128)(2,1)S(1)}, bf16[224,768]{1,0:T(8,128)(2,1)S(1)}, u32[]{:S(2)}, u32[]{:S(2)}) collective-permute-start(bf16[224,768]{1,0:T(8,128)(2,1)S(1)} %get-tuple-element.157.refs_14_.refs_27_), channel_id=1, source_target_pairs={{0,1},{1,2},{2,3},{3,0},{4,5},{5,6},{6,7},{7,4},{8,9},{9,10},{10,1... | collective-permute-start | bytes 1032200 | tf_op jit(solution)/shard_map/ppermute | solution.py:817
  11.5 16.9 %collective-permute-start = (bf16[224,768]{1,0:T(8,128)(2,1)S(1)}, bf16[224,768]{1,0:T(8,128)(2,1)S(1)}, u32[]{:S(2)}, u32[]{:S(2)}) collective-permute-start(bf16[224,768]{1,0:T(8,128)(2,1)S(1)} %get-tuple-element.157.refs_14_.refs_27_), channel_id=1, source_target_pairs={{0,3},{1,0},{2,1},{3,2},{4,7},{5,4},{6,5},{7,6},{8,11},{9,8},{10,9... | collective-permute-start | bytes 1032200 | tf_op jit(solution)/shard_map/ppermute | solution.py:817
  28.4 15.0 %collective-permute-start.6 = (bf16[224,768]{1,0:T(8,128)(2,1)S(1)}, bf16[224,768]{1,0:T(8,128)(2,1)S(1)}, u32[]{:S(2)}, u32[]{:S(2)}) collective-permute-start(bf16[224,768]{1,0:T(8,128)(2,1)S(1)} %get-tuple-element.163), channel_id=1, source_target_pairs={{0,2},{1,3},{2,0},{3,1},{4,6},{5,7},{6,4},{7,5},{8,10},{9,11},{10,... | collective-permute-start | bytes 1032200 | tf_op jit(solution)/shard_map/ppermute | solution.py:817
  28.6 14.8 %collective-permute-start.3 = (bf16[224,768]{1,0:T(8,128)(2,1)S(1)}, bf16[224,768]{1,0:T(8,128)(2,1)S(1)}, u32[]{:S(2)}, u32[]{:S(2)}) collective-permute-start(bf16[224,768]{1,0:T(8,128)(2,1)S(1)} %get-tuple-element.161.refs_4_), channel_id=1, source_target_pairs={{0,16},{4,20},{8,24},{12,28},{16,0},{20,4},{24,8},{28,12},{1,17},{... | collective-permute-start | bytes 1032200 | tf_op jit(solution)/shard_map/ppermute | solution.py:726
  29.8 13.6 %collective-permute-start.2 = (bf16[224,768]{1,0:T(8,128)(2,1)S(1)}, bf16[224,768]{1,0:T(8,128)(2,1)S(1)}, u32[]{:S(2)}, u32[]{:S(2)}) collective-permute-start(bf16[224,768]{1,0:T(8,128)(2,1)S(1)} %get-tuple-element.161.refs_4_), channel_id=1, source_target_pairs={{0,8},{4,12},{8,0},{12,4},{16,24},{20,28},{24,16},{28,20},{1,9},{5... | collective-permute-start | bytes 1032200 | tf_op jit(solution)/shard_map/ppermute | solution.py:726
  31.0 12.5 %collective-permute-start.5 = (bf16[224,768]{1,0:T(8,128)(2,1)S(1)}, bf16[224,768]{1,0:T(8,128)(2,1)S(1)}, u32[]{:S(2)}, u32[]{:S(2)}) collective-permute-start(bf16[224,768]{1,0:T(8,128)(2,1)S(1)} %get-tuple-element.162.refs_6_), channel_id=1, source_target_pairs={{0,16},{4,20},{8,24},{12,28},{16,0},{20,4},{24,8},{28,12},{1,17},{... | collective-permute-start | bytes 1032200 | tf_op jit(solution)/shard_map/ppermute | solution.py:726
  31.3 13.2 %collective-permute-start.4 = (bf16[224,768]{1,0:T(8,128)(2,1)S(1)}, bf16[224,768]{1,0:T(8,128)(2,1)S(1)}, u32[]{:S(2)}, u32[]{:S(2)}) collective-permute-start(bf16[224,768]{1,0:T(8,128)(2,1)S(1)} %get-tuple-element.162.refs_6_), channel_id=1, source_target_pairs={{0,8},{4,12},{8,0},{12,4},{16,24},{20,28},{24,16},{28,20},{1,9},{5... | collective-permute-start | bytes 1032200 | tf_op jit(solution)/shard_map/ppermute | solution.py:726
  44.5 6.1 %collective-permute-start.7 = (bf16[224,768]{1,0:T(8,128)(2,1)S(1)}, bf16[224,768]{1,0:T(8,128)(2,1)S(1)}, u32[]{:S(2)}, u32[]{:S(2)}) collective-permute-start(bf16[224,768]{1,0:T(8,128)(2,1)S(1)} %get-tuple-element.165.refs_4_), channel_id=1, source_target_pairs={{0,16},{4,20},{8,24},{12,28},{16,0},{20,4},{24,8},{28,12},{1,17},{... | collective-permute-start | bytes 1032200 | tf_op jit(solution)/shard_map/ppermute | solution.py:726
  45.1 6.4 %collective-permute-start.8 = (bf16[224,768]{1,0:T(8,128)(2,1)S(1)}, bf16[224,768]{1,0:T(8,128)(2,1)S(1)}, u32[]{:S(2)}, u32[]{:S(2)}) collective-permute-start(bf16[224,768]{1,0:T(8,128)(2,1)S(1)} %get-tuple-element.166.refs_7_), channel_id=1, source_target_pairs={{0,8},{4,12},{8,0},{12,4},{16,24},{20,28},{24,16},{28,20},{1,9},{5... | collective-permute-start | bytes 1032200 | tf_op jit(solution)/shard_map/ppermute | solution.py:726
  46.3 12.9 %collective-permute-start.18 = (bf16[224,768]{1,0:T(8,128)(2,1)S(1)}, bf16[224,768]{1,0:T(8,128)(2,1)S(1)}, u32[]{:S(2)}, u32[]{:S(2)}) collective-permute-start(bf16[224,768]{1,0:T(8,128)(2,1)S(1)} %get-tuple-element.196.refs_32_), channel_id=1, source_target_pairs={{0,16},{4,20},{8,24},{12,28},{16,0},{20,4},{24,8},{28,12},{1,17},{... | collective-permute-start | bytes 1032200 | tf_op jit(solution)/shard_map/ppermute | solution.py:726
  50.2 12.2 %collective-permute-start.17 = (bf16[224,768]{1,0:T(8,128)(2,1)S(1)}, bf16[224,768]{1,0:T(8,128)(2,1)S(1)}, u32[]{:S(2)}, u32[]{:S(2)}) collective-permute-start(bf16[224,768]{1,0:T(8,128)(2,1)S(1)} %get-tuple-element.196.refs_32_), channel_id=1, source_target_pairs={{0,8},{4,12},{8,0},{12,4},{16,24},{20,28},{24,16},{28,20},{1,9},{5... | collective-permute-start | bytes 1032200 | tf_op jit(solution)/shard_map/ppermute | solution.py:726
  51.5 11.4 %collective-permute-start.10 = (bf16[224,768]{1,0:T(8,128)(2,1)S(1)}, bf16[224,768]{1,0:T(8,128)(2,1)S(1)}, u32[]{:S(2)}, u32[]{:S(2)}) collective-permute-start(bf16[224,768]{1,0:T(8,128)(2,1)S(1)} %get-tuple-element.173.refs_4_), channel_id=1, source_target_pairs={{0,4},{4,0},{8,12},{12,8},{16,20},{20,16},{24,28},{28,24},{1,5},{5... | collective-permute-start | bytes 1032200 | tf_op jit(solution)/shard_map/ppermute | solution.py:726
  58.6 4.3 %collective-permute-start.11 = (bf16[224,768]{1,0:T(8,128)(2,1)S(1)}, bf16[224,768]{1,0:T(8,128)(2,1)S(1)}, u32[]{:S(2)}, u32[]{:S(2)}) collective-permute-start(bf16[224,768]{1,0:T(8,128)(2,1)S(1)} %get-tuple-element.174.refs_5_), channel_id=1, source_target_pairs={{0,4},{4,0},{8,12},{12,8},{16,20},{20,16},{24,28},{28,24},{1,5},{5... | collective-permute-start | bytes 1032200 | tf_op jit(solution)/shard_map/ppermute | solution.py:726
  58.7 4.7 %collective-permute-start.12 = (bf16[224,768]{1,0:T(8,128)(2,1)S(1)}, bf16[224,768]{1,0:T(8,128)(2,1)S(1)}, u32[]{:S(2)}, u32[]{:S(2)}) collective-permute-start(bf16[224,768]{1,0:T(8,128)(2,1)S(1)} %get-tuple-element.175.refs_6_), channel_id=1, source_target_pairs={{0,4},{4,0},{8,12},{12,8},{16,20},{20,16},{24,28},{28,24},{1,5},{5... | collective-permute-start | bytes 1032200 | tf_op jit(solution)/shard_map/ppermute | solution.py:726
  59.2 4.4 %collective-permute-start.14 = (bf16[224,768]{1,0:T(8,128)(2,1)S(1)}, bf16[224,768]{1,0:T(8,128)(2,1)S(1)}, u32[]{:S(2)}, u32[]{:S(2)}) collective-permute-start(bf16[224,768]{1,0:T(8,128)(2,1)S(1)} %get-tuple-element.178.refs_4_), channel_id=1, source_target_pairs={{0,4},{4,0},{8,12},{12,8},{16,20},{20,16},{24,28},{28,24},{1,5},{5... | collective-permute-start | bytes 1032200 | tf_op jit(solution)/shard_map/ppermute | solution.py:726
  62.9 3.8 %collective-permute-start.9 = (bf16[224,768]{1,0:T(8,128)(2,1)S(1)}, bf16[224,768]{1,0:T(8,128)(2,1)S(1)}, u32[]{:S(2)}, u32[]{:S(2)}) collective-permute-start(bf16[224,768]{1,0:T(8,128)(2,1)S(1)} %get-tuple-element.172.refs_3_.refs_28_), channel_id=1, source_target_pairs={{0,4},{4,0},{8,12},{12,8},{16,20},{20,16},{24,28},{28,24},{1,5},{5... | collective-permute-start | bytes 1032200 | tf_op jit(solution)/shard_map/ppermute | solution.py:726
  63.4 3.7 %collective-permute-start.13 = (bf16[224,768]{1,0:T(8,128)(2,1)S(1)}, bf16[224,768]{1,0:T(8,128)(2,1)S(1)}, u32[]{:S(2)}, u32[]{:S(2)}) collective-permute-start(bf16[224,768]{1,0:T(8,128)(2,1)S(1)} %get-tuple-element.177.refs_3_.refs_29_), channel_id=1, source_target_pairs={{0,4},{4,0},{8,12},{12,8},{16,20},{20,16},{24,28},{28,24},{1,5},{5... | collective-permute-start | bytes 1032200 | tf_op jit(solution)/shard_map/ppermute | solution.py:726
  63.6 8.7 %collective-permute-start.20 = (bf16[128,768]{1,0:T(8,128)(2,1)S(1)}, bf16[128,768]{1,0:T(8,128)(2,1)S(1)}, u32[]{:S(2)}, u32[]{:S(2)}) collective-permute-start(bf16[128,768]{1,0:T(8,128)(2,1)S(1)} %slice.113), channel_id=1, source_target_pairs={{0,8},{4,12},{8,0},{12,4},{16,24},{20,28},{24,16},{28,20},{1,9},{5... | collective-permute-start | bytes 589832 | tf_op jit(solution)/shard_map/ppermute | solution.py:726
  64.8 8.1 %collective-permute-start.21 = (bf16[224,768]{1,0:T(8,128)(2,1)S(1)}, bf16[224,768]{1,0:T(8,128)(2,1)S(1)}, u32[]{:S(2)}, u32[]{:S(2)}) collective-permute-start(bf16[224,768]{1,0:T(8,128)(2,1)S(1)} %get-tuple-element.196.refs_32_), channel_id=1, source_target_pairs={{0,4},{4,0},{8,12},{12,8},{16,20},{20,16},{24,28},{28,24},{1,5},{5... | collective-permute-start | bytes 1032200 | tf_op jit(solution)/shard_map/ppermute | solution.py:726
  65.6 6.7 %collective-permute-start.19 = (bf16[96,768]{1,0:T(8,128)(2,1)S(1)}, bf16[96,768]{1,0:T(8,128)(2,1)S(1)}, u32[]{:S(2)}, u32[]{:S(2)}) collective-permute-start(bf16[96,768]{1,0:T(8,128)(2,1)S(1)} %slice.112), channel_id=1, source_target_pairs={{0,16},{4,20},{8,24},{12,28},{16,0},{20,4},{24,8},{28,12},{1,17},{... | collective-permute-start | bytes 442376 | tf_op jit(solution)/shard_map/ppermute | solution.py:726
  66.8 6.2 %collective-permute-start.23 = (bf16[224,768]{1,0:T(8,128)(2,1)S(1)}, bf16[224,768]{1,0:T(8,128)(2,1)S(1)}, u32[]{:S(2)}, u32[]{:S(2)}) collective-permute-start(bf16[224,768]{1,0:T(8,128)(2,1)S(1)} %collective-permute-done.18.refs_34_), channel_id=1, source_target_pairs={{0,4},{4,0},{8,12},{12,8},{16,20},{20,16},{24,28},{28,24},{1,5},{5... | collective-permute-start | bytes 1032200 | tf_op jit(solution)/shard_map/ppermute | solution.py:726
  67.1 5.8 %collective-permute-start.22 = (bf16[224,768]{1,0:T(8,128)(2,1)S(1)}, bf16[224,768]{1,0:T(8,128)(2,1)S(1)}, u32[]{:S(2)}, u32[]{:S(2)}) collective-permute-start(bf16[224,768]{1,0:T(8,128)(2,1)S(1)} %collective-permute-done.17.refs_33_), channel_id=1, source_target_pairs={{0,4},{4,0},{8,12},{12,8},{16,20},{20,16},{24,28},{28,24},{1,5},{5... | collective-permute-start | bytes 1032200 | tf_op jit(solution)/shard_map/ppermute | solution.py:726
  88.7 15.4 %collective-permute-start.26 = (bf16[4,448,768]{2,1,0:T(8,128)(2,1)S(1)}, bf16[4,448,768]{2,1,0:T(8,128)(2,1)S(1)}, u32[]{:S(2)}, u32[]{:S(2)}) collective-permute-start(bf16[4,448,768]{2,1,0:T(8,128)(2,1)S(1)} %get-tuple-element.211), channel_id=1, source_target_pairs={{0,4},{4,0},{8,12},{12,8},{16,20},{20,16},{24,28},{28,24},{1,5},{5... | collective-permute-start | bytes 8257544 | tf_op jit(solution)/shard_map/ppermute | solution.py:726
  89.1 15.0 %collective-permute-start.27 = (bf16[4,384,768]{2,1,0:T(8,128)(2,1)S(1)}, bf16[4,384,768]{2,1,0:T(8,128)(2,1)S(1)}, u32[]{:S(2)}, u32[]{:S(2)}) collective-permute-start(bf16[4,384,768]{2,1,0:T(8,128)(2,1)S(1)} %get-tuple-element.212), channel_id=1, source_target_pairs={{0,4},{4,0},{8,12},{12,8},{16,20},{20,16},{24,28},{28,24},{1,5},{5... | collective-permute-start | bytes 7077896 | tf_op jit(solution)/shard_map/ppermute | solution.py:726
  111.0 9.6 %collective-permute-start.28 = (bf16[4,448,768]{2,1,0:T(8,128)(2,1)S(1)}, bf16[4,448,768]{2,1,0:T(8,128)(2,1)S(1)}, u32[]{:S(2)}, u32[]{:S(2)}) collective-permute-start(bf16[4,448,768]{2,1,0:T(8,128)(2,1)S(1)} %get-tuple-element.232), channel_id=1, source_target_pairs={{0,4},{4,0},{8,12},{12,8},{16,20},{20,16},{24,28},{28,24},{1,5},{5... | collective-permute-start | bytes 8257544 | tf_op jit(solution)/shard_map/ppermute | solution.py:726
  111.3 34.7 %collective-permute-start.37 = (bf16[2,4,96,768]{3,2,1,0:T(8,128)(2,1)S(1)}, bf16[2,4,96,768]{3,2,1,0:T(8,128)(2,1)S(1)}, u32[]{:S(2)}, u32[]{:S(2)}) collective-permute-start(bf16[2,4,96,768]{3,2,1,0:T(8,128)(2,1)S(1)} %get-tuple-element.244), channel_id=1, source_target_pairs={{0,16},{4,20},{8,24},{12,28},{16,0},{20,4},{24,8},{28,12},{1,17},{... | collective-permute-start | bytes 3538952 | tf_op jit(solution)/shard_map/ppermute | solution.py:726
  114.5 19.5 %collective-permute-start.29 = (bf16[480,768]{1,0:T(8,128)(2,1)S(1)}, bf16[480,768]{1,0:T(8,128)(2,1)S(1)}, u32[]{:S(2)}, u32[]{:S(2)}) collective-permute-start(bf16[480,768]{1,0:T(8,128)(2,1)S(1)} %get-tuple-element.236), channel_id=1, source_target_pairs={{1,0},{2,1},{3,2},{5,4},{6,5},{7,6},{9,8},{10,9},{11,10},{13,12},{... | collective-permute-start | bytes 2211848 | tf_op jit(solution)/shard_map/ppermute | solution.py:938
  118.1 19.1 %collective-permute-start.30 = (bf16[480,768]{1,0:T(8,128)(2,1)S(1)}, bf16[480,768]{1,0:T(8,128)(2,1)S(1)}, u32[]{:S(2)}, u32[]{:S(2)}) collective-permute-start(bf16[480,768]{1,0:T(8,128)(2,1)S(1)} %get-tuple-element.237), channel_id=1, source_target_pairs={{0,1},{1,2},{2,3},{4,5},{5,6},{6,7},{8,9},{9,10},{10,11},{12,13},{... | collective-permute-start | bytes 2211848 | tf_op jit(solution)/shard_map/ppermute | solution.py:939
  120.0 30.9 %collective-permute-start.34 = (bf16[2,4,112,768]{3,2,1,0:T(8,128)(2,1)S(1)}, bf16[2,4,112,768]{3,2,1,0:T(8,128)(2,1)S(1)}, u32[]{:S(2)}, u32[]{:S(2)}) collective-permute-start(bf16[2,4,112,768]{3,2,1,0:T(8,128)(2,1)S(1)} %get-tuple-element.241), channel_id=1, source_target_pairs={{0,8},{4,12},{8,0},{12,4},{16,24},{20,28},{24,16},{28,20},{1,9},{5... | collective-permute-start | bytes 4128776 | tf_op jit(solution)/shard_map/ppermute | solution.py:726
  140.1 18.1 %collective-permute-start.32 = (bf16[480,768]{1,0:T(8,128)(2,1)S(1)}, bf16[480,768]{1,0:T(8,128)(2,1)S(1)}, u32[]{:S(2)}, u32[]{:S(2)}) collective-permute-start(bf16[480,768]{1,0:T(8,128)(2,1)S(1)} %get-tuple-element.238.refs_2_), channel_id=1, source_target_pairs={{3,2},{2,1},{1,0},{7,6},{6,5},{5,4},{11,10},{10,9},{9,8},{15,14},{... | collective-permute-start | bytes 2211848 | tf_op jit(solution)/shard_map/ppermute | solution.py:954
  142.1 18.4 %collective-permute-start.31 = (bf16[480,768]{1,0:T(8,128)(2,1)S(1)}, bf16[480,768]{1,0:T(8,128)(2,1)S(1)}, u32[]{:S(2)}, u32[]{:S(2)}) collective-permute-start(bf16[480,768]{1,0:T(8,128)(2,1)S(1)} %get-tuple-element.238.refs_2_), channel_id=1, source_target_pairs={{0,1},{1,2},{2,3},{4,5},{5,6},{6,7},{8,9},{9,10},{10,11},{12,13},{... | collective-permute-start | bytes 2211848 | tf_op jit(solution)/shard_map/ppermute | solution.py:953
  145.4 20.2 %collective-permute-start.33 = (bf16[2,2,112,768]{3,2,1,0:T(8,128)(2,1)S(1)}, bf16[2,2,112,768]{3,2,1,0:T(8,128)(2,1)S(1)}, u32[]{:S(2)}, u32[]{:S(2)}) collective-permute-start(bf16[2,2,112,768]{3,2,1,0:T(8,128)(2,1)S(1)} %get-tuple-element.240), channel_id=1, source_target_pairs={{0,8},{4,12},{8,0},{12,4},{16,24},{20,28},{24,16},{28,20},{1,9},{5... | collective-permute-start | bytes 2064392 | tf_op jit(solution)/shard_map/ppermute | solution.py:726
  146.1 20.5 %collective-permute-start.36 = (bf16[2,2,112,768]{3,2,1,0:T(8,128)(2,1)S(1)}, bf16[2,2,112,768]{3,2,1,0:T(8,128)(2,1)S(1)}, u32[]{:S(2)}, u32[]{:S(2)}) collective-permute-start(bf16[2,2,112,768]{3,2,1,0:T(8,128)(2,1)S(1)} %get-tuple-element.243), channel_id=1, source_target_pairs={{0,16},{4,20},{8,24},{12,28},{16,0},{20,4},{24,8},{28,12},{1,17},{... | collective-permute-start | bytes 2064392 | tf_op jit(solution)/shard_map/ppermute | solution.py:726
  158.3 20.4 %collective-permute-start.43 = (bf16[480,768]{1,0:T(8,128)(2,1)S(1)}, bf16[480,768]{1,0:T(8,128)(2,1)}, u32[]{:S(2)}, u32[]{:S(2)}) collective-permute-start(bf16[480,768]{1,0:T(8,128)(2,1)S(1)} %collective-permute-done.32.refs_1_.refs_6_), channel_id=1, source_target_pairs={{2,1},{1,0},{6,5},{5,4},{10,9},{9,8},{14,13},{13,12},{18,17},{17,1... | collective-permute-start | bytes 2211848 | tf_op jit(solution)/shard_map/ppermute | solution.py:954
  160.5 20.1 %collective-permute-start.42 = (bf16[480,768]{1,0:T(8,128)(2,1)S(1)}, bf16[480,768]{1,0:T(8,128)(2,1)}, u32[]{:S(2)}, u32[]{:S(2)}) collective-permute-start(bf16[480,768]{1,0:T(8,128)(2,1)S(1)} %collective-permute-done.31.refs_0_.refs_3_), channel_id=1, source_target_pairs={{1,2},{2,3},{5,6},{6,7},{9,10},{10,11},{13,14},{14,15},{17,18},{18... | collective-permute-start | bytes 2211848 | tf_op jit(solution)/shard_map/ppermute | solution.py:953
  165.8 6.6 %collective-permute-start.35 = (bf16[2,112,768]{2,1,0:T(8,128)(2,1)S(1)}, bf16[2,112,768]{2,1,0:T(8,128)(2,1)S(1)}, u32[]{:S(2)}, u32[]{:S(2)}) collective-permute-start(bf16[2,112,768]{2,1,0:T(8,128)(2,1)S(1)} %get-tuple-element.282), channel_id=1, source_target_pairs={{0,16},{4,20},{8,24},{12,28},{16,0},{20,4},{24,8},{28,12},{1,17},{... | collective-permute-start | bytes 1032200 | tf_op jit(solution)/shard_map/ppermute | solution.py:726
  166.8 6.6 %collective-permute-start.38 = (bf16[2,112,768]{2,1,0:T(8,128)(2,1)S(1)}, bf16[2,112,768]{2,1,0:T(8,128)(2,1)S(1)}, u32[]{:S(2)}, u32[]{:S(2)}) collective-permute-start(bf16[2,112,768]{2,1,0:T(8,128)(2,1)S(1)} %get-tuple-element.280), channel_id=1, source_target_pairs={{0,8},{4,12},{8,0},{12,4},{16,24},{20,28},{24,16},{28,20},{1,9},{5... | collective-permute-start | bytes 1032200 | tf_op jit(solution)/shard_map/ppermute | solution.py:726
  174.5 13.8 %collective-permute-start.39 = (bf16[112,768]{1,0:T(8,128)(2,1)S(1)}, bf16[112,768]{1,0:T(8,128)(2,1)S(1)}, u32[]{:S(2)}, u32[]{:S(2)}) collective-permute-start(bf16[112,768]{1,0:T(8,128)(2,1)S(1)} %get-tuple-element.246), channel_id=1, source_target_pairs={{0,1},{1,2},{2,3},{3,0},{4,5},{5,6},{6,7},{7,4},{8,9},{9,10},{10,1... | collective-permute-start | bytes 516104 | tf_op jit(solution)/shard_map/ppermute | solution.py:959
  176.8 15.3 %collective-permute-start.40 = (bf16[112,768]{1,0:T(8,128)(2,1)S(1)}, bf16[112,768]{1,0:T(8,128)(2,1)S(1)}, u32[]{:S(2)}, u32[]{:S(2)}) collective-permute-start(bf16[112,768]{1,0:T(8,128)(2,1)S(1)} %get-tuple-element.247), channel_id=1, source_target_pairs={{0,2},{1,3},{2,0},{3,1},{4,6},{5,7},{6,4},{7,5},{8,10},{9,11},{10,... | collective-permute-start | bytes 516104 | tf_op jit(solution)/shard_map/ppermute | solution.py:959
  178.7 14.1 %collective-permute-start.41 = (bf16[112,768]{1,0:T(8,128)(2,1)S(1)}, bf16[112,768]{1,0:T(8,128)(2,1)S(1)}, u32[]{:S(2)}, u32[]{:S(2)}) collective-permute-start(bf16[112,768]{1,0:T(8,128)(2,1)S(1)} %get-tuple-element.248), channel_id=1, source_target_pairs={{0,3},{1,0},{2,1},{3,2},{4,7},{5,4},{6,5},{7,6},{8,11},{9,8},{10,9... | collective-permute-start | bytes 516104 | tf_op jit(solution)/shard_map/ppermute | solution.py:959
  182.9 20.9 %collective-permute-start.58 = (bf16[4,112,768]{2,1,0:T(8,128)(2,1)S(1)}, bf16[4,112,768]{2,1,0:T(8,128)(2,1)S(1)}, u32[]{:S(2)}, u32[]{:S(2)}) collective-permute-start(bf16[4,112,768]{2,1,0:T(8,128)(2,1)S(1)} %get-tuple-element.276), channel_id=1, source_target_pairs={{0,16},{4,20},{8,24},{12,28},{16,0},{20,4},{24,8},{28,12},{1,17},{... | collective-permute-start | bytes 2064392 | tf_op jit(solution)/shard_map/ppermute | solution.py:726
  184.4 19.4 %collective-permute-start.59 = (bf16[4,96,768]{2,1,0:T(8,128)(2,1)S(1)}, bf16[4,96,768]{2,1,0:T(8,128)(2,1)S(1)}, u32[]{:S(2)}, u32[]{:S(2)}) collective-permute-start(bf16[4,96,768]{2,1,0:T(8,128)(2,1)S(1)} %get-tuple-element.278), channel_id=1, source_target_pairs={{0,8},{4,12},{8,0},{12,4},{16,24},{20,28},{24,16},{28,20},{1,9},{5... | collective-permute-start | bytes 1769480 | tf_op jit(solution)/shard_map/ppermute | solution.py:726
  192.9 4.6 %collective-permute-start.46 = (bf16[112,768]{1,0:T(8,128)(2,1)S(1)}, bf16[112,768]{1,0:T(8,128)(2,1)S(1)}, u32[]{:S(2)}, u32[]{:S(2)}) collective-permute-start(bf16[112,768]{1,0:T(8,128)(2,1)S(1)} %add_convert_fusion.9), channel_id=1, source_target_pairs={{0,1},{1,2},{2,3},{3,0},{4,5},{5,6},{6,7},{7,4},{8,9},{9,10},{10,1... | collective-permute-start | bytes 516104 | tf_op jit(solution)/shard_map/ppermute | solution.py:817
  193.0 10.4 %collective-permute-start.45 = (bf16[112,768]{1,0:T(8,128)(2,1)S(1)}, bf16[112,768]{1,0:T(8,128)(2,1)S(1)}, u32[]{:S(2)}, u32[]{:S(2)}) collective-permute-start(bf16[112,768]{1,0:T(8,128)(2,1)S(1)} %add_convert_fusion.9), channel_id=1, source_target_pairs={{0,2},{1,3},{2,0},{3,1},{4,6},{5,7},{6,4},{7,5},{8,10},{9,11},{10,... | collective-permute-start | bytes 516104 | tf_op jit(solution)/shard_map/ppermute | solution.py:817
  195.2 8.5 %collective-permute-start.44 = (bf16[112,768]{1,0:T(8,128)(2,1)S(1)}, bf16[112,768]{1,0:T(8,128)(2,1)S(1)}, u32[]{:S(2)}, u32[]{:S(2)}) collective-permute-start(bf16[112,768]{1,0:T(8,128)(2,1)S(1)} %add_convert_fusion.9), channel_id=1, source_target_pairs={{0,3},{1,0},{2,1},{3,2},{4,7},{5,4},{6,5},{7,6},{8,11},{9,8},{10,9... | collective-permute-start | bytes 516104 | tf_op jit(solution)/shard_map/ppermute | solution.py:817
  205.8 15.8 %collective-permute-start.48 = (bf16[4,112,768]{2,1,0:T(8,128)(2,1)S(1)}, bf16[4,112,768]{2,1,0:T(8,128)(2,1)S(1)}, u32[]{:S(2)}, u32[]{:S(2)}) collective-permute-start(bf16[4,112,768]{2,1,0:T(8,128)(2,1)S(1)} %pad_maximum_fusion.refs_1_), channel_id=1, source_target_pairs={{0,16},{4,20},{8,24},{12,28},{16,0},{20,4},{24,8},{28,12},{1,17},{... | collective-permute-start | bytes 2064392 | tf_op jit(solution)/shard_map/ppermute | solution.py:726
  211.3 12.2 %collective-permute-start.47 = (bf16[4,112,768]{2,1,0:T(8,128)(2,1)S(1)}, bf16[4,112,768]{2,1,0:T(8,128)(2,1)S(1)}, u32[]{:S(2)}, u32[]{:S(2)}) collective-permute-start(bf16[4,112,768]{2,1,0:T(8,128)(2,1)S(1)} %pad_maximum_fusion.refs_1_), channel_id=1, source_target_pairs={{0,8},{4,12},{8,0},{12,4},{16,24},{20,28},{24,16},{28,20},{1,9},{5... | collective-permute-start | bytes 2064392 | tf_op jit(solution)/shard_map/ppermute | solution.py:726
  211.9 28.3 %collective-permute-start.51 = (bf16[4,112,768]{2,1,0:T(8,128)(2,1)S(1)}, bf16[4,112,768]{2,1,0:T(8,128)(2,1)S(1)}, u32[]{:S(2)}, u32[]{:S(2)}) collective-permute-start(bf16[4,112,768]{2,1,0:T(8,128)(2,1)S(1)} %pad_maximum_fusion.refs_1_), channel_id=1, source_target_pairs={{0,4},{4,0},{8,12},{12,8},{16,20},{20,16},{24,28},{28,24},{1,5},{5... | collective-permute-start | bytes 2064392 | tf_op jit(solution)/shard_map/ppermute | solution.py:726
  221.6 11.5 %collective-permute-start.50 = (bf16[2,112,768]{2,1,0:T(8,128)(2,1)S(1)}, bf16[2,112,768]{2,1,0:T(8,128)(2,1)S(1)}, u32[]{:S(2)}, u32[]{:S(2)}) collective-permute-start(bf16[2,112,768]{2,1,0:T(8,128)(2,1)S(1)} %slice.123), channel_id=1, source_target_pairs={{0,8},{4,12},{8,0},{12,4},{16,24},{20,28},{24,16},{28,20},{1,9},{5... | collective-permute-start | bytes 1032200 | tf_op jit(solution)/shard_map/ppermute | solution.py:726
  223.5 13.0 %collective-permute-start.49 = (bf16[2,112,768]{2,1,0:T(8,128)(2,1)S(1)}, bf16[2,112,768]{2,1,0:T(8,128)(2,1)S(1)}, u32[]{:S(2)}, u32[]{:S(2)}) collective-permute-start(bf16[2,112,768]{2,1,0:T(8,128)(2,1)S(1)} %slice.122), channel_id=1, source_target_pairs={{0,16},{4,20},{8,24},{12,28},{16,0},{20,4},{24,8},{28,12},{1,17},{... | collective-permute-start | bytes 1032200 | tf_op jit(solution)/shard_map/ppermute | solution.py:726
  224.6 19.3 %collective-permute-start.53 = (bf16[4,112,768]{2,1,0:T(8,128)(2,1)S(1)}, bf16[4,112,768]{2,1,0:T(8,128)(2,1)S(1)}, u32[]{:S(2)}, u32[]{:S(2)}) collective-permute-start(bf16[4,112,768]{2,1,0:T(8,128)(2,1)S(1)} %collective-permute-done.48.refs_3_), channel_id=1, source_target_pairs={{0,4},{4,0},{8,12},{12,8},{16,20},{20,16},{24,28},{28,24},{1,5},{5... | collective-permute-start | bytes 2064392 | tf_op jit(solution)/shard_map/ppermute | solution.py:726
  233.0 10.9 %collective-permute-start.52 = (bf16[4,112,768]{2,1,0:T(8,128)(2,1)S(1)}, bf16[4,112,768]{2,1,0:T(8,128)(2,1)S(1)}, u32[]{:S(2)}, u32[]{:S(2)}) collective-permute-start(bf16[4,112,768]{2,1,0:T(8,128)(2,1)S(1)} %collective-permute-done.47.refs_2_), channel_id=1, source_target_pairs={{0,4},{4,0},{8,12},{12,8},{16,20},{20,16},{24,28},{28,24},{1,5},{5... | collective-permute-start | bytes 2064392 | tf_op jit(solution)/shard_map/ppermute | solution.py:726
  233.1 9.3 %collective-permute-start.55 = (bf16[2,112,768]{2,1,0:T(8,128)(2,1)S(1)}, bf16[2,112,768]{2,1,0:T(8,128)(2,1)S(1)}, u32[]{:S(2)}, u32[]{:S(2)}) collective-permute-start(bf16[2,112,768]{2,1,0:T(8,128)(2,1)S(1)} %collective-permute-done.50.refs_5_), channel_id=1, source_target_pairs={{0,4},{4,0},{8,12},{12,8},{16,20},{20,16},{24,28},{28,24},{1,5},{5... | collective-permute-start | bytes 1032200 | tf_op jit(solution)/shard_map/ppermute | solution.py:726
  236.5 7.4 %collective-permute-start.54 = (bf16[2,112,768]{2,1,0:T(8,128)(2,1)S(1)}, bf16[2,112,768]{2,1,0:T(8,128)(2,1)S(1)}, u32[]{:S(2)}, u32[]{:S(2)}) collective-permute-start(bf16[2,112,768]{2,1,0:T(8,128)(2,1)S(1)} %collective-permute-done.49.refs_4_), channel_id=1, source_target_pairs={{0,4},{4,0},{8,12},{12,8},{16,20},{20,16},{24,28},{28,24},{1,5},{5... | collective-permute-start | bytes 1032200 | tf_op jit(solution)/shard_map/ppermute | solution.py:726
  240.2 23.1 %collective-permute-start.57 = (bf16[480,768]{1,0:T(8,128)(2,1)}, bf16[480,768]{1,0:T(8,128)(2,1)}, u32[]{:S(2)}, u32[]{:S(2)}) collective-permute-start(bf16[480,768]{1,0:T(8,128)(2,1)} %collective-permute-done.43.refs_7_), channel_id=1, source_target_pairs={{1,0},{5,4},{9,8},{13,12},{17,16},{21,20},{25,24},{29,28}} | collective-permute-start | bytes 2211848 | tf_op jit(solution)/shard_map/ppermute | solution.py:954
  242.4 21.6 %collective-permute-start.56 = (bf16[480,768]{1,0:T(8,128)(2,1)}, bf16[480,768]{1,0:T(8,128)(2,1)}, u32[]{:S(2)}, u32[]{:S(2)}) collective-permute-start(bf16[480,768]{1,0:T(8,128)(2,1)} %collective-permute-done.42.refs_4_), channel_id=1, source_target_pairs={{2,3},{6,7},{10,11},{14,15},{18,19},{22,23},{26,27},{30,31}} | collective-permute-start | bytes 2211848 | tf_op jit(solution)/shard_map/ppermute | solution.py:953
  252.1 9.2 %collective-permute-start.60 = (bf16[208,768]{1,0:T(8,128)(2,1)S(1)}, bf16[208,768]{1,0:T(8,128)(2,1)S(1)}, u32[]{:S(2)}, u32[]{:S(2)}) collective-permute-start(bf16[208,768]{1,0:T(8,128)(2,1)S(1)} %fusion.8.refs_1_), channel_id=1, source_target_pairs={{0,8},{4,12},{8,0},{12,4},{16,24},{20,28},{24,16},{28,20},{1,9},{5... | collective-permute-start | bytes 958472 | tf_op jit(solution)/shard_map/ppermute | solution.py:726
  252.8 9.8 %collective-permute-start.61 = (bf16[208,768]{1,0:T(8,128)(2,1)S(1)}, bf16[208,768]{1,0:T(8,128)(2,1)S(1)}, u32[]{:S(2)}, u32[]{:S(2)}) collective-permute-start(bf16[208,768]{1,0:T(8,128)(2,1)S(1)} %fusion.8.refs_1_), channel_id=1, source_target_pairs={{0,16},{4,20},{8,24},{12,28},{16,0},{20,4},{24,8},{28,12},{1,17},{... | collective-permute-start | bytes 958472 | tf_op jit(solution)/shard_map/ppermute | solution.py:726
  261.4 7.5 %collective-permute-start.62 = (bf16[112,768]{1,0:T(8,128)(2,1)S(1)}, bf16[112,768]{1,0:T(8,128)(2,1)S(1)}, u32[]{:S(2)}, u32[]{:S(2)}) collective-permute-start(bf16[112,768]{1,0:T(8,128)(2,1)S(1)} %slice.128), channel_id=1, source_target_pairs={{0,16},{4,20},{8,24},{12,28},{16,0},{20,4},{24,8},{28,12},{1,17},{... | collective-permute-start | bytes 516104 | tf_op jit(solution)/shard_map/ppermute | solution.py:726
  261.4 8.6 %collective-permute-start.64 = (bf16[208,768]{1,0:T(8,128)(2,1)S(1)}, bf16[208,768]{1,0:T(8,128)(2,1)}, u32[]{:S(2)}, u32[]{:S(2)}) collective-permute-start(bf16[208,768]{1,0:T(8,128)(2,1)S(1)} %fusion.8.refs_1_), channel_id=1, source_target_pairs={{0,4},{4,0},{8,12},{12,8},{16,20},{20,16},{24,28},{28,24},{1,5},{5... | collective-permute-start | bytes 958472 | tf_op jit(solution)/shard_map/ppermute | solution.py:726
  262.7 6.2 %collective-permute-start.63 = (bf16[96,768]{1,0:T(8,128)(2,1)S(1)}, bf16[96,768]{1,0:T(8,128)(2,1)S(1)}, u32[]{:S(2)}, u32[]{:S(2)}) collective-permute-start(bf16[96,768]{1,0:T(8,128)(2,1)S(1)} %slice.129), channel_id=1, source_target_pairs={{0,8},{4,12},{8,0},{12,4},{16,24},{20,28},{24,16},{28,20},{1,9},{5... | collective-permute-start | bytes 442376 | tf_op jit(solution)/shard_map/ppermute | solution.py:726
  263.3 6.8 %collective-permute-start.66 = (bf16[208,768]{1,0:T(8,128)(2,1)S(1)}, bf16[208,768]{1,0:T(8,128)(2,1)}, u32[]{:S(2)}, u32[]{:S(2)}) collective-permute-start(bf16[208,768]{1,0:T(8,128)(2,1)S(1)} %collective-permute-done.61.refs_3_), channel_id=1, source_target_pairs={{0,4},{4,0},{8,12},{12,8},{16,20},{20,16},{24,28},{28,24},{1,5},{5... | collective-permute-start | bytes 958472 | tf_op jit(solution)/shard_map/ppermute | solution.py:726
  264.0 6.1 %collective-permute-start.65 = (bf16[208,768]{1,0:T(8,128)(2,1)S(1)}, bf16[208,768]{1,0:T(8,128)(2,1)}, u32[]{:S(2)}, u32[]{:S(2)}) collective-permute-start(bf16[208,768]{1,0:T(8,128)(2,1)S(1)} %collective-permute-done.60.refs_2_), channel_id=1, source_target_pairs={{0,4},{4,0},{8,12},{12,8},{16,20},{20,16},{24,28},{28,24},{1,5},{5... | collective-permute-start | bytes 958472 | tf_op jit(solution)/shard_map/ppermute | solution.py:726
  (29 other events, 147.8 us)
Sparse Core Ops, SparseCore 0:
  205.8 36.3 reduce-scatter.1

commit v6 on v5

--- a/solution.py
+++ b/solution.py
@@ -94,27 +94,34 @@
     return jnp.where(key < limit, scores, masked_score)
 
 
-def pack_kernel(place, weights, layout, bias, mine):
+def pack_kernel(place, weights, layout, bias, bias_l, mine, rest):
     mine[:192] = weights[...]
-    width_l = layout.shape[1]
-    high = bias[...].astype(BF).astype(F32)
-    middle = (bias[...] - high).astype(BF).astype(F32)
-    low = bias[...] - high - middle
-    biases = jnp.concatenate([high, middle, low, jnp.zeros_like(low)], axis=0)
-    mine[192:, :] = jnp.zeros((32, mine.shape[1]), BF)
-    empty = jnp.zeros((8, width_l), F32)
     both = layout[...].astype(F32)
-    mine[192:, :width_l] = jnp.concatenate([both[:24], empty], axis=0).astype(BF)
-    mine[192:, 256 : 256 + width_l] = jnp.concatenate([both[24:], empty], axis=0).astype(BF)
-    mine[192:, 512:640] = biases.astype(BF)
-
-
-def biases_of(rest):
-    split = rest[:, 512:640].astype(F32)
-    rows = split[:8] + split[8:16] + split[16:24]
-    text = jnp.concatenate([rows[i : i + 1] for i in range(6)], axis=1)
-    layout = jnp.concatenate([rows[i : i + 1] for i in (6, 7)], axis=1)
-    return text, layout
+    for i, (row, lane) in enumerate(((0, 0), (0, 384), (8, 0))):
+        rest[row : row + 8, lane : lane + 192] = both[8 * i : 8 * i + 8]
+        rest[row : row + 8, lane + 192 : lane + 384] = both[24 + 8 * i : 32 + 8 * i]
+
+    def split(values):
+        high = values.astype(BF).astype(F32)
+        middle = (values - high).astype(BF).astype(F32)
+        return high, middle, values - high - middle
+
+    for i, part in enumerate(split(bias[...])):
+        rest[8 + 2 * i : 9 + 2 * i, 384:] = part[:, :384]
+        rest[9 + 2 * i : 10 + 2 * i, 384:] = part[:, 384:]
+    high, middle, low = split(bias_l[...])
+    rest[14:15, 384:576] = high
+    rest[14:15, 576:] = middle
+    rest[15:16, 384:576] = low
+    rest[15:16, 576:] = jnp.zeros_like(low)
+    mine[192:, :] = rest[...].astype(BF)
+
+
+def biases_of(piece):
+    split = piece[192:208, 384:768].astype(F32)[8:]
+    text = [split[i : i + 1] + split[i + 2 : i + 3] + split[i + 4 : i + 5] for i in (0, 1)]
+    left, right = piece[192:208, 384:576].astype(F32), piece[192:208, 576:768].astype(F32)
+    return jnp.concatenate(text, axis=1), left[14:15] + right[14:15] + left[15:16]
 
 
 def identity(size):
@@ -187,7 +194,7 @@
             )
         return carry
 
-    lax.fori_loop(0, HEADS // 2, one_pair, 0)
+    lax.fori_loop(0, HEADS // 2, one_pair, 0, unroll=2)
     cl[...] = cl_acc[:, :layout_width].astype(BF)
 
 
@@ -235,7 +242,7 @@
     normed = normalised(first)[0] * gl[0:1, :] + sl[0:1, :]
     low_l[...] = normed.astype(BF)
     normed_l[...] = normed + bl[3:4, :]
-    shard_forward(low_t, widen, biases_of(hidden[192:, :])[0], narrow, active, slope, total)
+    shard_forward(low_t, widen, biases_of(hidden)[0], narrow, active, slope, total)
 
 
 def piece_rows(info, rel):
@@ -251,9 +258,14 @@
 
 def place_layout(info, plan, refs, both):
     for ref, (rel, low, high) in zip(refs, plan):
-        if high == 224:
-            at = pl.multiple_of((info[HALF + rel // 4] + info[PIECE + rel % 4]) // 4, 8)
-            both[pl.ds(at, 24), :] = ref[192 - low :, :512].astype(F32)[:24]
+        if high == 208:
+            at = (info[HALF + rel // 4] + info[PIECE + rel % 4]) // 4
+            for i, (row, lane) in enumerate(((0, 0), (0, 384), (8, 0))):
+                rows = pl.ds(pl.multiple_of(at + 8 * i, 8), 8)
+                for half in (0, 1):
+                    lanes = slice(lane + 192 * half, lane + 192 * half + 192)
+                    got = ref[192 - low : 208 - low, lanes].astype(F32)
+                    both[rows, 256 * half : 256 * half + 192] = got[row : row + 8]
 
 
 def shard_kernel(plan, info, low, total_in, *refs):
@@ -263,7 +275,7 @@
     place_layout(info, plan, pieces, both)
     layout[...] = both[...].astype(BF)
     total[...] = total_in[...]
-    bias = biases_of(pieces[0][192:, :])[0]
+    bias = biases_of(pieces[0])[0]
     shard_forward(low, weights.at[0], bias, weights.at[1], active, slope, total)
 
 
@@ -306,14 +318,14 @@
     keep = jnp.concatenate(keep, axis=0)
 
     width_l = low_l.shape[1]
-    hidden_bias = [biases_of(ref[192:, :]) for ref in (mine, first_piece, pieces[0], third_piece)]
+    hidden_bias = [biases_of(ref) for ref in (mine, first_piece, pieces[0], third_piece)]
     place_layout(info, plan, pieces, both)
     last_l = both[...].astype(BF)
     layouts = [(widen_own_l[...], narrow_own_l[...])]
     layouts += [(v[:, :width_l], v[:, 256 : 256 + width_l]) for v in (layout_one[...], last_l, layout_three[...])]
     for s in range(shards):
         widen, narrow = layouts[s]
-        shard_forward(low_l, widen, hidden_bias[s][1][:, :width_l], narrow, active_l.at[s], slope_l.at[s], dnormed_l)
+        shard_forward(low_l, widen, hidden_bias[s][1], narrow, active_l.at[s], slope_l.at[s], dnormed_l)
     cot_l = tn(cot_lt[...], identity(width_l))
     upper_back(dnormed_l, gain_l, shift_l, cot_l, keep, result_l, dout_l, sums_l)
     result_lt[...] = nt(identity(width_l), result_l[...]).astype(BF)
@@ -523,7 +535,7 @@
             vl_acc[keys_at, group_lanes] += both[:, LANES:]
         return carry
 
-    lax.fori_loop(0, HEADS // 2, one_pair, 0)
+    lax.fori_loop(0, HEADS // 2, one_pair, 0, unroll=2)
     middle = pl.ds(pad, window)
     dk[middle, :] = k_acc[...].astype(BF)
     dv[middle, :] = v_acc[...].astype(BF)
@@ -803,7 +815,6 @@
 
     shift_from = lambda k: [(i, (i - k) % groups) for i in range(groups)]
     shift_to = lambda k: [(i, (i + k) % groups) for i in range(groups)]
-    bias = jnp.concatenate([text_hidden_bias, layout_hidden_bias, jnp.zeros((8 * LANES - hid - hid_l,), F32)])
     across = around(planes)
     row = row_of(0, 0, 0)
     mine, packed_up = call(
@@ -811,8 +822,9 @@
         (jnp.zeros((1,), jnp.int32),
          jnp.concatenate([lax.dynamic_slice_in_dim(v, row, piece, 0) for v in (text_widen, text_narrow)], axis=0),
          jnp.concatenate([lax.dynamic_slice_in_dim(v, row // 4, piece // 4, 0) for v in (layout_widen, layout_narrow)], axis=0),
-         bias.reshape(8, LANES)),
-        (shape((2 * piece + 32, width)),),
+         text_hidden_bias[None, :], layout_hidden_bias[None, :]),
+        (shape((2 * piece + EXTRA, width)),),
+        scratch=(pltpu.VMEM((EXTRA, width), F32),),
     )
     from_group = lambda v, k: lax.ppermute(v, "tensor", shift_from(k))
     come = {k: from_group(mine, k) for k in (1, 3)}

time: 287 us -> 284 us (0.990)
  starting transfers between devices: 92.2 us -> 87.2 us
    ppermute x52, starting transfers between devices: 60.8 us -> 57.3 us  [around(): return lambda v, bit: lax.ppermute(v, 'dp', flip(planes, bit))]
  transfers between devices with their start and end apart: 70 -> 70, of which waited for: 25 -> 20; matrix products, arithmetic and copies ran while one was open for 3% -> 3% of each run, Pallas kernels for 20% -> 20%
where the time goes in v6:
time: 284 us; the launch traced here: 278 us
  starting transfers between devices  87.2 us (31%)
  Pallas kernels  82.2 us (29%)
  waiting for transfers between devices  74.9 us (26%)
  between operations  18.3 us (6%)
  local copies, waits for them, and re-layouts  12.2 us (4%)
  other arithmetic  3.55 us (1%)
    pallas_call x19, Pallas kernels, call(): pl.pallas_call(with_token, out_shape=tuple((shape(o.shape, o.dtype) for o...  82.2 us
    ppermute x52, starting transfers between devices, around(): return lambda v, bit: lax.ppermute(v, 'dp', flip(planes, bit))  57.3 us
    ppermute x52, waiting for transfers between devices, around(): return lambda v, bit: lax.ppermute(v, 'dp', flip(planes, bit))  29.6 us
    ppermute x6, waiting for transfers between devices, per_device(): from_group = lambda v, k: lax.ppermute(v, 'tensor', shift_from(k))  17.3 us
    ppermute x1, waiting for transfers between devices, per_device(): lax.ppermute(left, 'tensor', [(i + 1, i) for i in range(groups - 1)])  10.5 us
    ppermute x3, starting transfers between devices, per_device(): lax.ppermute(v, 'tensor', [(i, i + 1) for i in range(far, groups - 1)])  9.88 us
    ppermute x3, waiting for transfers between devices, per_device(): to_group = lambda v, k: lax.ppermute(v, 'tensor', shift_to(k))  8.1 us
    ppermute x3, waiting for transfers between devices, per_device(): lax.ppermute(v, 'tensor', [(i, i - 1) for i in range(groups - 1 - far, 0,...  6.4 us
  transfers between devices with their start and end apart: 70, of which 20 were waited for; matrix products, arithmetic and copies ran while one was open for 3% of the time, Pallas kernels for 20%

profile of v6, /device:TPU:9, one launch (start us, length us, event | category | flops | bytes accessed | tf_op | source)
XLA Modules:
  0.0 278.4 jit_solution(13481437817274070247)
XLA Ops:
  8.8 1.2 constant_dynamic-slice_fusion.1
  10.8 1.3 collective-permute-start.1
  13.5 2.0 copy-done.1
  17.5 4.7 %project.1 = (bf16[384,768]{1,0:T(8,128)(2,1)S(1)}, bf16[1024,768]{1,0:T(8,128)(2,1)S(1)}, bf16[1024,768]{1,0:T(8,128)(2,1)S(1)}, bf16[384,256]{1,0:T(8,128)(2,1...) custom-call(f32[8,128]{1,0:T(8,128)S(1)} %get-tuple-element.147.refs, ...), custom_call_target="tpu_custom_call" | custom-call | flops 1000000000 | tf_op jit(solution)/shard_map/project/pallas_call | solution.py:703
  22.3 5.7 %collective-permute-done.refs_1_ = bf16[208,768]{1,0:T(8,128)(2,1)S(1)} collective-permute-done((bf16[208,768]{1,0:T(8,128)(2,1)S(1)}, bf16[208,768]{1,0:T(8,128)(2,1)S(1)}, u32[]{:S(2)}, u32[]{:S(2)}) %collective-permute-start) | collective-permute-done | bytes 319520 | tf_op jit(solution)/shard_map/ppermute | solution.py:829
  28.2 1.2 collective-permute-start.3
  29.4 1.2 collective-permute-start.2
  31.1 7.3 %attend.1 = (bf16[384,768]{1,0:T(8,128)(2,1)S(1)}, bf16[384,192]{1,0:T(8,128)(2,1)S(1)}, f32[384,128]{1,0:T(8,128)S(1)}, f32[8,128]{1,0:T(8,128)S(1)}) custom-call(s32[26]{0:T(128)S(1)} %concatenate.9.refs_1_.refs_0_.refs_2_.refs_3_, bf16[384,768]{1,0:T(8,128)(2,1)S(1)} %get-tuple-element.149.refs_1_.refs_2_, ...), custom_call_target="tpu_custom_call" | custom-call | flops 1800000000 | tf_op jit(solution)/shard_map/attend/pallas_call | solution.py:703
  38.5 3.5 %collective-permute-done.6.refs_5_ = bf16[208,768]{1,0:T(8,128)(2,1)S(1)} collective-permute-done((bf16[208,768]{1,0:T(8,128)(2,1)S(1)}, bf16[208,768]{1,0:T(8,128)(2,1)S(1)}, u32[]{:S(2)}, u32[]{:S(2)}) %collective-permute-start.6) | collective-permute-done | bytes 319520 | tf_op jit(solution)/shard_map/ppermute | solution.py:829
  43.6 1.2 collective-permute-start.8
  45.7 3.0 %first_norm.1 = (f32[384,768]{1,0:T(8,128)S(1)}, f32[384,192]{1,0:T(8,128)S(1)}, bf16[384,768]{1,0:T(8,128)(2,1)S(1)}, bf16[384,192]{1,0:T(8,128)(2,1)S(1)}, f32...) custom-call(s32[26]{0:T(128)S(1)} %concatenate.9.refs_1_.refs_0_.ref, ...), custom_call_target="tpu_custom_call" | custom-call | flops 600000000 | tf_op jit(solution)/shard_map/first_norm/pallas_call | solution.py:703
  49.7 6.6 %collective-permute-start.10 = (bf16[208,768]{1,0:T(8,128)(2,1)S(1)}, bf16[208,768]{1,0:T(8,128)(2,1)S(1)}, u32[]{:S(2)}, u32[]{:S(2)}) collective-permute-start(bf16[208,768]{1,0:T(8,128)(2,1)S(1)} %get-tuple-element.173.refs_4_), channel_id=1, source_target_pairs={{0,4},{4,0},{8,12},{12,8},{16,20},{20,16},{24,28},{28,24},{1,5},{5... | collective-permute-start | bytes 958472 | tf_op jit(solution)/shard_map/ppermute | solution.py:738
  56.9 2.9 %collective-permute-start.14 = (bf16[208,768]{1,0:T(8,128)(2,1)S(1)}, bf16[208,768]{1,0:T(8,128)(2,1)S(1)}, u32[]{:S(2)}, u32[]{:S(2)}) collective-permute-start(bf16[208,768]{1,0:T(8,128)(2,1)S(1)} %get-tuple-element.178.refs_4_), channel_id=1, source_target_pairs={{0,4},{4,0},{8,12},{12,8},{16,20},{20,16},{24,28},{28,24},{1,5},{5... | collective-permute-start | bytes 958472 | tf_op jit(solution)/shard_map/ppermute | solution.py:738
  61.2 1.3 collective-permute-start.20
  63.3 1.2 collective-permute-start.19
  65.0 2.8 shard.2
  67.8 2.2 shard.3
  70.7 1.2 collective-permute-done.24.refs_40_
  71.9 11.6 %turn.1 = (bf16[384,768]{1,0:T(8,128)(2,1)}, bf16[384,768]{1,0:T(8,128)(2,1)S(1)}, bf16[4,384,768]{2,1,0:T(8,128)(2,1)S(1)}, f32[4,768]{1,0:T(4,128)S(1)}, f32[4...) custom-call(s32[26]{0:T(128)S(1)} %concatenate.9.refs_1_.refs_0_.ref, ...), custom_call_target="tpu_custom_call" | custom-call | flops 2400000000 | tf_op jit(solution)/shard_map/turn/pallas_call | solution.py:703
  83.4 3.2 %ffn_send.1 = (bf16[4,448,768]{2,1,0:T(8,128)(2,1)S(1)}, bf16[4,384,768]{2,1,0:T(8,128)(2,1)S(1)}, f32[8,128]{1,0:T(8,128)S(1)}) custom-call(s32[26]{0:T(128)S(1)} %concatenate.9.refs_1_.refs_0_.refs_2_.refs_3_, bf16[384,768]{1,0:T(8,128)(2,1)S(1)} %get-tuple-element.185.refs_11_.refs_1_.refs_2_, ...), custom_call_target="tpu_custom_call" | custom-call | flops 800000000 | tf_op jit(solution)/shard_map/ffn_send/pallas_call | solution.py:703
  87.2 14.1 %attend_back.1 = (bf16[384,768]{1,0:T(8,128)(2,1)S(1)}, bf16[1792,768]{1,0:T(8,128)(2,1)S(1)}, bf16[1792,768]{1,0:T(8,128)(2,1)S(1)}, bf16[384,256]{1,0:T(8,128)...) custom-call(f32[8,128]{1,0:T(8,128)S(1)} %get-tuple-element.206.refs_0_, ...), custom_call_target="tpu_custom_call" | custom-call | flops 3000000000 | tf_op jit(solution)/shard_map/attend_back/pallas_call | solution.py:703
  101.4 3.6 %ffn_keep.1 = (bf16[2,4,112,768]{3,2,1,0:T(8,128)(2,1)S(1)}, bf16[2,4,96,768]{3,2,1,0:T(8,128)(2,1)S(1)}, bf16[2,4,112,768]{3,2,1,0:T(8,128)(2,1)S(1)}, bf16[2,4,96,768]{3,2,1,0:T(8,128)(2,1)S(1)}, f32[8,128]{1,0:T(8,128)S(1)}) custom-call(f32[8,128]{1,0:T(8,128)S(1)} %get-tuple-element.210.refs_0_, s32[26]{0:T(128)S(1)} %concatenate.9.refs_1_.refs_0_.refs_2_.refs_3_, ...), custom_call_target="tpu_custom_call" | custom-call | flops 800000000 | tf_op jit(solution)/shard_map/ffn_keep/pallas_call | solution.py:703
  105.0 3.3 %copied_send.1 = (bf16[4,448,768]{2,1,0:T(8,128)(2,1)S(1)}, bf16[512,768]{1,0:T(8,128)(2,1)S(1)}, f32[8,128]{1,0:T(8,128)S(1)}) custom-call(f32[8,128]{1,0:T(8,128)S(1)} %get-tuple-element.213.refs_0_, s32[26]{0:T(128)S(1)} %concatenate.9.refs_1_.refs_0_.refs_2_.refs_3_, bf16[1536,768]{1,0:T(8,128)(2,1)S(1)} %copy-done, ...), custom_call_target="tpu_custom_call" | custom-call | flops 800000000 | tf_op jit(solution)/shard_map/copied_send/pallas_call | solution.py:703
  109.0 2.8 %sides.1 = (bf16[480,768]{1,0:T(8,128)(2,1)S(1)}, bf16[480,768]{1,0:T(8,128)(2,1)S(1)}, f32[8,128]{1,0:T(8,128)S(1)}) custom-call(f32[8,128]{1,0:T(8,128)S(1)} %get-tuple-element.228.refs_0_, s32[26]{0:T(128)S(1)} %concatenate.9.refs_1_.refs_0_.refs_2_.refs_3_, bf16[768,2304]{1,0:T(8,128)(2,1)S(1)} %copy-done.2, ...), custom_call_target="tpu_custom_call" | custom-call | flops 600000000 | tf_op jit(solution)/shard_map/sides/pallas_call | solution.py:703
  111.8 3.3 %collective-permute-start.29 = (bf16[480,768]{1,0:T(8,128)(2,1)S(1)}, bf16[480,768]{1,0:T(8,128)(2,1)S(1)}, u32[]{:S(2)}, u32[]{:S(2)}) collective-permute-start(bf16[480,768]{1,0:T(8,128)(2,1)S(1)} %get-tuple-element.236), channel_id=1, source_target_pairs={{1,0},{2,1},{3,2},{5,4},{6,5},{7,6},{9,8},{10,9},{11,10},{13,12},{... | collective-permute-start | bytes 2211848 | tf_op jit(solution)/shard_map/ppermute | solution.py:950
  115.1 2.0 collective-permute-start.30
  117.7 2.9 %copied_keep.1 = (bf16[2,2,112,768]{3,2,1,0:T(8,128)(2,1)S(1)}, bf16[2,2,112,768]{3,2,1,0:T(8,128)(2,1)S(1)}, bf16[2,2,112,768]{3,2,1,0:T(8,128)(2,1)S(1)}, bf16...) custom-call(f32[8,128]{1,0:T(8,128)S(1)} %get-tuple-element.230.refs_0_, s32[26]{0:T(128)S(1)} %concatenate.9.refs_1_.refs_0_.refs_2_.refs_3_, ...), custom_call_target="tpu_custom_call" | custom-call | flops 600000000 | tf_op jit(solution)/shard_map/copied_keep/pallas_call | solution.py:703
  120.7 10.5 %collective-permute-done.29.refs_12_ = bf16[480,768]{1,0:T(8,128)(2,1)S(1)} collective-permute-done((bf16[480,768]{1,0:T(8,128)(2,1)S(1)}, bf16[480,768]{1,0:T(8,128)(2,1)S(1)}, u32[]{:S(2)}, u32[]{:S(2)}) %collective-permute-start.29) | collective-permute-done | bytes 737312 | tf_op jit(solution)/shard_map/ppermute | solution.py:950
  131.2 3.0 %collective-permute-done.30.refs_13_ = bf16[480,768]{1,0:T(8,128)(2,1)S(1)} collective-permute-done((bf16[480,768]{1,0:T(8,128)(2,1)S(1)}, bf16[480,768]{1,0:T(8,128)(2,1)S(1)}, u32[]{:S(2)}, u32[]{:S(2)}) %collective-permute-start.30) | collective-permute-done | bytes 737312 | tf_op jit(solution)/shard_map/ppermute | solution.py:951
  134.2 3.0 %own.1 = (bf16[480,768]{1,0:T(8,128)(2,1)S(1)}, f32[8,128]{1,0:T(8,128)}) custom-call(f32[8,128]{1,0:T(8,128)S(1)} %get-tuple-element.233.refs_0_, s32[26]{0:T(128)S(1)} %concatenate.9.refs_1_.refs_0_.refs_2_.refs_3_, bf16[768,2304]{1,0:T(8,128)(2,1)S(1)} %copy-done.2, bf16[192,768]{1,0:T(8,128)(2,1)S(1)} %get-tuple-element.229.refs_3_, ...), custom_call_target="tpu_custom_call" | custom-call | flops 600000000 | tf_op jit(solution)/shard_map/own/pallas_call | solution.py:703
  137.1 1.9 collective-permute-start.32
  139.1 3.4 %collective-permute-start.31 = (bf16[480,768]{1,0:T(8,128)(2,1)S(1)}, bf16[480,768]{1,0:T(8,128)(2,1)S(1)}, u32[]{:S(2)}, u32[]{:S(2)}) collective-permute-start(bf16[480,768]{1,0:T(8,128)(2,1)S(1)} %get-tuple-element.238.refs_2_), channel_id=1, source_target_pairs={{0,1},{1,2},{2,3},{4,5},{5,6},{6,7},{8,9},{9,10},{10,11},{12,13},{... | collective-permute-start | bytes 2211848 | tf_op jit(solution)/shard_map/ppermute | solution.py:965
  144.6 3.1 %collective-permute-done.34 = bf16[2,4,112,768]{3,2,1,0:T(8,128)(2,1)S(1)} collective-permute-done((bf16[2,4,112,768]{3,2,1,0:T(8,128)(2,1)S(1)}, bf16[2,4,112,768]{3,2,1,0:T(8,128)(2,1)S(1)}, u32[]{:S(2)}, u32[]{:S(2)}) %collective-permute-start.34) | collective-permute-done | bytes 1376288 | tf_op jit(solution)/shard_map/ppermute | solution.py:738
  148.9 6.4 %collective-permute-done.32.refs_1_.refs_6_ = bf16[480,768]{1,0:T(8,128)(2,1)S(1)} collective-permute-done((bf16[480,768]{1,0:T(8,128)(2,1)S(1)}, bf16[480,768]{1,0:T(8,128)(2,1)S(1)}, u32[]{:S(2)}, u32[]{:S(2)}) %collective-permute-start.32) | collective-permute-done | bytes 737312 | tf_op jit(solution)/shard_map/ppermute | solution.py:966
  155.3 2.2 collective-permute-start.43
  157.5 5.0 %collective-permute-start.42 = (bf16[480,768]{1,0:T(8,128)(2,1)S(1)}, bf16[480,768]{1,0:T(8,128)(2,1)}, u32[]{:S(2)}, u32[]{:S(2)}) collective-permute-start(bf16[480,768]{1,0:T(8,128)(2,1)S(1)} %collective-permute-done.31.refs_0_.refs_3_), channel_id=1, source_target_pairs={{1,2},{2,3},{5,6},{6,7},{9,10},{10,11},{13,14},{14,15},{17,18},{18... | collective-permute-start | bytes 2211848 | tf_op jit(solution)/shard_map/ppermute | solution.py:965
  162.7 1.3 collective-permute-start.35
  164.8 4.5 %collective-permute-done.35.refs_4_ = bf16[2,112,768]{2,1,0:T(8,128)(2,1)S(1)} collective-permute-done((bf16[2,112,768]{2,1,0:T(8,128)(2,1)S(1)}, bf16[2,112,768]{2,1,0:T(8,128)(2,1)S(1)}, u32[]{:S(2)}, u32[]{:S(2)}) %collective-permute-start.35) | collective-permute-done | bytes 344096 | tf_op jit(solution)/shard_map/ppermute | solution.py:738
  169.3 1.9 collective-permute-done.38.refs_6_
  171.2 1.1 copied_spread.1
  172.3 1.5 collective-permute-start.39
  173.8 1.9 collective-permute-start.40
  175.7 1.2 slice.121
  177.6 1.2 slice.120
  182.0 7.1 %collective-permute-done.40 = bf16[112,768]{1,0:T(8,128)(2,1)S(1)} collective-permute-done((bf16[112,768]{1,0:T(8,128)(2,1)S(1)}, bf16[112,768]{1,0:T(8,128)(2,1)S(1)}, u32[]{:S(2)}, u32[]{:S(2)}) %collective-permute-start.40) | collective-permute-done | bytes 172064 | tf_op jit(solution)/shard_map/ppermute | solution.py:971
  190.3 1.9 collective-permute-start.45
  192.1 1.4 collective-permute-start.44
  193.5 4.1 %collective-permute-done.46.refs_2_ = bf16[112,768]{1,0:T(8,128)(2,1)S(1)} collective-permute-done((bf16[112,768]{1,0:T(8,128)(2,1)S(1)}, bf16[112,768]{1,0:T(8,128)(2,1)S(1)}, u32[]{:S(2)}, u32[]{:S(2)}) %collective-permute-start.46) | collective-permute-done | bytes 172064 | tf_op jit(solution)/shard_map/ppermute | solution.py:829
  197.7 4.0 %collective-permute-done.45.refs_1_ = bf16[112,768]{1,0:T(8,128)(2,1)S(1)} collective-permute-done((bf16[112,768]{1,0:T(8,128)(2,1)S(1)}, bf16[112,768]{1,0:T(8,128)(2,1)S(1)}, u32[]{:S(2)}, u32[]{:S(2)}) %collective-permute-start.45) | collective-permute-done | bytes 172064 | tf_op jit(solution)/shard_map/ppermute | solution.py:829
  201.7 1.9 ffn_spread.1
  203.7 4.6 %collective-permute-start.48 = (bf16[4,112,768]{2,1,0:T(8,128)(2,1)S(1)}, bf16[4,112,768]{2,1,0:T(8,128)(2,1)S(1)}, u32[]{:S(2)}, u32[]{:S(2)}) collective-permute-start(bf16[4,112,768]{2,1,0:T(8,128)(2,1)S(1)} %pad_maximum_fusion.refs_1_), channel_id=1, source_target_pairs={{0,16},{4,20},{8,24},{12,28},{16,0},{20,4},{24,8},{28,12},{1,17},{... | collective-permute-start | bytes 2064392 | tf_op jit(solution)/shard_map/ppermute | solution.py:738
  208.8 4.1 %collective-permute-start.51 = (bf16[4,112,768]{2,1,0:T(8,128)(2,1)S(1)}, bf16[4,112,768]{2,1,0:T(8,128)(2,1)S(1)}, u32[]{:S(2)}, u32[]{:S(2)}) collective-permute-start(bf16[4,112,768]{2,1,0:T(8,128)(2,1)S(1)} %pad_maximum_fusion.refs_1_), channel_id=1, source_target_pairs={{0,4},{4,0},{8,12},{12,8},{16,20},{20,16},{24,28},{28,24},{1,5},{5... | collective-permute-start | bytes 2064392 | tf_op jit(solution)/shard_map/ppermute | solution.py:738
  212.9 6.4 %collective-permute-done.48.refs_3_ = bf16[4,112,768]{2,1,0:T(8,128)(2,1)S(1)} collective-permute-done((bf16[4,112,768]{2,1,0:T(8,128)(2,1)S(1)}, bf16[4,112,768]{2,1,0:T(8,128)(2,1)S(1)}, u32[]{:S(2)}, u32[]{:S(2)}) %collective-permute-start.48) | collective-permute-done | bytes 688160 | tf_op jit(solution)/shard_map/ppermute | solution.py:738
  221.2 1.2 collective-permute-start.49
  222.5 7.5 %collective-permute-start.53 = (bf16[4,112,768]{2,1,0:T(8,128)(2,1)S(1)}, bf16[4,112,768]{2,1,0:T(8,128)(2,1)S(1)}, u32[]{:S(2)}, u32[]{:S(2)}) collective-permute-start(bf16[4,112,768]{2,1,0:T(8,128)(2,1)S(1)} %collective-permute-done.48.refs_3_), channel_id=1, source_target_pairs={{0,4},{4,0},{8,12},{12,8},{16,20},{20,16},{24,28},{28,24},{1,5},{5... | collective-permute-start | bytes 2064392 | tf_op jit(solution)/shard_map/ppermute | solution.py:738
  230.0 3.5 %collective-permute-start.55 = (bf16[2,112,768]{2,1,0:T(8,128)(2,1)S(1)}, bf16[2,112,768]{2,1,0:T(8,128)(2,1)S(1)}, u32[]{:S(2)}, u32[]{:S(2)}) collective-permute-start(bf16[2,112,768]{2,1,0:T(8,128)(2,1)S(1)} %collective-permute-done.50.refs_5_), channel_id=1, source_target_pairs={{0,4},{4,0},{8,12},{12,8},{16,20},{20,16},{24,28},{28,24},{1,5},{5... | collective-permute-start | bytes 1032200 | tf_op jit(solution)/shard_map/ppermute | solution.py:738
  233.5 3.6 %collective-permute-start.54 = (bf16[2,112,768]{2,1,0:T(8,128)(2,1)S(1)}, bf16[2,112,768]{2,1,0:T(8,128)(2,1)S(1)}, u32[]{:S(2)}, u32[]{:S(2)}) collective-permute-start(bf16[2,112,768]{2,1,0:T(8,128)(2,1)S(1)} %collective-permute-done.49.refs_4_), channel_id=1, source_target_pairs={{0,4},{4,0},{8,12},{12,8},{16,20},{20,16},{24,28},{28,24},{1,5},{5... | collective-permute-start | bytes 1032200 | tf_op jit(solution)/shard_map/ppermute | solution.py:738
  237.1 2.2 collective-permute-start.57
  239.3 1.5 collective-permute-start.56
  240.8 6.0 %copied_final.1 = (f32[768,2304]{1,0:T(8,128)}, f32[768,768]{1,0:T(8,128)}, f32[192,576]{1,0:T(8,128)}, f32[192,192]{1,0:T(8,128)}, f32[4,768]{1,0:T(4,128)}, /*...) custom-call(s32[26]{0:T(128)S(1)} %concatenate.9.refs_1_.refs_0_.ref, ...), custom_call_target="tpu_custom_call" | custom-call | flops 1200000000 | tf_op jit(solution)/shard_map/copied_final/pallas_call | solution.py:703
  249.3 9.0 %collective-permute-done.60.refs_2_ = bf16[208,768]{1,0:T(8,128)(2,1)S(1)} collective-permute-done((bf16[208,768]{1,0:T(8,128)(2,1)S(1)}, bf16[208,768]{1,0:T(8,128)(2,1)S(1)}, u32[]{:S(2)}, u32[]{:S(2)}) %collective-permute-start.60) | collective-permute-done | bytes 319520 | tf_op jit(solution)/shard_map/ppermute | solution.py:738
  259.5 1.4 collective-permute-start.66
  261.0 4.8 %input_final.1 = (f32[1536,768]{1,0:T(8,128)}, f32[192,1536]{1,0:T(8,128)}, f32[8,128]{1,0:T(8,128)S(1)}) custom-call(f32[8,128]{1,0:T(8,128)S(1)} %get-tuple-element.249.refs_0_, s32[26]{0:T(128)S(1)} %concatenate.9.refs_1_.refs_0_.refs_2_.refs_3_, bf16[480,768]{1,0:T(8,128)(2,1)S(1)} %get-tuple-element.238.refs_2_, ...), custom_call_target="tpu_custom_call" | custom-call | flops 800000000 | tf_op jit(solution)/shard_map/input_final/pallas_call | solution.py:703
  267.7 3.6 %ffn_final.1 = (f32[768,768]{1,0:T(8,128)}, f32[768,768]{1,0:T(8,128)}, f32[192,192]{1,0:T(8,128)}, f32[192,192]{1,0:T(8,128)}, f32[8,128]{1,0:T(8,128)}) custom-call(s32[26]{0:T(128)S(1)} %concatenate.9.refs_1_.refs_0_.refs_2_.refs_3_, bf16[208,768]{1,0:T(8,128)(2,1)S(1)} %fusion.8.refs_1_, bf16[208,768]{1,0:T(8,128)(2,1)S(1)} %collective-permute-done.60.refs_2_, ...), custom_call_target="tpu_custom_call" | custom-call | flops 600000000 | tf_op jit(solution)/shard_map/ffn_final/pallas_call | solution.py:703
  (180 shorter events, 29.9 us)
Async XLA Ops:
  7.2 240.8 %reduce-scatter.2.cloned.1.call-start = ((), (), s32[]{:S(2)}) async-start(), calls=%async_computation.1 | async-start | bytes 1597440 | tf_op jit(solution)/shard_map/reduce_scatter | solution.py:990
  10.8 11.5 %collective-permute-start.1 = (bf16[208,768]{1,0:T(8,128)(2,1)S(1)}, bf16[208,768]{1,0:T(8,128)(2,1)S(1)}, u32[]{:S(2)}, u32[]{:S(2)}) collective-permute-start(bf16[208,768]{1,0:T(8,128)(2,1)S(1)} %get-tuple-element.157.refs_14_.refs_27_), channel_id=1, source_target_pairs={{0,1},{1,2},{2,3},{3,0},{4,5},{5,6},{6,7},{7,4},{8,9},{9,10},{10,1... | collective-permute-start | bytes 958472 | tf_op jit(solution)/shard_map/ppermute | solution.py:829
  12.1 15.9 %collective-permute-start = (bf16[208,768]{1,0:T(8,128)(2,1)S(1)}, bf16[208,768]{1,0:T(8,128)(2,1)S(1)}, u32[]{:S(2)}, u32[]{:S(2)}) collective-permute-start(bf16[208,768]{1,0:T(8,128)(2,1)S(1)} %get-tuple-element.157.refs_14_.refs_27_), channel_id=1, source_target_pairs={{0,3},{1,0},{2,1},{3,2},{4,7},{5,4},{6,5},{7,6},{8,11},{9,8},{10,9... | collective-permute-start | bytes 958472 | tf_op jit(solution)/shard_map/ppermute | solution.py:829
  28.0 14.0 %collective-permute-start.6 = (bf16[208,768]{1,0:T(8,128)(2,1)S(1)}, bf16[208,768]{1,0:T(8,128)(2,1)S(1)}, u32[]{:S(2)}, u32[]{:S(2)}) collective-permute-start(bf16[208,768]{1,0:T(8,128)(2,1)S(1)} %get-tuple-element.163), channel_id=1, source_target_pairs={{0,2},{1,3},{2,0},{3,1},{4,6},{5,7},{6,4},{7,5},{8,10},{9,11},{10,... | collective-permute-start | bytes 958472 | tf_op jit(solution)/shard_map/ppermute | solution.py:829
  28.2 13.8 %collective-permute-start.3 = (bf16[208,768]{1,0:T(8,128)(2,1)S(1)}, bf16[208,768]{1,0:T(8,128)(2,1)S(1)}, u32[]{:S(2)}, u32[]{:S(2)}) collective-permute-start(bf16[208,768]{1,0:T(8,128)(2,1)S(1)} %get-tuple-element.161.refs_4_), channel_id=1, source_target_pairs={{0,16},{4,20},{8,24},{12,28},{16,0},{20,4},{24,8},{28,12},{1,17},{... | collective-permute-start | bytes 958472 | tf_op jit(solution)/shard_map/ppermute | solution.py:738
  29.4 12.5 %collective-permute-start.2 = (bf16[208,768]{1,0:T(8,128)(2,1)S(1)}, bf16[208,768]{1,0:T(8,128)(2,1)S(1)}, u32[]{:S(2)}, u32[]{:S(2)}) collective-permute-start(bf16[208,768]{1,0:T(8,128)(2,1)S(1)} %get-tuple-element.161.refs_4_), channel_id=1, source_target_pairs={{0,8},{4,12},{8,0},{12,4},{16,24},{20,28},{24,16},{28,20},{1,9},{5... | collective-permute-start | bytes 958472 | tf_op jit(solution)/shard_map/ppermute | solution.py:738
  30.6 11.4 %collective-permute-start.5 = (bf16[208,768]{1,0:T(8,128)(2,1)S(1)}, bf16[208,768]{1,0:T(8,128)(2,1)S(1)}, u32[]{:S(2)}, u32[]{:S(2)}) collective-permute-start(bf16[208,768]{1,0:T(8,128)(2,1)S(1)} %get-tuple-element.162.refs_6_), channel_id=1, source_target_pairs={{0,16},{4,20},{8,24},{12,28},{16,0},{20,4},{24,8},{28,12},{1,17},{... | collective-permute-start | bytes 958472 | tf_op jit(solution)/shard_map/ppermute | solution.py:738
  30.9 12.1 %collective-permute-start.4 = (bf16[208,768]{1,0:T(8,128)(2,1)S(1)}, bf16[208,768]{1,0:T(8,128)(2,1)S(1)}, u32[]{:S(2)}, u32[]{:S(2)}) collective-permute-start(bf16[208,768]{1,0:T(8,128)(2,1)S(1)} %get-tuple-element.162.refs_6_), channel_id=1, source_target_pairs={{0,8},{4,12},{8,0},{12,4},{16,24},{20,28},{24,16},{28,20},{1,9},{5... | collective-permute-start | bytes 958472 | tf_op jit(solution)/shard_map/ppermute | solution.py:738
  43.0 6.1 %collective-permute-start.7 = (bf16[208,768]{1,0:T(8,128)(2,1)S(1)}, bf16[208,768]{1,0:T(8,128)(2,1)S(1)}, u32[]{:S(2)}, u32[]{:S(2)}) collective-permute-start(bf16[208,768]{1,0:T(8,128)(2,1)S(1)} %get-tuple-element.165.refs_4_), channel_id=1, source_target_pairs={{0,16},{4,20},{8,24},{12,28},{16,0},{20,4},{24,8},{28,12},{1,17},{... | collective-permute-start | bytes 958472 | tf_op jit(solution)/shard_map/ppermute | solution.py:738
  43.6 6.1 %collective-permute-start.8 = (bf16[208,768]{1,0:T(8,128)(2,1)S(1)}, bf16[208,768]{1,0:T(8,128)(2,1)S(1)}, u32[]{:S(2)}, u32[]{:S(2)}) collective-permute-start(bf16[208,768]{1,0:T(8,128)(2,1)S(1)} %get-tuple-element.166.refs_7_), channel_id=1, source_target_pairs={{0,8},{4,12},{8,0},{12,4},{16,24},{20,28},{24,16},{28,20},{1,9},{5... | collective-permute-start | bytes 958472 | tf_op jit(solution)/shard_map/ppermute | solution.py:738
  44.8 12.1 %collective-permute-start.18 = (bf16[208,768]{1,0:T(8,128)(2,1)S(1)}, bf16[208,768]{1,0:T(8,128)(2,1)S(1)}, u32[]{:S(2)}, u32[]{:S(2)}) collective-permute-start(bf16[208,768]{1,0:T(8,128)(2,1)S(1)} %get-tuple-element.196.refs_32_), channel_id=1, source_target_pairs={{0,16},{4,20},{8,24},{12,28},{16,0},{20,4},{24,8},{28,12},{1,17},{... | collective-permute-start | bytes 958472 | tf_op jit(solution)/shard_map/ppermute | solution.py:738
  48.8 11.1 %collective-permute-start.17 = (bf16[208,768]{1,0:T(8,128)(2,1)S(1)}, bf16[208,768]{1,0:T(8,128)(2,1)S(1)}, u32[]{:S(2)}, u32[]{:S(2)}) collective-permute-start(bf16[208,768]{1,0:T(8,128)(2,1)S(1)} %get-tuple-element.196.refs_32_), channel_id=1, source_target_pairs={{0,8},{4,12},{8,0},{12,4},{16,24},{20,28},{24,16},{28,20},{1,9},{5... | collective-permute-start | bytes 958472 | tf_op jit(solution)/shard_map/ppermute | solution.py:738
  49.7 10.8 %collective-permute-start.10 = (bf16[208,768]{1,0:T(8,128)(2,1)S(1)}, bf16[208,768]{1,0:T(8,128)(2,1)S(1)}, u32[]{:S(2)}, u32[]{:S(2)}) collective-permute-start(bf16[208,768]{1,0:T(8,128)(2,1)S(1)} %get-tuple-element.173.refs_4_), channel_id=1, source_target_pairs={{0,4},{4,0},{8,12},{12,8},{16,20},{20,16},{24,28},{28,24},{1,5},{5... | collective-permute-start | bytes 958472 | tf_op jit(solution)/shard_map/ppermute | solution.py:738
  56.4 4.2 %collective-permute-start.11 = (bf16[208,768]{1,0:T(8,128)(2,1)S(1)}, bf16[208,768]{1,0:T(8,128)(2,1)S(1)}, u32[]{:S(2)}, u32[]{:S(2)}) collective-permute-start(bf16[208,768]{1,0:T(8,128)(2,1)S(1)} %get-tuple-element.174.refs_5_), channel_id=1, source_target_pairs={{0,4},{4,0},{8,12},{12,8},{16,20},{20,16},{24,28},{28,24},{1,5},{5... | collective-permute-start | bytes 958472 | tf_op jit(solution)/shard_map/ppermute | solution.py:738
  56.4 4.6 %collective-permute-start.12 = (bf16[208,768]{1,0:T(8,128)(2,1)S(1)}, bf16[208,768]{1,0:T(8,128)(2,1)S(1)}, u32[]{:S(2)}, u32[]{:S(2)}) collective-permute-start(bf16[208,768]{1,0:T(8,128)(2,1)S(1)} %get-tuple-element.175.refs_6_), channel_id=1, source_target_pairs={{0,4},{4,0},{8,12},{12,8},{16,20},{20,16},{24,28},{28,24},{1,5},{5... | collective-permute-start | bytes 958472 | tf_op jit(solution)/shard_map/ppermute | solution.py:738
  56.9 4.3 %collective-permute-start.14 = (bf16[208,768]{1,0:T(8,128)(2,1)S(1)}, bf16[208,768]{1,0:T(8,128)(2,1)S(1)}, u32[]{:S(2)}, u32[]{:S(2)}) collective-permute-start(bf16[208,768]{1,0:T(8,128)(2,1)S(1)} %get-tuple-element.178.refs_4_), channel_id=1, source_target_pairs={{0,4},{4,0},{8,12},{12,8},{16,20},{20,16},{24,28},{28,24},{1,5},{5... | collective-permute-start | bytes 958472 | tf_op jit(solution)/shard_map/ppermute | solution.py:738
  60.6 3.9 %collective-permute-start.9 = (bf16[208,768]{1,0:T(8,128)(2,1)S(1)}, bf16[208,768]{1,0:T(8,128)(2,1)S(1)}, u32[]{:S(2)}, u32[]{:S(2)}) collective-permute-start(bf16[208,768]{1,0:T(8,128)(2,1)S(1)} %get-tuple-element.172.refs_3_.refs_28_), channel_id=1, source_target_pairs={{0,4},{4,0},{8,12},{12,8},{16,20},{20,16},{24,28},{28,24},{1,5},{5... | collective-permute-start | bytes 958472 | tf_op jit(solution)/shard_map/ppermute | solution.py:738
  61.1 3.8 %collective-permute-start.13 = (bf16[208,768]{1,0:T(8,128)(2,1)S(1)}, bf16[208,768]{1,0:T(8,128)(2,1)S(1)}, u32[]{:S(2)}, u32[]{:S(2)}) collective-permute-start(bf16[208,768]{1,0:T(8,128)(2,1)S(1)} %get-tuple-element.177.refs_3_.refs_29_), channel_id=1, source_target_pairs={{0,4},{4,0},{8,12},{12,8},{16,20},{20,16},{24,28},{28,24},{1,5},{5... | collective-permute-start | bytes 958472 | tf_op jit(solution)/shard_map/ppermute | solution.py:738
  61.2 8.9 %collective-permute-start.20 = (bf16[112,768]{1,0:T(8,128)(2,1)S(1)}, bf16[112,768]{1,0:T(8,128)(2,1)S(1)}, u32[]{:S(2)}, u32[]{:S(2)}) collective-permute-start(bf16[112,768]{1,0:T(8,128)(2,1)S(1)} %slice.113), channel_id=1, source_target_pairs={{0,8},{4,12},{8,0},{12,4},{16,24},{20,28},{24,16},{28,20},{1,9},{5... | collective-permute-start | bytes 516104 | tf_op jit(solution)/shard_map/ppermute | solution.py:738
  62.5 8.2 %collective-permute-start.21 = (bf16[208,768]{1,0:T(8,128)(2,1)S(1)}, bf16[208,768]{1,0:T(8,128)(2,1)S(1)}, u32[]{:S(2)}, u32[]{:S(2)}) collective-permute-start(bf16[208,768]{1,0:T(8,128)(2,1)S(1)} %get-tuple-element.196.refs_32_), channel_id=1, source_target_pairs={{0,4},{4,0},{8,12},{12,8},{16,20},{20,16},{24,28},{28,24},{1,5},{5... | collective-permute-start | bytes 958472 | tf_op jit(solution)/shard_map/ppermute | solution.py:738
  63.3 6.8 %collective-permute-start.19 = (bf16[96,768]{1,0:T(8,128)(2,1)S(1)}, bf16[96,768]{1,0:T(8,128)(2,1)S(1)}, u32[]{:S(2)}, u32[]{:S(2)}) collective-permute-start(bf16[96,768]{1,0:T(8,128)(2,1)S(1)} %slice.112), channel_id=1, source_target_pairs={{0,16},{4,20},{8,24},{12,28},{16,0},{20,4},{24,8},{28,12},{1,17},{... | collective-permute-start | bytes 442376 | tf_op jit(solution)/shard_map/ppermute | solution.py:738
  64.5 6.1 %collective-permute-start.23 = (bf16[208,768]{1,0:T(8,128)(2,1)S(1)}, bf16[208,768]{1,0:T(8,128)(2,1)S(1)}, u32[]{:S(2)}, u32[]{:S(2)}) collective-permute-start(bf16[208,768]{1,0:T(8,128)(2,1)S(1)} %collective-permute-done.18.refs_34_), channel_id=1, source_target_pairs={{0,4},{4,0},{8,12},{12,8},{16,20},{20,16},{24,28},{28,24},{1,5},{5... | collective-permute-start | bytes 958472 | tf_op jit(solution)/shard_map/ppermute | solution.py:738
  64.9 5.8 %collective-permute-start.22 = (bf16[208,768]{1,0:T(8,128)(2,1)S(1)}, bf16[208,768]{1,0:T(8,128)(2,1)S(1)}, u32[]{:S(2)}, u32[]{:S(2)}) collective-permute-start(bf16[208,768]{1,0:T(8,128)(2,1)S(1)} %collective-permute-done.17.refs_33_), channel_id=1, source_target_pairs={{0,4},{4,0},{8,12},{12,8},{16,20},{20,16},{24,28},{28,24},{1,5},{5... | collective-permute-start | bytes 958472 | tf_op jit(solution)/shard_map/ppermute | solution.py:738
  86.7 14.7 %collective-permute-start.26 = (bf16[4,448,768]{2,1,0:T(8,128)(2,1)S(1)}, bf16[4,448,768]{2,1,0:T(8,128)(2,1)S(1)}, u32[]{:S(2)}, u32[]{:S(2)}) collective-permute-start(bf16[4,448,768]{2,1,0:T(8,128)(2,1)S(1)} %get-tuple-element.211), channel_id=1, source_target_pairs={{0,4},{4,0},{8,12},{12,8},{16,20},{20,16},{24,28},{28,24},{1,5},{5... | collective-permute-start | bytes 8257544 | tf_op jit(solution)/shard_map/ppermute | solution.py:738
  87.0 14.4 %collective-permute-start.27 = (bf16[4,384,768]{2,1,0:T(8,128)(2,1)S(1)}, bf16[4,384,768]{2,1,0:T(8,128)(2,1)S(1)}, u32[]{:S(2)}, u32[]{:S(2)}) collective-permute-start(bf16[4,384,768]{2,1,0:T(8,128)(2,1)S(1)} %get-tuple-element.212), channel_id=1, source_target_pairs={{0,4},{4,0},{8,12},{12,8},{16,20},{20,16},{24,28},{28,24},{1,5},{5... | collective-permute-start | bytes 7077896 | tf_op jit(solution)/shard_map/ppermute | solution.py:738
  108.3 9.4 %collective-permute-start.28 = (bf16[4,448,768]{2,1,0:T(8,128)(2,1)S(1)}, bf16[4,448,768]{2,1,0:T(8,128)(2,1)S(1)}, u32[]{:S(2)}, u32[]{:S(2)}) collective-permute-start(bf16[4,448,768]{2,1,0:T(8,128)(2,1)S(1)} %get-tuple-element.232), channel_id=1, source_target_pairs={{0,4},{4,0},{8,12},{12,8},{16,20},{20,16},{24,28},{28,24},{1,5},{5... | collective-permute-start | bytes 8257544 | tf_op jit(solution)/shard_map/ppermute | solution.py:738
  108.6 34.3 %collective-permute-start.37 = (bf16[2,4,96,768]{3,2,1,0:T(8,128)(2,1)S(1)}, bf16[2,4,96,768]{3,2,1,0:T(8,128)(2,1)S(1)}, u32[]{:S(2)}, u32[]{:S(2)}) collective-permute-start(bf16[2,4,96,768]{3,2,1,0:T(8,128)(2,1)S(1)} %get-tuple-element.244), channel_id=1, source_target_pairs={{0,16},{4,20},{8,24},{12,28},{16,0},{20,4},{24,8},{28,12},{1,17},{... | collective-permute-start | bytes 3538952 | tf_op jit(solution)/shard_map/ppermute | solution.py:738
  111.8 19.4 %collective-permute-start.29 = (bf16[480,768]{1,0:T(8,128)(2,1)S(1)}, bf16[480,768]{1,0:T(8,128)(2,1)S(1)}, u32[]{:S(2)}, u32[]{:S(2)}) collective-permute-start(bf16[480,768]{1,0:T(8,128)(2,1)S(1)} %get-tuple-element.236), channel_id=1, source_target_pairs={{1,0},{2,1},{3,2},{5,4},{6,5},{7,6},{9,8},{10,9},{11,10},{13,12},{... | collective-permute-start | bytes 2211848 | tf_op jit(solution)/shard_map/ppermute | solution.py:950
  115.1 19.1 %collective-permute-start.30 = (bf16[480,768]{1,0:T(8,128)(2,1)S(1)}, bf16[480,768]{1,0:T(8,128)(2,1)S(1)}, u32[]{:S(2)}, u32[]{:S(2)}) collective-permute-start(bf16[480,768]{1,0:T(8,128)(2,1)S(1)} %get-tuple-element.237), channel_id=1, source_target_pairs={{0,1},{1,2},{2,3},{4,5},{5,6},{6,7},{8,9},{9,10},{10,11},{12,13},{... | collective-permute-start | bytes 2211848 | tf_op jit(solution)/shard_map/ppermute | solution.py:951
  117.1 30.7 %collective-permute-start.34 = (bf16[2,4,112,768]{3,2,1,0:T(8,128)(2,1)S(1)}, bf16[2,4,112,768]{3,2,1,0:T(8,128)(2,1)S(1)}, u32[]{:S(2)}, u32[]{:S(2)}) collective-permute-start(bf16[2,4,112,768]{3,2,1,0:T(8,128)(2,1)S(1)} %get-tuple-element.241), channel_id=1, source_target_pairs={{0,8},{4,12},{8,0},{12,4},{16,24},{20,28},{24,16},{28,20},{1,9},{5... | collective-permute-start | bytes 4128776 | tf_op jit(solution)/shard_map/ppermute | solution.py:738
  137.1 18.1 %collective-permute-start.32 = (bf16[480,768]{1,0:T(8,128)(2,1)S(1)}, bf16[480,768]{1,0:T(8,128)(2,1)S(1)}, u32[]{:S(2)}, u32[]{:S(2)}) collective-permute-start(bf16[480,768]{1,0:T(8,128)(2,1)S(1)} %get-tuple-element.238.refs_2_), channel_id=1, source_target_pairs={{3,2},{2,1},{1,0},{7,6},{6,5},{5,4},{11,10},{10,9},{9,8},{15,14},{... | collective-permute-start | bytes 2211848 | tf_op jit(solution)/shard_map/ppermute | solution.py:966
  139.1 18.4 %collective-permute-start.31 = (bf16[480,768]{1,0:T(8,128)(2,1)S(1)}, bf16[480,768]{1,0:T(8,128)(2,1)S(1)}, u32[]{:S(2)}, u32[]{:S(2)}) collective-permute-start(bf16[480,768]{1,0:T(8,128)(2,1)S(1)} %get-tuple-element.238.refs_2_), channel_id=1, source_target_pairs={{0,1},{1,2},{2,3},{4,5},{5,6},{6,7},{8,9},{9,10},{10,11},{12,13},{... | collective-permute-start | bytes 2211848 | tf_op jit(solution)/shard_map/ppermute | solution.py:965
  142.4 20.1 %collective-permute-start.33 = (bf16[2,2,112,768]{3,2,1,0:T(8,128)(2,1)S(1)}, bf16[2,2,112,768]{3,2,1,0:T(8,128)(2,1)S(1)}, u32[]{:S(2)}, u32[]{:S(2)}) collective-permute-start(bf16[2,2,112,768]{3,2,1,0:T(8,128)(2,1)S(1)} %get-tuple-element.240), channel_id=1, source_target_pairs={{0,8},{4,12},{8,0},{12,4},{16,24},{20,28},{24,16},{28,20},{1,9},{5... | collective-permute-start | bytes 2064392 | tf_op jit(solution)/shard_map/ppermute | solution.py:738
  143.0 21.0 %collective-permute-start.36 = (bf16[2,2,112,768]{3,2,1,0:T(8,128)(2,1)S(1)}, bf16[2,2,112,768]{3,2,1,0:T(8,128)(2,1)S(1)}, u32[]{:S(2)}, u32[]{:S(2)}) collective-permute-start(bf16[2,2,112,768]{3,2,1,0:T(8,128)(2,1)S(1)} %get-tuple-element.243), channel_id=1, source_target_pairs={{0,16},{4,20},{8,24},{12,28},{16,0},{20,4},{24,8},{28,12},{1,17},{... | collective-permute-start | bytes 2064392 | tf_op jit(solution)/shard_map/ppermute | solution.py:738
  155.3 20.4 %collective-permute-start.43 = (bf16[480,768]{1,0:T(8,128)(2,1)S(1)}, bf16[480,768]{1,0:T(8,128)(2,1)}, u32[]{:S(2)}, u32[]{:S(2)}) collective-permute-start(bf16[480,768]{1,0:T(8,128)(2,1)S(1)} %collective-permute-done.32.refs_1_.refs_6_), channel_id=1, source_target_pairs={{2,1},{1,0},{6,5},{5,4},{10,9},{9,8},{14,13},{13,12},{18,17},{17,1... | collective-permute-start | bytes 2211848 | tf_op jit(solution)/shard_map/ppermute | solution.py:966
  157.5 20.1 %collective-permute-start.42 = (bf16[480,768]{1,0:T(8,128)(2,1)S(1)}, bf16[480,768]{1,0:T(8,128)(2,1)}, u32[]{:S(2)}, u32[]{:S(2)}) collective-permute-start(bf16[480,768]{1,0:T(8,128)(2,1)S(1)} %collective-permute-done.31.refs_0_.refs_3_), channel_id=1, source_target_pairs={{1,2},{2,3},{5,6},{6,7},{9,10},{10,11},{13,14},{14,15},{17,18},{18... | collective-permute-start | bytes 2211848 | tf_op jit(solution)/shard_map/ppermute | solution.py:965
  162.7 6.6 %collective-permute-start.35 = (bf16[2,112,768]{2,1,0:T(8,128)(2,1)S(1)}, bf16[2,112,768]{2,1,0:T(8,128)(2,1)S(1)}, u32[]{:S(2)}, u32[]{:S(2)}) collective-permute-start(bf16[2,112,768]{2,1,0:T(8,128)(2,1)S(1)} %get-tuple-element.282), channel_id=1, source_target_pairs={{0,16},{4,20},{8,24},{12,28},{16,0},{20,4},{24,8},{28,12},{1,17},{... | collective-permute-start | bytes 1032200 | tf_op jit(solution)/shard_map/ppermute | solution.py:738
  164.2 7.0 %collective-permute-start.38 = (bf16[2,112,768]{2,1,0:T(8,128)(2,1)S(1)}, bf16[2,112,768]{2,1,0:T(8,128)(2,1)S(1)}, u32[]{:S(2)}, u32[]{:S(2)}) collective-permute-start(bf16[2,112,768]{2,1,0:T(8,128)(2,1)S(1)} %get-tuple-element.280), channel_id=1, source_target_pairs={{0,8},{4,12},{8,0},{12,4},{16,24},{20,28},{24,16},{28,20},{1,9},{5... | collective-permute-start | bytes 1032200 | tf_op jit(solution)/shard_map/ppermute | solution.py:738
  172.3 9.7 %collective-permute-start.39 = (bf16[112,768]{1,0:T(8,128)(2,1)S(1)}, bf16[112,768]{1,0:T(8,128)(2,1)S(1)}, u32[]{:S(2)}, u32[]{:S(2)}) collective-permute-start(bf16[112,768]{1,0:T(8,128)(2,1)S(1)} %get-tuple-element.246), channel_id=1, source_target_pairs={{0,1},{1,2},{2,3},{3,0},{4,5},{5,6},{6,7},{7,4},{8,9},{9,10},{10,1... | collective-permute-start | bytes 516104 | tf_op jit(solution)/shard_map/ppermute | solution.py:971
  173.8 15.3 %collective-permute-start.40 = (bf16[112,768]{1,0:T(8,128)(2,1)S(1)}, bf16[112,768]{1,0:T(8,128)(2,1)S(1)}, u32[]{:S(2)}, u32[]{:S(2)}) collective-permute-start(bf16[112,768]{1,0:T(8,128)(2,1)S(1)} %get-tuple-element.247), channel_id=1, source_target_pairs={{0,2},{1,3},{2,0},{3,1},{4,6},{5,7},{6,4},{7,5},{8,10},{9,11},{10,... | collective-permute-start | bytes 516104 | tf_op jit(solution)/shard_map/ppermute | solution.py:971
  175.7 14.4 %collective-permute-start.41 = (bf16[112,768]{1,0:T(8,128)(2,1)S(1)}, bf16[112,768]{1,0:T(8,128)(2,1)S(1)}, u32[]{:S(2)}, u32[]{:S(2)}) collective-permute-start(bf16[112,768]{1,0:T(8,128)(2,1)S(1)} %get-tuple-element.248), channel_id=1, source_target_pairs={{0,3},{1,0},{2,1},{3,2},{4,7},{5,4},{6,5},{7,6},{8,11},{9,8},{10,9... | collective-permute-start | bytes 516104 | tf_op jit(solution)/shard_map/ppermute | solution.py:971
  179.9 21.8 %collective-permute-start.58 = (bf16[4,112,768]{2,1,0:T(8,128)(2,1)S(1)}, bf16[4,112,768]{2,1,0:T(8,128)(2,1)S(1)}, u32[]{:S(2)}, u32[]{:S(2)}) collective-permute-start(bf16[4,112,768]{2,1,0:T(8,128)(2,1)S(1)} %get-tuple-element.276), channel_id=1, source_target_pairs={{0,16},{4,20},{8,24},{12,28},{16,0},{20,4},{24,8},{28,12},{1,17},{... | collective-permute-start | bytes 2064392 | tf_op jit(solution)/shard_map/ppermute | solution.py:738
  181.4 20.3 %collective-permute-start.59 = (bf16[4,96,768]{2,1,0:T(8,128)(2,1)S(1)}, bf16[4,96,768]{2,1,0:T(8,128)(2,1)S(1)}, u32[]{:S(2)}, u32[]{:S(2)}) collective-permute-start(bf16[4,96,768]{2,1,0:T(8,128)(2,1)S(1)} %get-tuple-element.278), channel_id=1, source_target_pairs={{0,8},{4,12},{8,0},{12,4},{16,24},{20,28},{24,16},{28,20},{1,9},{5... | collective-permute-start | bytes 1769480 | tf_op jit(solution)/shard_map/ppermute | solution.py:738
  190.2 7.5 %collective-permute-start.46 = (bf16[112,768]{1,0:T(8,128)(2,1)S(1)}, bf16[112,768]{1,0:T(8,128)(2,1)S(1)}, u32[]{:S(2)}, u32[]{:S(2)}) collective-permute-start(bf16[112,768]{1,0:T(8,128)(2,1)S(1)} %add_convert_fusion.9), channel_id=1, source_target_pairs={{0,1},{1,2},{2,3},{3,0},{4,5},{5,6},{6,7},{7,4},{8,9},{9,10},{10,1... | collective-permute-start | bytes 516104 | tf_op jit(solution)/shard_map/ppermute | solution.py:829
  190.3 11.4 %collective-permute-start.45 = (bf16[112,768]{1,0:T(8,128)(2,1)S(1)}, bf16[112,768]{1,0:T(8,128)(2,1)S(1)}, u32[]{:S(2)}, u32[]{:S(2)}) collective-permute-start(bf16[112,768]{1,0:T(8,128)(2,1)S(1)} %add_convert_fusion.9), channel_id=1, source_target_pairs={{0,2},{1,3},{2,0},{3,1},{4,6},{5,7},{6,4},{7,5},{8,10},{9,11},{10,... | collective-permute-start | bytes 516104 | tf_op jit(solution)/shard_map/ppermute | solution.py:829
  192.1 9.5 %collective-permute-start.44 = (bf16[112,768]{1,0:T(8,128)(2,1)S(1)}, bf16[112,768]{1,0:T(8,128)(2,1)S(1)}, u32[]{:S(2)}, u32[]{:S(2)}) collective-permute-start(bf16[112,768]{1,0:T(8,128)(2,1)S(1)} %add_convert_fusion.9), channel_id=1, source_target_pairs={{0,3},{1,0},{2,1},{3,2},{4,7},{5,4},{6,5},{7,6},{8,11},{9,8},{10,9... | collective-permute-start | bytes 516104 | tf_op jit(solution)/shard_map/ppermute | solution.py:829
  203.7 15.5 %collective-permute-start.48 = (bf16[4,112,768]{2,1,0:T(8,128)(2,1)S(1)}, bf16[4,112,768]{2,1,0:T(8,128)(2,1)S(1)}, u32[]{:S(2)}, u32[]{:S(2)}) collective-permute-start(bf16[4,112,768]{2,1,0:T(8,128)(2,1)S(1)} %pad_maximum_fusion.refs_1_), channel_id=1, source_target_pairs={{0,16},{4,20},{8,24},{12,28},{16,0},{20,4},{24,8},{28,12},{1,17},{... | collective-permute-start | bytes 2064392 | tf_op jit(solution)/shard_map/ppermute | solution.py:738
  208.3 12.9 %collective-permute-start.47 = (bf16[4,112,768]{2,1,0:T(8,128)(2,1)S(1)}, bf16[4,112,768]{2,1,0:T(8,128)(2,1)S(1)}, u32[]{:S(2)}, u32[]{:S(2)}) collective-permute-start(bf16[4,112,768]{2,1,0:T(8,128)(2,1)S(1)} %pad_maximum_fusion.refs_1_), channel_id=1, source_target_pairs={{0,8},{4,12},{8,0},{12,4},{16,24},{20,28},{24,16},{28,20},{1,9},{5... | collective-permute-start | bytes 2064392 | tf_op jit(solution)/shard_map/ppermute | solution.py:738
  208.8 28.4 %collective-permute-start.51 = (bf16[4,112,768]{2,1,0:T(8,128)(2,1)S(1)}, bf16[4,112,768]{2,1,0:T(8,128)(2,1)S(1)}, u32[]{:S(2)}, u32[]{:S(2)}) collective-permute-start(bf16[4,112,768]{2,1,0:T(8,128)(2,1)S(1)} %pad_maximum_fusion.refs_1_), channel_id=1, source_target_pairs={{0,4},{4,0},{8,12},{12,8},{16,20},{20,16},{24,28},{28,24},{1,5},{5... | collective-permute-start | bytes 2064392 | tf_op jit(solution)/shard_map/ppermute | solution.py:738
  219.3 10.7 %collective-permute-start.50 = (bf16[2,112,768]{2,1,0:T(8,128)(2,1)S(1)}, bf16[2,112,768]{2,1,0:T(8,128)(2,1)S(1)}, u32[]{:S(2)}, u32[]{:S(2)}) collective-permute-start(bf16[2,112,768]{2,1,0:T(8,128)(2,1)S(1)} %slice.123), channel_id=1, source_target_pairs={{0,8},{4,12},{8,0},{12,4},{16,24},{20,28},{24,16},{28,20},{1,9},{5... | collective-permute-start | bytes 1032200 | tf_op jit(solution)/shard_map/ppermute | solution.py:738
  221.2 12.3 %collective-permute-start.49 = (bf16[2,112,768]{2,1,0:T(8,128)(2,1)S(1)}, bf16[2,112,768]{2,1,0:T(8,128)(2,1)S(1)}, u32[]{:S(2)}, u32[]{:S(2)}) collective-permute-start(bf16[2,112,768]{2,1,0:T(8,128)(2,1)S(1)} %slice.122), channel_id=1, source_target_pairs={{0,16},{4,20},{8,24},{12,28},{16,0},{20,4},{24,8},{28,12},{1,17},{... | collective-permute-start | bytes 1032200 | tf_op jit(solution)/shard_map/ppermute | solution.py:738
  222.5 18.3 %collective-permute-start.53 = (bf16[4,112,768]{2,1,0:T(8,128)(2,1)S(1)}, bf16[4,112,768]{2,1,0:T(8,128)(2,1)S(1)}, u32[]{:S(2)}, u32[]{:S(2)}) collective-permute-start(bf16[4,112,768]{2,1,0:T(8,128)(2,1)S(1)} %collective-permute-done.48.refs_3_), channel_id=1, source_target_pairs={{0,4},{4,0},{8,12},{12,8},{16,20},{20,16},{24,28},{28,24},{1,5},{5... | collective-permute-start | bytes 2064392 | tf_op jit(solution)/shard_map/ppermute | solution.py:738
  229.9 10.9 %collective-permute-start.52 = (bf16[4,112,768]{2,1,0:T(8,128)(2,1)S(1)}, bf16[4,112,768]{2,1,0:T(8,128)(2,1)S(1)}, u32[]{:S(2)}, u32[]{:S(2)}) collective-permute-start(bf16[4,112,768]{2,1,0:T(8,128)(2,1)S(1)} %collective-permute-done.47.refs_2_), channel_id=1, source_target_pairs={{0,4},{4,0},{8,12},{12,8},{16,20},{20,16},{24,28},{28,24},{1,5},{5... | collective-permute-start | bytes 2064392 | tf_op jit(solution)/shard_map/ppermute | solution.py:738
  230.0 9.3 %collective-permute-start.55 = (bf16[2,112,768]{2,1,0:T(8,128)(2,1)S(1)}, bf16[2,112,768]{2,1,0:T(8,128)(2,1)S(1)}, u32[]{:S(2)}, u32[]{:S(2)}) collective-permute-start(bf16[2,112,768]{2,1,0:T(8,128)(2,1)S(1)} %collective-permute-done.50.refs_5_), channel_id=1, source_target_pairs={{0,4},{4,0},{8,12},{12,8},{16,20},{20,16},{24,28},{28,24},{1,5},{5... | collective-permute-start | bytes 1032200 | tf_op jit(solution)/shard_map/ppermute | solution.py:738
  233.5 7.3 %collective-permute-start.54 = (bf16[2,112,768]{2,1,0:T(8,128)(2,1)S(1)}, bf16[2,112,768]{2,1,0:T(8,128)(2,1)S(1)}, u32[]{:S(2)}, u32[]{:S(2)}) collective-permute-start(bf16[2,112,768]{2,1,0:T(8,128)(2,1)S(1)} %collective-permute-done.49.refs_4_), channel_id=1, source_target_pairs={{0,4},{4,0},{8,12},{12,8},{16,20},{20,16},{24,28},{28,24},{1,5},{5... | collective-permute-start | bytes 1032200 | tf_op jit(solution)/shard_map/ppermute | solution.py:738
  237.1 22.4 %collective-permute-start.57 = (bf16[480,768]{1,0:T(8,128)(2,1)}, bf16[480,768]{1,0:T(8,128)(2,1)}, u32[]{:S(2)}, u32[]{:S(2)}) collective-permute-start(bf16[480,768]{1,0:T(8,128)(2,1)} %collective-permute-done.43.refs_7_), channel_id=1, source_target_pairs={{1,0},{5,4},{9,8},{13,12},{17,16},{21,20},{25,24},{29,28}} | collective-permute-start | bytes 2211848 | tf_op jit(solution)/shard_map/ppermute | solution.py:966
  239.3 21.6 %collective-permute-start.56 = (bf16[480,768]{1,0:T(8,128)(2,1)}, bf16[480,768]{1,0:T(8,128)(2,1)}, u32[]{:S(2)}, u32[]{:S(2)}) collective-permute-start(bf16[480,768]{1,0:T(8,128)(2,1)} %collective-permute-done.42.refs_4_), channel_id=1, source_target_pairs={{2,3},{6,7},{10,11},{14,15},{18,19},{22,23},{26,27},{30,31}} | collective-permute-start | bytes 2211848 | tf_op jit(solution)/shard_map/ppermute | solution.py:965
  249.0 9.2 %collective-permute-start.60 = (bf16[208,768]{1,0:T(8,128)(2,1)S(1)}, bf16[208,768]{1,0:T(8,128)(2,1)S(1)}, u32[]{:S(2)}, u32[]{:S(2)}) collective-permute-start(bf16[208,768]{1,0:T(8,128)(2,1)S(1)} %fusion.8.refs_1_), channel_id=1, source_target_pairs={{0,8},{4,12},{8,0},{12,4},{16,24},{20,28},{24,16},{28,20},{1,9},{5... | collective-permute-start | bytes 958472 | tf_op jit(solution)/shard_map/ppermute | solution.py:738
  249.3 9.9 %collective-permute-start.61 = (bf16[208,768]{1,0:T(8,128)(2,1)S(1)}, bf16[208,768]{1,0:T(8,128)(2,1)S(1)}, u32[]{:S(2)}, u32[]{:S(2)}) collective-permute-start(bf16[208,768]{1,0:T(8,128)(2,1)S(1)} %fusion.8.refs_1_), channel_id=1, source_target_pairs={{0,16},{4,20},{8,24},{12,28},{16,0},{20,4},{24,8},{28,12},{1,17},{... | collective-permute-start | bytes 958472 | tf_op jit(solution)/shard_map/ppermute | solution.py:738
  258.3 7.5 %collective-permute-start.62 = (bf16[112,768]{1,0:T(8,128)(2,1)S(1)}, bf16[112,768]{1,0:T(8,128)(2,1)S(1)}, u32[]{:S(2)}, u32[]{:S(2)}) collective-permute-start(bf16[112,768]{1,0:T(8,128)(2,1)S(1)} %slice.128), channel_id=1, source_target_pairs={{0,16},{4,20},{8,24},{12,28},{16,0},{20,4},{24,8},{28,12},{1,17},{... | collective-permute-start | bytes 516104 | tf_op jit(solution)/shard_map/ppermute | solution.py:738
  258.4 8.6 %collective-permute-start.64 = (bf16[208,768]{1,0:T(8,128)(2,1)S(1)}, bf16[208,768]{1,0:T(8,128)(2,1)}, u32[]{:S(2)}, u32[]{:S(2)}) collective-permute-start(bf16[208,768]{1,0:T(8,128)(2,1)S(1)} %fusion.8.refs_1_), channel_id=1, source_target_pairs={{0,4},{4,0},{8,12},{12,8},{16,20},{20,16},{24,28},{28,24},{1,5},{5... | collective-permute-start | bytes 958472 | tf_op jit(solution)/shard_map/ppermute | solution.py:738
  259.2 6.5 %collective-permute-start.63 = (bf16[96,768]{1,0:T(8,128)(2,1)S(1)}, bf16[96,768]{1,0:T(8,128)(2,1)S(1)}, u32[]{:S(2)}, u32[]{:S(2)}) collective-permute-start(bf16[96,768]{1,0:T(8,128)(2,1)S(1)} %slice.129), channel_id=1, source_target_pairs={{0,8},{4,12},{8,0},{12,4},{16,24},{20,28},{24,16},{28,20},{1,9},{5... | collective-permute-start | bytes 442376 | tf_op jit(solution)/shard_map/ppermute | solution.py:738
  259.5 7.5 %collective-permute-start.66 = (bf16[208,768]{1,0:T(8,128)(2,1)S(1)}, bf16[208,768]{1,0:T(8,128)(2,1)}, u32[]{:S(2)}, u32[]{:S(2)}) collective-permute-start(bf16[208,768]{1,0:T(8,128)(2,1)S(1)} %collective-permute-done.61.refs_3_), channel_id=1, source_target_pairs={{0,4},{4,0},{8,12},{12,8},{16,20},{20,16},{24,28},{28,24},{1,5},{5... | collective-permute-start | bytes 958472 | tf_op jit(solution)/shard_map/ppermute | solution.py:738
  260.9 6.1 %collective-permute-start.65 = (bf16[208,768]{1,0:T(8,128)(2,1)S(1)}, bf16[208,768]{1,0:T(8,128)(2,1)}, u32[]{:S(2)}, u32[]{:S(2)}) collective-permute-start(bf16[208,768]{1,0:T(8,128)(2,1)S(1)} %collective-permute-done.60.refs_2_), channel_id=1, source_target_pairs={{0,4},{4,0},{8,12},{12,8},{16,20},{20,16},{24,28},{28,24},{1,5},{5... | collective-permute-start | bytes 958472 | tf_op jit(solution)/shard_map/ppermute | solution.py:738
  (30 other events, 146.2 us)
Sparse Core Ops, SparseCore 0:
  203.8 34.3 reduce-scatter.1

commit v7 on v6

--- a/solution.py
+++ b/solution.py
@@ -194,7 +194,7 @@
             )
         return carry
 
-    lax.fori_loop(0, HEADS // 2, one_pair, 0, unroll=2)
+    lax.fori_loop(0, HEADS // 2, one_pair, 0, unroll=3)
     cl[...] = cl_acc[:, :layout_width].astype(BF)
 
 
@@ -535,7 +535,7 @@
             vl_acc[keys_at, group_lanes] += both[:, LANES:]
         return carry
 
-    lax.fori_loop(0, HEADS // 2, one_pair, 0, unroll=2)
+    lax.fori_loop(0, HEADS // 2, one_pair, 0, unroll=3)
     middle = pl.ds(pad, window)
     dk[middle, :] = k_acc[...].astype(BF)
     dv[middle, :] = v_acc[...].astype(BF)

time: 284 us -> 284 us (level)
  the two profiles are of different devices: /device:TPU:9 before, /device:TPU:17 now
where the time goes in v7:
time: 284 us; the launch traced here: 279 us
  starting transfers between devices  93.9 us (33%)
  Pallas kernels  81.4 us (29%)
  waiting for transfers between devices  69.8 us (25%)
  between operations  18.4 us (6%)
  local copies, waits for them, and re-layouts  12.2 us (4%)
  other arithmetic  3.55 us (1%)
    pallas_call x19, Pallas kernels, call(): pl.pallas_call(with_token, out_shape=tuple((shape(o.shape, o.dtype) for o...  81.4 us
    ppermute x52, starting transfers between devices, around(): return lambda v, bit: lax.ppermute(v, 'dp', flip(planes, bit))  59.4 us
    ppermute x52, waiting for transfers between devices, around(): return lambda v, bit: lax.ppermute(v, 'dp', flip(planes, bit))  32.9 us
    ppermute x6, waiting for transfers between devices, per_device(): from_group = lambda v, k: lax.ppermute(v, 'tensor', shift_from(k))  13.4 us
    ppermute x1, waiting for transfers between devices, per_device(): lax.ppermute(left, 'tensor', [(i + 1, i) for i in range(groups - 1)])  10.7 us
    ppermute x3, starting transfers between devices, per_device(): lax.ppermute(v, 'tensor', [(i, i + 1) for i in range(far, groups - 1)])  9.33 us
    ppermute x3, starting transfers between devices, per_device(): lax.ppermute(v, 'tensor', [(i, i - 1) for i in range(groups - 1 - far, 0,...  8.95 us
    ppermute x6, starting transfers between devices, per_device(): from_group = lambda v, k: lax.ppermute(v, 'tensor', shift_from(k))  7.41 us
  transfers between devices with their start and end apart: 70, of which 21 were waited for; matrix products, arithmetic and copies ran while one was open for 3% of the time, Pallas kernels for 19%

profile of v7, /device:TPU:17, one launch (start us, length us, event | category | flops | bytes accessed | tf_op | source)
XLA Modules:
  0.0 279.4 jit_solution(1608399339840333968)
XLA Ops:
  8.8 1.2 constant_dynamic-slice_fusion.1
  10.8 1.3 collective-permute-start.1
  13.5 2.0 copy-done.1
  17.5 4.7 %project.1 = (bf16[384,768]{1,0:T(8,128)(2,1)S(1)}, bf16[1024,768]{1,0:T(8,128)(2,1)S(1)}, bf16[1024,768]{1,0:T(8,128)(2,1)S(1)}, bf16[384,256]{1,0:T(8,128)(2,1...) custom-call(f32[8,128]{1,0:T(8,128)S(1)} %get-tuple-element.147.refs, ...), custom_call_target="tpu_custom_call" | custom-call | flops 1000000000 | tf_op jit(solution)/shard_map/project/pallas_call | solution.py:703
  22.3 4.0 %collective-permute-done.refs_1_ = bf16[208,768]{1,0:T(8,128)(2,1)S(1)} collective-permute-done((bf16[208,768]{1,0:T(8,128)(2,1)S(1)}, bf16[208,768]{1,0:T(8,128)(2,1)S(1)}, u32[]{:S(2)}, u32[]{:S(2)}) %collective-permute-start) | collective-permute-done | bytes 319520 | tf_op jit(solution)/shard_map/ppermute | solution.py:829
  26.2 1.6 collective-permute-start.6
  27.8 1.2 collective-permute-start.3
  29.1 1.2 collective-permute-start.2
  30.8 7.1 %attend.1 = (bf16[384,768]{1,0:T(8,128)(2,1)S(1)}, bf16[384,192]{1,0:T(8,128)(2,1)S(1)}, f32[384,128]{1,0:T(8,128)S(1)}, f32[8,128]{1,0:T(8,128)S(1)}) custom-call(s32[26]{0:T(128)S(1)} %concatenate.9.refs_1_.refs_0_.refs_2_.refs_3_, bf16[384,768]{1,0:T(8,128)(2,1)S(1)} %get-tuple-element.149.refs_1_.refs_2_, ...), custom_call_target="tpu_custom_call" | custom-call | flops 1800000000 | tf_op jit(solution)/shard_map/attend/pallas_call | solution.py:703
  37.9 2.8 collective-permute-done.6.refs_5_
  40.7 1.6 collective-permute-done.5.refs_3_
  43.6 1.2 collective-permute-start.8
  44.8 1.2 collective-permute-start.18
  46.0 3.0 %first_norm.1 = (f32[384,768]{1,0:T(8,128)S(1)}, f32[384,192]{1,0:T(8,128)S(1)}, bf16[384,768]{1,0:T(8,128)(2,1)S(1)}, bf16[384,192]{1,0:T(8,128)(2,1)S(1)}, f32...) custom-call(s32[26]{0:T(128)S(1)} %concatenate.9.refs_1_.refs_0_.ref, ...), custom_call_target="tpu_custom_call" | custom-call | flops 600000000 | tf_op jit(solution)/shard_map/first_norm/pallas_call | solution.py:703
  49.8 6.6 %collective-permute-start.10 = (bf16[208,768]{1,0:T(8,128)(2,1)S(1)}, bf16[208,768]{1,0:T(8,128)(2,1)S(1)}, u32[]{:S(2)}, u32[]{:S(2)}) collective-permute-start(bf16[208,768]{1,0:T(8,128)(2,1)S(1)} %get-tuple-element.173.refs_4_), channel_id=1, source_target_pairs={{0,4},{4,0},{8,12},{12,8},{16,20},{20,16},{24,28},{28,24},{1,5},{5... | collective-permute-start | bytes 958472 | tf_op jit(solution)/shard_map/ppermute | solution.py:738
  56.9 3.2 %collective-permute-start.14 = (bf16[208,768]{1,0:T(8,128)(2,1)S(1)}, bf16[208,768]{1,0:T(8,128)(2,1)S(1)}, u32[]{:S(2)}, u32[]{:S(2)}) collective-permute-start(bf16[208,768]{1,0:T(8,128)(2,1)S(1)} %get-tuple-element.178.refs_4_), channel_id=1, source_target_pairs={{0,4},{4,0},{8,12},{12,8},{16,20},{20,16},{24,28},{28,24},{1,5},{5... | collective-permute-start | bytes 958472 | tf_op jit(solution)/shard_map/ppermute | solution.py:738
  61.3 1.2 collective-permute-start.20
  64.8 2.8 shard.2
  67.6 2.2 shard.3
  70.4 1.2 collective-permute-done.24.refs_40_
  71.6 11.2 %turn.1 = (bf16[384,768]{1,0:T(8,128)(2,1)}, bf16[384,768]{1,0:T(8,128)(2,1)S(1)}, bf16[4,384,768]{2,1,0:T(8,128)(2,1)S(1)}, f32[4,768]{1,0:T(4,128)S(1)}, f32[4...) custom-call(s32[26]{0:T(128)S(1)} %concatenate.9.refs_1_.refs_0_.ref, ...), custom_call_target="tpu_custom_call" | custom-call | flops 2400000000 | tf_op jit(solution)/shard_map/turn/pallas_call | solution.py:703
  82.9 3.2 %ffn_send.1 = (bf16[4,448,768]{2,1,0:T(8,128)(2,1)S(1)}, bf16[4,384,768]{2,1,0:T(8,128)(2,1)S(1)}, f32[8,128]{1,0:T(8,128)S(1)}) custom-call(s32[26]{0:T(128)S(1)} %concatenate.9.refs_1_.refs_0_.refs_2_.refs_3_, bf16[384,768]{1,0:T(8,128)(2,1)S(1)} %get-tuple-element.185.refs_11_.refs_1_.refs_2_, ...), custom_call_target="tpu_custom_call" | custom-call | flops 800000000 | tf_op jit(solution)/shard_map/ffn_send/pallas_call | solution.py:703
  86.7 14.0 %attend_back.1 = (bf16[384,768]{1,0:T(8,128)(2,1)S(1)}, bf16[1792,768]{1,0:T(8,128)(2,1)S(1)}, bf16[1792,768]{1,0:T(8,128)(2,1)S(1)}, bf16[384,256]{1,0:T(8,128)...) custom-call(f32[8,128]{1,0:T(8,128)S(1)} %get-tuple-element.206.refs_0_, ...), custom_call_target="tpu_custom_call" | custom-call | flops 3000000000 | tf_op jit(solution)/shard_map/attend_back/pallas_call | solution.py:703
  100.7 3.6 %ffn_keep.1 = (bf16[2,4,112,768]{3,2,1,0:T(8,128)(2,1)S(1)}, bf16[2,4,96,768]{3,2,1,0:T(8,128)(2,1)S(1)}, bf16[2,4,112,768]{3,2,1,0:T(8,128)(2,1)S(1)}, bf16[2,4,96,768]{3,2,1,0:T(8,128)(2,1)S(1)}, f32[8,128]{1,0:T(8,128)S(1)}) custom-call(f32[8,128]{1,0:T(8,128)S(1)} %get-tuple-element.210.refs_0_, s32[26]{0:T(128)S(1)} %concatenate.9.refs_1_.refs_0_.refs_2_.refs_3_, ...), custom_call_target="tpu_custom_call" | custom-call | flops 800000000 | tf_op jit(solution)/shard_map/ffn_keep/pallas_call | solution.py:703
  104.3 3.3 %copied_send.1 = (bf16[4,448,768]{2,1,0:T(8,128)(2,1)S(1)}, bf16[512,768]{1,0:T(8,128)(2,1)S(1)}, f32[8,128]{1,0:T(8,128)S(1)}) custom-call(f32[8,128]{1,0:T(8,128)S(1)} %get-tuple-element.213.refs_0_, s32[26]{0:T(128)S(1)} %concatenate.9.refs_1_.refs_0_.refs_2_.refs_3_, bf16[1536,768]{1,0:T(8,128)(2,1)S(1)} %copy-done, ...), custom_call_target="tpu_custom_call" | custom-call | flops 800000000 | tf_op jit(solution)/shard_map/copied_send/pallas_call | solution.py:703
  108.4 2.8 %sides.1 = (bf16[480,768]{1,0:T(8,128)(2,1)S(1)}, bf16[480,768]{1,0:T(8,128)(2,1)S(1)}, f32[8,128]{1,0:T(8,128)S(1)}) custom-call(f32[8,128]{1,0:T(8,128)S(1)} %get-tuple-element.228.refs_0_, s32[26]{0:T(128)S(1)} %concatenate.9.refs_1_.refs_0_.refs_2_.refs_3_, bf16[768,2304]{1,0:T(8,128)(2,1)S(1)} %copy-done.2, ...), custom_call_target="tpu_custom_call" | custom-call | flops 600000000 | tf_op jit(solution)/shard_map/sides/pallas_call | solution.py:703
  111.3 2.1 collective-permute-start.29
  113.4 3.2 %collective-permute-start.30 = (bf16[480,768]{1,0:T(8,128)(2,1)S(1)}, bf16[480,768]{1,0:T(8,128)(2,1)S(1)}, u32[]{:S(2)}, u32[]{:S(2)}) collective-permute-start(bf16[480,768]{1,0:T(8,128)(2,1)S(1)} %get-tuple-element.237), channel_id=1, source_target_pairs={{0,1},{1,2},{2,3},{4,5},{5,6},{6,7},{8,9},{9,10},{10,11},{12,13},{... | collective-permute-start | bytes 2211848 | tf_op jit(solution)/shard_map/ppermute | solution.py:951
  117.1 2.9 %copied_keep.1 = (bf16[2,2,112,768]{3,2,1,0:T(8,128)(2,1)S(1)}, bf16[2,2,112,768]{3,2,1,0:T(8,128)(2,1)S(1)}, bf16[2,2,112,768]{3,2,1,0:T(8,128)(2,1)S(1)}, bf16...) custom-call(f32[8,128]{1,0:T(8,128)S(1)} %get-tuple-element.230.refs_0_, s32[26]{0:T(128)S(1)} %concatenate.9.refs_1_.refs_0_.refs_2_.refs_3_, ...), custom_call_target="tpu_custom_call" | custom-call | flops 600000000 | tf_op jit(solution)/shard_map/copied_keep/pallas_call | solution.py:703
  120.1 10.7 %collective-permute-done.29.refs_12_ = bf16[480,768]{1,0:T(8,128)(2,1)S(1)} collective-permute-done((bf16[480,768]{1,0:T(8,128)(2,1)S(1)}, bf16[480,768]{1,0:T(8,128)(2,1)S(1)}, u32[]{:S(2)}, u32[]{:S(2)}) %collective-permute-start.29) | collective-permute-done | bytes 737312 | tf_op jit(solution)/shard_map/ppermute | solution.py:950
  130.7 1.8 collective-permute-done.30.refs_13_
  132.6 3.0 %own.1 = (bf16[480,768]{1,0:T(8,128)(2,1)S(1)}, f32[8,128]{1,0:T(8,128)}) custom-call(f32[8,128]{1,0:T(8,128)S(1)} %get-tuple-element.233.refs_0_, s32[26]{0:T(128)S(1)} %concatenate.9.refs_1_.refs_0_.refs_2_.refs_3_, bf16[768,2304]{1,0:T(8,128)(2,1)S(1)} %copy-done.2, bf16[192,768]{1,0:T(8,128)(2,1)S(1)} %get-tuple-element.229.refs_3_, ...), custom_call_target="tpu_custom_call" | custom-call | flops 600000000 | tf_op jit(solution)/shard_map/own/pallas_call | solution.py:703
  135.5 3.3 %collective-permute-start.32 = (bf16[480,768]{1,0:T(8,128)(2,1)S(1)}, bf16[480,768]{1,0:T(8,128)(2,1)S(1)}, u32[]{:S(2)}, u32[]{:S(2)}) collective-permute-start(bf16[480,768]{1,0:T(8,128)(2,1)S(1)} %get-tuple-element.238.refs_2_), channel_id=1, source_target_pairs={{3,2},{2,1},{1,0},{7,6},{6,5},{5,4},{11,10},{10,9},{9,8},{15,14},{... | collective-permute-start | bytes 2211848 | tf_op jit(solution)/shard_map/ppermute | solution.py:966
  138.8 2.0 collective-permute-start.31
  143.7 3.6 %collective-permute-done.34 = bf16[2,4,112,768]{3,2,1,0:T(8,128)(2,1)S(1)} collective-permute-done((bf16[2,4,112,768]{3,2,1,0:T(8,128)(2,1)S(1)}, bf16[2,4,112,768]{3,2,1,0:T(8,128)(2,1)S(1)}, u32[]{:S(2)}, u32[]{:S(2)}) %collective-permute-start.34) | collective-permute-done | bytes 1376288 | tf_op jit(solution)/shard_map/ppermute | solution.py:738
  148.5 5.3 %collective-permute-done.32.refs_1_.refs_6_ = bf16[480,768]{1,0:T(8,128)(2,1)S(1)} collective-permute-done((bf16[480,768]{1,0:T(8,128)(2,1)S(1)}, bf16[480,768]{1,0:T(8,128)(2,1)S(1)}, u32[]{:S(2)}, u32[]{:S(2)}) %collective-permute-start.32) | collective-permute-done | bytes 737312 | tf_op jit(solution)/shard_map/ppermute | solution.py:966
  153.7 4.1 %collective-permute-start.43 = (bf16[480,768]{1,0:T(8,128)(2,1)S(1)}, bf16[480,768]{1,0:T(8,128)(2,1)}, u32[]{:S(2)}, u32[]{:S(2)}) collective-permute-start(bf16[480,768]{1,0:T(8,128)(2,1)S(1)} %collective-permute-done.32.refs_1_.refs_6_), channel_id=1, source_target_pairs={{2,1},{1,0},{6,5},{5,4},{10,9},{9,8},{14,13},{13,12},{18,17},{17,1... | collective-permute-start | bytes 2211848 | tf_op jit(solution)/shard_map/ppermute | solution.py:966
  157.9 2.2 collective-permute-start.42
  160.0 2.0 collective-permute-done.33
  164.0 5.9 %collective-permute-done.35.refs_4_ = bf16[2,112,768]{2,1,0:T(8,128)(2,1)S(1)} collective-permute-done((bf16[2,112,768]{2,1,0:T(8,128)(2,1)S(1)}, bf16[2,112,768]{2,1,0:T(8,128)(2,1)S(1)}, u32[]{:S(2)}, u32[]{:S(2)}) %collective-permute-start.35) | collective-permute-done | bytes 344096 | tf_op jit(solution)/shard_map/ppermute | solution.py:738
  170.9 1.1 copied_spread.1
  173.2 2.3 collective-permute-start.41
  175.5 1.2 slice.121
  177.4 1.2 slice.120
  181.7 4.3 %collective-permute-done.39 = bf16[112,768]{1,0:T(8,128)(2,1)S(1)} collective-permute-done((bf16[112,768]{1,0:T(8,128)(2,1)S(1)}, bf16[112,768]{1,0:T(8,128)(2,1)S(1)}, u32[]{:S(2)}, u32[]{:S(2)}) %collective-permute-start.39) | collective-permute-done | bytes 172064 | tf_op jit(solution)/shard_map/ppermute | solution.py:971
  186.0 1.5 collective-permute-done.41
  187.6 3.1 %collective-permute-start.46 = (bf16[112,768]{1,0:T(8,128)(2,1)S(1)}, bf16[112,768]{1,0:T(8,128)(2,1)S(1)}, u32[]{:S(2)}, u32[]{:S(2)}) collective-permute-start(bf16[112,768]{1,0:T(8,128)(2,1)S(1)} %add_convert_fusion.9), channel_id=1, source_target_pairs={{0,1},{1,2},{2,3},{3,0},{4,5},{5,6},{6,7},{7,4},{8,9},{9,10},{10,1... | collective-permute-start | bytes 516104 | tf_op jit(solution)/shard_map/ppermute | solution.py:829
  191.9 6.6 %collective-permute-done.46.refs_2_ = bf16[112,768]{1,0:T(8,128)(2,1)S(1)} collective-permute-done((bf16[112,768]{1,0:T(8,128)(2,1)S(1)}, bf16[112,768]{1,0:T(8,128)(2,1)S(1)}, u32[]{:S(2)}, u32[]{:S(2)}) %collective-permute-start.46) | collective-permute-done | bytes 172064 | tf_op jit(solution)/shard_map/ppermute | solution.py:829
  198.6 1.9 ffn_spread.1
  200.6 5.5 %collective-permute-start.48 = (bf16[4,112,768]{2,1,0:T(8,128)(2,1)S(1)}, bf16[4,112,768]{2,1,0:T(8,128)(2,1)S(1)}, u32[]{:S(2)}, u32[]{:S(2)}) collective-permute-start(bf16[4,112,768]{2,1,0:T(8,128)(2,1)S(1)} %pad_maximum_fusion.refs_1_), channel_id=1, source_target_pairs={{0,16},{4,20},{8,24},{12,28},{16,0},{20,4},{24,8},{28,12},{1,17},{... | collective-permute-start | bytes 2064392 | tf_op jit(solution)/shard_map/ppermute | solution.py:738
  206.5 4.5 %collective-permute-start.51 = (bf16[4,112,768]{2,1,0:T(8,128)(2,1)S(1)}, bf16[4,112,768]{2,1,0:T(8,128)(2,1)S(1)}, u32[]{:S(2)}, u32[]{:S(2)}) collective-permute-start(bf16[4,112,768]{2,1,0:T(8,128)(2,1)S(1)} %pad_maximum_fusion.refs_1_), channel_id=1, source_target_pairs={{0,4},{4,0},{8,12},{12,8},{16,20},{20,16},{24,28},{28,24},{1,5},{5... | collective-permute-start | bytes 2064392 | tf_op jit(solution)/shard_map/ppermute | solution.py:738
  210.9 5.6 %collective-permute-done.48.refs_3_ = bf16[4,112,768]{2,1,0:T(8,128)(2,1)S(1)} collective-permute-done((bf16[4,112,768]{2,1,0:T(8,128)(2,1)S(1)}, bf16[4,112,768]{2,1,0:T(8,128)(2,1)S(1)}, u32[]{:S(2)}, u32[]{:S(2)}) %collective-permute-start.48) | collective-permute-done | bytes 688160 | tf_op jit(solution)/shard_map/ppermute | solution.py:738
  218.5 1.3 collective-permute-start.49
  219.8 8.0 %collective-permute-start.53 = (bf16[4,112,768]{2,1,0:T(8,128)(2,1)S(1)}, bf16[4,112,768]{2,1,0:T(8,128)(2,1)S(1)}, u32[]{:S(2)}, u32[]{:S(2)}) collective-permute-start(bf16[4,112,768]{2,1,0:T(8,128)(2,1)S(1)} %collective-permute-done.48.refs_3_), channel_id=1, source_target_pairs={{0,4},{4,0},{8,12},{12,8},{16,20},{20,16},{24,28},{28,24},{1,5},{5... | collective-permute-start | bytes 2064392 | tf_op jit(solution)/shard_map/ppermute | solution.py:738
  227.8 3.4 %collective-permute-start.55 = (bf16[2,112,768]{2,1,0:T(8,128)(2,1)S(1)}, bf16[2,112,768]{2,1,0:T(8,128)(2,1)S(1)}, u32[]{:S(2)}, u32[]{:S(2)}) collective-permute-start(bf16[2,112,768]{2,1,0:T(8,128)(2,1)S(1)} %collective-permute-done.50.refs_5_), channel_id=1, source_target_pairs={{0,4},{4,0},{8,12},{12,8},{16,20},{20,16},{24,28},{28,24},{1,5},{5... | collective-permute-start | bytes 1032200 | tf_op jit(solution)/shard_map/ppermute | solution.py:738
  231.3 3.7 %collective-permute-start.54 = (bf16[2,112,768]{2,1,0:T(8,128)(2,1)S(1)}, bf16[2,112,768]{2,1,0:T(8,128)(2,1)S(1)}, u32[]{:S(2)}, u32[]{:S(2)}) collective-permute-start(bf16[2,112,768]{2,1,0:T(8,128)(2,1)S(1)} %collective-permute-done.49.refs_4_), channel_id=1, source_target_pairs={{0,4},{4,0},{8,12},{12,8},{16,20},{20,16},{24,28},{28,24},{1,5},{5... | collective-permute-start | bytes 1032200 | tf_op jit(solution)/shard_map/ppermute | solution.py:738
  234.9 1.5 collective-permute-start.57
  236.5 5.1 %collective-permute-start.56 = (bf16[480,768]{1,0:T(8,128)(2,1)}, bf16[480,768]{1,0:T(8,128)(2,1)}, u32[]{:S(2)}, u32[]{:S(2)}) collective-permute-start(bf16[480,768]{1,0:T(8,128)(2,1)} %collective-permute-done.42.refs_4_), channel_id=1, source_target_pairs={{2,3},{6,7},{10,11},{14,15},{18,19},{22,23},{26,27},{30,31}} | collective-permute-start | bytes 2211848 | tf_op jit(solution)/shard_map/ppermute | solution.py:965
  241.6 6.0 %copied_final.1 = (f32[768,2304]{1,0:T(8,128)}, f32[768,768]{1,0:T(8,128)}, f32[192,576]{1,0:T(8,128)}, f32[192,192]{1,0:T(8,128)}, f32[4,768]{1,0:T(4,128)}, /*...) custom-call(s32[26]{0:T(128)S(1)} %concatenate.9.refs_1_.refs_0_.ref, ...), custom_call_target="tpu_custom_call" | custom-call | flops 1200000000 | tf_op jit(solution)/shard_map/copied_final/pallas_call | solution.py:703
  250.0 8.7 %collective-permute-done.60.refs_2_ = bf16[208,768]{1,0:T(8,128)(2,1)S(1)} collective-permute-done((bf16[208,768]{1,0:T(8,128)(2,1)S(1)}, bf16[208,768]{1,0:T(8,128)(2,1)S(1)}, u32[]{:S(2)}, u32[]{:S(2)}) %collective-permute-start.60) | collective-permute-done | bytes 319520 | tf_op jit(solution)/shard_map/ppermute | solution.py:738
  258.8 1.2 collective-permute-start.64
  260.2 1.4 collective-permute-start.66
  261.8 4.8 %input_final.1 = (f32[1536,768]{1,0:T(8,128)}, f32[192,1536]{1,0:T(8,128)}, f32[8,128]{1,0:T(8,128)S(1)}) custom-call(f32[8,128]{1,0:T(8,128)S(1)} %get-tuple-element.249.refs_0_, s32[26]{0:T(128)S(1)} %concatenate.9.refs_1_.refs_0_.refs_2_.refs_3_, bf16[480,768]{1,0:T(8,128)(2,1)S(1)} %get-tuple-element.238.refs_2_, ...), custom_call_target="tpu_custom_call" | custom-call | flops 800000000 | tf_op jit(solution)/shard_map/input_final/pallas_call | solution.py:703
  268.5 3.6 %ffn_final.1 = (f32[768,768]{1,0:T(8,128)}, f32[768,768]{1,0:T(8,128)}, f32[192,192]{1,0:T(8,128)}, f32[192,192]{1,0:T(8,128)}, f32[8,128]{1,0:T(8,128)}) custom-call(s32[26]{0:T(128)S(1)} %concatenate.9.refs_1_.refs_0_.refs_2_.refs_3_, bf16[208,768]{1,0:T(8,128)(2,1)S(1)} %fusion.8.refs_1_, bf16[208,768]{1,0:T(8,128)(2,1)S(1)} %collective-permute-done.60.refs_2_, ...), custom_call_target="tpu_custom_call" | custom-call | flops 600000000 | tf_op jit(solution)/shard_map/ffn_final/pallas_call | solution.py:703
  (180 shorter events, 31.9 us)
Async XLA Ops:
  7.2 241.6 %reduce-scatter.2.cloned.1.call-start = ((), (), s32[]{:S(2)}) async-start(), calls=%async_computation.1 | async-start | bytes 1597440 | tf_op jit(solution)/shard_map/reduce_scatter | solution.py:990
  10.8 11.5 %collective-permute-start.1 = (bf16[208,768]{1,0:T(8,128)(2,1)S(1)}, bf16[208,768]{1,0:T(8,128)(2,1)S(1)}, u32[]{:S(2)}, u32[]{:S(2)}) collective-permute-start(bf16[208,768]{1,0:T(8,128)(2,1)S(1)} %get-tuple-element.157.refs_14_.refs_27_), channel_id=1, source_target_pairs={{0,1},{1,2},{2,3},{3,0},{4,5},{5,6},{6,7},{7,4},{8,9},{9,10},{10,1... | collective-permute-start | bytes 958472 | tf_op jit(solution)/shard_map/ppermute | solution.py:829
  12.1 14.2 %collective-permute-start = (bf16[208,768]{1,0:T(8,128)(2,1)S(1)}, bf16[208,768]{1,0:T(8,128)(2,1)S(1)}, u32[]{:S(2)}, u32[]{:S(2)}) collective-permute-start(bf16[208,768]{1,0:T(8,128)(2,1)S(1)} %get-tuple-element.157.refs_14_.refs_27_), channel_id=1, source_target_pairs={{0,3},{1,0},{2,1},{3,2},{4,7},{5,4},{6,5},{7,6},{8,11},{9,8},{10,9... | collective-permute-start | bytes 958472 | tf_op jit(solution)/shard_map/ppermute | solution.py:829
  26.2 14.4 %collective-permute-start.6 = (bf16[208,768]{1,0:T(8,128)(2,1)S(1)}, bf16[208,768]{1,0:T(8,128)(2,1)S(1)}, u32[]{:S(2)}, u32[]{:S(2)}) collective-permute-start(bf16[208,768]{1,0:T(8,128)(2,1)S(1)} %get-tuple-element.163), channel_id=1, source_target_pairs={{0,2},{1,3},{2,0},{3,1},{4,6},{5,7},{6,4},{7,5},{8,10},{9,11},{10,... | collective-permute-start | bytes 958472 | tf_op jit(solution)/shard_map/ppermute | solution.py:829
  27.8 12.9 %collective-permute-start.3 = (bf16[208,768]{1,0:T(8,128)(2,1)S(1)}, bf16[208,768]{1,0:T(8,128)(2,1)S(1)}, u32[]{:S(2)}, u32[]{:S(2)}) collective-permute-start(bf16[208,768]{1,0:T(8,128)(2,1)S(1)} %get-tuple-element.161.refs_4_), channel_id=1, source_target_pairs={{0,16},{4,20},{8,24},{12,28},{16,0},{20,4},{24,8},{28,12},{1,17},{... | collective-permute-start | bytes 958472 | tf_op jit(solution)/shard_map/ppermute | solution.py:738
  29.1 11.6 %collective-permute-start.2 = (bf16[208,768]{1,0:T(8,128)(2,1)S(1)}, bf16[208,768]{1,0:T(8,128)(2,1)S(1)}, u32[]{:S(2)}, u32[]{:S(2)}) collective-permute-start(bf16[208,768]{1,0:T(8,128)(2,1)S(1)} %get-tuple-element.161.refs_4_), channel_id=1, source_target_pairs={{0,8},{4,12},{8,0},{12,4},{16,24},{20,28},{24,16},{28,20},{1,9},{5... | collective-permute-start | bytes 958472 | tf_op jit(solution)/shard_map/ppermute | solution.py:738
  30.3 12.0 %collective-permute-start.5 = (bf16[208,768]{1,0:T(8,128)(2,1)S(1)}, bf16[208,768]{1,0:T(8,128)(2,1)S(1)}, u32[]{:S(2)}, u32[]{:S(2)}) collective-permute-start(bf16[208,768]{1,0:T(8,128)(2,1)S(1)} %get-tuple-element.162.refs_6_), channel_id=1, source_target_pairs={{0,16},{4,20},{8,24},{12,28},{16,0},{20,4},{24,8},{28,12},{1,17},{... | collective-permute-start | bytes 958472 | tf_op jit(solution)/shard_map/ppermute | solution.py:738
  30.5 12.8 %collective-permute-start.4 = (bf16[208,768]{1,0:T(8,128)(2,1)S(1)}, bf16[208,768]{1,0:T(8,128)(2,1)S(1)}, u32[]{:S(2)}, u32[]{:S(2)}) collective-permute-start(bf16[208,768]{1,0:T(8,128)(2,1)S(1)} %get-tuple-element.162.refs_6_), channel_id=1, source_target_pairs={{0,8},{4,12},{8,0},{12,4},{16,24},{20,28},{24,16},{28,20},{1,9},{5... | collective-permute-start | bytes 958472 | tf_op jit(solution)/shard_map/ppermute | solution.py:738
  43.3 6.4 %collective-permute-start.7 = (bf16[208,768]{1,0:T(8,128)(2,1)S(1)}, bf16[208,768]{1,0:T(8,128)(2,1)S(1)}, u32[]{:S(2)}, u32[]{:S(2)}) collective-permute-start(bf16[208,768]{1,0:T(8,128)(2,1)S(1)} %get-tuple-element.165.refs_4_), channel_id=1, source_target_pairs={{0,16},{4,20},{8,24},{12,28},{16,0},{20,4},{24,8},{28,12},{1,17},{... | collective-permute-start | bytes 958472 | tf_op jit(solution)/shard_map/ppermute | solution.py:738
  43.6 6.2 %collective-permute-start.8 = (bf16[208,768]{1,0:T(8,128)(2,1)S(1)}, bf16[208,768]{1,0:T(8,128)(2,1)S(1)}, u32[]{:S(2)}, u32[]{:S(2)}) collective-permute-start(bf16[208,768]{1,0:T(8,128)(2,1)S(1)} %get-tuple-element.166.refs_7_), channel_id=1, source_target_pairs={{0,8},{4,12},{8,0},{12,4},{16,24},{20,28},{24,16},{28,20},{1,9},{5... | collective-permute-start | bytes 958472 | tf_op jit(solution)/shard_map/ppermute | solution.py:738
  44.8 12.1 %collective-permute-start.18 = (bf16[208,768]{1,0:T(8,128)(2,1)S(1)}, bf16[208,768]{1,0:T(8,128)(2,1)S(1)}, u32[]{:S(2)}, u32[]{:S(2)}) collective-permute-start(bf16[208,768]{1,0:T(8,128)(2,1)S(1)} %get-tuple-element.196.refs_32_), channel_id=1, source_target_pairs={{0,16},{4,20},{8,24},{12,28},{16,0},{20,4},{24,8},{28,12},{1,17},{... | collective-permute-start | bytes 958472 | tf_op jit(solution)/shard_map/ppermute | solution.py:738
  49.1 11.0 %collective-permute-start.17 = (bf16[208,768]{1,0:T(8,128)(2,1)S(1)}, bf16[208,768]{1,0:T(8,128)(2,1)S(1)}, u32[]{:S(2)}, u32[]{:S(2)}) collective-permute-start(bf16[208,768]{1,0:T(8,128)(2,1)S(1)} %get-tuple-element.196.refs_32_), channel_id=1, source_target_pairs={{0,8},{4,12},{8,0},{12,4},{16,24},{20,28},{24,16},{28,20},{1,9},{5... | collective-permute-start | bytes 958472 | tf_op jit(solution)/shard_map/ppermute | solution.py:738
  49.8 10.6 %collective-permute-start.10 = (bf16[208,768]{1,0:T(8,128)(2,1)S(1)}, bf16[208,768]{1,0:T(8,128)(2,1)S(1)}, u32[]{:S(2)}, u32[]{:S(2)}) collective-permute-start(bf16[208,768]{1,0:T(8,128)(2,1)S(1)} %get-tuple-element.173.refs_4_), channel_id=1, source_target_pairs={{0,4},{4,0},{8,12},{12,8},{16,20},{20,16},{24,28},{28,24},{1,5},{5... | collective-permute-start | bytes 958472 | tf_op jit(solution)/shard_map/ppermute | solution.py:738
  56.4 4.2 %collective-permute-start.11 = (bf16[208,768]{1,0:T(8,128)(2,1)S(1)}, bf16[208,768]{1,0:T(8,128)(2,1)S(1)}, u32[]{:S(2)}, u32[]{:S(2)}) collective-permute-start(bf16[208,768]{1,0:T(8,128)(2,1)S(1)} %get-tuple-element.174.refs_5_), channel_id=1, source_target_pairs={{0,4},{4,0},{8,12},{12,8},{16,20},{20,16},{24,28},{28,24},{1,5},{5... | collective-permute-start | bytes 958472 | tf_op jit(solution)/shard_map/ppermute | solution.py:738
  56.4 4.5 %collective-permute-start.12 = (bf16[208,768]{1,0:T(8,128)(2,1)S(1)}, bf16[208,768]{1,0:T(8,128)(2,1)S(1)}, u32[]{:S(2)}, u32[]{:S(2)}) collective-permute-start(bf16[208,768]{1,0:T(8,128)(2,1)S(1)} %get-tuple-element.175.refs_6_), channel_id=1, source_target_pairs={{0,4},{4,0},{8,12},{12,8},{16,20},{20,16},{24,28},{28,24},{1,5},{5... | collective-permute-start | bytes 958472 | tf_op jit(solution)/shard_map/ppermute | solution.py:738
  56.9 4.5 %collective-permute-start.14 = (bf16[208,768]{1,0:T(8,128)(2,1)S(1)}, bf16[208,768]{1,0:T(8,128)(2,1)S(1)}, u32[]{:S(2)}, u32[]{:S(2)}) collective-permute-start(bf16[208,768]{1,0:T(8,128)(2,1)S(1)} %get-tuple-element.178.refs_4_), channel_id=1, source_target_pairs={{0,4},{4,0},{8,12},{12,8},{16,20},{20,16},{24,28},{28,24},{1,5},{5... | collective-permute-start | bytes 958472 | tf_op jit(solution)/shard_map/ppermute | solution.py:738
  60.6 3.7 %collective-permute-start.9 = (bf16[208,768]{1,0:T(8,128)(2,1)S(1)}, bf16[208,768]{1,0:T(8,128)(2,1)S(1)}, u32[]{:S(2)}, u32[]{:S(2)}) collective-permute-start(bf16[208,768]{1,0:T(8,128)(2,1)S(1)} %get-tuple-element.172.refs_3_.refs_28_), channel_id=1, source_target_pairs={{0,4},{4,0},{8,12},{12,8},{16,20},{20,16},{24,28},{28,24},{1,5},{5... | collective-permute-start | bytes 958472 | tf_op jit(solution)/shard_map/ppermute | solution.py:738
  60.9 3.7 %collective-permute-start.13 = (bf16[208,768]{1,0:T(8,128)(2,1)S(1)}, bf16[208,768]{1,0:T(8,128)(2,1)S(1)}, u32[]{:S(2)}, u32[]{:S(2)}) collective-permute-start(bf16[208,768]{1,0:T(8,128)(2,1)S(1)} %get-tuple-element.177.refs_3_.refs_29_), channel_id=1, source_target_pairs={{0,4},{4,0},{8,12},{12,8},{16,20},{20,16},{24,28},{28,24},{1,5},{5... | collective-permute-start | bytes 958472 | tf_op jit(solution)/shard_map/ppermute | solution.py:738
  61.3 8.5 %collective-permute-start.20 = (bf16[112,768]{1,0:T(8,128)(2,1)S(1)}, bf16[112,768]{1,0:T(8,128)(2,1)S(1)}, u32[]{:S(2)}, u32[]{:S(2)}) collective-permute-start(bf16[112,768]{1,0:T(8,128)(2,1)S(1)} %slice.113), channel_id=1, source_target_pairs={{0,8},{4,12},{8,0},{12,4},{16,24},{20,28},{24,16},{28,20},{1,9},{5... | collective-permute-start | bytes 516104 | tf_op jit(solution)/shard_map/ppermute | solution.py:738
  62.5 7.9 %collective-permute-start.21 = (bf16[208,768]{1,0:T(8,128)(2,1)S(1)}, bf16[208,768]{1,0:T(8,128)(2,1)S(1)}, u32[]{:S(2)}, u32[]{:S(2)}) collective-permute-start(bf16[208,768]{1,0:T(8,128)(2,1)S(1)} %get-tuple-element.196.refs_32_), channel_id=1, source_target_pairs={{0,4},{4,0},{8,12},{12,8},{16,20},{20,16},{24,28},{28,24},{1,5},{5... | collective-permute-start | bytes 958472 | tf_op jit(solution)/shard_map/ppermute | solution.py:738
  63.3 6.5 %collective-permute-start.19 = (bf16[96,768]{1,0:T(8,128)(2,1)S(1)}, bf16[96,768]{1,0:T(8,128)(2,1)S(1)}, u32[]{:S(2)}, u32[]{:S(2)}) collective-permute-start(bf16[96,768]{1,0:T(8,128)(2,1)S(1)} %slice.112), channel_id=1, source_target_pairs={{0,16},{4,20},{8,24},{12,28},{16,0},{20,4},{24,8},{28,12},{1,17},{... | collective-permute-start | bytes 442376 | tf_op jit(solution)/shard_map/ppermute | solution.py:738
  64.3 6.1 %collective-permute-start.23 = (bf16[208,768]{1,0:T(8,128)(2,1)S(1)}, bf16[208,768]{1,0:T(8,128)(2,1)S(1)}, u32[]{:S(2)}, u32[]{:S(2)}) collective-permute-start(bf16[208,768]{1,0:T(8,128)(2,1)S(1)} %collective-permute-done.18.refs_34_), channel_id=1, source_target_pairs={{0,4},{4,0},{8,12},{12,8},{16,20},{20,16},{24,28},{28,24},{1,5},{5... | collective-permute-start | bytes 958472 | tf_op jit(solution)/shard_map/ppermute | solution.py:738
  64.6 5.8 %collective-permute-start.22 = (bf16[208,768]{1,0:T(8,128)(2,1)S(1)}, bf16[208,768]{1,0:T(8,128)(2,1)S(1)}, u32[]{:S(2)}, u32[]{:S(2)}) collective-permute-start(bf16[208,768]{1,0:T(8,128)(2,1)S(1)} %collective-permute-done.17.refs_33_), channel_id=1, source_target_pairs={{0,4},{4,0},{8,12},{12,8},{16,20},{20,16},{24,28},{28,24},{1,5},{5... | collective-permute-start | bytes 958472 | tf_op jit(solution)/shard_map/ppermute | solution.py:738
  86.1 14.6 %collective-permute-start.26 = (bf16[4,448,768]{2,1,0:T(8,128)(2,1)S(1)}, bf16[4,448,768]{2,1,0:T(8,128)(2,1)S(1)}, u32[]{:S(2)}, u32[]{:S(2)}) collective-permute-start(bf16[4,448,768]{2,1,0:T(8,128)(2,1)S(1)} %get-tuple-element.211), channel_id=1, source_target_pairs={{0,4},{4,0},{8,12},{12,8},{16,20},{20,16},{24,28},{28,24},{1,5},{5... | collective-permute-start | bytes 8257544 | tf_op jit(solution)/shard_map/ppermute | solution.py:738
  86.4 14.3 %collective-permute-start.27 = (bf16[4,384,768]{2,1,0:T(8,128)(2,1)S(1)}, bf16[4,384,768]{2,1,0:T(8,128)(2,1)S(1)}, u32[]{:S(2)}, u32[]{:S(2)}) collective-permute-start(bf16[4,384,768]{2,1,0:T(8,128)(2,1)S(1)} %get-tuple-element.212), channel_id=1, source_target_pairs={{0,4},{4,0},{8,12},{12,8},{16,20},{20,16},{24,28},{28,24},{1,5},{5... | collective-permute-start | bytes 7077896 | tf_op jit(solution)/shard_map/ppermute | solution.py:738
  107.6 9.5 %collective-permute-start.28 = (bf16[4,448,768]{2,1,0:T(8,128)(2,1)S(1)}, bf16[4,448,768]{2,1,0:T(8,128)(2,1)S(1)}, u32[]{:S(2)}, u32[]{:S(2)}) collective-permute-start(bf16[4,448,768]{2,1,0:T(8,128)(2,1)S(1)} %get-tuple-element.232), channel_id=1, source_target_pairs={{0,4},{4,0},{8,12},{12,8},{16,20},{20,16},{24,28},{28,24},{1,5},{5... | collective-permute-start | bytes 8257544 | tf_op jit(solution)/shard_map/ppermute | solution.py:738
  107.9 33.5 %collective-permute-start.37 = (bf16[2,4,96,768]{3,2,1,0:T(8,128)(2,1)S(1)}, bf16[2,4,96,768]{3,2,1,0:T(8,128)(2,1)S(1)}, u32[]{:S(2)}, u32[]{:S(2)}) collective-permute-start(bf16[2,4,96,768]{3,2,1,0:T(8,128)(2,1)S(1)} %get-tuple-element.244), channel_id=1, source_target_pairs={{0,16},{4,20},{8,24},{12,28},{16,0},{20,4},{24,8},{28,12},{1,17},{... | collective-permute-start | bytes 3538952 | tf_op jit(solution)/shard_map/ppermute | solution.py:738
  111.3 19.5 %collective-permute-start.29 = (bf16[480,768]{1,0:T(8,128)(2,1)S(1)}, bf16[480,768]{1,0:T(8,128)(2,1)S(1)}, u32[]{:S(2)}, u32[]{:S(2)}) collective-permute-start(bf16[480,768]{1,0:T(8,128)(2,1)S(1)} %get-tuple-element.236), channel_id=1, source_target_pairs={{1,0},{2,1},{3,2},{5,4},{6,5},{7,6},{9,8},{10,9},{11,10},{13,12},{... | collective-permute-start | bytes 2211848 | tf_op jit(solution)/shard_map/ppermute | solution.py:950
  113.4 19.1 %collective-permute-start.30 = (bf16[480,768]{1,0:T(8,128)(2,1)S(1)}, bf16[480,768]{1,0:T(8,128)(2,1)S(1)}, u32[]{:S(2)}, u32[]{:S(2)}) collective-permute-start(bf16[480,768]{1,0:T(8,128)(2,1)S(1)} %get-tuple-element.237), channel_id=1, source_target_pairs={{0,1},{1,2},{2,3},{4,5},{5,6},{6,7},{8,9},{9,10},{10,11},{12,13},{... | collective-permute-start | bytes 2211848 | tf_op jit(solution)/shard_map/ppermute | solution.py:951
  116.6 30.7 %collective-permute-start.34 = (bf16[2,4,112,768]{3,2,1,0:T(8,128)(2,1)S(1)}, bf16[2,4,112,768]{3,2,1,0:T(8,128)(2,1)S(1)}, u32[]{:S(2)}, u32[]{:S(2)}) collective-permute-start(bf16[2,4,112,768]{3,2,1,0:T(8,128)(2,1)S(1)} %get-tuple-element.241), channel_id=1, source_target_pairs={{0,8},{4,12},{8,0},{12,4},{16,24},{20,28},{24,16},{28,20},{1,9},{5... | collective-permute-start | bytes 4128776 | tf_op jit(solution)/shard_map/ppermute | solution.py:738
  135.5 18.2 %collective-permute-start.32 = (bf16[480,768]{1,0:T(8,128)(2,1)S(1)}, bf16[480,768]{1,0:T(8,128)(2,1)S(1)}, u32[]{:S(2)}, u32[]{:S(2)}) collective-permute-start(bf16[480,768]{1,0:T(8,128)(2,1)S(1)} %get-tuple-element.238.refs_2_), channel_id=1, source_target_pairs={{3,2},{2,1},{1,0},{7,6},{6,5},{5,4},{11,10},{10,9},{9,8},{15,14},{... | collective-permute-start | bytes 2211848 | tf_op jit(solution)/shard_map/ppermute | solution.py:966
  138.8 19.0 %collective-permute-start.31 = (bf16[480,768]{1,0:T(8,128)(2,1)S(1)}, bf16[480,768]{1,0:T(8,128)(2,1)S(1)}, u32[]{:S(2)}, u32[]{:S(2)}) collective-permute-start(bf16[480,768]{1,0:T(8,128)(2,1)S(1)} %get-tuple-element.238.refs_2_), channel_id=1, source_target_pairs={{0,1},{1,2},{2,3},{4,5},{5,6},{6,7},{8,9},{9,10},{10,11},{12,13},{... | collective-permute-start | bytes 2211848 | tf_op jit(solution)/shard_map/ppermute | solution.py:965
  140.9 21.2 %collective-permute-start.33 = (bf16[2,2,112,768]{3,2,1,0:T(8,128)(2,1)S(1)}, bf16[2,2,112,768]{3,2,1,0:T(8,128)(2,1)S(1)}, u32[]{:S(2)}, u32[]{:S(2)}) collective-permute-start(bf16[2,2,112,768]{3,2,1,0:T(8,128)(2,1)S(1)} %get-tuple-element.240), channel_id=1, source_target_pairs={{0,8},{4,12},{8,0},{12,4},{16,24},{20,28},{24,16},{28,20},{1,9},{5... | collective-permute-start | bytes 2064392 | tf_op jit(solution)/shard_map/ppermute | solution.py:738
  141.5 21.8 %collective-permute-start.36 = (bf16[2,2,112,768]{3,2,1,0:T(8,128)(2,1)S(1)}, bf16[2,2,112,768]{3,2,1,0:T(8,128)(2,1)S(1)}, u32[]{:S(2)}, u32[]{:S(2)}) collective-permute-start(bf16[2,2,112,768]{3,2,1,0:T(8,128)(2,1)S(1)} %get-tuple-element.243), channel_id=1, source_target_pairs={{0,16},{4,20},{8,24},{12,28},{16,0},{20,4},{24,8},{28,12},{1,17},{... | collective-permute-start | bytes 2064392 | tf_op jit(solution)/shard_map/ppermute | solution.py:738
  153.7 21.8 %collective-permute-start.43 = (bf16[480,768]{1,0:T(8,128)(2,1)S(1)}, bf16[480,768]{1,0:T(8,128)(2,1)}, u32[]{:S(2)}, u32[]{:S(2)}) collective-permute-start(bf16[480,768]{1,0:T(8,128)(2,1)S(1)} %collective-permute-done.32.refs_1_.refs_6_), channel_id=1, source_target_pairs={{2,1},{1,0},{6,5},{5,4},{10,9},{9,8},{14,13},{13,12},{18,17},{17,1... | collective-permute-start | bytes 2211848 | tf_op jit(solution)/shard_map/ppermute | solution.py:966
  157.9 19.5 %collective-permute-start.42 = (bf16[480,768]{1,0:T(8,128)(2,1)S(1)}, bf16[480,768]{1,0:T(8,128)(2,1)}, u32[]{:S(2)}, u32[]{:S(2)}) collective-permute-start(bf16[480,768]{1,0:T(8,128)(2,1)S(1)} %collective-permute-done.31.refs_0_.refs_3_), channel_id=1, source_target_pairs={{1,2},{2,3},{5,6},{6,7},{9,10},{10,11},{13,14},{14,15},{17,18},{18... | collective-permute-start | bytes 2211848 | tf_op jit(solution)/shard_map/ppermute | solution.py:965
  162.2 7.7 %collective-permute-start.35 = (bf16[2,112,768]{2,1,0:T(8,128)(2,1)S(1)}, bf16[2,112,768]{2,1,0:T(8,128)(2,1)S(1)}, u32[]{:S(2)}, u32[]{:S(2)}) collective-permute-start(bf16[2,112,768]{2,1,0:T(8,128)(2,1)S(1)} %get-tuple-element.282), channel_id=1, source_target_pairs={{0,16},{4,20},{8,24},{12,28},{16,0},{20,4},{24,8},{28,12},{1,17},{... | collective-permute-start | bytes 1032200 | tf_op jit(solution)/shard_map/ppermute | solution.py:738
  163.5 7.5 %collective-permute-start.38 = (bf16[2,112,768]{2,1,0:T(8,128)(2,1)S(1)}, bf16[2,112,768]{2,1,0:T(8,128)(2,1)S(1)}, u32[]{:S(2)}, u32[]{:S(2)}) collective-permute-start(bf16[2,112,768]{2,1,0:T(8,128)(2,1)S(1)} %get-tuple-element.280), channel_id=1, source_target_pairs={{0,8},{4,12},{8,0},{12,4},{16,24},{20,28},{24,16},{28,20},{1,9},{5... | collective-permute-start | bytes 1032200 | tf_op jit(solution)/shard_map/ppermute | solution.py:738
  172.1 13.9 %collective-permute-start.39 = (bf16[112,768]{1,0:T(8,128)(2,1)S(1)}, bf16[112,768]{1,0:T(8,128)(2,1)S(1)}, u32[]{:S(2)}, u32[]{:S(2)}) collective-permute-start(bf16[112,768]{1,0:T(8,128)(2,1)S(1)} %get-tuple-element.246), channel_id=1, source_target_pairs={{0,1},{1,2},{2,3},{3,0},{4,5},{5,6},{6,7},{7,4},{8,9},{9,10},{10,1... | collective-permute-start | bytes 516104 | tf_op jit(solution)/shard_map/ppermute | solution.py:971
  172.1 13.9 %collective-permute-start.40 = (bf16[112,768]{1,0:T(8,128)(2,1)S(1)}, bf16[112,768]{1,0:T(8,128)(2,1)S(1)}, u32[]{:S(2)}, u32[]{:S(2)}) collective-permute-start(bf16[112,768]{1,0:T(8,128)(2,1)S(1)} %get-tuple-element.247), channel_id=1, source_target_pairs={{0,2},{1,3},{2,0},{3,1},{4,6},{5,7},{6,4},{7,5},{8,10},{9,11},{10,... | collective-permute-start | bytes 516104 | tf_op jit(solution)/shard_map/ppermute | solution.py:971
  173.2 14.3 %collective-permute-start.41 = (bf16[112,768]{1,0:T(8,128)(2,1)S(1)}, bf16[112,768]{1,0:T(8,128)(2,1)S(1)}, u32[]{:S(2)}, u32[]{:S(2)}) collective-permute-start(bf16[112,768]{1,0:T(8,128)(2,1)S(1)} %get-tuple-element.248), channel_id=1, source_target_pairs={{0,3},{1,0},{2,1},{3,2},{4,7},{5,4},{6,5},{7,6},{8,11},{9,8},{10,9... | collective-permute-start | bytes 516104 | tf_op jit(solution)/shard_map/ppermute | solution.py:971
  179.7 18.8 %collective-permute-start.58 = (bf16[4,112,768]{2,1,0:T(8,128)(2,1)S(1)}, bf16[4,112,768]{2,1,0:T(8,128)(2,1)S(1)}, u32[]{:S(2)}, u32[]{:S(2)}) collective-permute-start(bf16[4,112,768]{2,1,0:T(8,128)(2,1)S(1)} %get-tuple-element.276), channel_id=1, source_target_pairs={{0,16},{4,20},{8,24},{12,28},{16,0},{20,4},{24,8},{28,12},{1,17},{... | collective-permute-start | bytes 2064392 | tf_op jit(solution)/shard_map/ppermute | solution.py:738
  181.2 17.3 %collective-permute-start.59 = (bf16[4,96,768]{2,1,0:T(8,128)(2,1)S(1)}, bf16[4,96,768]{2,1,0:T(8,128)(2,1)S(1)}, u32[]{:S(2)}, u32[]{:S(2)}) collective-permute-start(bf16[4,96,768]{2,1,0:T(8,128)(2,1)S(1)} %get-tuple-element.278), channel_id=1, source_target_pairs={{0,8},{4,12},{8,0},{12,4},{16,24},{20,28},{24,16},{28,20},{1,9},{5... | collective-permute-start | bytes 1769480 | tf_op jit(solution)/shard_map/ppermute | solution.py:738
  187.6 10.9 %collective-permute-start.46 = (bf16[112,768]{1,0:T(8,128)(2,1)S(1)}, bf16[112,768]{1,0:T(8,128)(2,1)S(1)}, u32[]{:S(2)}, u32[]{:S(2)}) collective-permute-start(bf16[112,768]{1,0:T(8,128)(2,1)S(1)} %add_convert_fusion.9), channel_id=1, source_target_pairs={{0,1},{1,2},{2,3},{3,0},{4,5},{5,6},{6,7},{7,4},{8,9},{9,10},{10,1... | collective-permute-start | bytes 516104 | tf_op jit(solution)/shard_map/ppermute | solution.py:829
  190.7 7.9 %collective-permute-start.45 = (bf16[112,768]{1,0:T(8,128)(2,1)S(1)}, bf16[112,768]{1,0:T(8,128)(2,1)S(1)}, u32[]{:S(2)}, u32[]{:S(2)}) collective-permute-start(bf16[112,768]{1,0:T(8,128)(2,1)S(1)} %add_convert_fusion.9), channel_id=1, source_target_pairs={{0,2},{1,3},{2,0},{3,1},{4,6},{5,7},{6,4},{7,5},{8,10},{9,11},{10,... | collective-permute-start | bytes 516104 | tf_op jit(solution)/shard_map/ppermute | solution.py:829
  191.0 7.5 %collective-permute-start.44 = (bf16[112,768]{1,0:T(8,128)(2,1)S(1)}, bf16[112,768]{1,0:T(8,128)(2,1)S(1)}, u32[]{:S(2)}, u32[]{:S(2)}) collective-permute-start(bf16[112,768]{1,0:T(8,128)(2,1)S(1)} %add_convert_fusion.9), channel_id=1, source_target_pairs={{0,3},{1,0},{2,1},{3,2},{4,7},{5,4},{6,5},{7,6},{8,11},{9,8},{10,9... | collective-permute-start | bytes 516104 | tf_op jit(solution)/shard_map/ppermute | solution.py:829
  200.6 15.9 %collective-permute-start.48 = (bf16[4,112,768]{2,1,0:T(8,128)(2,1)S(1)}, bf16[4,112,768]{2,1,0:T(8,128)(2,1)S(1)}, u32[]{:S(2)}, u32[]{:S(2)}) collective-permute-start(bf16[4,112,768]{2,1,0:T(8,128)(2,1)S(1)} %pad_maximum_fusion.refs_1_), channel_id=1, source_target_pairs={{0,16},{4,20},{8,24},{12,28},{16,0},{20,4},{24,8},{28,12},{1,17},{... | collective-permute-start | bytes 2064392 | tf_op jit(solution)/shard_map/ppermute | solution.py:738
  206.0 12.4 %collective-permute-start.47 = (bf16[4,112,768]{2,1,0:T(8,128)(2,1)S(1)}, bf16[4,112,768]{2,1,0:T(8,128)(2,1)S(1)}, u32[]{:S(2)}, u32[]{:S(2)}) collective-permute-start(bf16[4,112,768]{2,1,0:T(8,128)(2,1)S(1)} %pad_maximum_fusion.refs_1_), channel_id=1, source_target_pairs={{0,8},{4,12},{8,0},{12,4},{16,24},{20,28},{24,16},{28,20},{1,9},{5... | collective-permute-start | bytes 2064392 | tf_op jit(solution)/shard_map/ppermute | solution.py:738
  206.5 28.5 %collective-permute-start.51 = (bf16[4,112,768]{2,1,0:T(8,128)(2,1)S(1)}, bf16[4,112,768]{2,1,0:T(8,128)(2,1)S(1)}, u32[]{:S(2)}, u32[]{:S(2)}) collective-permute-start(bf16[4,112,768]{2,1,0:T(8,128)(2,1)S(1)} %pad_maximum_fusion.refs_1_), channel_id=1, source_target_pairs={{0,4},{4,0},{8,12},{12,8},{16,20},{20,16},{24,28},{28,24},{1,5},{5... | collective-permute-start | bytes 2064392 | tf_op jit(solution)/shard_map/ppermute | solution.py:738
  216.5 11.3 %collective-permute-start.50 = (bf16[2,112,768]{2,1,0:T(8,128)(2,1)S(1)}, bf16[2,112,768]{2,1,0:T(8,128)(2,1)S(1)}, u32[]{:S(2)}, u32[]{:S(2)}) collective-permute-start(bf16[2,112,768]{2,1,0:T(8,128)(2,1)S(1)} %slice.123), channel_id=1, source_target_pairs={{0,8},{4,12},{8,0},{12,4},{16,24},{20,28},{24,16},{28,20},{1,9},{5... | collective-permute-start | bytes 1032200 | tf_op jit(solution)/shard_map/ppermute | solution.py:738
  218.5 12.8 %collective-permute-start.49 = (bf16[2,112,768]{2,1,0:T(8,128)(2,1)S(1)}, bf16[2,112,768]{2,1,0:T(8,128)(2,1)S(1)}, u32[]{:S(2)}, u32[]{:S(2)}) collective-permute-start(bf16[2,112,768]{2,1,0:T(8,128)(2,1)S(1)} %slice.122), channel_id=1, source_target_pairs={{0,16},{4,20},{8,24},{12,28},{16,0},{20,4},{24,8},{28,12},{1,17},{... | collective-permute-start | bytes 1032200 | tf_op jit(solution)/shard_map/ppermute | solution.py:738
  219.8 21.8 %collective-permute-start.53 = (bf16[4,112,768]{2,1,0:T(8,128)(2,1)S(1)}, bf16[4,112,768]{2,1,0:T(8,128)(2,1)S(1)}, u32[]{:S(2)}, u32[]{:S(2)}) collective-permute-start(bf16[4,112,768]{2,1,0:T(8,128)(2,1)S(1)} %collective-permute-done.48.refs_3_), channel_id=1, source_target_pairs={{0,4},{4,0},{8,12},{12,8},{16,20},{20,16},{24,28},{28,24},{1,5},{5... | collective-permute-start | bytes 2064392 | tf_op jit(solution)/shard_map/ppermute | solution.py:738
  227.8 13.9 %collective-permute-start.52 = (bf16[4,112,768]{2,1,0:T(8,128)(2,1)S(1)}, bf16[4,112,768]{2,1,0:T(8,128)(2,1)S(1)}, u32[]{:S(2)}, u32[]{:S(2)}) collective-permute-start(bf16[4,112,768]{2,1,0:T(8,128)(2,1)S(1)} %collective-permute-done.47.refs_2_), channel_id=1, source_target_pairs={{0,4},{4,0},{8,12},{12,8},{16,20},{20,16},{24,28},{28,24},{1,5},{5... | collective-permute-start | bytes 2064392 | tf_op jit(solution)/shard_map/ppermute | solution.py:738
  227.8 8.6 %collective-permute-start.55 = (bf16[2,112,768]{2,1,0:T(8,128)(2,1)S(1)}, bf16[2,112,768]{2,1,0:T(8,128)(2,1)S(1)}, u32[]{:S(2)}, u32[]{:S(2)}) collective-permute-start(bf16[2,112,768]{2,1,0:T(8,128)(2,1)S(1)} %collective-permute-done.50.refs_5_), channel_id=1, source_target_pairs={{0,4},{4,0},{8,12},{12,8},{16,20},{20,16},{24,28},{28,24},{1,5},{5... | collective-permute-start | bytes 1032200 | tf_op jit(solution)/shard_map/ppermute | solution.py:738
  231.3 10.3 %collective-permute-start.54 = (bf16[2,112,768]{2,1,0:T(8,128)(2,1)S(1)}, bf16[2,112,768]{2,1,0:T(8,128)(2,1)S(1)}, u32[]{:S(2)}, u32[]{:S(2)}) collective-permute-start(bf16[2,112,768]{2,1,0:T(8,128)(2,1)S(1)} %collective-permute-done.49.refs_4_), channel_id=1, source_target_pairs={{0,4},{4,0},{8,12},{12,8},{16,20},{20,16},{24,28},{28,24},{1,5},{5... | collective-permute-start | bytes 1032200 | tf_op jit(solution)/shard_map/ppermute | solution.py:738
  234.9 25.3 %collective-permute-start.57 = (bf16[480,768]{1,0:T(8,128)(2,1)}, bf16[480,768]{1,0:T(8,128)(2,1)}, u32[]{:S(2)}, u32[]{:S(2)}) collective-permute-start(bf16[480,768]{1,0:T(8,128)(2,1)} %collective-permute-done.43.refs_7_), channel_id=1, source_target_pairs={{1,0},{5,4},{9,8},{13,12},{17,16},{21,20},{25,24},{29,28}} | collective-permute-start | bytes 2211848 | tf_op jit(solution)/shard_map/ppermute | solution.py:966
  236.5 25.2 %collective-permute-start.56 = (bf16[480,768]{1,0:T(8,128)(2,1)}, bf16[480,768]{1,0:T(8,128)(2,1)}, u32[]{:S(2)}, u32[]{:S(2)}) collective-permute-start(bf16[480,768]{1,0:T(8,128)(2,1)} %collective-permute-done.42.refs_4_), channel_id=1, source_target_pairs={{2,3},{6,7},{10,11},{14,15},{18,19},{22,23},{26,27},{30,31}} | collective-permute-start | bytes 2211848 | tf_op jit(solution)/shard_map/ppermute | solution.py:965
  249.8 8.9 %collective-permute-start.60 = (bf16[208,768]{1,0:T(8,128)(2,1)S(1)}, bf16[208,768]{1,0:T(8,128)(2,1)S(1)}, u32[]{:S(2)}, u32[]{:S(2)}) collective-permute-start(bf16[208,768]{1,0:T(8,128)(2,1)S(1)} %fusion.8.refs_1_), channel_id=1, source_target_pairs={{0,8},{4,12},{8,0},{12,4},{16,24},{20,28},{24,16},{28,20},{1,9},{5... | collective-permute-start | bytes 958472 | tf_op jit(solution)/shard_map/ppermute | solution.py:738
  250.0 10.0 %collective-permute-start.61 = (bf16[208,768]{1,0:T(8,128)(2,1)S(1)}, bf16[208,768]{1,0:T(8,128)(2,1)S(1)}, u32[]{:S(2)}, u32[]{:S(2)}) collective-permute-start(bf16[208,768]{1,0:T(8,128)(2,1)S(1)} %fusion.8.refs_1_), channel_id=1, source_target_pairs={{0,16},{4,20},{8,24},{12,28},{16,0},{20,4},{24,8},{28,12},{1,17},{... | collective-permute-start | bytes 958472 | tf_op jit(solution)/shard_map/ppermute | solution.py:738
  258.8 7.8 %collective-permute-start.62 = (bf16[112,768]{1,0:T(8,128)(2,1)S(1)}, bf16[112,768]{1,0:T(8,128)(2,1)S(1)}, u32[]{:S(2)}, u32[]{:S(2)}) collective-permute-start(bf16[112,768]{1,0:T(8,128)(2,1)S(1)} %slice.128), channel_id=1, source_target_pairs={{0,16},{4,20},{8,24},{12,28},{16,0},{20,4},{24,8},{28,12},{1,17},{... | collective-permute-start | bytes 516104 | tf_op jit(solution)/shard_map/ppermute | solution.py:738
  258.8 8.9 %collective-permute-start.64 = (bf16[208,768]{1,0:T(8,128)(2,1)S(1)}, bf16[208,768]{1,0:T(8,128)(2,1)}, u32[]{:S(2)}, u32[]{:S(2)}) collective-permute-start(bf16[208,768]{1,0:T(8,128)(2,1)S(1)} %fusion.8.refs_1_), channel_id=1, source_target_pairs={{0,4},{4,0},{8,12},{12,8},{16,20},{20,16},{24,28},{28,24},{1,5},{5... | collective-permute-start | bytes 958472 | tf_op jit(solution)/shard_map/ppermute | solution.py:738
  260.0 6.5 %collective-permute-start.63 = (bf16[96,768]{1,0:T(8,128)(2,1)S(1)}, bf16[96,768]{1,0:T(8,128)(2,1)S(1)}, u32[]{:S(2)}, u32[]{:S(2)}) collective-permute-start(bf16[96,768]{1,0:T(8,128)(2,1)S(1)} %slice.129), channel_id=1, source_target_pairs={{0,8},{4,12},{8,0},{12,4},{16,24},{20,28},{24,16},{28,20},{1,9},{5... | collective-permute-start | bytes 442376 | tf_op jit(solution)/shard_map/ppermute | solution.py:738
  260.2 7.5 %collective-permute-start.66 = (bf16[208,768]{1,0:T(8,128)(2,1)S(1)}, bf16[208,768]{1,0:T(8,128)(2,1)}, u32[]{:S(2)}, u32[]{:S(2)}) collective-permute-start(bf16[208,768]{1,0:T(8,128)(2,1)S(1)} %collective-permute-done.61.refs_3_), channel_id=1, source_target_pairs={{0,4},{4,0},{8,12},{12,8},{16,20},{20,16},{24,28},{28,24},{1,5},{5... | collective-permute-start | bytes 958472 | tf_op jit(solution)/shard_map/ppermute | solution.py:738
  261.7 6.1 %collective-permute-start.65 = (bf16[208,768]{1,0:T(8,128)(2,1)S(1)}, bf16[208,768]{1,0:T(8,128)(2,1)}, u32[]{:S(2)}, u32[]{:S(2)}) collective-permute-start(bf16[208,768]{1,0:T(8,128)(2,1)S(1)} %collective-permute-done.60.refs_2_), channel_id=1, source_target_pairs={{0,4},{4,0},{8,12},{12,8},{16,20},{20,16},{24,28},{28,24},{1,5},{5... | collective-permute-start | bytes 958472 | tf_op jit(solution)/shard_map/ppermute | solution.py:738
  (30 other events, 151.2 us)
Sparse Core Ops, SparseCore 0:
  200.6 38.6 reduce-scatter.1
